TPU v7x, 32 devices: a whole 2x2x4 slice. The times are simulated.
32 devices in a mesh: dp: 8 (over z, y), code: 4 (over x, core).
Axes of the slice: x: 2, y: 2, z: 4, core: 2. Of those that a mesh axis runs over, the one named last changes fastest.
Arguments:
- codebook: bfloat16 [25088, 768], P(('dp', 'code')), may hold values from -6 to 6
- projector: bfloat16 [768, 256], replicated, may hold values from -0.21875 to 0.21875
- latents: bfloat16 [64, 16, 16, 256], P(('dp', 'code')), may hold values from -6 to 6
- wanted: int32 [32, 32, 8], P(('dp', 'code')), may hold values from 0 to 783
- wanted_count: int32 [32, 32], P(('dp', 'code')), may hold values from 1 to 8, as said below
- token_pick: int32 [64, 16, 16], P(('dp', 'code')), may hold values from 0 to 255
- kernel: bfloat16 [3, 3, 256, 512], replicated, may hold values from -0.125 to 0.125
- bias: bfloat16 [512], replicated, may hold values from -3 to 3
- cotangent: bfloat16 [64, 16, 16, 512], P(('dp', 'code')), may hold values from -6 to 6
Outputs:
- hidden: bfloat16 [64, 16, 16, 512], P(('dp', 'code'))
- grad_latents: bfloat16 [64, 16, 16, 256], P(('dp', 'code'))
- proj_step: float32 [768, 256], replicated
- kernel_step: float32 [3, 3, 256, 512], replicated
- bias_step: float32 [512], replicated
Inputs may be any that keep to these rules, and one draw needn't show every extreme that they name: `wanted_count`: for one owner chosen in each draw every requester's list is full; the others hold 1 to 8 live entries. `wanted`: offsets into the owner's 784 entries; entries past the live count are unused.
All inputs are finite; a program needn't handle non-finite values.
Results may differ from a plain program's by a relative error of at most 0.0046.
Values may be sent and summed in bfloat16 or wider, within the bound.
No kernel may reach another device: no remote copies, remote signals or barrier semaphores. Data moves between devices by JAX's collectives and lax.ppermute only.
A program may use at most 64 MiB of HBM per device.

v0:
```python
import jax
import jax.numpy as jnp
from jax import lax
from jax.sharding import PartitionSpec as P

commit_weight = 0.25
norm_eps = 1e-06


def unit_scale(values, count):
    return values / jnp.sqrt(jnp.sum(values * values) / count + norm_eps)


def split_product(left, right):
    upper = right.astype(jnp.bfloat16)
    lower = (right - upper.astype(jnp.float32)).astype(jnp.bfloat16)
    dims = (((0,), (0,)), ((), ()))
    first = lax.dot_general(left, upper, dims, preferred_element_type=jnp.float32)
    return first + lax.dot_general(left, lower, dims, preferred_element_type=jnp.float32)


def on_device(
    codebook, projector, latents, wanted, wanted_count, token_pick, kernel, bias, cotangent
):
    devices = lax.axis_size(("dp", "code"))
    images, rows, width, zch = latents.shape
    channels = kernel.shape[3]
    feat = codebook.shape[1]
    rows_dev = codebook.shape[0]
    cap = wanted.shape[2]
    slots = devices * cap
    tokens = images * rows * width
    block = min(512, tokens)
    requests = wanted.reshape(devices, cap)
    counts = wanted_count.reshape(devices)
    pick = token_pick.reshape(tokens)
    owner = pick // cap
    owner_hit = owner[:, None] == jnp.arange(devices, dtype=jnp.int32)[None, :]
    count = jnp.sum(jnp.where(owner_hit, counts[None, :], 0), axis=1)
    slot = owner * cap + pick % cap % count
    asked = lax.all_to_all(
        requests, ("dp", "code"), split_axis=0, concat_axis=0, tiled=True
    ).reshape(slots)
    select = (asked[:, None] == jnp.arange(rows_dev, dtype=jnp.int32)[None, :]).astype(jnp.bfloat16)
    local_codes = jnp.dot(codebook, projector, preferred_element_type=jnp.float32).astype(
        jnp.bfloat16
    )
    answer = jnp.dot(select, local_codes, preferred_element_type=jnp.float32).astype(jnp.bfloat16)
    slot_codes = lax.all_to_all(
        answer.reshape(devices, cap, zch), ("dp", "code"), split_axis=0, concat_axis=0, tiled=True
    ).reshape(slots, zch)
    slot_blocks = slot.reshape(tokens // block, block)
    slot_ids = jnp.arange(slots, dtype=jnp.int32)

    def pick_codes(block_slots):
        onehot = (block_slots[:, None] == slot_ids[None, :]).astype(jnp.bfloat16)
        return jnp.dot(onehot, slot_codes, preferred_element_type=jnp.float32).astype(jnp.bfloat16)

    quant = lax.map(pick_codes, slot_blocks).reshape(images, rows, width, zch)
    quant_f = quant.astype(jnp.float32)
    latent_f = latents.astype(jnp.float32)
    grad_quant = 2.0 * (quant_f - latent_f)
    grad_blocks = grad_quant.reshape(tokens // block, block, zch)

    def collect_grads(total, inputs):
        block_slots, block_grads = inputs
        onehot = (block_slots[:, None] == slot_ids[None, :]).astype(jnp.bfloat16)
        return (total + split_product(onehot, block_grads), None)

    slot_grads, _ = lax.scan(
        collect_grads, jnp.zeros((slots, zch), jnp.float32), (slot_blocks, grad_blocks)
    )
    returned = (
        lax.all_to_all(
            slot_grads.reshape(devices, cap, zch).astype(jnp.bfloat16),
            ("dp", "code"),
            split_axis=0,
            concat_axis=0,
            tiled=True,
        )
        .astype(jnp.float32)
        .reshape(slots, zch)
    )
    grad_rows = split_product(select, returned)
    grad_proj = split_product(codebook, grad_rows)
    padded = jnp.pad(quant, ((0, 0), (1, 1), (1, 1), (0, 0)))
    padded_grad = jnp.pad(cotangent, ((0, 0), (1, 1), (1, 1), (0, 0)))
    output = jnp.zeros((images, rows, width, channels), jnp.float32)
    grad_input = jnp.zeros((images, rows, width, zch), jnp.float32)
    taps = []
    for row_off in range(3):
        for col_off in range(3):
            window = padded[:, row_off : row_off + rows, col_off : col_off + width]
            output = output + jnp.einsum(
                "nhwc,co->nhwo",
                window,
                kernel[row_off, col_off],
                preferred_element_type=jnp.float32,
            )
            grad_window = padded_grad[
                :, 2 - row_off : 2 - row_off + rows, 2 - col_off : 2 - col_off + width
            ]
            grad_input = grad_input + jnp.einsum(
                "nhwo,co->nhwc",
                grad_window,
                kernel[row_off, col_off],
                preferred_element_type=jnp.float32,
            )
            taps.append(
                jnp.einsum("nhwc,nhwo->co", window, cotangent, preferred_element_type=jnp.float32)
            )
    hidden = (output + bias.astype(jnp.float32)).astype(jnp.bfloat16)
    grad_kernel = jnp.stack(taps).reshape(3, 3, zch, channels)
    grad_bias = jnp.sum(cotangent.astype(jnp.float32), axis=(0, 1, 2))
    grad_latents = (grad_input + 2.0 * commit_weight * (latent_f - quant_f)).astype(jnp.bfloat16)
    kernel_count = 9 * zch * channels
    total_proj, total_kernel, total_bias = lax.psum(
        (grad_proj, grad_kernel, grad_bias), ("dp", "code")
    )
    kernel_step = unit_scale(total_kernel, kernel_count)
    proj_step = unit_scale(total_proj, feat * zch)
    bias_step = unit_scale(total_bias, channels)
    return (hidden, grad_latents, proj_step, kernel_step, bias_step)


def solution(mesh):
    in_specs = (
        P(("dp", "code"), None),
        P(),
        P(("dp", "code"), None, None, None),
        P(("dp", "code"), None, None),
        P(("dp", "code"), None),
        P(("dp", "code"), None, None),
        P(),
        P(),
        P(("dp", "code"), None, None, None),
    )
    out_specs = (
        P(("dp", "code"), None, None, None),
        P(("dp", "code"), None, None, None),
        P(),
        P(),
        P(),
    )
    return jax.shard_map(
        on_device, mesh=mesh, in_specs=in_specs, out_specs=out_specs, check_vma=False
    )
```

profile of v0, /device:TPU:0, one launch (start us, length us, event | category | flops | bytes accessed | tf_op | source)
XLA Modules:
  0.0 272.0 jit_solution(16462433711174080784)
XLA Ops:
  7.2 0.0 copy-start
  7.2 0.0 copy-start.1
  7.2 1.5 copy.73
  8.7 7.3 %all-to-all-start = ((s32[32,1,8]{2,1,0:T(1,128)}), s32[32,1,8]{2,1,0:T(1,128)S(1)}, u32[]{:S(2)}, u32[]{:S(2)}) async-start(s32[32,1,8]{2,1,0:T(1,128)} %bitcast.1), calls=%async_computation | async-start | bytes 32768 | tf_op jit(solution)/shard_map/all_to_all | solution.py:41
  16.0 0.8 reshape.76
  16.8 0.9 select_reduce_fusion
  17.7 0.1 fusion.93
  17.8 1.2 convert_reduce_fusion
  19.0 1.4 fusion.22
  20.4 1.4 convolution_add_fusion.17
  21.9 0.3 convolution_add_fusion.16
  22.3 0.3 convolution_add_fusion.15
  22.6 0.3 convolution_add_fusion.14
  23.0 0.4 convolution_add_fusion.13
  23.3 0.4 convolution_add_fusion.12
  23.7 40.5 %psum.23 = f32[512]{0:T(512)S(1)} all-reduce(f32[512]{0:T(512)S(1)} %convert_reduce_fusion), channel_id=1, replica_groups=mesh['dp'=8,'code'=4] {'dp','code'}, use_global_device_ids=true, to_apply=%region_6.7 | all-reduce | flops 512 | bytes 4096 | tf_op jit(solution)/shard_map/psum | solution.py:117
  64.2 0.6 multiply_reduce_fusion.2
  65.5 0.6 broadcast_divide_fusion.2
  66.1 0.5 broadcast.62
  66.6 0.7 reduce.3
  67.3 0.1 eq.75
  67.4 1.5 fusion.18
  69.0 4.5 %all-to-all-start.1 = ((bf16[32,8,256]{2,1,0:T(8,128)(2,1)}), bf16[32,8,256]{2,1,0:T(8,128)(2,1)S(1)}, u32[]{:S(2)}, u32[]{:S(2)}) async-start(bf16[32,8,256]{2,1,0:T(8,128)(2,1)} %fusion.18), calls=%async_computation.1 | async-start | bytes 262144 | tf_op jit(solution)/shard_map/all_to_all | solution.py:49
  73.4 1.3 convolution_add_fusion.11
  74.7 6.9 %all-to-all-done.1 = bf16[32,8,256]{2,1,0:T(8,128)(2,1)S(1)} async-done(((bf16[32,8,256]{2,1,0:T(8,128)(2,1)}), bf16[32,8,256]{2,1,0:T(8,128)(2,1)S(1)}, u32[]{:S(2)}, u32[]{:S(2)}) %all-to-all-start.1) | async-done | bytes 131104 | tf_op jit(solution)/shard_map/all_to_all | solution.py:49
  81.7 0.3 convolution_convert_fusion.1
  81.9 1.0 pad_slice_fusion.8
  83.0 1.1 fusion.11
  84.1 1.1 fusion.10
  85.2 1.1 fusion.9
  86.3 1.1 fusion.8
  87.5 1.1 fusion.7
  88.6 0.1 fusion.21
  88.7 0.4 fusion.24
  89.1 1.1 fusion.17
  90.2 2.6 all-to-all-start.2
  92.8 0.2 all-reduce.5.cloned.1.call-start
  93.1 1.1 fusion.6
  94.2 1.1 fusion.5
  95.3 1.1 fusion.4
  96.4 1.1 fusion.3
  97.6 3.5 %all-to-all-done.2 = bf16[32,8,256]{2,1,0:T(8,128)(2,1)S(1)} async-done(((bf16[32,8,256]{2,1,0:T(8,128)(2,1)}), bf16[32,8,256]{2,1,0:T(8,128)(2,1)S(1)}, u32[]{:S(2)}, u32[]{:S(2)}) %all-to-all-start.2) | async-done | bytes 131104 | tf_op jit(solution)/shard_map/all_to_all | solution.py:74
  101.1 0.5 fusion.19
  101.5 0.5 convolution_add_fusion.8
  102.0 0.6 fusion.78
  102.7 1.5 fusion.2
  104.2 0.0 all-reduce.5.cloned.1.call-update
  104.2 0.0 copy-start.3
  104.2 1.4 fusion.45
  105.6 2.0 fusion.14
  107.6 0.3 convolution_add_fusion.7
  107.9 0.3 convolution_add_fusion.6
  108.2 0.3 convolution_add_fusion.5
  108.5 0.3 convolution_add_fusion.4
  108.8 0.3 convolution_add_fusion.3
  109.1 0.3 convolution_add_fusion.2
  109.4 0.3 convolution_add_fusion.1
  109.7 1.1 fusion.1
  110.8 141.3 %all-reduce.5.cloned.1.call-done = (f32[768,256]{0,1:T(8,128)}, f32[3,3,256,512]{3,2,1,0:T(8,128)}) async-done(((f32[768,256]{0,1:T(8,128)}, f32[3,3,256,512]{3,2,1,0:T(8,128)}), (f32[768,256]{0,1:T(8,128)}, f32[3,3,256,512]{3,2,1,0:T(8,128)})) %all-reduce.5.cloned.1.call-update) | async-done | bytes 5505040 | tf_op jit(solution)/shard_map/psum | solution.py:117
  252.2 4.2 %multiply_reduce_fusion = f32[]{:T(128)} fusion(f32[3,3,256,512]{3,2,1,0:T(8,128)} %get-tuple-element.56), kind=kLoop, calls=%fused_computation | loop fusion | flops 2359295 | bytes 4718596 | tf_op jit(solution)/shard_map/reduce_sum | solution.py:11
  257.0 5.4 %broadcast_divide_fusion = f32[3,3,256,512]{3,2,1,0:T(8,128)} fusion(f32[3,3,256,512]{3,2,1,0:T(8,128)} %get-tuple-element.56, f32[]{:T(128)S(6)} %sqrt.10), kind=kLoop, calls=%fused_computation.1 | loop fusion | flops 1179648 | bytes 9437188 | tf_op jit(solution)/shard_map/div | solution.py:11
  262.4 0.8 multiply_reduce_fusion.1
  263.9 0.1 broadcast_divide_fusion.1
  264.0 1.1 copy.92
  (21 shorter events, 0.1 us)
Async XLA Ops:
  7.2 60.3 %copy-start = (bf16[784,768]{1,0:T(8,128)(2,1)S(1)}, bf16[784,768]{1,0:T(8,128)(2,1)}, u32[]{:S(2)}) copy-start(bf16[784,768]{1,0:T(8,128)(2,1)} %param.9) | copy-start | bytes 3612676
  7.2 14.7 %copy-start.1 = (bf16[2,16,16,512]{3,2,1,0:T(8,128)(2,1)S(1)}, bf16[2,16,16,512]{3,2,1,0:T(8,128)(2,1)}, u32[]{:S(2)}) copy-start(bf16[2,16,16,512]{3,2,1,0:T(8,128)(2,1)} %param.17) | copy-start | bytes 1572868
  8.7 57.4 %all-to-all-start = ((s32[32,1,8]{2,1,0:T(1,128)}), s32[32,1,8]{2,1,0:T(1,128)S(1)}, u32[]{:S(2)}, u32[]{:S(2)}) async-start(s32[32,1,8]{2,1,0:T(1,128)} %bitcast.1), calls=%async_computation | async-start | bytes 32768 | tf_op jit(solution)/shard_map/all_to_all | solution.py:41
  16.8 5.1 %copy-start.2 = (bf16[3,3,256,512]{3,2,1,0:T(8,128)(2,1)S(1)}, bf16[3,3,256,512]{3,2,1,0:T(8,128)(2,1)}, u32[]{:S(2)}) copy-start(bf16[3,3,256,512]{3,2,1,0:T(8,128)(2,1)} %param.15) | copy-start | bytes 7077892
  22.6 43.5 %copy-start.8 = (bf16[512]{0:T(512)(128)(2,1)S(1)}, bf16[512]{0:T(512)(128)(2,1)}, u32[]{:S(2)}) copy-start(bf16[512]{0:T(512)(128)(2,1)} %param.16) | copy-start | bytes 3076
  22.6 44.8 %copy-start.9 = (bf16[768,256]{1,0:T(8,128)(2,1)S(1)}, bf16[768,256]{1,0:T(8,128)(2,1)}, u32[]{:S(2)}) copy-start(bf16[768,256]{1,0:T(8,128)(2,1)} %param.10) | copy-start | bytes 1179652
  69.0 12.7 %all-to-all-start.1 = ((bf16[32,8,256]{2,1,0:T(8,128)(2,1)}), bf16[32,8,256]{2,1,0:T(8,128)(2,1)S(1)}, u32[]{:S(2)}, u32[]{:S(2)}) async-start(bf16[32,8,256]{2,1,0:T(8,128)(2,1)} %fusion.18), calls=%async_computation.1 | async-start | bytes 262144 | tf_op jit(solution)/shard_map/all_to_all | solution.py:49
  87.5 1.1 copy-start.5
  90.2 10.8 %all-to-all-start.2 = ((bf16[32,8,256]{2,1,0:T(8,128)(2,1)}), bf16[32,8,256]{2,1,0:T(8,128)(2,1)S(1)}, u32[]{:S(2)}, u32[]{:S(2)}) async-start(bf16[32,8,256]{2,1,0:T(8,128)(2,1)} %fusion.17), calls=%async_computation.2 | async-start | bytes 262144 | tf_op jit(solution)/shard_map/all_to_all | solution.py:74
  92.8 159.3 %all-reduce.5.cloned.1.call-start = ((), (), s32[]{:S(2)}) async-start(), calls=%async_computation.3 | async-start | bytes 11010048 | tf_op jit(solution)/shard_map/psum | solution.py:117
  93.1 1.1 copy-start.7
  94.2 1.1 copy-start.6
  104.2 3.4 %copy-start.3 = (bf16[3,3,256,512]{3,2,1,0:T(8,128)(2,1)S(1)}, bf16[3,3,256,512]{3,2,1,0:T(8,128)(2,1)}, u32[]{:S(2)}) copy-start(bf16[3,3,256,512]{3,2,1,0:T(8,128)(2,1)} %param.15) | copy-start | bytes 7077892
  257.0 5.4 %copy-start.4 = (f32[768,256]{0,1:T(8,128)S(1)}, f32[768,256]{0,1:T(8,128)}, u32[]{:S(2)}) copy-start(f32[768,256]{0,1:T(8,128)} %get-tuple-element.55) | copy-start | bytes 2359300
Sparse Core Ops, SparseCore 0:
  104.3 147.8 all-reduce.4
where the time goes:
time: 273 us; the launch traced here: 272 us
  waiting for transfers between devices  152 us (56%)
  blocking collectives  40.5 us (15%)
  matrix products  28.9 us (11%)
  between operations  16.4 us (6%)
  starting transfers between devices  14.6 us (5%)
  other arithmetic  14.6 us (5%)
  local copies, waits for them, and re-layouts  5.14 us (2%)
    psum x1, waiting for transfers between devices, on_device(): lax.psum((grad_proj, grad_kernel, grad_bias), ('dp', 'code'))  141 us
    psum x1, blocking collectives, on_device(): lax.psum((grad_proj, grad_kernel, grad_bias), ('dp', 'code'))  40.5 us
    dot_general x9, matrix products, on_device(): jnp.einsum('nhwc,nhwo->co', window, cotangent, preferred_element_type=jnp...  10.1 us
    dot_general x9, matrix products, on_device(): jnp.einsum('nhwo,co->nhwc', grad_window, kernel[row_off, col_off], prefer...  7.88 us
    all_to_all x1, starting transfers between devices, on_device(): lax.all_to_all(requests, ('dp', 'code'), split_axis=0, concat_axis=0, til...  7.3 us
    all_to_all x1, waiting for transfers between devices, on_device(): lax.all_to_all(answer.reshape(devices, cap, zch), ('dp', 'code'), split_a...  6.94 us
    div x3, other arithmetic, unit_scale(): return values / jnp.sqrt(jnp.sum(values * values) / count + norm_eps)  6.02 us
    reduce_sum x3, other arithmetic, unit_scale(): return values / jnp.sqrt(jnp.sum(values * values) / count + norm_eps)  5.55 us
  transfers between devices with their start and end apart: 4, of which 3 were waited for; matrix products, arithmetic and copies ran while one was open for 8% of the time, Pallas kernels for 0%

commit v1 on v0

--- a/solution.py
+++ b/solution.py
@@ -1,14 +1,182 @@
+import functools
+
 import jax
 import jax.numpy as jnp
 from jax import lax
+from jax.experimental import pallas as pl
+from jax.experimental.pallas import tpu as pltpu
 from jax.sharding import PartitionSpec as P
 
 commit_weight = 0.25
 norm_eps = 1e-06
-
-
-def unit_scale(values, count):
-    return values / jnp.sqrt(jnp.sum(values * values) / count + norm_eps)
+AXES = ("dp", "code")
+PARTS = 4
+
+
+class Grid:
+    def __init__(self, n_dp, n_code):
+        self.n_dp, self.n_code = n_dp, n_code
+        self.outer = n_code // 4
+        self.planes = (n_dp // 2) * self.outer
+        self.total = n_dp * n_code
+
+    def linear(self, r, i):
+        dh, ch = r // self.outer, r % self.outer
+        return (dh * 2 + i // 4) * self.n_code + ch * 4 + i % 4
+
+    def perm(self, move):
+        return [
+            (self.linear(r, i), self.linear(*move(r, i)))
+            for r in range(self.planes)
+            for i in range(8)
+        ]
+
+    def flip(self, bit):
+        return self.perm(lambda r, i: (r, i ^ bit))
+
+    def turn(self, k):
+        return self.perm(lambda r, i: (r // PARTS * PARTS + (r + k) % PARTS, i))
+
+    def far(self, k):
+        groups = self.planes // PARTS
+        return self.perm(lambda r, i: ((r // PARTS + k) % groups * PARTS + r % PARTS, i))
+
+    def place(self):
+        dp, code = lax.axis_index("dp"), lax.axis_index("code")
+        return (dp // 2) * self.outer + code // 4, (dp % 2) * 4 + code % 4
+
+
+def send(x, perm):
+    return lax.ppermute(x, AXES, perm)
+
+
+def half(x, axis, index):
+    return lax.dynamic_index_in_dim(x, index, axis, keepdims=False)
+
+
+def exchange(x, axis, own, perm):
+    sent = half(x, axis, 1 - own).astype(jnp.bfloat16)
+    return half(x, axis, own) + send(sent, perm).astype(jnp.float32)
+
+
+def reduce_planes(grid, x, r):
+    part = r % PARTS
+    got = half(x, 0, part)
+    for k in range(1, PARTS):
+        sent = half(x, 0, (part + k) % PARTS).astype(jnp.bfloat16)
+        got = got + send(sent, grid.turn(k)).astype(jnp.float32)
+    groups = grid.planes // PARTS
+    if groups > 1:
+        rest = [got] + [send(got, grid.far(k)) for k in range(1, groups)]
+        order = (r // PARTS - jnp.arange(groups)) % groups
+        got = jnp.sum(jnp.take(jnp.stack(rest), order, axis=0), axis=0)
+    return got
+
+
+def reduce_scatter(grid, x, r, i):
+    x = x.reshape(2, 2, 2, PARTS, *x.shape[2:])
+    core, col, row = i % 2, i // 2 % 2, i // 4
+    x = exchange(x, 2, core, grid.flip(1))
+    cut = PARTS // 2
+    first = exchange(x[:, :, :cut], 1, col, grid.flip(2))
+    second = exchange(x[:, :, cut:], 0, row, grid.flip(4))
+    first = exchange(first, 0, row, grid.flip(4))
+    second = exchange(second, 0, col, grid.flip(2))
+    return reduce_planes(grid, jnp.concatenate([first, second]), r)
+
+
+def all_gather(grid, own):
+    zs = jnp.stack([own] + [send(own, grid.turn(k)) for k in range(1, PARTS)])
+    xs, ys = send(zs, grid.flip(2)), send(zs, grid.flip(4))
+    cut = PARTS // 2
+    near, far = send(xs[:cut], grid.flip(4)), send(ys[cut:], grid.flip(2))
+    mine = jnp.concatenate([zs, xs, ys, near, far])
+    return mine, send(mine, grid.flip(1))
+
+
+def butterfly(grid, x):
+    bit = 1
+    while bit < grid.total:
+        x = x + send(x, [(d, d ^ bit) for d in range(grid.total)])
+        bit *= 2
+    return x
+
+
+def finish_kernel(order_ref, mine_ref, other_ref, kernel_ref, proj_ref, *, krows, prows, kcount, pcount):
+    slice_rows = krows // 9
+    ksum = jnp.zeros((8, 128), jnp.float32)
+    psum = jnp.zeros((8, 128), jnp.float32)
+
+    def load(e):
+        src = order_ref[e]
+        core = src // 16
+        return src, core
+
+    def body(e, sums):
+        src, core = load(e)
+
+        def total(ref):
+            v = ref[src % 16].astype(jnp.float32)
+            v = v * v
+            return (
+                jnp.sum(v[:krows].reshape(krows // 8, 8, 128), axis=0),
+                jnp.sum(v[krows : krows + prows].reshape(prows // 8, 8, 128), axis=0),
+            )
+
+        a, b = lax.cond(core == 0, lambda: total(mine_ref), lambda: total(other_ref))
+        return sums[0] + a, sums[1] + b
+
+    ksum, psum = lax.fori_loop(0, 32, body, (ksum, psum))
+
+    def factor(v, count):
+        s = jnp.sum(jnp.sum(v, axis=0, keepdims=True), axis=1, keepdims=True)
+        return 1.0 / jnp.sqrt(s / count + norm_eps)
+
+    kf, pf = factor(ksum, kcount), factor(psum, pcount)
+    for e in range(32):
+        i, q = e // 4, e % 4
+        src, core = load(e)
+        row = (i // 2 % 2) * 2 + i // 4
+        row = row * 4 * prows + q * prows
+        col = (i % 2) * 128
+
+        def put(ref):
+            v = ref[src % 16].astype(jnp.float32)
+            kernel_ref[:, i * slice_rows : (i + 1) * slice_rows, q * 128 : (q + 1) * 128] = (
+                v[:krows] * kf
+            ).reshape(9, slice_rows, 128)
+            proj_ref[row : row + prows, col : col + 128] = v[krows : krows + prows] * pf
+
+        pl.when(core == 0)(functools.partial(put, mine_ref))
+        pl.when(core == 1)(functools.partial(put, other_ref))
+
+
+def finish(order, mine, other, zch, channels, feat):
+    krows, prows = 9 * zch // 8, feat // 16
+    body = functools.partial(
+        finish_kernel,
+        krows=krows,
+        prows=prows,
+        kcount=9 * zch * channels,
+        pcount=feat * zch,
+    )
+    return pl.pallas_call(
+        body,
+        out_shape=(
+            jax.ShapeDtypeStruct((9, zch, channels), jnp.float32),
+            jax.ShapeDtypeStruct((feat, zch), jnp.float32),
+        ),
+        in_specs=[
+            pl.BlockSpec(memory_space=pltpu.SMEM),
+            pl.BlockSpec(memory_space=pltpu.VMEM),
+            pl.BlockSpec(memory_space=pltpu.VMEM),
+        ],
+        out_specs=(
+            pl.BlockSpec(memory_space=pltpu.VMEM),
+            pl.BlockSpec(memory_space=pltpu.VMEM),
+        ),
+        compiler_params=pltpu.CompilerParams(vmem_limit_bytes=24 << 20),
+    )(order, mine, other)
 
 
 def split_product(left, right):
@@ -20,7 +188,7 @@
 
 
 def on_device(
-    codebook, projector, latents, wanted, wanted_count, token_pick, kernel, bias, cotangent
+    grid, codebook, projector, latents, wanted, wanted_count, token_pick, kernel, bias, cotangent
 ):
     devices = lax.axis_size(("dp", "code"))
     images, rows, width, zch = latents.shape
@@ -30,7 +198,6 @@
     cap = wanted.shape[2]
     slots = devices * cap
     tokens = images * rows * width
-    block = min(512, tokens)
     requests = wanted.reshape(devices, cap)
     counts = wanted_count.reshape(devices)
     pick = token_pick.reshape(tokens)
@@ -49,27 +216,14 @@
     slot_codes = lax.all_to_all(
         answer.reshape(devices, cap, zch), ("dp", "code"), split_axis=0, concat_axis=0, tiled=True
     ).reshape(slots, zch)
-    slot_blocks = slot.reshape(tokens // block, block)
     slot_ids = jnp.arange(slots, dtype=jnp.int32)
-
-    def pick_codes(block_slots):
-        onehot = (block_slots[:, None] == slot_ids[None, :]).astype(jnp.bfloat16)
-        return jnp.dot(onehot, slot_codes, preferred_element_type=jnp.float32).astype(jnp.bfloat16)
-
-    quant = lax.map(pick_codes, slot_blocks).reshape(images, rows, width, zch)
+    onehot = (slot[:, None] == slot_ids[None, :]).astype(jnp.bfloat16)
+    quant = jnp.dot(onehot, slot_codes, preferred_element_type=jnp.float32).astype(jnp.bfloat16)
+    quant = quant.reshape(images, rows, width, zch)
     quant_f = quant.astype(jnp.float32)
     latent_f = latents.astype(jnp.float32)
     grad_quant = 2.0 * (quant_f - latent_f)
-    grad_blocks = grad_quant.reshape(tokens // block, block, zch)
-
-    def collect_grads(total, inputs):
-        block_slots, block_grads = inputs
-        onehot = (block_slots[:, None] == slot_ids[None, :]).astype(jnp.bfloat16)
-        return (total + split_product(onehot, block_grads), None)
-
-    slot_grads, _ = lax.scan(
-        collect_grads, jnp.zeros((slots, zch), jnp.float32), (slot_blocks, grad_blocks)
-    )
+    slot_grads = split_product(onehot, grad_quant.reshape(tokens, zch))
     returned = (
         lax.all_to_all(
             slot_grads.reshape(devices, cap, zch).astype(jnp.bfloat16),
@@ -110,20 +264,35 @@
                 jnp.einsum("nhwc,nhwo->co", window, cotangent, preferred_element_type=jnp.float32)
             )
     hidden = (output + bias.astype(jnp.float32)).astype(jnp.bfloat16)
-    grad_kernel = jnp.stack(taps).reshape(3, 3, zch, channels)
-    grad_bias = jnp.sum(cotangent.astype(jnp.float32), axis=(0, 1, 2))
+    grad_kernel = jnp.stack(taps)
+    grad_bias = butterfly(grid, jnp.sum(cotangent.astype(jnp.float32), axis=(0, 1, 2)))
     grad_latents = (grad_input + 2.0 * commit_weight * (latent_f - quant_f)).astype(jnp.bfloat16)
-    kernel_count = 9 * zch * channels
-    total_proj, total_kernel, total_bias = lax.psum(
-        (grad_proj, grad_kernel, grad_bias), ("dp", "code")
-    )
-    kernel_step = unit_scale(total_kernel, kernel_count)
-    proj_step = unit_scale(total_proj, feat * zch)
-    bias_step = unit_scale(total_bias, channels)
+
+    r, i = grid.place()
+    krows, prows, wide = 9 * zch // 8, feat // 16, channels // PARTS
+    kpart = (
+        grad_kernel.reshape(9, 8, zch // 8, PARTS, wide)
+        .transpose(1, 3, 0, 2, 4)
+        .reshape(8, PARTS, krows, wide)
+    )
+    ppart = (
+        grad_proj.reshape(2, 2, PARTS, prows, 2, zch // 2)
+        .transpose(1, 0, 4, 2, 3, 5)
+        .reshape(8, PARTS, prows, zch // 2)
+    )
+    total = reduce_scatter(grid, jnp.concatenate([kpart, ppart], axis=2), r, i)
+    mine, other = all_gather(grid, total.astype(jnp.bfloat16))
+    e = jnp.arange(32, dtype=jnp.int32)
+    rel_i, rel_r = (e // 4) ^ i, (r - e % 4) % 4
+    order = (rel_i % 2) * 16 + (rel_i // 2) * 4 + rel_r
+    kernel_step, proj_step = finish(order, mine, other, zch, channels, feat)
+    kernel_step = kernel_step.reshape(3, 3, zch, channels)
+    bias_step = grad_bias / jnp.sqrt(jnp.sum(grad_bias * grad_bias) / channels + norm_eps)
     return (hidden, grad_latents, proj_step, kernel_step, bias_step)
 
 
 def solution(mesh):
+    grid = Grid(mesh.shape["dp"], mesh.shape["code"])
     in_specs = (
         P(("dp", "code"), None),
         P(),
@@ -143,5 +312,9 @@
         P(),
     )
     return jax.shard_map(
-        on_device, mesh=mesh, in_specs=in_specs, out_specs=out_specs, check_vma=False
-    )
+        functools.partial(on_device, grid),
+        mesh=mesh,
+        in_specs=in_specs,
+        out_specs=out_specs,
+        check_vma=False,
+    )

time: 273 us -> 182 us (0.67)
  waiting for transfers between devices: 152 us -> 39.1 us
  blocking collectives: 40.5 us -> 0 us
  local copies, waits for them, and re-layouts: 5.14 us -> 38.7 us
  starting transfers between devices: 14.6 us -> 46.5 us
  between operations: 16.4 us -> 1.93 us
  matrix products: 28.9 us -> 38.5 us
  Pallas kernels: 0 us -> 5.77 us
  other arithmetic: 14.6 us -> 9.77 us
    psum x1 -> x0, waiting for transfers between devices: 141 us -> none  [on_device(): lax.psum((grad_proj, grad_kernel, grad_bias), ('dp', 'code'))]
    psum x1 -> x0, blocking collectives: 40.5 us -> none  [on_device(): lax.psum((grad_proj, grad_kernel, grad_bias), ('dp', 'code'))]
    ppermute x0 -> x21, waiting for transfers between devices: none -> 32.2 us  [send(): return lax.ppermute(x, AXES, perm)]
    ppermute x0 -> x21, starting transfers between devices: none -> 30.7 us  [send(): return lax.ppermute(x, AXES, perm)]
    another operation x0 -> x10, local copies, waits for them, and re-layouts: none -> 15.9 us  [the longest x9 14.5 us: on_device(): grad_kernel = jnp.stack(taps)]
    unnamed x22 -> x40, local copies, waits for them, and re-layouts: 2.7 us -> 8.77 us
    dot_general x9, matrix products: 10.1 us -> 15.9 us  [on_device(): jnp.einsum('nhwc,nhwo->co', window, cotangent, preferred_element_type=jnp...]
    pallas_call x0 -> x1, Pallas kernels: none -> 5.77 us  [finish(): pl.pallas_call(body, out_shape=(jax.ShapeDtypeStruct((9, zch, channels),...]
  transfers between devices with their start and end apart: 4 -> 24, of which waited for: 3 -> 17; matrix products, arithmetic and copies ran while one was open for 8% -> 46% of each run, Pallas kernels for 0% -> 0%
where the time goes in v1:
time: 182 us; the launch traced here: 180 us
  starting transfers between devices  46.5 us (26%)
  waiting for transfers between devices  39.1 us (21%)
  local copies, waits for them, and re-layouts  38.7 us (21%)
  matrix products  38.5 us (21%)
  other arithmetic  9.77 us (5%)
  Pallas kernels  5.77 us (3%)
  between operations  1.93 us (1%)
    ppermute x21, waiting for transfers between devices, send(): return lax.ppermute(x, AXES, perm)  32.2 us
    ppermute x21, starting transfers between devices, send(): return lax.ppermute(x, AXES, perm)  30.7 us
    dot_general x9, matrix products, on_device(): jnp.einsum('nhwc,nhwo->co', window, cotangent, preferred_element_type=jnp...  15.9 us
    another operation x9, local copies, waits for them, and re-layouts, on_device(): grad_kernel = jnp.stack(taps)  14.5 us
    dot_general x9, matrix products, on_device(): jnp.einsum('nhwo,co->nhwc', grad_window, kernel[row_off, col_off], prefer...  11.7 us
    unnamed x40, local copies, waits for them, and re-layouts  8.77 us
    all_to_all x1, starting transfers between devices, on_device(): lax.all_to_all(requests, ('dp', 'code'), split_axis=0, concat_axis=0, til...  7.3 us
    all_to_all x1, waiting for transfers between devices, on_device(): lax.all_to_all(answer.reshape(devices, cap, zch), ('dp', 'code'), split_a...  6.92 us
  transfers between devices with their start and end apart: 24, of which 17 were waited for; matrix products, arithmetic and copies ran while one was open for 46% of the time, Pallas kernels for 0%

profile of v1, /device:TPU:0, one launch (start us, length us, event | category | flops | bytes accessed | tf_op | source)
XLA Modules:
  0.0 180.2 jit_solution(6917207187043597300)
XLA Ops:
  0.7 1.5 copy.98
  2.1 7.3 %all-to-all-start = ((s32[32,1,8]{2,1,0:T(1,128)}), s32[32,1,8]{2,1,0:T(1,128)S(1)}, u32[]{:S(2)}, u32[]{:S(2)}) async-start(s32[32,1,8]{2,1,0:T(1,128)} %bitcast.1), calls=%async_computation | async-start | bytes 32768 | tf_op jit(solution)/shard_map/all_to_all | solution.py:208
  12.6 1.4 fusion.21
  14.1 1.4 convolution_add_fusion.17
  15.5 1.3 convolution_add_fusion.16
  16.8 1.3 convolution_add_fusion.15
  18.2 1.3 convolution_add_fusion.14
  21.7 1.5 fusion.16
  23.3 5.7 %all-to-all-start.1 = ((bf16[32,8,256]{2,1,0:T(8,128)(2,1)}), bf16[32,8,256]{2,1,0:T(8,128)(2,1)S(1)}, u32[]{:S(2)}, u32[]{:S(2)}) async-start(bf16[32,8,256]{2,1,0:T(8,128)(2,1)} %fusion.16), calls=%async_computation.1 | async-start | bytes 262144 | tf_op jit(solution)/shard_map/all_to_all | solution.py:216
  29.0 1.3 convolution_add_fusion.13
  30.3 6.9 %all-to-all-done.1 = bf16[32,8,256]{2,1,0:T(8,128)(2,1)S(1)} async-done(((bf16[32,8,256]{2,1,0:T(8,128)(2,1)}), bf16[32,8,256]{2,1,0:T(8,128)(2,1)S(1)}, u32[]{:S(2)}, u32[]{:S(2)}) %all-to-all-start.1) | async-done | bytes 131104 | tf_op jit(solution)/shard_map/all_to_all | solution.py:216
  37.5 1.3 pad_slice_fusion.8
  42.0 2.1 %convolution_bitcast_fusion.7 = f32[256,512]{1,0:T(8,128)} fusion(bf16[2,16,16,256]{3,2,1,0:T(8,128)(2,1)} %get-tuple-element.21, bf16[2,16,16,512]{3,2,1,0:T(8,128)(2,1)S(1)} %copy-done.1), kind=kOutput, calls=%fused_computation.40 | convolution fusion | flops 134217728 | bytes 1310720 | tf_op jit(solution)/shard_map/nhwc,nhwo->co/dot_general | solution.py:264
  45.3 2.1 %convolution_bitcast_fusion.6 = f32[256,512]{1,0:T(8,128)} fusion(bf16[2,16,16,256]{3,2,1,0:T(8,128)(2,1)} %get-tuple-element.22, bf16[2,16,16,512]{3,2,1,0:T(8,128)(2,1)S(1)} %copy-done.1), kind=kOutput, calls=%fused_computation.39 | convolution fusion | flops 134217728 | bytes 1310720 | tf_op jit(solution)/shard_map/nhwc,nhwo->co/dot_general | solution.py:264
  47.3 2.0 %stack.45 = f32[1,8,32,4,128]{4,3,2,1,0:T(4,128)} reshape(f32[256,512]{1,0:T(8,128)} %convolution_bitcast_fusion.6) | data formatting | bytes 1048576 | tf_op jit(solution)/shard_map/stack | solution.py:267
  49.3 2.1 %convolution_bitcast_fusion.5 = f32[256,512]{1,0:T(8,128)} fusion(bf16[2,16,16,256]{3,2,1,0:T(8,128)(2,1)} %get-tuple-element.23, bf16[2,16,16,512]{3,2,1,0:T(8,128)(2,1)S(1)} %copy-done.1), kind=kOutput, calls=%fused_computation.38 | convolution fusion | flops 134217728 | bytes 1310720 | tf_op jit(solution)/shard_map/nhwc,nhwo->co/dot_general | solution.py:264
  51.4 2.0 %stack.46 = f32[1,8,32,4,128]{4,3,2,1,0:T(4,128)} reshape(f32[256,512]{1,0:T(8,128)} %convolution_bitcast_fusion.5) | data formatting | bytes 1048576 | tf_op jit(solution)/shard_map/stack | solution.py:267
  53.4 1.4 reshape.162
  54.8 2.1 %convolution_bitcast_fusion.3 = f32[256,512]{1,0:T(8,128)} fusion(bf16[2,16,16,256]{3,2,1,0:T(8,128)(2,1)} %get-tuple-element.24, bf16[2,16,16,512]{3,2,1,0:T(8,128)(2,1)S(1)} %copy-done.1), kind=kOutput, calls=%fused_computation.35 | convolution fusion | flops 134217728 | bytes 1310720 | tf_op jit(solution)/shard_map/nhwc,nhwo->co/dot_general | solution.py:264
  56.9 2.0 %stack.47 = f32[1,8,32,4,128]{4,3,2,1,0:T(4,128)} reshape(f32[256,512]{1,0:T(8,128)} %convolution_bitcast_fusion.3) | data formatting | bytes 1048576 | tf_op jit(solution)/shard_map/stack | solution.py:267
  58.9 2.1 %convolution_bitcast_fusion.2 = f32[256,512]{1,0:T(8,128)} fusion(bf16[2,16,16,256]{3,2,1,0:T(8,128)(2,1)} %get-tuple-element.25, bf16[2,16,16,512]{3,2,1,0:T(8,128)(2,1)S(1)} %copy-done.1), kind=kOutput, calls=%fused_computation.34 | convolution fusion | flops 134217728 | bytes 1310720 | tf_op jit(solution)/shard_map/nhwc,nhwo->co/dot_general | solution.py:264
  61.0 2.0 %stack.48 = f32[1,8,32,4,128]{4,3,2,1,0:T(4,128)} reshape(f32[256,512]{1,0:T(8,128)} %convolution_bitcast_fusion.2) | data formatting | bytes 1048576 | tf_op jit(solution)/shard_map/stack | solution.py:267
  64.1 2.0 %stack.49 = f32[1,8,32,4,128]{4,3,2,1,0:T(4,128)} reshape(f32[256,512]{1,0:T(8,128)} %convolution_bitcast_fusion.1) | data formatting | bytes 1048576 | tf_op jit(solution)/shard_map/stack | solution.py:267
  66.1 2.1 %convolution_bitcast_fusion = f32[256,512]{1,0:T(8,128)} fusion(bf16[2,16,16,256]{3,2,1,0:T(8,128)(2,1)} %get-tuple-element.20, bf16[2,16,16,512]{3,2,1,0:T(8,128)(2,1)S(1)} %copy-done.1), kind=kOutput, calls=%fused_computation.32 | convolution fusion | flops 134217728 | bytes 1310720 | tf_op jit(solution)/shard_map/nhwc,nhwo->co/dot_general | solution.py:264
  69.9 2.8 %all-to-all-start.2 = ((bf16[32,8,256]{2,1,0:T(8,128)(2,1)}), bf16[32,8,256]{2,1,0:T(8,128)(2,1)S(1)}, u32[]{:S(2)}, u32[]{:S(2)}) async-start(bf16[32,8,256]{2,1,0:T(8,128)(2,1)} %fusion.15), calls=%async_computation.2 | async-start | bytes 262144 | tf_op jit(solution)/shard_map/all_to_all | solution.py:228
  73.5 1.9 %copy_dynamic-update-slice_fusion.5 = f32[9,8,32,4,128]{4,2,3,1,0:T(8,128)} fusion(f32[9,8,32,4,128]{4,2,3,1,0:T(8,128)} %copy_dynamic-update-slice_fusion.6, f32[1,8,32,4,128]{4,3,2,1,0:T(4,128)} %stack.45), kind=kLoop, calls=%fused_computation.99 | loop fusion | bytes 1048576
  76.3 1.2 fusion.9
  82.2 5.2 %copy.125 = f32[8,4,9,32,128]{4,3,2,1,0:T(8,128)} copy(f32[8,4,9,32,128]{4,3,1,0,2:T(8,128)} %bitcast.240) | data formatting | bytes 9437184 | tf_op jit(solution)/shard_map/transpose | solution.py:275
  90.8 2.4 %reshape.166 = f32[2,2,4,48,2,128]{5,4,3,2,1,0:T(2,128)} reshape(f32[768,256]{1,0:T(8,128)} %copy.126) | data formatting | bytes 1572864 | tf_op jit(solution)/shard_map/reshape | solution.py:279
  94.4 2.9 %fusion.5 = bf16[2,2,4,336,128]{4,3,2,1,0:T(8,128)(2,1)} fusion(s32[]{:T(128)S(6)} %select_n.167, f32[2,2,2,4,48,128]{5,4,3,1,0,2:T(8,128)S(1)} %bitcast.238, f32[2,2,2,4,288,128]{5,4,3,2,1,0:T(8,128)} %bitcast.236), kind=kLoop, calls=%fused_computation.17 | loop fusion | flops 2752512 | bytes 6881284 | tf_op jit(solution)/shard_map/convert_element_type | solution.py:58
  97.4 1.3 convolution_add_fusion.12
  98.7 1.7 collective-permute-start.17
  100.4 1.3 convolution_add_fusion.11
  102.4 1.6 collective-permute-start.18
  104.0 1.9 %collective-permute-done.18 = f32[512]{0:T(512)S(1)} collective-permute-done((f32[512]{0:T(512)S(1)}, f32[512]{0:T(512)S(1)}, u32[]{:S(2)}, u32[]{:S(2)}) %collective-permute-start.18) | collective-permute-done | bytes 2080 | tf_op jit(solution)/shard_map/ppermute | solution.py:50
  105.9 1.7 collective-permute-start.19
  107.6 1.9 %collective-permute-done.19 = f32[512]{0:T(512)S(1)} collective-permute-done((f32[512]{0:T(512)S(1)}, f32[512]{0:T(512)S(1)}, u32[]{:S(2)}, u32[]{:S(2)}) %collective-permute-start.19) | collective-permute-done | bytes 2080 | tf_op jit(solution)/shard_map/ppermute | solution.py:50
  109.5 2.6 %collective-permute-start.20 = (f32[512]{0:T(512)S(1)}, f32[512]{0:T(512)S(1)}, u32[]{:S(2)}, u32[]{:S(2)}) collective-permute-start(f32[512]{0:T(512)S(1)} %add.323), channel_id=1, source_target_pairs={{0,16},{1,17},{2,18},{3,19},{4,20},{5,21},{6,22},{7,23},{8,24},{9,... | collective-permute-start | bytes 6152 | tf_op jit(solution)/shard_map/ppermute | solution.py:50
  112.2 1.8 %collective-permute-done.20 = f32[512]{0:T(512)S(1)} collective-permute-done((f32[512]{0:T(512)S(1)}, f32[512]{0:T(512)S(1)}, u32[]{:S(2)}, u32[]{:S(2)}) %collective-permute-start.20) | collective-permute-done | bytes 2080 | tf_op jit(solution)/shard_map/ppermute | solution.py:50
  115.9 1.2 fusion.48
  118.4 2.3 %fusion.4 = f32[2,2,4,336,128]{4,3,2,1,0:T(8,128)S(1)} fusion(s32[]{:T(128)S(6)} %select_n.166, f32[2,2,2,4,48,128]{5,4,3,1,0,2:T(8,128)S(1)} %bitcast.239, bf16[2,2,4,336,128]{4,3,2,1,0:T(8,128)(2,1)} %collective-permute-done, f32[2,2,2,4,288,128]{5,4,3,2,1,0:T(8,128)} %bitcast.237), kind=kLoop, calls=%fused_computation.8 | loop fusion | flops 2064384 | bytes 9633796 | tf_op jit(solution)/shard_map/add | solution.py:59
  121.0 1.7 collective-permute-start.1
  123.1 1.6 collective-permute-start.3
  124.6 3.9 %collective-permute-done.1 = bf16[2,2,336,128]{3,2,1,0:T(8,128)(2,1)S(1)} collective-permute-done((bf16[2,2,336,128]{3,2,1,0:T(8,128)(2,1)S(1)}, bf16[2,2,336,128]{3,2,1,0:T(8,128)(2,1)S(1)}, u32[]{:S(2)}, u32[]{:S(2)}) %collective-permute-start.1) | collective-permute-done | bytes 344096 | tf_op jit(solution)/shard_map/ppermute | solution.py:50
  128.6 1.8 %collective-permute-start.2 = (bf16[2,336,128]{2,1,0:T(8,128)(2,1)S(1)}, bf16[2,336,128]{2,1,0:T(8,128)(2,1)S(1)}, u32[]{:S(2)}, u32[]{:S(2)}) collective-permute-start(bf16[2,336,128]{2,1,0:T(8,128)(2,1)S(1)} %fusion.82), channel_id=1, source_target_pairs={{0,4},{1,5},{2,6},{3,7},{4,0},{5,1},{6,2},{7,3},{8,12},{9,13},{10,... | collective-permute-start | bytes 516104 | tf_op jit(solution)/shard_map/ppermute | solution.py:50
  131.6 1.4 collective-permute-start.4
  134.1 3.0 %collective-permute-done.4 = bf16[2,336,128]{2,1,0:T(8,128)(2,1)S(1)} collective-permute-done((bf16[2,336,128]{2,1,0:T(8,128)(2,1)S(1)}, bf16[2,336,128]{2,1,0:T(8,128)(2,1)S(1)}, u32[]{:S(2)}, u32[]{:S(2)}) %collective-permute-start.4) | collective-permute-done | bytes 172064 | tf_op jit(solution)/shard_map/ppermute | solution.py:50
  137.2 1.6 collective-permute-start.5
  138.8 2.5 %collective-permute-start.6 = (bf16[336,128]{1,0:T(8,128)(2,1)S(1)}, bf16[336,128]{1,0:T(8,128)(2,1)S(1)}, u32[]{:S(2)}, u32[]{:S(2)}) collective-permute-start(bf16[336,128]{1,0:T(8,128)(2,1)S(1)} %get-tuple-element.18), channel_id=1, source_target_pairs={{0,16},{1,17},{2,18},{3,19},{4,20},{5,21},{6,22},{7,23},{8,24},{9,... | collective-permute-start | bytes 258056 | tf_op jit(solution)/shard_map/ppermute | solution.py:50
  141.3 1.4 collective-permute-start.7
  143.0 1.6 collective-permute-done.5
  144.6 3.4 %collective-permute-done.6 = bf16[336,128]{1,0:T(8,128)(2,1)S(1)} collective-permute-done((bf16[336,128]{1,0:T(8,128)(2,1)S(1)}, bf16[336,128]{1,0:T(8,128)(2,1)S(1)}, u32[]{:S(2)}, u32[]{:S(2)}) %collective-permute-start.6) | collective-permute-done | bytes 86048 | tf_op jit(solution)/shard_map/ppermute | solution.py:50
  148.1 2.3 %collective-permute-start.8 = (bf16[336,128]{1,0:T(8,128)(2,1)S(1)}, bf16[336,128]{1,0:T(8,128)(2,1)S(1)}, u32[]{:S(2)}, u32[]{:S(2)}) collective-permute-start(bf16[336,128]{1,0:T(8,128)(2,1)S(1)} %get-tuple-element.12), channel_id=1, source_target_pairs={{0,8},{1,9},{2,10},{3,11},{4,12},{5,13},{6,14},{7,15},{8,16},{9,17... | collective-permute-start | bytes 258056 | tf_op jit(solution)/shard_map/ppermute | solution.py:50
  151.4 1.4 collective-permute-start.10
  153.1 1.3 collective-permute-done.8
  154.4 1.9 %collective-permute-done.9 = bf16[336,128]{1,0:T(8,128)(2,1)S(1)} collective-permute-done((bf16[336,128]{1,0:T(8,128)(2,1)S(1)}, bf16[336,128]{1,0:T(8,128)(2,1)S(1)}, u32[]{:S(2)}, u32[]{:S(2)}) %collective-permute-start.9) | collective-permute-done | bytes 86048 | tf_op jit(solution)/shard_map/ppermute | solution.py:50
  156.8 1.5 collective-permute-start.11
  158.3 1.5 collective-permute-start.12
  159.9 4.3 %collective-permute-done.11 = bf16[4,336,128]{2,1,0:T(8,128)(2,1)S(1)} collective-permute-done((bf16[4,336,128]{2,1,0:T(8,128)(2,1)S(1)}, bf16[4,336,128]{2,1,0:T(8,128)(2,1)S(1)}, u32[]{:S(2)}, u32[]{:S(2)}) %collective-permute-start.11) | collective-permute-done | bytes 344096 | tf_op jit(solution)/shard_map/ppermute | solution.py:50
  164.2 1.6 collective-permute-start.13
  165.8 1.5 collective-permute-start.14
  167.4 2.3 %collective-permute-done.13 = bf16[2,336,128]{2,1,0:T(8,128)(2,1)S(1)} collective-permute-done((bf16[2,336,128]{2,1,0:T(8,128)(2,1)S(1)}, bf16[2,336,128]{2,1,0:T(8,128)(2,1)S(1)}, u32[]{:S(2)}, u32[]{:S(2)}) %collective-permute-start.13) | collective-permute-done | bytes 172064 | tf_op jit(solution)/shard_map/ppermute | solution.py:50
  169.7 1.6 collective-permute-done.14
  174.5 5.8 %shard_map.128 = (f32[9,256,512]{2,1,0:T(8,128)}, f32[768,256]{1,0:T(8,128)}) custom-call(s32[32]{0:T(128)S(1)} %fusion.114.order_ref, bf16[16,336,128]{2,1,0:T(8,128)(2,1)S(1)} %constant_dynamic-update-slice_fusion.mine_ref, bf16[16,336,128]{2,1,0:T(8,128)(2,1)S(1)} %collective-permute-done.15.other_ref), custom_call_target="tpu_custom_call" | custom-call | tf_op jit(solution)/shard_map/pallas_call | solution.py:163
  (111 shorter events, 35.5 us)
Async XLA Ops:
  0.6 21.1 %copy-start = (bf16[784,768]{1,0:T(8,128)(2,1)S(1)}, bf16[784,768]{1,0:T(8,128)(2,1)}, u32[]{:S(2)}) copy-start(bf16[784,768]{1,0:T(8,128)(2,1)} %param.9) | copy-start | bytes 3612676
  0.6 14.9 %copy-start.1 = (bf16[2,16,16,512]{3,2,1,0:T(8,128)(2,1)S(1)}, bf16[2,16,16,512]{3,2,1,0:T(8,128)(2,1)}, u32[]{:S(2)}) copy-start(bf16[2,16,16,512]{3,2,1,0:T(8,128)(2,1)} %param.17) | copy-start | bytes 1572868
  2.1 18.3 %all-to-all-start = ((s32[32,1,8]{2,1,0:T(1,128)}), s32[32,1,8]{2,1,0:T(1,128)S(1)}, u32[]{:S(2)}, u32[]{:S(2)}) async-start(s32[32,1,8]{2,1,0:T(1,128)} %bitcast.1), calls=%async_computation | async-start | bytes 32768 | tf_op jit(solution)/shard_map/all_to_all | solution.py:208
  10.6 88.1 %collective-permute-start.16 = (f32[512]{0:T(512)S(1)}, f32[512]{0:T(512)S(1)}, u32[]{:S(2)}, u32[]{:S(2)}) collective-permute-start(f32[512]{0:T(512)S(1)} %convert_reduce_fusion), channel_id=1, source_target_pairs={{0,1},{1,0},{2,3},{3,2},{4,5},{5,4},{6,7},{7,6},{8,9},{9,8},{10,11... | collective-permute-start | bytes 6152 | tf_op jit(solution)/shard_map/ppermute | solution.py:50
  16.8 4.9 %copy-start.12 = (bf16[768,256]{1,0:T(8,128)(2,1)S(1)}, bf16[768,256]{1,0:T(8,128)(2,1)}, u32[]{:S(2)}) copy-start(bf16[768,256]{1,0:T(8,128)(2,1)} %param.10) | copy-start | bytes 1179652
  23.3 14.0 %all-to-all-start.1 = ((bf16[32,8,256]{2,1,0:T(8,128)(2,1)}), bf16[32,8,256]{2,1,0:T(8,128)(2,1)S(1)}, u32[]{:S(2)}, u32[]{:S(2)}) async-start(bf16[32,8,256]{2,1,0:T(8,128)(2,1)} %fusion.16), calls=%async_computation.1 | async-start | bytes 262144 | tf_op jit(solution)/shard_map/all_to_all | solution.py:216
  66.1 2.1 %copy-start.8 = (bf16[2,16,16,256]{3,2,1,0:T(8,128)(2,1)S(1)}, bf16[2,16,16,256]{3,2,1,0:T(8,128)(2,1)}, u32[]{:S(2)}) copy-start(bf16[2,16,16,256]{3,2,1,0:T(8,128)(2,1)} %param.11) | copy-start | bytes 786436
  69.9 17.6 %all-to-all-start.2 = ((bf16[32,8,256]{2,1,0:T(8,128)(2,1)}), bf16[32,8,256]{2,1,0:T(8,128)(2,1)S(1)}, u32[]{:S(2)}, u32[]{:S(2)}) async-start(bf16[32,8,256]{2,1,0:T(8,128)(2,1)} %fusion.15), calls=%async_computation.2 | async-start | bytes 262144 | tf_op jit(solution)/shard_map/all_to_all | solution.py:228
  72.6 2.8 %copy-start.5 = (f32[1,8,32,4,128]{4,3,2,1,0:T(4,128)S(1)}, f32[1,8,32,4,128]{4,3,2,1,0:T(4,128)}, u32[]{:S(2)}) copy-start(f32[1,8,32,4,128]{4,3,2,1,0:T(4,128)} %stack.46) | copy-start | bytes 1572868
  72.6 3.6 %copy-start.7 = (bf16[8,32,16,2,16]{1,0,4,2,3:T(8,128)(2,1)S(1)}, bf16[8,32,16,2,16]{1,0,4,2,3:T(8,128)(2,1)}, u32[]{:S(2)}) copy-start(bf16[8,32,16,2,16]{1,0,4,2,3:T(8,128)(2,1)} %reshape.162) | copy-start | bytes 786436
  72.7 3.6 %copy-start.10 = (bf16[4,128,16,2,16]{1,0,4,2,3:T(4,128)(2,1)S(1)}, bf16[4,128,16,2,16]{1,0,4,2,3:T(4,128)(2,1)}, u32[]{:S(2)}) copy-start(bf16[4,128,16,2,16]{1,0,4,2,3:T(4,128)(2,1)} %dot_general.143) | copy-start | bytes 1572868
  76.3 1.3 copy-start.3
  76.3 2.1 %copy-start.4 = (f32[1,8,32,4,128]{4,3,2,1,0:T(4,128)S(1)}, f32[1,8,32,4,128]{4,3,2,1,0:T(4,128)}, u32[]{:S(2)}) copy-start(f32[1,8,32,4,128]{4,3,2,1,0:T(4,128)} %stack.48) | copy-start | bytes 1572868
  77.6 1.7 copy-start.6
  97.4 14.8 %copy-start.11 = (bf16[512]{0:T(512)(128)(2,1)S(1)}, bf16[512]{0:T(512)(128)(2,1)}, u32[]{:S(2)}) copy-start(bf16[512]{0:T(512)(128)(2,1)} %param.16) | copy-start | bytes 3076
  97.4 21.0 %collective-permute-start = (bf16[2,2,4,336,128]{4,3,2,1,0:T(8,128)(2,1)}, bf16[2,2,4,336,128]{4,3,2,1,0:T(8,128)(2,1)}, u32[]{:S(2)}, u32[]{:S(2)}) collective-permute-start(bf16[2,2,4,336,128]{4,3,2,1,0:T(8,128)(2,1)} %fusion.5), channel_id=1, source_target_pairs={{0,1},{1,0},{2,3},{3,2},{4,5},{5,4},{6,7},{7,6},{8,9},{9,8},{10,11... | collective-permute-start | bytes 4128776 | tf_op jit(solution)/shard_map/ppermute | solution.py:50
  98.7 3.7 %collective-permute-start.17 = (f32[512]{0:T(512)S(1)}, f32[512]{0:T(512)S(1)}, u32[]{:S(2)}, u32[]{:S(2)}) collective-permute-start(f32[512]{0:T(512)S(1)} %add.320), channel_id=1, source_target_pairs={{0,2},{1,3},{2,0},{3,1},{4,6},{5,7},{6,4},{7,5},{8,10},{9,11},{10,... | collective-permute-start | bytes 6152 | tf_op jit(solution)/shard_map/ppermute | solution.py:50
  102.4 3.6 %collective-permute-start.18 = (f32[512]{0:T(512)S(1)}, f32[512]{0:T(512)S(1)}, u32[]{:S(2)}, u32[]{:S(2)}) collective-permute-start(f32[512]{0:T(512)S(1)} %add.321), channel_id=1, source_target_pairs={{0,4},{1,5},{2,6},{3,7},{4,0},{5,1},{6,2},{7,3},{8,12},{9,13},{10,... | collective-permute-start | bytes 6152 | tf_op jit(solution)/shard_map/ppermute | solution.py:50
  105.9 3.6 %collective-permute-start.19 = (f32[512]{0:T(512)S(1)}, f32[512]{0:T(512)S(1)}, u32[]{:S(2)}, u32[]{:S(2)}) collective-permute-start(f32[512]{0:T(512)S(1)} %add.322), channel_id=1, source_target_pairs={{0,8},{1,9},{2,10},{3,11},{4,12},{5,13},{6,14},{7,15},{8,0},{9,1},... | collective-permute-start | bytes 6152 | tf_op jit(solution)/shard_map/ppermute | solution.py:50
  109.5 4.5 %collective-permute-start.20 = (f32[512]{0:T(512)S(1)}, f32[512]{0:T(512)S(1)}, u32[]{:S(2)}, u32[]{:S(2)}) collective-permute-start(f32[512]{0:T(512)S(1)} %add.323), channel_id=1, source_target_pairs={{0,16},{1,17},{2,18},{3,19},{4,20},{5,21},{6,22},{7,23},{8,24},{9,... | collective-permute-start | bytes 6152 | tf_op jit(solution)/shard_map/ppermute | solution.py:50
  120.7 2.0 %copy-start.2 = (bf16[3,3,256,512]{3,2,1,0:T(8,128)(2,1)S(1)}, bf16[3,3,256,512]{3,2,1,0:T(8,128)(2,1)}, u32[]{:S(2)}) copy-start(bf16[3,3,256,512]{3,2,1,0:T(8,128)(2,1)} %param.15) | copy-start | bytes 7077892
  121.0 7.5 %collective-permute-start.1 = (bf16[2,2,336,128]{3,2,1,0:T(8,128)(2,1)S(1)}, bf16[2,2,336,128]{3,2,1,0:T(8,128)(2,1)S(1)}, u32[]{:S(2)}, u32[]{:S(2)}) collective-permute-start(bf16[2,2,336,128]{3,2,1,0:T(8,128)(2,1)S(1)} %fusion.29), channel_id=1, source_target_pairs={{0,2},{1,3},{2,0},{3,1},{4,6},{5,7},{6,4},{7,5},{8,10},{9,11},{10,... | collective-permute-start | bytes 1032200 | tf_op jit(solution)/shard_map/ppermute | solution.py:50
  123.1 8.5 %collective-permute-start.3 = (bf16[2,2,336,128]{3,2,1,0:T(8,128)(2,1)S(1)}, bf16[2,2,336,128]{3,2,1,0:T(8,128)(2,1)S(1)}, u32[]{:S(2)}, u32[]{:S(2)}) collective-permute-start(bf16[2,2,336,128]{3,2,1,0:T(8,128)(2,1)S(1)} %fusion.30), channel_id=1, source_target_pairs={{0,4},{1,5},{2,6},{3,7},{4,0},{5,1},{6,2},{7,3},{8,12},{9,13},{10,... | collective-permute-start | bytes 1032200 | tf_op jit(solution)/shard_map/ppermute | solution.py:50
  128.6 5.5 %collective-permute-start.2 = (bf16[2,336,128]{2,1,0:T(8,128)(2,1)S(1)}, bf16[2,336,128]{2,1,0:T(8,128)(2,1)S(1)}, u32[]{:S(2)}, u32[]{:S(2)}) collective-permute-start(bf16[2,336,128]{2,1,0:T(8,128)(2,1)S(1)} %fusion.82), channel_id=1, source_target_pairs={{0,4},{1,5},{2,6},{3,7},{4,0},{5,1},{6,2},{7,3},{8,12},{9,13},{10,... | collective-permute-start | bytes 516104 | tf_op jit(solution)/shard_map/ppermute | solution.py:50
  131.6 5.5 %collective-permute-start.4 = (bf16[2,336,128]{2,1,0:T(8,128)(2,1)S(1)}, bf16[2,336,128]{2,1,0:T(8,128)(2,1)S(1)}, u32[]{:S(2)}, u32[]{:S(2)}) collective-permute-start(bf16[2,336,128]{2,1,0:T(8,128)(2,1)S(1)} %fusion.83), channel_id=1, source_target_pairs={{0,2},{1,3},{2,0},{3,1},{4,6},{5,7},{6,4},{7,5},{8,10},{9,11},{10,... | collective-permute-start | bytes 516104 | tf_op jit(solution)/shard_map/ppermute | solution.py:50
  137.2 7.4 %collective-permute-start.5 = (bf16[336,128]{1,0:T(8,128)(2,1)S(1)}, bf16[336,128]{1,0:T(8,128)(2,1)S(1)}, u32[]{:S(2)}, u32[]{:S(2)}) collective-permute-start(bf16[336,128]{1,0:T(8,128)(2,1)S(1)} %get-tuple-element.17), channel_id=1, source_target_pairs={{0,8},{1,9},{2,10},{3,11},{4,12},{5,13},{6,14},{7,15},{8,16},{9,17... | collective-permute-start | bytes 258056 | tf_op jit(solution)/shard_map/ppermute | solution.py:50
  138.8 9.2 %collective-permute-start.6 = (bf16[336,128]{1,0:T(8,128)(2,1)S(1)}, bf16[336,128]{1,0:T(8,128)(2,1)S(1)}, u32[]{:S(2)}, u32[]{:S(2)}) collective-permute-start(bf16[336,128]{1,0:T(8,128)(2,1)S(1)} %get-tuple-element.18), channel_id=1, source_target_pairs={{0,16},{1,17},{2,18},{3,19},{4,20},{5,21},{6,22},{7,23},{8,24},{9,... | collective-permute-start | bytes 258056 | tf_op jit(solution)/shard_map/ppermute | solution.py:50
  141.3 6.7 %collective-permute-start.7 = (bf16[336,128]{1,0:T(8,128)(2,1)S(1)}, bf16[336,128]{1,0:T(8,128)(2,1)S(1)}, u32[]{:S(2)}, u32[]{:S(2)}) collective-permute-start(bf16[336,128]{1,0:T(8,128)(2,1)S(1)} %get-tuple-element.19), channel_id=1, source_target_pairs={{0,24},{1,25},{2,26},{3,27},{4,28},{5,29},{6,30},{7,31},{8,0},{9,1... | collective-permute-start | bytes 258056 | tf_op jit(solution)/shard_map/ppermute | solution.py:50
  148.1 6.3 %collective-permute-start.8 = (bf16[336,128]{1,0:T(8,128)(2,1)S(1)}, bf16[336,128]{1,0:T(8,128)(2,1)S(1)}, u32[]{:S(2)}, u32[]{:S(2)}) collective-permute-start(bf16[336,128]{1,0:T(8,128)(2,1)S(1)} %get-tuple-element.12), channel_id=1, source_target_pairs={{0,8},{1,9},{2,10},{3,11},{4,12},{5,13},{6,14},{7,15},{8,16},{9,17... | collective-permute-start | bytes 258056 | tf_op jit(solution)/shard_map/ppermute | solution.py:50
  150.4 6.0 %collective-permute-start.9 = (bf16[336,128]{1,0:T(8,128)(2,1)S(1)}, bf16[336,128]{1,0:T(8,128)(2,1)S(1)}, u32[]{:S(2)}, u32[]{:S(2)}) collective-permute-start(bf16[336,128]{1,0:T(8,128)(2,1)S(1)} %get-tuple-element.12), channel_id=1, source_target_pairs={{0,16},{1,17},{2,18},{3,19},{4,20},{5,21},{6,22},{7,23},{8,24},{9,... | collective-permute-start | bytes 258056 | tf_op jit(solution)/shard_map/ppermute | solution.py:50
  151.4 5.4 %collective-permute-start.10 = (bf16[336,128]{1,0:T(8,128)(2,1)S(1)}, bf16[336,128]{1,0:T(8,128)(2,1)S(1)}, u32[]{:S(2)}, u32[]{:S(2)}) collective-permute-start(bf16[336,128]{1,0:T(8,128)(2,1)S(1)} %get-tuple-element.12), channel_id=1, source_target_pairs={{0,24},{1,25},{2,26},{3,27},{4,28},{5,29},{6,30},{7,31},{8,0},{9,1... | collective-permute-start | bytes 258056 | tf_op jit(solution)/shard_map/ppermute | solution.py:50
  153.1 18.2 %copy-start.9 = (bf16[2,16,16,256]{3,2,1,0:T(8,128)(2,1)S(1)}, bf16[2,16,16,256]{3,2,1,0:T(8,128)(2,1)}, u32[]{:S(2)}) copy-start(bf16[2,16,16,256]{3,2,1,0:T(8,128)(2,1)} %param.11) | copy-start | bytes 786436
  156.8 7.3 %collective-permute-start.11 = (bf16[4,336,128]{2,1,0:T(8,128)(2,1)S(1)}, bf16[4,336,128]{2,1,0:T(8,128)(2,1)S(1)}, u32[]{:S(2)}, u32[]{:S(2)}) collective-permute-start(bf16[4,336,128]{2,1,0:T(8,128)(2,1)S(1)} %pad_maximum_fusion), channel_id=1, source_target_pairs={{0,2},{1,3},{2,0},{3,1},{4,6},{5,7},{6,4},{7,5},{8,10},{9,11},{10,... | collective-permute-start | bytes 1032200 | tf_op jit(solution)/shard_map/ppermute | solution.py:50
  158.3 7.4 %collective-permute-start.12 = (bf16[4,336,128]{2,1,0:T(8,128)(2,1)S(1)}, bf16[4,336,128]{2,1,0:T(8,128)(2,1)S(1)}, u32[]{:S(2)}, u32[]{:S(2)}) collective-permute-start(bf16[4,336,128]{2,1,0:T(8,128)(2,1)S(1)} %pad_maximum_fusion), channel_id=1, source_target_pairs={{0,4},{1,5},{2,6},{3,7},{4,0},{5,1},{6,2},{7,3},{8,12},{9,13},{10,... | collective-permute-start | bytes 1032200 | tf_op jit(solution)/shard_map/ppermute | solution.py:50
  164.2 5.5 %collective-permute-start.13 = (bf16[2,336,128]{2,1,0:T(8,128)(2,1)S(1)}, bf16[2,336,128]{2,1,0:T(8,128)(2,1)S(1)}, u32[]{:S(2)}, u32[]{:S(2)}) collective-permute-start(bf16[2,336,128]{2,1,0:T(8,128)(2,1)S(1)} %slice.129), channel_id=1, source_target_pairs={{0,4},{1,5},{2,6},{3,7},{4,0},{5,1},{6,2},{7,3},{8,12},{9,13},{10,... | collective-permute-start | bytes 516104 | tf_op jit(solution)/shard_map/ppermute | solution.py:50
  165.8 5.5 %collective-permute-start.14 = (bf16[2,336,128]{2,1,0:T(8,128)(2,1)S(1)}, bf16[2,336,128]{2,1,0:T(8,128)(2,1)S(1)}, u32[]{:S(2)}, u32[]{:S(2)}) collective-permute-start(bf16[2,336,128]{2,1,0:T(8,128)(2,1)S(1)} %slice.130), channel_id=1, source_target_pairs={{0,2},{1,3},{2,0},{3,1},{4,6},{5,7},{6,4},{7,5},{8,10},{9,11},{10,... | collective-permute-start | bytes 516104 | tf_op jit(solution)/shard_map/ppermute | solution.py:50
  171.3 3.2 %collective-permute-start.15 = (bf16[16,336,128]{2,1,0:T(8,128)(2,1)S(1)}, bf16[16,336,128]{2,1,0:T(8,128)(2,1)S(1)}, u32[]{:S(2)}, u32[]{:S(2)}) collective-permute-start(bf16[16,336,128]{2,1,0:T(8,128)(2,1)S(1)} %constant_dynamic-update-slice_fusion.mine_ref), channel_id=1, source_target_pairs={{0,1},{1,0},{2,3},{3,2},{4,5},{5,4},{6,7},{7,6},{8,9},{9,8},{10,11... | collective-permute-start | bytes 4128776 | tf_op jit(solution)/shard_map/ppermute | solution.py:50

commit v2 on v0

v2 whole, which is shorter than its diff:
```python
import functools

import jax
import jax.numpy as jnp
from jax import lax
from jax.experimental import pallas as pl
from jax.experimental.pallas import tpu as pltpu
from jax.sharding import PartitionSpec as P

commit_weight = 0.25
norm_eps = 1e-06
AXES = ("dp", "code")
PARTS = 4


class Grid:
    def __init__(self, n_dp, n_code):
        self.n_dp, self.n_code = n_dp, n_code
        self.outer = n_code // 4
        self.planes = (n_dp // 2) * self.outer
        self.total = n_dp * n_code

    def linear(self, r, i):
        dh, ch = r // self.outer, r % self.outer
        return (dh * 2 + i // 4) * self.n_code + ch * 4 + i % 4

    def perm(self, move):
        return [
            (self.linear(r, i), self.linear(*move(r, i)))
            for r in range(self.planes)
            for i in range(8)
        ]

    def flip(self, bit):
        return self.perm(lambda r, i: (r, i ^ bit))

    def turn(self, k):
        return self.perm(lambda r, i: (r // PARTS * PARTS + (r + k) % PARTS, i))

    def far(self, k):
        groups = self.planes // PARTS
        return self.perm(lambda r, i: ((r // PARTS + k) % groups * PARTS + r % PARTS, i))

    def order(self, x):
        rest = x.shape[2:]
        x = x.reshape(self.n_dp // 2, self.outer, 2, 4, *rest)
        return jnp.swapaxes(x, 1, 2).reshape(self.total, *rest)

    def place(self):
        dp, code = lax.axis_index("dp"), lax.axis_index("code")
        return (dp // 2) * self.outer + code // 4, (dp % 2) * 4 + code % 4


def send(x, perm):
    return lax.ppermute(x, AXES, perm)


def all_gather(grid, own):
    zs = jnp.stack([own] + [send(own, grid.turn(k)) for k in range(1, PARTS)])
    xs, ys = send(zs, grid.flip(2)), send(zs, grid.flip(4))
    cut = PARTS // 2
    near, far = send(xs[:cut], grid.flip(4)), send(ys[cut:], grid.flip(2))
    mine = jnp.concatenate([zs, xs, ys, near, far])
    return mine, send(mine, grid.flip(1))


def vmem(count):
    return [pl.BlockSpec(memory_space=pltpu.VMEM)] * count


SMEM_SPEC = pl.BlockSpec(memory_space=pltpu.SMEM)
LIMIT = pltpu.CompilerParams(vmem_limit_bytes=40 << 20)


def cost(flops, nbytes):
    return pl.CostEstimate(flops=flops, bytes_accessed=nbytes, transcendentals=0)


def spread(x, grid):
    return lax.all_to_all(x, AXES, split_axis=0, concat_axis=0, tiled=True)


def answer_kernel(grid, cap, asked_ref, book_ref, codes_ref, out_ref):
    devices = grid.total
    slots = devices * cap
    entries = book_ref.shape[0]
    asked = jnp.broadcast_to(asked_ref[...][:, None, :], (devices, cap, cap)).reshape(slots, cap)
    place = lax.broadcasted_iota(jnp.int32, (slots, cap), 0) % cap
    lane = lax.broadcasted_iota(jnp.int32, (slots, cap), 1)
    column = jnp.sum(jnp.where(lane == place, asked, 0), axis=1, keepdims=True)
    hit = column == lax.broadcasted_iota(jnp.int32, (slots, entries), 1)
    select = hit.astype(jnp.float32).astype(jnp.bfloat16)
    codes = jnp.dot(select, codes_ref[...], preferred_element_type=jnp.float32)
    rows = jnp.dot(select, book_ref[...], preferred_element_type=jnp.float32)
    feat = rows.shape[1]
    thirds = feat // 256
    rows = rows.reshape(devices, cap, feat)
    block = lax.broadcasted_iota(jnp.int32, (cap, 128), 1) // 32
    turned = {}
    for v in range(2):
        part = codes[:, v * 128 : (v + 1) * 128]
        for s in range(4):
            moved = part if s == 0 else pltpu.roll(part, s * 32, 1)
            turned[v, s] = moved.reshape(devices, cap, 128)
    for r in range(grid.planes):
        for i in range(8):
            dest = grid.linear(r, i)
            v, a = i // 4, i % 4
            halves = []
            for h in range(2):
                value = turned[v, (0 - a) % 4][grid.linear(r, 4 * h)]
                for b in range(1, 4):
                    other = turned[v, (b - a) % 4][grid.linear(r, 4 * h + b)]
                    value = jnp.where(block == b, other, value)
                halves.append(value)
            own = [jnp.concatenate(halves, axis=1)]
            own += [rows[dest][:, t * 256 : (t + 1) * 256] for t in range(thirds)]
            out_ref[dest] = jnp.concatenate(own, axis=0).astype(jnp.bfloat16)


def answer(grid, asked, book, codes):
    devices, cap = asked.shape
    feat = book.shape[1]
    height = cap * (1 + feat // 256)
    return pl.pallas_call(
        functools.partial(answer_kernel, grid, cap),
        out_shape=jax.ShapeDtypeStruct((devices, height, 256), jnp.bfloat16),
        in_specs=vmem(3),
        out_specs=vmem(1)[0],
        compiler_params=LIMIT,
        cost_estimate=cost(2 * devices * cap * book.shape[0] * (feat + 256), 3 << 20),
    )(asked, book, codes)


def weights_kernel(grid, cap, place_ref, got_ref, slot_ref, *refs):
    cots, (own_ref, *send_refs), (acc_ref, xt_ref) = refs[:10], refs[10:-2], refs[-2:]
    devices = grid.total
    slots = devices * cap
    zch = got_ref.shape[2]
    wide = zch // 8
    tokens, channels = cots[0].shape
    i, part = place_ref[0], place_ref[1]
    slices = got_ref[...].astype(jnp.float32)[:, :cap].reshape(slots, zch)
    xt_ref[...] = slices.T
    token = lax.broadcasted_iota(jnp.int32, (1, tokens), 1)
    line, cell = token // 16 % 16, token % 16
    slot_id = lax.broadcasted_iota(jnp.int32, (slots, tokens), 0)
    ones = (lax.broadcasted_iota(jnp.int32, (16, tokens), 0) == 0).astype(jnp.float32)
    whole = {0: cots[0], 2: cots[1], 4: cots[2], 1: cots[5], 3: cots[6], 5: cots[7]}
    for j in range(8):
        member = i ^ j
        xt = xt_ref[pl.ds(pl.multiple_of(member * wide, wide), wide), :].astype(jnp.bfloat16)
        hit = (slot_id == slot_ref[j : j + 1, :]).astype(jnp.float32).astype(jnp.bfloat16)
        quant = jnp.dot(xt, hit, preferred_element_type=jnp.float32)
        taps = []
        for down in (-1, 0, 1):
            for right in (-1, 0, 1):
                shift = (-(down * 16 + right)) % tokens
                moved = quant if shift == 0 else pltpu.roll(quant, shift, 1)
                valid = (line + down >= 0) & (line + down < 16) & (cell + right >= 0) & (cell + right < 16)
                taps.append(moved * valid.astype(jnp.float32))
        left = jnp.concatenate(taps + [ones], axis=0).astype(jnp.bfloat16)
        if j in whole:
            value = jnp.dot(left, whole[j][...], preferred_element_type=jnp.float32)
        else:
            top, bottom = (cots[3], cots[4]) if j == 6 else (cots[8], cots[9])
            cut = tokens // 2
            value = jnp.dot(left[:, :cut], top[...], preferred_element_type=jnp.float32)
            value += jnp.dot(left[:, cut:], bottom[...], preferred_element_type=jnp.float32)
        if j == 0:
            acc_ref[...] = value
        else:
            acc_ref[...] += value
    krows = 9 * wide
    piece = channels // PARTS
    own_ref[...] = acc_ref[:, pl.ds(pl.multiple_of(part * piece, piece), piece)]
    row = lax.broadcasted_iota(jnp.int32, (16, piece), 0)
    for k, send_ref in enumerate(send_refs, 1):
        other = (part + k) % PARTS
        value = acc_ref[:, pl.ds(pl.multiple_of(other * piece, piece), piece)]
        upper = value.astype(jnp.bfloat16).astype(jnp.float32)
        lower = (value - upper)[krows : krows + 1]
        send_ref[:krows] = value[:krows].astype(jnp.bfloat16)
        last = jnp.where(row == 1, lower, value[krows:])
        send_ref[krows:] = last.astype(jnp.bfloat16)


def group_weights(grid, place, got, slot, cots, cap):
    zch, channels = got.shape[2], cots[0].shape[1]
    height = 9 * zch // 8 + 16
    piece = channels // PARTS
    slots = grid.total * cap
    return pl.pallas_call(
        functools.partial(weights_kernel, grid, cap),
        out_shape=[jax.ShapeDtypeStruct((height, piece), jnp.float32)]
        + [jax.ShapeDtypeStruct((height, piece), jnp.bfloat16)] * (PARTS - 1),
        in_specs=[SMEM_SPEC] + vmem(12),
        out_specs=vmem(PARTS),
        scratch_shapes=[
            pltpu.VMEM((height, channels), jnp.float32),
            pltpu.VMEM((zch, slots), jnp.float32),
        ],
        compiler_params=LIMIT,
        cost_estimate=cost(2 * 9 * zch * 512 * channels, 8 << 20),
    )(place, got, slot, *cots)


def own_kernel(grid, cap, got_ref, projector_ref, sums_ref, uses_ref, codes_ref, parts_ref):
    slots = grid.total * cap
    feat, zch = projector_ref.shape
    thirds = feat // 256
    got = got_ref[...].astype(jnp.float32)
    rows = []
    codes = jnp.zeros((slots, zch), jnp.float32)
    for t in range(thirds):
        rows.append(got[:, cap * (t + 1) : cap * (t + 2)].reshape(slots, 256).astype(jnp.bfloat16))
        codes += jnp.dot(
            rows[t], projector_ref[t * 256 : (t + 1) * 256], preferred_element_type=jnp.float32
        )
    codes = codes.astype(jnp.bfloat16)
    codes_ref[...] = codes
    grads = 2.0 * (uses_ref[...] * codes.astype(jnp.float32) - sums_ref[...])
    upper = grads.astype(jnp.bfloat16)
    lower = (grads - upper.astype(jnp.float32)).astype(jnp.bfloat16)
    dims = (((0,), (0,)), ((), ()))
    total = []
    for t in range(thirds):
        value = lax.dot_general(rows[t], upper, dims, preferred_element_type=jnp.float32)
        value += lax.dot_general(rows[t], lower, dims, preferred_element_type=jnp.float32)
        total.append(value.astype(jnp.bfloat16))
    total = jnp.concatenate(total, axis=0)
    prows, wide = feat // 16, zch // 2
    for r in range(grid.planes):
        for i in range(8):
            row, col = proj_place(i, r % PARTS, prows)
            parts_ref[grid.linear(r, i)] = total[row : row + prows, col * wide : (col + 1) * wide]


def proj_place(i, q, prows):
    return (((i // 2) % 2) * 2 + i // 4) * PARTS * prows + q * prows, i % 2


def own_part(grid, got, projector, sums, uses, cap):
    feat, zch = projector.shape
    slots = grid.total * cap
    return pl.pallas_call(
        functools.partial(own_kernel, grid, cap),
        out_shape=(
            jax.ShapeDtypeStruct((slots, zch), jnp.bfloat16),
            jax.ShapeDtypeStruct((grid.total, feat // 16, zch // 2), jnp.bfloat16),
        ),
        in_specs=vmem(4),
        out_specs=tuple(vmem(2)),
        compiler_params=LIMIT,
        cost_estimate=cost(6 * slots * feat * zch, 3 << 20),
    )(got, projector, sums, uses)


def combine_kernel(krows, own_ref, proj_ref, *refs):
    got_refs, out_ref = refs[:-1], refs[-1]
    total = own_ref[...]
    for ref in got_refs:
        total = total + ref[...].astype(jnp.float32)
    kernel = total[:krows]
    proj = jnp.sum(proj_ref[...].astype(jnp.float32), axis=0)
    bias = total[krows : krows + 1] + total[krows + 1 : krows + 2]
    row = lax.broadcasted_iota(jnp.int32, (16, own_ref.shape[1]), 0)
    extra = jnp.zeros(row.shape, jnp.float32)
    sums = (
        bias,
        jnp.sum(kernel * kernel, axis=0, keepdims=True),
        jnp.sum(proj * proj, axis=0, keepdims=True),
    )
    for n, value in enumerate(sums):
        upper = value.astype(jnp.bfloat16).astype(jnp.float32)
        middle = (value - upper).astype(jnp.bfloat16).astype(jnp.float32)
        for k, piece in enumerate((upper, middle, value - upper - middle)):
            extra = jnp.where(row == 3 * n + k, piece, extra)
    out_ref[:krows] = kernel.astype(jnp.bfloat16)
    out_ref[krows : krows + 16] = extra.astype(jnp.bfloat16)
    out_ref[krows + 16 :] = proj.astype(jnp.bfloat16)


def combine(krows, own, got, proj):
    height = own.shape[0] + proj.shape[1]
    return pl.pallas_call(
        functools.partial(combine_kernel, krows),
        out_shape=jax.ShapeDtypeStruct((height, own.shape[1]), jnp.bfloat16),
        in_specs=vmem(2 + len(got)),
        out_specs=vmem(1)[0],
        compiler_params=LIMIT,
    )(own, proj, *got)


def reduce_planes(grid, own, sends, r):
    got = [send(s, grid.turn(k)) for k, s in enumerate(sends, 1)]
    groups = grid.planes // PARTS
    if groups > 1:
        own = own + sum(g.astype(jnp.float32) for g in got)
        rest = [own] + [send(own, grid.far(k)) for k in range(1, groups)]
        order = (r // PARTS - jnp.arange(groups)) % groups
        own = jnp.sum(jnp.take(jnp.stack(rest), order, axis=0), axis=0)
        got = []
    return own, got


def finish_kernel(krows, counts, place_ref, mine_ref, other_ref, kernel_ref, proj_ref, bias_ref, keep_ref):
    i, part = place_ref[0], place_ref[1]
    wide = krows // 9
    prows = mine_ref.shape[1] - krows - 16
    sources = []
    for ref, core in ((mine_ref, 0), (other_ref, 1)):
        for n in range(16):
            place = i ^ (n // 4 * 2 + core)
            q = (part + PARTS - n % 4) % PARTS
            sources.append((ref, n, place, q))
            keep_ref[place * PARTS + q] = ref[n, krows : krows + 16].astype(jnp.float32)
    kept = jnp.sum(keep_ref[...], axis=0)

    def factor(values, count):
        total = jnp.sum(jnp.sum(values, axis=0, keepdims=True), axis=1, keepdims=True)
        return 1.0 / jnp.sqrt(total / count + norm_eps)

    kfactor, pfactor = factor(kept[3:6], counts[0]), factor(kept[6:9], counts[1])
    for ref, n, place, q in sources:
        value = ref[n].astype(jnp.float32)
        lanes = pl.ds(pl.multiple_of(q * 128, 128), 128)
        kernel_ref[:, pl.ds(pl.multiple_of(place * wide, wide), wide), lanes] = (
            value[:krows] * kfactor
        ).reshape(9, wide, 128)
        row, col = proj_place(place, q, prows)
        proj_ref[pl.ds(pl.multiple_of(row, 8), prows), pl.ds(pl.multiple_of(col * 128, 128), 128)] = (
            value[krows + 16 :] * pfactor
        )
    bias = [jnp.sum(keep_ref[q, 0:3], axis=0, keepdims=True) for q in range(PARTS)]
    bias = jnp.concatenate(bias, axis=1)
    bias_ref[...] = bias * factor(bias * bias, counts[2])


def finish(place, mine, other, zch, channels, feat):
    krows = 9 * zch // 8
    counts = (9 * zch * channels, feat * zch, channels)
    return pl.pallas_call(
        functools.partial(finish_kernel, krows, counts),
        out_shape=(
            jax.ShapeDtypeStruct((9, zch, channels), jnp.float32),
            jax.ShapeDtypeStruct((feat, zch), jnp.float32),
            jax.ShapeDtypeStruct((1, channels), jnp.float32),
        ),
        in_specs=[SMEM_SPEC] + vmem(2),
        out_specs=tuple(vmem(3)),
        scratch_shapes=[pltpu.VMEM((32, 16, 128), jnp.float32)],
        compiler_params=LIMIT,
    )(place, mine, other)


def gather_group(grid, own):
    col, row = send(own, grid.flip(2)), send(own, grid.flip(4))
    cut = own.shape[0] // 2
    first, second = send(col[:cut], grid.flip(4)), send(row[cut:], grid.flip(2))
    mine = [own, col, row, first, second]
    return mine + [send(x, grid.flip(1)) for x in mine]


def on_device(
    grid, codebook, projector, latents, wanted, wanted_count, token_pick, kernel, bias, cotangent
):
    devices = grid.total
    images, rows, width, zch = latents.shape
    channels = kernel.shape[3]
    feat = codebook.shape[1]
    cap = wanted.shape[2]
    slots = devices * cap
    tokens = images * rows * width
    r, i = grid.place()
    place = jnp.stack([i, r % PARTS]).astype(jnp.int32)
    asked = spread(wanted.reshape(devices, cap), grid).reshape(devices, cap)
    cots = gather_group(grid, cotangent.reshape(tokens, channels))
    counts = wanted_count.reshape(devices)
    pick = token_pick.reshape(tokens)
    owner = pick // cap
    owner_hit = owner[:, None] == jnp.arange(devices, dtype=jnp.int32)[None, :]
    count = jnp.sum(jnp.where(owner_hit, counts[None, :], 0), axis=1)
    slot = owner * cap + pick % cap % count
    group_slot = slot.reshape(1, tokens)
    for bit in (1, 2, 4):
        group_slot = jnp.concatenate([group_slot, send(group_slot, grid.flip(bit))])
    local_codes = jnp.dot(codebook, projector, preferred_element_type=jnp.float32).astype(
        jnp.bfloat16
    )
    slot_ids = jnp.arange(slots, dtype=jnp.int32)
    onehot = (slot[:, None] == slot_ids[None, :]).astype(jnp.bfloat16)
    sums = lax.dot_general(
        onehot,
        latents.reshape(tokens, zch),
        (((0,), (0,)), ((), ())),
        preferred_element_type=jnp.float32,
    )
    uses = jnp.sum((slot_ids[:, None] == slot[None, :]).astype(jnp.float32), axis=1, keepdims=True)
    got = spread(answer(grid, asked, codebook, local_codes), grid)
    own, *sends = group_weights(grid, place, got, group_slot, cots, cap)
    codes, parts = own_part(grid, got, projector, sums, uses, cap)
    own, received = reduce_planes(grid, own, sends, r)
    parts = spread(parts, grid)
    krows = 9 * zch // 8
    mine, other = all_gather(grid, combine(krows, own, received, parts))
    kernel_step, proj_step, bias_step = finish(place, mine, other, zch, channels, feat)

    quant = jnp.dot(onehot, codes, preferred_element_type=jnp.float32).astype(jnp.bfloat16)
    quant = quant.reshape(images, rows, width, zch)
    quant_f = quant.astype(jnp.float32)
    latent_f = latents.astype(jnp.float32)
    padded = jnp.pad(quant, ((0, 0), (1, 1), (1, 1), (0, 0)))
    padded_grad = jnp.pad(cotangent, ((0, 0), (1, 1), (1, 1), (0, 0)))
    output = jnp.zeros((images, rows, width, channels), jnp.float32)
    grad_input = jnp.zeros((images, rows, width, zch), jnp.float32)
    for row_off in range(3):
        for col_off in range(3):
            window = padded[:, row_off : row_off + rows, col_off : col_off + width]
            output = output + jnp.einsum(
                "nhwc,co->nhwo",
                window,
                kernel[row_off, col_off],
                preferred_element_type=jnp.float32,
            )
            grad_window = padded_grad[
                :, 2 - row_off : 2 - row_off + rows, 2 - col_off : 2 - col_off + width
            ]
            grad_input = grad_input + jnp.einsum(
                "nhwo,co->nhwc",
                grad_window,
                kernel[row_off, col_off],
                preferred_element_type=jnp.float32,
            )
    hidden = (output + bias.astype(jnp.float32)).astype(jnp.bfloat16)
    grad_latents = (grad_input + 2.0 * commit_weight * (latent_f - quant_f)).astype(jnp.bfloat16)
    kernel_step = kernel_step.reshape(3, 3, zch, channels)
    return (hidden, grad_latents, proj_step, kernel_step, bias_step.reshape(channels))


def solution(mesh):
    grid = Grid(mesh.shape["dp"], mesh.shape["code"])
    in_specs = (
        P(("dp", "code"), None),
        P(),
        P(("dp", "code"), None, None, None),
        P(("dp", "code"), None, None),
        P(("dp", "code"), None),
        P(("dp", "code"), None, None),
        P(),
        P(),
        P(("dp", "code"), None, None, None),
    )
    out_specs = (
        P(("dp", "code"), None, None, None),
        P(("dp", "code"), None, None, None),
        P(),
        P(),
        P(),
    )
    return jax.shard_map(
        functools.partial(on_device, grid),
        mesh=mesh,
        in_specs=in_specs,
        out_specs=out_specs,
        check_vma=False,
    )
```

time: 273 us -> 108 us (0.40)
  waiting for transfers between devices: 152 us -> 27.8 us
  blocking collectives: 40.5 us -> 0 us
  starting transfers between devices: 14.6 us -> 40.2 us
  between operations: 16.4 us -> 1.15 us
  other arithmetic: 14.6 us -> 1.42 us
  matrix products: 28.9 us -> 17.2 us
  Pallas kernels: 0 us -> 11.2 us
    psum x1 -> x0, waiting for transfers between devices: 141 us -> none  [on_device(): lax.psum((grad_proj, grad_kernel, grad_bias), ('dp', 'code'))]
    psum x1 -> x0, blocking collectives: 40.5 us -> none  [on_device(): lax.psum((grad_proj, grad_kernel, grad_bias), ('dp', 'code'))]
    ppermute x0 -> x23, waiting for transfers between devices: none -> 27.8 us  [send(): return lax.ppermute(x, AXES, perm)]
    ppermute x0 -> x23, starting transfers between devices: none -> 27 us  [send(): return lax.ppermute(x, AXES, perm)]
    dot_general x17 -> x3, matrix products: 16.5 us -> 2.87 us  [the longest x1 1.36 us: on_device(): lax.dot_general(onehot, latents.reshape(tokens, zch), (((0,), (0,)), ((),...]
    pallas_call x0 -> x5, Pallas kernels: none -> 11.2 us  [the longest x1 5.15 us: group_weights(): pl.pallas_call(functools.partial(weights_kernel, grid, cap), out_shape=[j...]
    all_to_all x3, waiting for transfers between devices: 10.4 us -> 0.01 us  [spread(): return lax.all_to_all(x, AXES, split_axis=0, concat_axis=0, tiled=True)]
    reduce_sum x4 -> x1, other arithmetic: 6.71 us -> 0.13 us  [on_device(): jnp.sum((slot_ids[:, None] == slot[None, :]).astype(jnp.float32), axis=1,...]
  transfers between devices with their start and end apart: 4 -> 26, of which waited for: 3 -> 8; matrix products, arithmetic and copies ran while one was open for 8% -> 22% of each run, Pallas kernels for 0% -> 7%
where the time goes in v2:
time: 108 us; the launch traced here: 107 us
  starting transfers between devices  40.2 us (37%)
  waiting for transfers between devices  27.8 us (26%)
  matrix products  17.2 us (16%)
  Pallas kernels  11.2 us (10%)
  local copies, waits for them, and re-layouts  7.82 us (7%)
  other arithmetic  1.42 us (1%)
  between operations  1.15 us (1%)
    ppermute x23, waiting for transfers between devices, send(): return lax.ppermute(x, AXES, perm)  27.8 us
    ppermute x23, starting transfers between devices, send(): return lax.ppermute(x, AXES, perm)  27 us
    all_to_all x3, starting transfers between devices, spread(): return lax.all_to_all(x, AXES, split_axis=0, concat_axis=0, tiled=True)  13.2 us
    dot_general x9, matrix products, on_device(): jnp.einsum('nhwc,co->nhwo', window, kernel[row_off, col_off], preferred_e...  7.36 us
    dot_general x9, matrix products, on_device(): jnp.einsum('nhwo,co->nhwc', grad_window, kernel[row_off, col_off], prefer...  6.94 us
    pallas_call x1, Pallas kernels, group_weights(): pl.pallas_call(functools.partial(weights_kernel, grid, cap), out_shape=[j...  5.15 us
    unnamed x34, local copies, waits for them, and re-layouts  4.6 us
    pallas_call x1, Pallas kernels, finish(): pl.pallas_call(functools.partial(finish_kernel, krows, counts), out_shape...  3.62 us
  transfers between devices with their start and end apart: 26, of which 8 were waited for; matrix products, arithmetic and copies ran while one was open for 22% of the time, Pallas kernels for 7%

profile of v2, /device:TPU:0, one launch (start us, length us, event | category | flops | bytes accessed | tf_op | source)
XLA Modules:
  0.0 106.8 jit_solution(843578249899509465)
XLA Ops:
  0.6 3.0 %collective-permute-start.3 = (bf16[512,512]{1,0:T(8,128)(2,1)}, bf16[512,512]{1,0:T(8,128)(2,1)S(1)}, u32[]{:S(2)}, u32[]{:S(2)}) collective-permute-start(bf16[512,512]{1,0:T(8,128)(2,1)} %bitcast.107), channel_id=1, source_target_pairs={{0,2},{1,3},{2,0},{3,1},{4,6},{5,7},{6,4},{7,5},{8,10},{9,11},{10,... | collective-permute-start | bytes 1572872 | tf_op jit(solution)/shard_map/ppermute | solution.py:55
  3.6 1.5 %collective-permute-start.4 = (bf16[512,512]{1,0:T(8,128)(2,1)}, bf16[512,512]{1,0:T(8,128)(2,1)S(1)}, u32[]{:S(2)}, u32[]{:S(2)}) collective-permute-start(bf16[512,512]{1,0:T(8,128)(2,1)} %bitcast.108), channel_id=1, source_target_pairs={{0,4},{1,5},{2,6},{3,7},{4,0},{5,1},{6,2},{7,3},{8,12},{9,13},{10,... | collective-permute-start | bytes 1572872 | tf_op jit(solution)/shard_map/ppermute | solution.py:55
  5.2 0.8 reshape.249
  6.0 0.8 reshape.252
  6.8 0.7 select_reduce_fusion
  7.5 0.2 fusion.47
  7.8 0.6 collective-permute-start
  8.3 1.4 %copy.19 = s32[1,32,8]{2,1,0:T(8,128)} copy(s32[1,32,8]{1,2,0:T(8,128)} %param.12) | data formatting | bytes 2048 | tf_op args[3]
  9.7 4.0 %all-to-all-start = ((s32[32,1,8]{2,1,0:T(1,128)}), s32[32,1,8]{2,1,0:T(1,128)S(1)}, u32[]{:S(2)}, u32[]{:S(2)}) async-start(s32[32,1,8]{2,1,0:T(1,128)} %bitcast.1), calls=%async_computation | async-start | bytes 32768 | tf_op jit(solution)/shard_map/all_to_all | solution.py:80
  13.7 1.6 %fusion.4 = f32[2,16,16,256]{3,2,1,0:T(8,128)S(1)} fusion(bf16[2,16,16,512]{3,2,1,0:T(8,128)(2,1)} %param.17, bf16[3,3,256,512]{3,2,1,0:T(8,128)(2,1)} %param.15), kind=kOutput, calls=%fused_computation.38 | convolution fusion | flops 134217728 | bytes 1310720 | tf_op jit(solution)/shard_map/nhwo,co->nhwc/dot_general | solution.py:429
  15.3 1.4 %convolution_add_fusion.15 = f32[2,16,16,256]{3,2,1,0:T(8,128)S(1)} fusion(f32[2,16,16,256]{3,2,1,0:T(8,128)S(1)} %fusion.4, bf16[2,16,16,512]{3,2,1,0:T(8,128)(2,1)} %param.17, bf16[3,3,256,512]{3,2,1,0:T(8,128)(2,1)} %param.15), kind=kOutput, calls=%fused_computation.27 | convolution fusion | flops 134348800 | bytes 1835008 | tf_op jit(solution)/shard_map/nhwo,co->nhwc/dot_general | solution.py:429
  16.8 0.3 convolution_add_fusion.14
  17.1 0.3 convolution_add_fusion.13
  17.5 0.3 convolution_add_fusion.12
  17.8 0.3 convolution_add_fusion.11
  18.2 0.4 convolution_add_fusion.10
  18.8 1.2 %convolution_convert_fusion.codes_ref = bf16[784,256]{1,0:T(8,128)(2,1)} fusion(bf16[784,768]{1,0:T(8,128)(2,1)S(1)} %copy-done.1, bf16[768,256]{1,0:T(8,128)(2,1)S(1)} %copy-done.4), kind=kOutput, calls=%fused_computation.18 | convolution fusion | flops 308482048 | bytes 1998848 | tf_op jit(solution)/shard_map/dot_general | solution.py:388
  20.0 1.1 %convolution_add_fusion.9 = f32[2,16,16,256]{3,2,1,0:T(8,128)} fusion(f32[2,16,16,256]{3,2,1,0:T(8,128)S(1)} %convolution_add_fusion.10, bf16[2,16,16,512]{3,2,1,0:T(8,128)(2,1)S(1)} %copy-done, bf16[3,3,256,512]{3,2,1,0:T(8,128)(2,1)S(1)} %copy-done.8), kind=kOutput, calls=%fused_computation.21 | convolution fusion | flops 134348800 | bytes 1835008 | tf_op jit(solution)/shard_map/nhwo,co->nhwc/dot_general | solution.py:429
  21.2 1.0 copy-done.2
  22.2 1.6 %shard_map.128 = bf16[32,32,256]{2,1,0:T(8,128)(2,1)} custom-call(s32[32,8]{1,0:T(8,128)S(1)} %bitcast.112, bf16[784,768]{1,0:T(8,128)(2,1)S(1)} %copy-done.1, bf16[784,256]{1,0:T(8,128)(2,1)S(1)} %copy-done.2), custom_call_target="tpu_custom_call" | custom-call | flops 411041792 | bytes 3145728 | tf_op jit(solution)/shard_map/pallas_call | solution.py:125
  23.8 5.8 %all-to-all-start.1 = ((bf16[32,32,256]{2,1,0:T(8,128)(2,1)}), bf16[32,32,256]{2,1,0:T(8,128)(2,1)S(1)}, u32[]{:S(2)}, u32[]{:S(2)}) async-start(bf16[32,32,256]{2,1,0:T(8,128)(2,1)} %shard_map.128), calls=%async_computation.1 | async-start | bytes 1048576 | tf_op jit(solution)/shard_map/all_to_all | solution.py:80
  29.7 1.4 %fusion.5.sums_ref = f32[256,256]{1,0:T(8,128)S(1)} fusion(bf16[512,256]{1,0:T(8,128)(2,1)} %bitcast.123, s32[512]{0:T(512)S(1)} %fusion.46), kind=kOutput, calls=%fused_computation.42 | convolution fusion | flops 67239936 | bytes 526336 | tf_op jit(solution)/shard_map/dot_general | solution.py:393
  31.1 1.8 %collective-permute-start.1 = (s32[2,512]{1,0:T(2,128)S(1)}, s32[2,512]{1,0:T(2,128)S(1)}, u32[]{:S(2)}, u32[]{:S(2)}) collective-permute-start(s32[2,512]{1,0:T(2,128)S(1)} %pad_add_fusion.2), channel_id=1, source_target_pairs={{0,2},{1,3},{2,0},{3,1},{4,6},{5,7},{6,4},{7,5},{8,10},{9,11},{10,... | collective-permute-start | bytes 12296 | tf_op jit(solution)/shard_map/ppermute | solution.py:55
  33.2 0.7 slice.127
  33.9 1.5 %collective-permute-start.5 = (bf16[256,512]{1,0:T(8,128)(2,1)}, bf16[256,512]{1,0:T(8,128)(2,1)S(1)}, u32[]{:S(2)}, u32[]{:S(2)}) collective-permute-start(bf16[256,512]{1,0:T(8,128)(2,1)} %slice.127), channel_id=1, source_target_pairs={{0,4},{1,5},{2,6},{3,7},{4,0},{5,1},{6,2},{7,3},{8,12},{9,13},{10,... | collective-permute-start | bytes 786440 | tf_op jit(solution)/shard_map/ppermute | solution.py:55
  35.4 0.7 slice.128
  36.1 0.6 collective-permute-start.6
  36.7 0.3 collective-permute-start.2
  37.2 8.1 %collective-permute-done.2 = s32[4,512]{1,0:T(4,128)S(1)} collective-permute-done((s32[4,512]{1,0:T(4,128)S(1)}, s32[4,512]{1,0:T(4,128)S(1)}, u32[]{:S(2)}, u32[]{:S(2)}) %collective-permute-start.2) | collective-permute-done | bytes 8224 | tf_op jit(solution)/shard_map/ppermute | solution.py:55
  45.5 0.5 collective-permute-start.9
  46.0 0.4 collective-permute-start.11
  46.5 1.0 copy-done.5
  47.5 0.7 shard_map.129
  48.2 0.7 copy-done.3
  49.0 3.4 %all-to-all-start.2 = ((bf16[32,48,128]{2,1,0:T(8,128)(2,1)}), bf16[32,48,128]{2,1,0:T(8,128)(2,1)S(1)}, u32[]{:S(2)}, u32[]{:S(2)}) async-start(bf16[32,48,128]{2,1,0:T(8,128)(2,1)} %copy-done.3), calls=%async_computation.2 | async-start | bytes 786432 | tf_op jit(solution)/shard_map/all_to_all | solution.py:80
  52.4 0.3 convolution_convert_fusion.1
  52.7 1.3 %fusion.6 = f32[2,16,16,512]{3,2,1,0:T(8,128)S(1)} fusion(bf16[2,16,16,256]{3,2,1,0:T(8,128)(2,1)S(1)} %bitcast.113, bf16[3,3,256,512]{3,2,1,0:T(8,128)(2,1)} %param.15), kind=kOutput, calls=%fused_computation.44 | convolution fusion | flops 134217728 | bytes 1572864 | tf_op jit(solution)/shard_map/nhwc,co->nhwo/dot_general | solution.py:420
  54.0 1.2 %convolution_add_fusion.7 = f32[2,16,16,512]{3,2,1,0:T(8,128)S(1)} fusion(f32[2,16,16,512]{3,2,1,0:T(8,128)S(1)} %fusion.6, bf16[2,16,16,256]{3,2,1,0:T(8,128)(2,1)S(1)} %bitcast.114, bf16[3,3,256,512]{3,2,1,0:T(8,128)(2,1)} %param.15), kind=kOutput, calls=%fused_computation.16 | convolution fusion | flops 134479872 | bytes 2621440 | tf_op jit(solution)/shard_map/nhwc,co->nhwo/dot_general | solution.py:420
  55.3 1.3 %convolution_add_fusion.6 = f32[2,16,16,512]{3,2,1,0:T(8,128)S(1)} fusion(f32[2,16,16,512]{3,2,1,0:T(8,128)S(1)} %convolution_add_fusion.7, bf16[2,16,16,256]{3,2,1,0:T(8,128)(2,1)S(1)} %bitcast.115, bf16[3,3,256,512]{3,2,1,0:T(8,128)(2,1)} %param.15), kind=kOutput, calls=%fused_computation.15 | convolution fusion | flops 134479872 | bytes 2621440 | tf_op jit(solution)/shard_map/nhwc,co->nhwo/dot_general | solution.py:420
  56.6 5.1 %shard_map.130 = (f32[304,128]{1,0:T(8,128)S(1)}, bf16[304,128]{1,0:T(8,128)(2,1)S(1)}, bf16[304,128]{1,0:T(8,128)(2,1)S(1)}, bf16[304,128]{1,0:T(8,128)(2,1)S(1)}) custom-call(s32[2]{0:T(128)S(1)} %pad_add_fusion.3.place_ref, bf16[32,32,256]{2,1,0:T(8,128)(2,1)S(1)} %all-to-all-done.1.got_ref, s32[8,512]{1,0:T(8,128)S(1)} %pad_add_fusion.slot_ref, ...), custom_call_target="tpu_custom_call" | custom-call | flops 1207959552 | bytes 8388608 | tf_op jit(solution)/shard_map/pallas_call | solution.py:193
  61.7 1.8 %collective-permute-start.12 = (bf16[304,128]{1,0:T(8,128)(2,1)S(1)}, bf16[304,128]{1,0:T(8,128)(2,1)S(1)}, u32[]{:S(2)}, u32[]{:S(2)}) collective-permute-start(bf16[304,128]{1,0:T(8,128)(2,1)S(1)} %get-tuple-element.17), channel_id=1, source_target_pairs={{0,8},{1,9},{2,10},{3,11},{4,12},{5,13},{6,14},{7,15},{8,16},{9,17... | collective-permute-start | bytes 233480 | tf_op jit(solution)/shard_map/ppermute | solution.py:55
  63.6 2.4 %collective-permute-start.13 = (bf16[304,128]{1,0:T(8,128)(2,1)S(1)}, bf16[304,128]{1,0:T(8,128)(2,1)S(1)}, u32[]{:S(2)}, u32[]{:S(2)}) collective-permute-start(bf16[304,128]{1,0:T(8,128)(2,1)S(1)} %get-tuple-element.18), channel_id=1, source_target_pairs={{0,16},{1,17},{2,18},{3,19},{4,20},{5,21},{6,22},{7,23},{8,24},{9,... | collective-permute-start | bytes 233480 | tf_op jit(solution)/shard_map/ppermute | solution.py:55
  66.0 1.4 %collective-permute-start.14 = (bf16[304,128]{1,0:T(8,128)(2,1)S(1)}, bf16[304,128]{1,0:T(8,128)(2,1)S(1)}, u32[]{:S(2)}, u32[]{:S(2)}) collective-permute-start(bf16[304,128]{1,0:T(8,128)(2,1)S(1)} %get-tuple-element.19), channel_id=1, source_target_pairs={{0,24},{1,25},{2,26},{3,27},{4,28},{5,29},{6,30},{7,31},{8,0},{9,1... | collective-permute-start | bytes 233480 | tf_op jit(solution)/shard_map/ppermute | solution.py:55
  67.4 1.2 %convolution_add_fusion.5 = f32[2,16,16,512]{3,2,1,0:T(8,128)S(1)} fusion(f32[2,16,16,512]{3,2,1,0:T(8,128)S(1)} %convolution_add_fusion.6, bf16[2,16,16,256]{3,2,1,0:T(8,128)(2,1)S(1)} %bitcast.116, bf16[3,3,256,512]{3,2,1,0:T(8,128)(2,1)} %param.15), kind=kOutput, calls=%fused_computation.14 | convolution fusion | flops 134479872 | bytes 2621440 | tf_op jit(solution)/shard_map/nhwc,co->nhwo/dot_general | solution.py:420
  68.7 2.9 %collective-permute-done.13.refs_1_ = bf16[304,128]{1,0:T(8,128)(2,1)S(1)} collective-permute-done((bf16[304,128]{1,0:T(8,128)(2,1)S(1)}, bf16[304,128]{1,0:T(8,128)(2,1)S(1)}, u32[]{:S(2)}, u32[]{:S(2)}) %collective-permute-start.13) | collective-permute-done | bytes 77856 | tf_op jit(solution)/shard_map/ppermute | solution.py:55
  71.9 2.0 %collective-permute-start.15 = (bf16[352,128]{1,0:T(8,128)(2,1)S(1)}, bf16[352,128]{1,0:T(8,128)(2,1)S(1)}, u32[]{:S(2)}, u32[]{:S(2)}) collective-permute-start(bf16[352,128]{1,0:T(8,128)(2,1)S(1)} %shard_map.131), channel_id=1, source_target_pairs={{0,8},{1,9},{2,10},{3,11},{4,12},{5,13},{6,14},{7,15},{8,16},{9,17... | collective-permute-start | bytes 270344 | tf_op jit(solution)/shard_map/ppermute | solution.py:55
  73.9 1.7 %collective-permute-start.16 = (bf16[352,128]{1,0:T(8,128)(2,1)S(1)}, bf16[352,128]{1,0:T(8,128)(2,1)S(1)}, u32[]{:S(2)}, u32[]{:S(2)}) collective-permute-start(bf16[352,128]{1,0:T(8,128)(2,1)S(1)} %shard_map.131), channel_id=1, source_target_pairs={{0,16},{1,17},{2,18},{3,19},{4,20},{5,21},{6,22},{7,23},{8,24},{9,... | collective-permute-start | bytes 270344 | tf_op jit(solution)/shard_map/ppermute | solution.py:55
  75.6 0.8 collective-permute-start.17
  76.3 3.0 %collective-permute-done.15 = bf16[352,128]{1,0:T(8,128)(2,1)S(1)} collective-permute-done((bf16[352,128]{1,0:T(8,128)(2,1)S(1)}, bf16[352,128]{1,0:T(8,128)(2,1)S(1)}, u32[]{:S(2)}, u32[]{:S(2)}) %collective-permute-start.15) | collective-permute-done | bytes 90144 | tf_op jit(solution)/shard_map/ppermute | solution.py:55
  79.3 2.6 %collective-permute-done.16 = bf16[352,128]{1,0:T(8,128)(2,1)S(1)} collective-permute-done((bf16[352,128]{1,0:T(8,128)(2,1)S(1)}, bf16[352,128]{1,0:T(8,128)(2,1)S(1)}, u32[]{:S(2)}, u32[]{:S(2)}) %collective-permute-start.16) | collective-permute-done | bytes 90144 | tf_op jit(solution)/shard_map/ppermute | solution.py:55
  82.0 1.7 %collective-permute-start.18 = (bf16[4,352,128]{2,1,0:T(8,128)(2,1)S(1)}, bf16[4,352,128]{2,1,0:T(8,128)(2,1)S(1)}, u32[]{:S(2)}, u32[]{:S(2)}) collective-permute-start(bf16[4,352,128]{2,1,0:T(8,128)(2,1)S(1)} %pad_maximum_fusion), channel_id=1, source_target_pairs={{0,2},{1,3},{2,0},{3,1},{4,6},{5,7},{6,4},{7,5},{8,10},{9,11},{10,... | collective-permute-start | bytes 1081352 | tf_op jit(solution)/shard_map/ppermute | solution.py:55
  83.7 1.5 %collective-permute-start.19 = (bf16[4,352,128]{2,1,0:T(8,128)(2,1)S(1)}, bf16[4,352,128]{2,1,0:T(8,128)(2,1)S(1)}, u32[]{:S(2)}, u32[]{:S(2)}) collective-permute-start(bf16[4,352,128]{2,1,0:T(8,128)(2,1)S(1)} %pad_maximum_fusion), channel_id=1, source_target_pairs={{0,4},{1,5},{2,6},{3,7},{4,0},{5,1},{6,2},{7,3},{8,12},{9,13},{10,... | collective-permute-start | bytes 1081352 | tf_op jit(solution)/shard_map/ppermute | solution.py:55
  85.3 7.0 %collective-permute-done.18 = bf16[4,352,128]{2,1,0:T(8,128)(2,1)S(1)} collective-permute-done((bf16[4,352,128]{2,1,0:T(8,128)(2,1)S(1)}, bf16[4,352,128]{2,1,0:T(8,128)(2,1)S(1)}, u32[]{:S(2)}, u32[]{:S(2)}) %collective-permute-start.18) | collective-permute-done | bytes 360480 | tf_op jit(solution)/shard_map/ppermute | solution.py:55
  92.3 1.7 %collective-permute-start.20 = (bf16[2,352,128]{2,1,0:T(8,128)(2,1)S(1)}, bf16[2,352,128]{2,1,0:T(8,128)(2,1)S(1)}, u32[]{:S(2)}, u32[]{:S(2)}) collective-permute-start(bf16[2,352,128]{2,1,0:T(8,128)(2,1)S(1)} %slice.129), channel_id=1, source_target_pairs={{0,4},{1,5},{2,6},{3,7},{4,0},{5,1},{6,2},{7,3},{8,12},{9,13},{10,... | collective-permute-start | bytes 540680 | tf_op jit(solution)/shard_map/ppermute | solution.py:55
  94.1 1.5 %collective-permute-start.21 = (bf16[2,352,128]{2,1,0:T(8,128)(2,1)S(1)}, bf16[2,352,128]{2,1,0:T(8,128)(2,1)S(1)}, u32[]{:S(2)}, u32[]{:S(2)}) collective-permute-start(bf16[2,352,128]{2,1,0:T(8,128)(2,1)S(1)} %slice.130), channel_id=1, source_target_pairs={{0,2},{1,3},{2,0},{3,1},{4,6},{5,7},{6,4},{7,5},{8,10},{9,11},{10,... | collective-permute-start | bytes 540680 | tf_op jit(solution)/shard_map/ppermute | solution.py:55
  95.7 2.2 %collective-permute-done.20 = bf16[2,352,128]{2,1,0:T(8,128)(2,1)S(1)} collective-permute-done((bf16[2,352,128]{2,1,0:T(8,128)(2,1)S(1)}, bf16[2,352,128]{2,1,0:T(8,128)(2,1)S(1)}, u32[]{:S(2)}, u32[]{:S(2)}) %collective-permute-start.20) | collective-permute-done | bytes 180256 | tf_op jit(solution)/shard_map/ppermute | solution.py:55
  98.0 1.7 %collective-permute-done.21 = bf16[2,352,128]{2,1,0:T(8,128)(2,1)S(1)} collective-permute-done((bf16[2,352,128]{2,1,0:T(8,128)(2,1)S(1)}, bf16[2,352,128]{2,1,0:T(8,128)(2,1)S(1)}, u32[]{:S(2)}, u32[]{:S(2)}) %collective-permute-start.21) | collective-permute-done | bytes 180256 | tf_op jit(solution)/shard_map/ppermute | solution.py:55
  99.8 1.1 fusion.3
  100.9 0.3 convolution_add_fusion.4
  101.2 0.3 convolution_add_fusion.3
  101.5 0.3 convolution_add_fusion.2
  101.8 0.3 convolution_add_fusion.1
  102.1 1.1 %fusion.1 = bf16[2,16,16,512]{3,2,1,0:T(8,128)(2,1)} fusion(f32[2,16,16,512]{3,2,1,0:T(8,128)S(1)} %convolution_add_fusion.1, f32[512]{0:T(512)S(1)} %convert_element_type.32, bf16[2,16,16,256]{3,2,1,0:T(8,128)(2,1)S(1)} %bitcast.122, bf16[3,3,256,512]{3,2,1,0:T(8,128)(2,1)S(1)} %copy-done.9), kind=kOutput, calls=%fused_computation.17 | convolution fusion | flops 135004160 | bytes 2099200 | tf_op jit(solution)/shard_map/nhwc,co->nhwo/dot_general | solution.py:420
  103.2 3.6 %shard_map.132 = (f32[9,256,512]{2,1,0:T(8,128)}, f32[768,256]{1,0:T(8,128)}, f32[1,512]{1,0:T(1,128)}) custom-call(s32[2]{0:T(128)S(1)} %pad_add_fusion.3.place_ref, bf16[16,352,128]{2,1,0:T(8,128)(2,1)S(1)} %constant_dynamic-update-slice_fusion.mine_ref, bf16[16,352,128]{2,1,0:T(8,128)(2,1)S(1)} %collective-permute-done.22.other_ref), custom_call_target="tpu_custom_call" | custom-call | tf_op jit(solution)/shard_map/pallas_call | solution.py:343
  (67 shorter events, 1.7 us)
Async XLA Ops:
  0.6 16.1 %copy-start = (bf16[2,16,16,512]{3,2,1,0:T(8,128)(2,1)S(1)}, bf16[2,16,16,512]{3,2,1,0:T(8,128)(2,1)}, u32[]{:S(2)}) copy-start(bf16[2,16,16,512]{3,2,1,0:T(8,128)(2,1)} %param.17) | copy-start | bytes 1572868
  0.6 32.5 %collective-permute-start.3 = (bf16[512,512]{1,0:T(8,128)(2,1)}, bf16[512,512]{1,0:T(8,128)(2,1)S(1)}, u32[]{:S(2)}, u32[]{:S(2)}) collective-permute-start(bf16[512,512]{1,0:T(8,128)(2,1)} %bitcast.107), channel_id=1, source_target_pairs={{0,2},{1,3},{2,0},{3,1},{4,6},{5,7},{6,4},{7,5},{8,10},{9,11},{10,... | collective-permute-start | bytes 1572872 | tf_op jit(solution)/shard_map/ppermute | solution.py:55
  3.6 31.7 %collective-permute-start.4 = (bf16[512,512]{1,0:T(8,128)(2,1)}, bf16[512,512]{1,0:T(8,128)(2,1)S(1)}, u32[]{:S(2)}, u32[]{:S(2)}) collective-permute-start(bf16[512,512]{1,0:T(8,128)(2,1)} %bitcast.108), channel_id=1, source_target_pairs={{0,4},{1,5},{2,6},{3,7},{4,0},{5,1},{6,2},{7,3},{8,12},{9,13},{10,... | collective-permute-start | bytes 1572872 | tf_op jit(solution)/shard_map/ppermute | solution.py:55
  5.2 51.4 %collective-permute-start.7 = (bf16[512,512]{1,0:T(8,128)(2,1)}, bf16[512,512]{1,0:T(8,128)(2,1)S(1)}, u32[]{:S(2)}, u32[]{:S(2)}) collective-permute-start(bf16[512,512]{1,0:T(8,128)(2,1)} %bitcast.109), channel_id=1, source_target_pairs={{0,1},{1,0},{2,3},{3,2},{4,5},{5,4},{6,7},{7,6},{8,9},{9,8},{10,11... | collective-permute-start | bytes 1572872 | tf_op jit(solution)/shard_map/ppermute | solution.py:55
  7.8 23.4 %collective-permute-start = (s32[1,512]{1,0:T(1,128)S(1)}, s32[1,512]{1,0:T(1,128)S(1)}, u32[]{:S(2)}, u32[]{:S(2)}) collective-permute-start(s32[1,512]{1,0:T(1,128)S(1)} %fusion.47), channel_id=1, source_target_pairs={{0,1},{1,0},{2,3},{3,2},{4,5},{5,4},{6,7},{7,6},{8,9},{9,8},{10,11... | collective-permute-start | bytes 6152 | tf_op jit(solution)/shard_map/ppermute | solution.py:55
  9.7 11.5 %all-to-all-start = ((s32[32,1,8]{2,1,0:T(1,128)}), s32[32,1,8]{2,1,0:T(1,128)S(1)}, u32[]{:S(2)}, u32[]{:S(2)}) async-start(s32[32,1,8]{2,1,0:T(1,128)} %bitcast.1), calls=%async_computation | async-start | bytes 32768 | tf_op jit(solution)/shard_map/all_to_all | solution.py:80
  13.7 3.1 %copy-start.8 = (bf16[3,3,256,512]{3,2,1,0:T(8,128)(2,1)S(1)}, bf16[3,3,256,512]{3,2,1,0:T(8,128)(2,1)}, u32[]{:S(2)}) copy-start(bf16[3,3,256,512]{3,2,1,0:T(8,128)(2,1)} %param.15) | copy-start | bytes 7077892
  17.4 1.3 %copy-start.1 = (bf16[784,768]{1,0:T(8,128)(2,1)S(1)}, bf16[784,768]{1,0:T(8,128)(2,1)}, u32[]{:S(2)}) copy-start(bf16[784,768]{1,0:T(8,128)(2,1)} %book_ref.1) | copy-start | bytes 3612676
  17.5 1.3 %copy-start.4 = (bf16[768,256]{1,0:T(8,128)(2,1)S(1)}, bf16[768,256]{1,0:T(8,128)(2,1)}, u32[]{:S(2)}) copy-start(bf16[768,256]{1,0:T(8,128)(2,1)} %projector_ref.1) | copy-start | bytes 1179652
  21.2 1.0 copy-start.2
  22.2 15.0 %copy-start.12 = (bf16[512]{0:T(512)(128)(2,1)S(1)}, bf16[512]{0:T(512)(128)(2,1)}, u32[]{:S(2)}) copy-start(bf16[512]{0:T(512)(128)(2,1)} %param.16) | copy-start | bytes 3076
  23.8 22.7 %all-to-all-start.1 = ((bf16[32,32,256]{2,1,0:T(8,128)(2,1)}), bf16[32,32,256]{2,1,0:T(8,128)(2,1)S(1)}, u32[]{:S(2)}, u32[]{:S(2)}) async-start(bf16[32,32,256]{2,1,0:T(8,128)(2,1)} %shard_map.128), calls=%async_computation.1 | async-start | bytes 1048576 | tf_op jit(solution)/shard_map/all_to_all | solution.py:80
  31.1 5.5 %collective-permute-start.1 = (s32[2,512]{1,0:T(2,128)S(1)}, s32[2,512]{1,0:T(2,128)S(1)}, u32[]{:S(2)}, u32[]{:S(2)}) collective-permute-start(s32[2,512]{1,0:T(2,128)S(1)} %pad_add_fusion.2), channel_id=1, source_target_pairs={{0,2},{1,3},{2,0},{3,1},{4,6},{5,7},{6,4},{7,5},{8,10},{9,11},{10,... | collective-permute-start | bytes 12296 | tf_op jit(solution)/shard_map/ppermute | solution.py:55
  33.9 12.1 %collective-permute-start.5 = (bf16[256,512]{1,0:T(8,128)(2,1)}, bf16[256,512]{1,0:T(8,128)(2,1)S(1)}, u32[]{:S(2)}, u32[]{:S(2)}) collective-permute-start(bf16[256,512]{1,0:T(8,128)(2,1)} %slice.127), channel_id=1, source_target_pairs={{0,4},{1,5},{2,6},{3,7},{4,0},{5,1},{6,2},{7,3},{8,12},{9,13},{10,... | collective-permute-start | bytes 786440 | tf_op jit(solution)/shard_map/ppermute | solution.py:55
  36.1 10.0 %collective-permute-start.6 = (bf16[256,512]{1,0:T(8,128)(2,1)}, bf16[256,512]{1,0:T(8,128)(2,1)}, u32[]{:S(2)}, u32[]{:S(2)}) collective-permute-start(bf16[256,512]{1,0:T(8,128)(2,1)} %slice.128), channel_id=1, source_target_pairs={{0,2},{1,3},{2,0},{3,1},{4,6},{5,7},{6,4},{7,5},{8,10},{9,11},{10,... | collective-permute-start | bytes 786440 | tf_op jit(solution)/shard_map/ppermute | solution.py:55
  36.7 8.7 %collective-permute-start.2 = (s32[4,512]{1,0:T(4,128)S(1)}, s32[4,512]{1,0:T(4,128)S(1)}, u32[]{:S(2)}, u32[]{:S(2)}) collective-permute-start(s32[4,512]{1,0:T(4,128)S(1)} %pad_add_fusion.1), channel_id=1, source_target_pairs={{0,4},{1,5},{2,6},{3,7},{4,0},{5,1},{6,2},{7,3},{8,12},{9,13},{10,... | collective-permute-start | bytes 24584 | tf_op jit(solution)/shard_map/ppermute | solution.py:55
  45.4 11.2 %collective-permute-start.8 = (bf16[512,512]{1,0:T(8,128)(2,1)S(1)}, bf16[512,512]{1,0:T(8,128)(2,1)}, u32[]{:S(2)}, u32[]{:S(2)}) collective-permute-start(bf16[512,512]{1,0:T(8,128)(2,1)S(1)} %collective-permute-done.3.refs_1_), channel_id=1, source_target_pairs={{0,1},{1,0},{2,3},{3,2},{4,5},{5,4},{6,7},{7,6},{8,9},{9,8},{10,11... | collective-permute-start | bytes 1572872 | tf_op jit(solution)/shard_map/ppermute | solution.py:55
  45.5 11.1 %collective-permute-start.9 = (bf16[512,512]{1,0:T(8,128)(2,1)S(1)}, bf16[512,512]{1,0:T(8,128)(2,1)}, u32[]{:S(2)}, u32[]{:S(2)}) collective-permute-start(bf16[512,512]{1,0:T(8,128)(2,1)S(1)} %collective-permute-done.4.refs_2_), channel_id=1, source_target_pairs={{0,1},{1,0},{2,3},{3,2},{4,5},{5,4},{6,7},{7,6},{8,9},{9,8},{10,11... | collective-permute-start | bytes 1572872 | tf_op jit(solution)/shard_map/ppermute | solution.py:55
  46.0 10.6 %collective-permute-start.10 = (bf16[256,512]{1,0:T(8,128)(2,1)S(1)}, bf16[256,512]{1,0:T(8,128)(2,1)}, u32[]{:S(2)}, u32[]{:S(2)}) collective-permute-start(bf16[256,512]{1,0:T(8,128)(2,1)S(1)} %collective-permute-done.5.refs_3_), channel_id=1, source_target_pairs={{0,1},{1,0},{2,3},{3,2},{4,5},{5,4},{6,7},{7,6},{8,9},{9,8},{10,11... | collective-permute-start | bytes 786440 | tf_op jit(solution)/shard_map/ppermute | solution.py:55
  46.0 10.5 %collective-permute-start.11 = (bf16[256,512]{1,0:T(8,128)(2,1)}, bf16[256,512]{1,0:T(8,128)(2,1)}, u32[]{:S(2)}, u32[]{:S(2)}) collective-permute-start(bf16[256,512]{1,0:T(8,128)(2,1)} %collective-permute-done.6.refs_4_), channel_id=1, source_target_pairs={{0,1},{1,0},{2,3},{3,2},{4,5},{5,4},{6,7},{7,6},{8,9},{9,8},{10,11... | collective-permute-start | bytes 786440 | tf_op jit(solution)/shard_map/ppermute | solution.py:55
  46.5 1.0 copy-start.5
  48.2 0.7 copy-start.3
  49.0 22.8 %all-to-all-start.2 = ((bf16[32,48,128]{2,1,0:T(8,128)(2,1)}), bf16[32,48,128]{2,1,0:T(8,128)(2,1)S(1)}, u32[]{:S(2)}, u32[]{:S(2)}) async-start(bf16[32,48,128]{2,1,0:T(8,128)(2,1)} %copy-done.3), calls=%async_computation.2 | async-start | bytes 786432 | tf_op jit(solution)/shard_map/all_to_all | solution.py:80
  52.7 14.7 %copy-start.6 = (bf16[512,256]{1,0:T(8,128)(2,1)}, bf16[512,256]{1,0:T(8,128)(2,1)S(1)}, u32[]{:S(2)}) copy-start(bf16[512,256]{1,0:T(8,128)(2,1)S(1)} %convolution_convert_fusion.1) | copy-start | bytes 786436
  61.7 6.9 %collective-permute-start.12 = (bf16[304,128]{1,0:T(8,128)(2,1)S(1)}, bf16[304,128]{1,0:T(8,128)(2,1)S(1)}, u32[]{:S(2)}, u32[]{:S(2)}) collective-permute-start(bf16[304,128]{1,0:T(8,128)(2,1)S(1)} %get-tuple-element.17), channel_id=1, source_target_pairs={{0,8},{1,9},{2,10},{3,11},{4,12},{5,13},{6,14},{7,15},{8,16},{9,17... | collective-permute-start | bytes 233480 | tf_op jit(solution)/shard_map/ppermute | solution.py:55
  63.6 8.0 %collective-permute-start.13 = (bf16[304,128]{1,0:T(8,128)(2,1)S(1)}, bf16[304,128]{1,0:T(8,128)(2,1)S(1)}, u32[]{:S(2)}, u32[]{:S(2)}) collective-permute-start(bf16[304,128]{1,0:T(8,128)(2,1)S(1)} %get-tuple-element.18), channel_id=1, source_target_pairs={{0,16},{1,17},{2,18},{3,19},{4,20},{5,21},{6,22},{7,23},{8,24},{9,... | collective-permute-start | bytes 233480 | tf_op jit(solution)/shard_map/ppermute | solution.py:55
  66.0 5.8 %collective-permute-start.14 = (bf16[304,128]{1,0:T(8,128)(2,1)S(1)}, bf16[304,128]{1,0:T(8,128)(2,1)S(1)}, u32[]{:S(2)}, u32[]{:S(2)}) collective-permute-start(bf16[304,128]{1,0:T(8,128)(2,1)S(1)} %get-tuple-element.19), channel_id=1, source_target_pairs={{0,24},{1,25},{2,26},{3,27},{4,28},{5,29},{6,30},{7,31},{8,0},{9,1... | collective-permute-start | bytes 233480 | tf_op jit(solution)/shard_map/ppermute | solution.py:55
  71.9 27.9 %copy-start.7 = (bf16[512,256]{1,0:T(8,128)(2,1)S(1)}, bf16[512,256]{1,0:T(8,128)(2,1)}, u32[]{:S(2)}) copy-start(bf16[512,256]{1,0:T(8,128)(2,1)} %copy-done.6) | copy-start | bytes 786436
  71.9 27.9 %copy-start.9 = (bf16[3,3,256,512]{3,2,1,0:T(8,128)(2,1)S(1)}, bf16[3,3,256,512]{3,2,1,0:T(8,128)(2,1)}, u32[]{:S(2)}) copy-start(bf16[3,3,256,512]{3,2,1,0:T(8,128)(2,1)} %param.15) | copy-start | bytes 7077892
  71.9 27.9 %copy-start.10 = (f32[2,16,16,256]{3,2,1,0:T(8,128)S(1)}, f32[2,16,16,256]{3,2,1,0:T(8,128)}, u32[]{:S(2)}) copy-start(f32[2,16,16,256]{3,2,1,0:T(8,128)} %convolution_add_fusion.9) | copy-start | bytes 1572868
  71.9 27.9 %copy-start.11 = (bf16[2,16,16,256]{3,2,1,0:T(8,128)(2,1)S(1)}, bf16[2,16,16,256]{3,2,1,0:T(8,128)(2,1)}, u32[]{:S(2)}) copy-start(bf16[2,16,16,256]{3,2,1,0:T(8,128)(2,1)} %param.11) | copy-start | bytes 786436
  71.9 7.4 %collective-permute-start.15 = (bf16[352,128]{1,0:T(8,128)(2,1)S(1)}, bf16[352,128]{1,0:T(8,128)(2,1)S(1)}, u32[]{:S(2)}, u32[]{:S(2)}) collective-permute-start(bf16[352,128]{1,0:T(8,128)(2,1)S(1)} %shard_map.131), channel_id=1, source_target_pairs={{0,8},{1,9},{2,10},{3,11},{4,12},{5,13},{6,14},{7,15},{8,16},{9,17... | collective-permute-start | bytes 270344 | tf_op jit(solution)/shard_map/ppermute | solution.py:55
  73.9 8.1 %collective-permute-start.16 = (bf16[352,128]{1,0:T(8,128)(2,1)S(1)}, bf16[352,128]{1,0:T(8,128)(2,1)S(1)}, u32[]{:S(2)}, u32[]{:S(2)}) collective-permute-start(bf16[352,128]{1,0:T(8,128)(2,1)S(1)} %shard_map.131), channel_id=1, source_target_pairs={{0,16},{1,17},{2,18},{3,19},{4,20},{5,21},{6,22},{7,23},{8,24},{9,... | collective-permute-start | bytes 270344 | tf_op jit(solution)/shard_map/ppermute | solution.py:55
  75.6 6.4 %collective-permute-start.17 = (bf16[352,128]{1,0:T(8,128)(2,1)S(1)}, bf16[352,128]{1,0:T(8,128)(2,1)S(1)}, u32[]{:S(2)}, u32[]{:S(2)}) collective-permute-start(bf16[352,128]{1,0:T(8,128)(2,1)S(1)} %shard_map.131), channel_id=1, source_target_pairs={{0,24},{1,25},{2,26},{3,27},{4,28},{5,29},{6,30},{7,31},{8,0},{9,1... | collective-permute-start | bytes 270344 | tf_op jit(solution)/shard_map/ppermute | solution.py:55
  82.0 10.3 %collective-permute-start.18 = (bf16[4,352,128]{2,1,0:T(8,128)(2,1)S(1)}, bf16[4,352,128]{2,1,0:T(8,128)(2,1)S(1)}, u32[]{:S(2)}, u32[]{:S(2)}) collective-permute-start(bf16[4,352,128]{2,1,0:T(8,128)(2,1)S(1)} %pad_maximum_fusion), channel_id=1, source_target_pairs={{0,2},{1,3},{2,0},{3,1},{4,6},{5,7},{6,4},{7,5},{8,10},{9,11},{10,... | collective-permute-start | bytes 1081352 | tf_op jit(solution)/shard_map/ppermute | solution.py:55
  83.7 10.3 %collective-permute-start.19 = (bf16[4,352,128]{2,1,0:T(8,128)(2,1)S(1)}, bf16[4,352,128]{2,1,0:T(8,128)(2,1)S(1)}, u32[]{:S(2)}, u32[]{:S(2)}) collective-permute-start(bf16[4,352,128]{2,1,0:T(8,128)(2,1)S(1)} %pad_maximum_fusion), channel_id=1, source_target_pairs={{0,4},{1,5},{2,6},{3,7},{4,0},{5,1},{6,2},{7,3},{8,12},{9,13},{10,... | collective-permute-start | bytes 1081352 | tf_op jit(solution)/shard_map/ppermute | solution.py:55
  92.3 5.6 %collective-permute-start.20 = (bf16[2,352,128]{2,1,0:T(8,128)(2,1)S(1)}, bf16[2,352,128]{2,1,0:T(8,128)(2,1)S(1)}, u32[]{:S(2)}, u32[]{:S(2)}) collective-permute-start(bf16[2,352,128]{2,1,0:T(8,128)(2,1)S(1)} %slice.129), channel_id=1, source_target_pairs={{0,4},{1,5},{2,6},{3,7},{4,0},{5,1},{6,2},{7,3},{8,12},{9,13},{10,... | collective-permute-start | bytes 540680 | tf_op jit(solution)/shard_map/ppermute | solution.py:55
  94.1 5.6 %collective-permute-start.21 = (bf16[2,352,128]{2,1,0:T(8,128)(2,1)S(1)}, bf16[2,352,128]{2,1,0:T(8,128)(2,1)S(1)}, u32[]{:S(2)}, u32[]{:S(2)}) collective-permute-start(bf16[2,352,128]{2,1,0:T(8,128)(2,1)S(1)} %slice.130), channel_id=1, source_target_pairs={{0,2},{1,3},{2,0},{3,1},{4,6},{5,7},{6,4},{7,5},{8,10},{9,11},{10,... | collective-permute-start | bytes 540680 | tf_op jit(solution)/shard_map/ppermute | solution.py:55
  99.7 3.5 %collective-permute-start.22 = (bf16[16,352,128]{2,1,0:T(8,128)(2,1)S(1)}, bf16[16,352,128]{2,1,0:T(8,128)(2,1)S(1)}, u32[]{:S(2)}, u32[]{:S(2)}) collective-permute-start(bf16[16,352,128]{2,1,0:T(8,128)(2,1)S(1)} %constant_dynamic-update-slice_fusion.mine_ref), channel_id=1, source_target_pairs={{0,1},{1,0},{2,3},{3,2},{4,5},{5,4},{6,7},{7,6},{8,9},{9,8},{10,11... | collective-permute-start | bytes 4325384 | tf_op jit(solution)/shard_map/ppermute | solution.py:55

commit v3 on v2

v3 whole, which is shorter than its diff:
```python
import functools

import jax
import jax.numpy as jnp
from jax import lax
from jax.experimental import pallas as pl
from jax.experimental.pallas import tpu as pltpu
from jax.sharding import PartitionSpec as P

commit_weight = 0.25
norm_eps = 1e-06
AXES = ("dp", "code")
PARTS = 4


class Grid:
    def __init__(self, n_dp, n_code):
        self.n_dp, self.n_code = n_dp, n_code
        self.outer = n_code // 4
        self.planes = (n_dp // 2) * self.outer
        self.total = n_dp * n_code

    def linear(self, r, i):
        dh, ch = r // self.outer, r % self.outer
        return (dh * 2 + i // 4) * self.n_code + ch * 4 + i % 4

    def perm(self, move):
        return [
            (self.linear(r, i), self.linear(*move(r, i)))
            for r in range(self.planes)
            for i in range(8)
        ]

    def flip(self, bit):
        return self.perm(lambda r, i: (r, i ^ bit))

    def turn(self, k):
        return self.perm(lambda r, i: (r // PARTS * PARTS + (r + k) % PARTS, i))

    def far(self, k):
        groups = self.planes // PARTS
        return self.perm(lambda r, i: ((r // PARTS + k) % groups * PARTS + r % PARTS, i))

    def order(self, x):
        rest = x.shape[2:]
        x = x.reshape(self.n_dp // 2, self.outer, 2, 4, *rest)
        return jnp.swapaxes(x, 1, 2).reshape(self.total, *rest)

    def place(self):
        dp, code = lax.axis_index("dp"), lax.axis_index("code")
        return (dp // 2) * self.outer + code // 4, (dp % 2) * 4 + code % 4


def send(x, perm):
    return lax.ppermute(x, AXES, perm)


def gather_planes(grid, own):
    zs = [send(own, grid.turn(k)) for k in range(1, PARTS)]
    x, y = send(own, grid.flip(2)), send(own, grid.flip(4))
    early = jnp.stack([own, x, y, send(x, grid.flip(4))])
    zs = jnp.stack(zs)
    return early, zs, send(zs, grid.flip(2)), send(zs, grid.flip(4))


def gather_places(grid, early, zs, xs, ys):
    second, first = send(ys[:2], grid.flip(2)), send(xs[2:], grid.flip(4))
    mine = [early, jnp.concatenate([zs, xs, ys]), jnp.concatenate([second, first])]
    return mine + [send(x, grid.flip(1)) for x in mine]


def vmem(count):
    return [pl.BlockSpec(memory_space=pltpu.VMEM)] * count


SMEM_SPEC = pl.BlockSpec(memory_space=pltpu.SMEM)
LIMIT = pltpu.CompilerParams(vmem_limit_bytes=40 << 20)


def cost(flops, nbytes):
    return pl.CostEstimate(flops=flops, bytes_accessed=nbytes, transcendentals=0)


def spread(x, grid):
    return lax.all_to_all(x, AXES, split_axis=0, concat_axis=0, tiled=True)


def token_kernel(
    cap, place_ref, pick_hbm, counts_hbm, wanted_hbm, latents_hbm, cot_hbm, near_ref, far_ref, slot_ref, ask_ref, *rest
):
    pick_ref, counts_ref, wanted_ref, latents_ref, cot_ref, sems = rest
    sources = (pick_hbm, counts_hbm, wanted_hbm, latents_hbm, cot_hbm)
    copies = [
        pltpu.make_async_copy(source, target, sems.at[n])
        for n, (source, target) in enumerate(zip(sources, rest[:-1]))
    ]
    for copy in copies:
        copy.start()
    for copy in copies[:4]:
        copy.wait()
    lines, width = pick_ref.shape
    devices = counts_ref.shape[1]
    tokens = lines * width
    pick = pick_ref[...]
    owner = pick // cap
    first = pick - owner * cap
    token = lax.broadcasted_iota(jnp.int32, (width, tokens), 1)
    wide = (token % width == lax.broadcasted_iota(jnp.int32, (width, tokens), 0)).astype(jnp.float32)
    wide = wide.astype(jnp.bfloat16)
    token = lax.broadcasted_iota(jnp.int32, (lines, tokens), 1)
    keep = token // width == lax.broadcasted_iota(jnp.int32, (lines, tokens), 0)

    def flat(x):
        x = x.astype(jnp.float32).astype(jnp.bfloat16)
        x = jnp.dot(x, wide, preferred_element_type=jnp.float32)
        return jnp.sum(jnp.where(keep, x, 0.0), axis=0, keepdims=True)

    owner, entry = flat(owner), flat(first)
    row = lax.broadcasted_iota(jnp.int32, (devices, devices), 0)
    col = lax.broadcasted_iota(jnp.int32, (devices, devices), 1)
    counts = jnp.where(row == col, counts_ref[...].astype(jnp.float32), 0.0)
    counts = jnp.sum(counts, axis=1, keepdims=True)
    owner_id = lax.broadcasted_iota(jnp.int32, (devices, tokens), 0)
    count = jnp.sum(
        jnp.where(owner_id == owner.astype(jnp.int32), counts, 0.0), axis=0, keepdims=True
    )
    for _ in range(cap - 1):
        entry = jnp.where(entry >= count, entry - count, entry)
    slot = (owner * cap + entry).astype(jnp.int32)
    slot_ref[...] = slot
    place = lax.broadcasted_iota(jnp.int32, (16, tokens), 0)
    wide = cot_ref.shape[1] // 2
    place = place[:, :wide]
    extra = jnp.zeros((16, wide), jnp.float32)
    for n, row in enumerate((owner[:, :wide], owner[:, wide:], entry[:, :wide], entry[:, wide:])):
        extra = jnp.where(place == n, row, extra)
    copies[4].wait()
    for ref, side in ((near_ref, place_ref[0] // 4), (far_ref, 1 - place_ref[0] // 4)):
        ref[:tokens] = cot_ref[:, pl.ds(pl.multiple_of(side * wide, wide), wide)]
        ref[tokens:] = extra.astype(jnp.bfloat16)
    hit = (lax.broadcasted_iota(jnp.int32, (devices * cap, tokens), 0) == slot).astype(jnp.float32)
    slots = devices * cap
    uses = jnp.sum(hit, axis=1, keepdims=True)
    sums = jnp.dot(hit.astype(jnp.bfloat16), latents_ref[...], preferred_element_type=jnp.float32)
    zch = sums.shape[1]
    wanted = wanted_ref[...].astype(jnp.float32).T
    wanted = jnp.broadcast_to(wanted[:, None, :], (devices, cap, cap)).reshape(slots, cap)
    place = lax.broadcasted_iota(jnp.int32, (slots, cap), 0) % cap
    lane = lax.broadcasted_iota(jnp.int32, (slots, cap), 1)
    wanted = jnp.sum(jnp.where(lane == place, wanted, 0.0), axis=1, keepdims=True)
    lane = lax.broadcasted_iota(jnp.int32, (slots, 128), 1)
    last = jnp.where(lane == 0, uses, jnp.where(lane == 1, wanted, 0.0))
    ask_ref[:, :, :zch] = sums.reshape(devices, cap, zch)
    ask_ref[:, :, zch:] = last.reshape(devices, cap, 128)


def token_part(place, pick, counts, wanted, latents, cots):
    tokens, channels = cots.shape
    cap, devices = wanted.shape
    slots = devices * cap
    return pl.pallas_call(
        functools.partial(token_kernel, cap),
        out_shape=(
            jax.ShapeDtypeStruct((tokens + 16, channels // 2), jnp.bfloat16),
            jax.ShapeDtypeStruct((tokens + 16, channels // 2), jnp.bfloat16),
            jax.ShapeDtypeStruct((1, tokens), jnp.int32),
            jax.ShapeDtypeStruct((devices, cap, latents.shape[1] + 128), jnp.float32),
        ),
        in_specs=[SMEM_SPEC] + [pl.BlockSpec(memory_space=pltpu.HBM)] * 5,
        out_specs=tuple(vmem(4)),
        scratch_shapes=[
            pltpu.VMEM(x.shape, x.dtype) for x in (pick, counts, wanted, latents, cots)
        ]
        + [pltpu.SemaphoreType.DMA((5,))],
        compiler_params=pltpu.CompilerParams(vmem_limit_bytes=62 << 20),
        cost_estimate=cost(2 * slots * tokens * latents.shape[1], 2 << 20),
    )(place, pick, counts, wanted, latents, cots)


def select_rows(asked, zch, entries):
    column = asked[:, zch + 1 : zch + 2].astype(jnp.int32)
    hit = column == lax.broadcasted_iota(jnp.int32, (asked.shape[0], entries), 1)
    return hit.astype(jnp.float32).astype(jnp.bfloat16)


def answer_kernel(grid, cap, asked_ref, codes_ref, out_ref):
    devices = grid.total
    entries, zch = codes_ref.shape
    select = select_rows(asked_ref[...].reshape(devices * cap, zch + 128), zch, entries)
    codes = jnp.dot(select, codes_ref[...], preferred_element_type=jnp.float32)
    whole = codes.reshape(devices, cap, zch)
    second = lax.broadcasted_iota(jnp.int32, (cap, 128), 1) >= 64
    turned = {}
    for v in range(2):
        part = codes[:, v * 128 : (v + 1) * 128]
        turned[v, 0] = part.reshape(devices, cap, 128)
        turned[v, 1] = pltpu.roll(part, 64, 1).reshape(devices, cap, 128)
    for r in range(grid.planes):
        for u in range(4):
            v, a = u // 2, u % 2
            slices = [
                jnp.where(
                    second,
                    turned[v, 1 - a][grid.linear(r, 2 * h + 1)],
                    turned[v, a][grid.linear(r, 2 * h)],
                )
                for h in range(4)
            ]
            for dest in (grid.linear(r, u), grid.linear(r, u + 4)):
                top = jnp.concatenate(slices[:3], axis=1)
                bottom = jnp.concatenate([slices[3], whole[dest]], axis=1)
                out_ref[dest] = jnp.concatenate([top, bottom], axis=0).astype(jnp.bfloat16)


def answer(grid, asked, codes):
    devices, cap, _ = asked.shape
    zch = codes.shape[1]
    return pl.pallas_call(
        functools.partial(answer_kernel, grid, cap),
        out_shape=jax.ShapeDtypeStruct((devices, 2 * cap, 384), jnp.bfloat16),
        in_specs=vmem(2),
        out_specs=vmem(1)[0],
        compiler_params=LIMIT,
        cost_estimate=cost(2 * devices * cap * codes.shape[0] * zch, 2 << 20),
    )(asked, codes)


def proj_kernel(place_ref, asked_ref, book_ref, codes_ref, keep_ref, send_ref, all_ref):
    entries, feat = book_ref.shape
    zch = codes_ref.shape[1]
    devices, cap, _ = asked_ref.shape
    asked = asked_ref[...].reshape(devices * cap, zch + 128)
    select = select_rows(asked, zch, entries)
    codes = jnp.dot(select, codes_ref[...], preferred_element_type=jnp.float32)
    rows = jnp.dot(select, book_ref[...], preferred_element_type=jnp.float32).astype(jnp.bfloat16)
    grads = 2.0 * (asked[:, zch : zch + 1] * codes - asked[:, :zch])
    upper = grads.astype(jnp.bfloat16)
    lower = (grads - upper.astype(jnp.float32)).astype(jnp.bfloat16)
    dims = (((0,), (0,)), ((), ()))
    total = lax.dot_general(rows, upper, dims, preferred_element_type=jnp.float32)
    all_ref[...] = total + lax.dot_general(rows, lower, dims, preferred_element_type=jnp.float32)
    core = place_ref[0] % 2
    keep_ref[...] = all_ref[:, pl.ds(pl.multiple_of(core * 128, 128), 128)]
    send_ref[...] = all_ref[:, pl.ds(pl.multiple_of((1 - core) * 128, 128), 128)]


def proj_part(place, asked, book, codes):
    feat, zch = book.shape[1], codes.shape[1]
    slots = asked.shape[0] * asked.shape[1]
    return pl.pallas_call(
        proj_kernel,
        out_shape=(jax.ShapeDtypeStruct((feat, 128), jnp.float32),) * 2,
        in_specs=[SMEM_SPEC] + vmem(3),
        out_specs=tuple(vmem(2)),
        scratch_shapes=[pltpu.VMEM((feat, zch), jnp.float32)],
        compiler_params=LIMIT,
        cost_estimate=cost(2 * slots * (book.shape[0] + 2 * zch) * feat, 4 << 20),
    )(place, asked, book, codes)


def half(x, axis, index):
    return lax.dynamic_index_in_dim(x, index, axis, keepdims=False)


def exchange(x, own, perm):
    sent = half(x, 0, 1 - own).astype(jnp.bfloat16)
    return half(x, 0, own) + send(sent, perm).astype(jnp.float32)


def proj_place(i, q, prows):
    return (((i // 2) % 2) * 2 + i // 4) * PARTS * prows + q * prows, i % 2


def weights_kernel(grid, cap, place_ref, got_ref, *refs):
    cots, (acc_ref, xt_ref) = refs[:8], refs[8:]
    devices = grid.total
    slots = devices * cap
    tokens, channels = cots[0].shape
    tokens -= 16
    cut = tokens // 2
    i, part = place_ref[0], place_ref[1]
    got = got_ref[...].astype(jnp.float32)
    xt_ref[:384] = got[:, :cap].reshape(slots, 384).T
    xt_ref[384:] = got[:, cap:, :128].reshape(slots, 128).T
    wide = 64
    krows = 9 * wide // 2
    token = lax.broadcasted_iota(jnp.int32, (1, tokens), 1)
    line, cell = token // 16 % 16, token % 16
    slot_id = lax.broadcasted_iota(jnp.int32, (slots, tokens), 0)
    ones = (lax.broadcasted_iota(jnp.int32, (16, tokens), 0) == 0).astype(jnp.float32)
    cots = {j: cots[j % 2 * 4 + j // 2] for j in range(8)}
    for j in range(8):
        member = i ^ j
        xt = xt_ref[pl.ds(pl.multiple_of(member * wide, wide), wide), :].astype(jnp.bfloat16)
        last = cots[j][tokens:].astype(jnp.float32)
        last = last[0:2] * cap + last[2:4]
        slot = jnp.concatenate([last[0:1], last[1:2]], axis=1).astype(jnp.int32)
        hit = (slot_id == slot).astype(jnp.float32).astype(jnp.bfloat16)
        quant = jnp.dot(xt, hit, preferred_element_type=jnp.float32)
        taps = []
        for down in (-1, 0, 1):
            for right in (-1, 0, 1):
                shift = (-(down * 16 + right)) % tokens
                moved = quant if shift == 0 else pltpu.roll(quant, shift, 1)
                valid = (line + down >= 0) & (line + down < 16) & (cell + right >= 0) & (cell + right < 16)
                taps.append(moved * valid.astype(jnp.float32))
        taps = [x[: wide // 2] for x in taps] + [x[wide // 2 :] for x in taps]
        left = jnp.concatenate(taps + [ones], axis=0).astype(jnp.bfloat16)
        value = jnp.dot(left, cots[j][:tokens], preferred_element_type=jnp.float32)
        if j == 0:
            acc_ref[...] = value
        else:
            acc_ref[...] += value


def pack_kernel(krows, place_ref, acc_ref, proj_ref, own_ref, *send_refs):
    part = place_ref[1]

    def piece(q):
        lanes = pl.ds(pl.multiple_of(q % 2 * 128, 128), 128)
        rows = pl.ds(pl.multiple_of(q // 2 * krows, 8), krows)
        return acc_ref[rows, lanes], acc_ref[2 * krows :, lanes]

    own_ref[:krows], own_ref[krows : krows + 16] = piece(part)
    own_ref[krows + 16 :] = proj_ref[part]
    row = lax.broadcasted_iota(jnp.int32, (16, 128), 0)
    for k, send_ref in enumerate(send_refs, 1):
        value, last = piece((part + k) % PARTS)
        upper = last.astype(jnp.bfloat16).astype(jnp.float32)
        lower = (last - upper)[0:1]
        send_ref[:krows] = value.astype(jnp.bfloat16)
        send_ref[krows : krows + 16] = jnp.where(row == 1, lower, last).astype(jnp.bfloat16)
        send_ref[krows + 16 :] = proj_ref[(part + k) % PARTS].astype(jnp.bfloat16)


def group_weights(grid, place, got, cots, cap):
    channels = cots[0].shape[1]
    slots = grid.total * cap
    return pl.pallas_call(
        functools.partial(weights_kernel, grid, cap),
        out_shape=jax.ShapeDtypeStruct((9 * 64 + 16, channels), jnp.float32),
        in_specs=[SMEM_SPEC] + vmem(9),
        out_specs=vmem(1)[0],
        scratch_shapes=[pltpu.VMEM((512, slots), jnp.float32)],
        compiler_params=LIMIT,
        cost_estimate=cost(2 * 9 * 512 * 512 * channels, 8 << 20),
    )(place, got, *cots)


def pack(place, acc, proj):
    krows = (acc.shape[0] - 16) // 2
    height = krows + 16 + proj.shape[1]
    return pl.pallas_call(
        functools.partial(pack_kernel, krows),
        out_shape=[jax.ShapeDtypeStruct((height, 128), jnp.float32)]
        + [jax.ShapeDtypeStruct((height, 128), jnp.bfloat16)] * (PARTS - 1),
        in_specs=[SMEM_SPEC] + vmem(2),
        out_specs=vmem(PARTS),
        compiler_params=LIMIT,
    )(place, acc, proj)


def combine_kernel(krows, own_ref, *refs):
    got_refs, out_ref = refs[:-1], refs[-1]
    total = own_ref[...]
    for ref in got_refs:
        total = total + ref[...].astype(jnp.float32)
    kernel = total[:krows]
    proj = total[krows + 16 :]
    bias = total[krows : krows + 1] + total[krows + 1 : krows + 2]
    row = lax.broadcasted_iota(jnp.int32, (16, own_ref.shape[1]), 0)
    extra = jnp.zeros(row.shape, jnp.float32)
    sums = (
        bias,
        jnp.sum(kernel * kernel, axis=0, keepdims=True),
        jnp.sum(proj * proj, axis=0, keepdims=True),
    )
    for n, value in enumerate(sums):
        upper = value.astype(jnp.bfloat16).astype(jnp.float32)
        middle = (value - upper).astype(jnp.bfloat16).astype(jnp.float32)
        for k, piece in enumerate((upper, middle, value - upper - middle)):
            extra = jnp.where(row == 3 * n + k, piece, extra)
    out_ref[:krows] = kernel.astype(jnp.bfloat16)
    out_ref[krows : krows + 16] = extra.astype(jnp.bfloat16)
    out_ref[krows + 16 :] = proj.astype(jnp.bfloat16)


def combine(krows, own, got):
    return pl.pallas_call(
        functools.partial(combine_kernel, krows),
        out_shape=jax.ShapeDtypeStruct(own.shape, jnp.bfloat16),
        in_specs=vmem(1 + len(got)),
        out_specs=vmem(1)[0],
        compiler_params=LIMIT,
    )(own, *got)


def reduce_planes(grid, own, sends, r):
    got = [send(s, grid.turn(k)) for k, s in enumerate(sends, 1)]
    groups = grid.planes // PARTS
    if groups > 1:
        own = own + sum(g.astype(jnp.float32) for g in got)
        rest = [own] + [send(own, grid.far(k)) for k in range(1, groups)]
        order = (r // PARTS - jnp.arange(groups)) % groups
        own = jnp.sum(jnp.take(jnp.stack(rest), order, axis=0), axis=0)
        got = []
    return own, got


def finish_kernel(krows, counts, place_ref, *refs):
    (kernel_ref, proj_ref, bias_ref, keep_ref), refs = refs[6:], refs[:6]
    i, part = place_ref[0], place_ref[1]
    wide = krows // 9
    prows = refs[0].shape[1] - krows - 16
    sources = []
    near = [(n, 2 * n, 0) for n in range(4)]
    middle = [(n, n // 3 * 2, n % 3 + 1) for n in range(9)]
    last = [(n, 6, n + 1) for n in range(3)]
    for m, ref in enumerate(refs):
        for n, bits, turn in (near, middle, last)[m % 3]:
            place = i ^ (bits + m // 3)
            q = (part + PARTS - turn) % PARTS
            sources.append((ref, n, place, q))
            keep_ref[place * PARTS + q] = ref[n, krows : krows + 16].astype(jnp.float32)
    kept = jnp.sum(keep_ref[...], axis=0)

    def factor(values, count):
        total = jnp.sum(jnp.sum(values, axis=0, keepdims=True), axis=1, keepdims=True)
        return 1.0 / jnp.sqrt(total / count + norm_eps)

    kfactor, pfactor = factor(kept[3:6], counts[0]), factor(kept[6:9], counts[1])
    for ref, n, place, q in sources:
        value = ref[n].astype(jnp.float32)
        lanes = pl.ds(pl.multiple_of(place // 4 * 256 + q % 2 * 128, 128), 128)
        start = place % 4 * 64 + q // 2 * 32
        kernel_ref[:, pl.ds(pl.multiple_of(start, 32), wide), lanes] = (
            value[:krows] * kfactor
        ).reshape(9, wide, 128)
        row, col = proj_place(place, q, prows)
        proj_ref[pl.ds(pl.multiple_of(row, 8), prows), pl.ds(pl.multiple_of(col * 128, 128), 128)] = (
            value[krows + 16 :] * pfactor
        )
    bias = [jnp.sum(keep_ref[n, 0:3], axis=0, keepdims=True) for n in (0, 1, 16, 17)]
    bias = jnp.concatenate(bias, axis=1)
    bias_ref[...] = bias * factor(bias * bias, counts[2])


def finish(place, blocks, zch, channels, feat):
    krows = 9 * zch // 8
    counts = (9 * zch * channels, feat * zch, channels)
    return pl.pallas_call(
        functools.partial(finish_kernel, krows, counts),
        out_shape=(
            jax.ShapeDtypeStruct((9, zch, channels), jnp.float32),
            jax.ShapeDtypeStruct((feat, zch), jnp.float32),
            jax.ShapeDtypeStruct((1, channels), jnp.float32),
        ),
        in_specs=[SMEM_SPEC] + vmem(6),
        out_specs=tuple(vmem(3)),
        scratch_shapes=[pltpu.VMEM((32, 16, 128), jnp.float32)],
        compiler_params=LIMIT,
    )(place, *blocks)


def gather_near(grid, near, far):
    return send(near, grid.flip(2)), send(far, grid.flip(4))


def gather_rest(grid, near, col, row):
    mine = [near, col, row, send(row, grid.flip(2))]
    return mine + [send(x, grid.flip(1)) for x in mine]


def on_device(
    grid, codebook, projector, latents, wanted, wanted_count, token_pick, kernel, bias, cotangent
):
    devices = grid.total
    images, rows, width, zch = latents.shape
    channels = kernel.shape[3]
    feat = codebook.shape[1]
    cap = wanted.shape[2]
    slots = devices * cap
    tokens = images * rows * width
    r, i = grid.place()
    place = jnp.stack([i, r % PARTS]).astype(jnp.int32)
    near, far, slot, ask = token_part(
        place,
        token_pick.reshape(images * rows, width),
        wanted_count,
        jnp.swapaxes(wanted.reshape(devices, cap), 0, 1),
        latents.reshape(tokens, zch),
        cotangent.reshape(tokens, channels),
    )
    asked = spread(ask, grid)
    col, row = gather_near(grid, near, far)
    local_codes = jnp.dot(codebook, projector, preferred_element_type=jnp.float32).astype(
        jnp.bfloat16
    )
    slot_ids = jnp.arange(slots, dtype=jnp.int32)
    onehot = (slot.reshape(tokens, 1) == slot_ids[None, :]).astype(jnp.bfloat16)
    replies = answer(grid, asked, local_codes)
    got = spread(replies, grid)
    asked, col, row, _ = lax.optimization_barrier((asked, col, row, replies))
    cots = gather_rest(grid, near, col, row)
    kept, sent = proj_part(place, asked, codebook, local_codes)
    proj = (kept + send(sent, grid.flip(1))).reshape(2, 2, PARTS, feat // 16, 128)
    cotangent, _ = lax.optimization_barrier((cotangent, replies))
    proj = exchange(proj, i // 2 % 2, grid.flip(2))
    got_half = send(half(proj, 0, 1 - i // 4).astype(jnp.bfloat16), grid.flip(4))
    acc = group_weights(grid, place, got, cots, cap)
    kept, acc = lax.optimization_barrier((half(proj, 0, i // 4), acc))
    own, *sends = pack(place, acc, kept + got_half.astype(jnp.float32))
    codes = got[:, cap:, 128:].reshape(slots, zch)
    codes, own, *sends = lax.optimization_barrier((codes, own, *sends))
    own, received = reduce_planes(grid, own, sends, r)
    quant = jnp.dot(onehot, codes, preferred_element_type=jnp.float32).astype(jnp.bfloat16)
    quant = quant.reshape(images, rows, width, zch)
    quant_f = quant.astype(jnp.float32)
    latent_f = latents.astype(jnp.float32)
    padded = jnp.pad(quant, ((0, 0), (1, 1), (1, 1), (0, 0)))
    padded_grad = jnp.pad(cotangent, ((0, 0), (1, 1), (1, 1), (0, 0)))
    output = jnp.zeros((images, rows, width, channels), jnp.float32)
    grad_input = jnp.zeros((images, rows, width, zch), jnp.float32)
    for row_off in range(3):
        for col_off in range(3):
            window = padded[:, row_off : row_off + rows, col_off : col_off + width]
            output = output + jnp.einsum(
                "nhwc,co->nhwo",
                window,
                kernel[row_off, col_off],
                preferred_element_type=jnp.float32,
            )
            grad_window = padded_grad[
                :, 2 - row_off : 2 - row_off + rows, 2 - col_off : 2 - col_off + width
            ]
            grad_input = grad_input + jnp.einsum(
                "nhwo,co->nhwc",
                grad_window,
                kernel[row_off, col_off],
                preferred_element_type=jnp.float32,
            )
    hidden = (output + bias.astype(jnp.float32)).astype(jnp.bfloat16)
    grad_latents = (grad_input + 2.0 * commit_weight * (latent_f - quant_f)).astype(jnp.bfloat16)
    krows = 9 * zch // 8
    planes = gather_planes(grid, combine(krows, own, received))
    *planes, hidden, grad_latents = lax.optimization_barrier((*planes, hidden, grad_latents))
    blocks = gather_places(grid, *planes)
    kernel_step, proj_step, bias_step = finish(place, blocks, zch, channels, feat)
    kernel_step = kernel_step.reshape(3, 3, zch, channels)
    return (hidden, grad_latents, proj_step, kernel_step, bias_step.reshape(channels))


def solution(mesh):
    grid = Grid(mesh.shape["dp"], mesh.shape["code"])
    in_specs = (
        P(("dp", "code"), None),
        P(),
        P(("dp", "code"), None, None, None),
        P(("dp", "code"), None, None),
        P(("dp", "code"), None),
        P(("dp", "code"), None, None),
        P(),
        P(),
        P(("dp", "code"), None, None, None),
    )
    out_specs = (
        P(("dp", "code"), None, None, None),
        P(("dp", "code"), None, None, None),
        P(),
        P(),
        P(),
    )
    return jax.shard_map(
        functools.partial(on_device, grid),
        mesh=mesh,
        in_specs=in_specs,
        out_specs=out_specs,
        check_vma=False,
    )
```

time: 108 us -> 98.6 us (0.913)
  starting transfers between devices: 40.2 us -> 32.6 us
  matrix products: 17.2 us -> 10.4 us
  waiting for transfers between devices: 27.8 us -> 34.3 us
  local copies, waits for them, and re-layouts: 7.82 us -> 2.87 us
  Pallas kernels: 11.2 us -> 15.4 us
    all_to_all x3 -> x2, waiting for transfers between devices: 0.01 us -> 7.27 us  [spread(): return lax.all_to_all(x, AXES, split_axis=0, concat_axis=0, tiled=True)]
    pallas_call x2 -> x4, Pallas kernels: 5.88 us -> 10.4 us  [the longest x1 5.03 us: group_weights(): pl.pallas_call(functools.partial(weights_kernel, grid, cap), out_shape=ja...]
    ppermute x23 -> x26, starting transfers between devices: 27 us -> 22.7 us  [send(): return lax.ppermute(x, AXES, perm)]
    dot_general x9, matrix products: 7.36 us -> 3.48 us  [on_device(): jnp.einsum('nhwc,co->nhwo', window, kernel[row_off, col_off], preferred_e...]
    all_to_all x3 -> x2, starting transfers between devices: 13.2 us -> 9.93 us  [spread(): return lax.all_to_all(x, AXES, split_axis=0, concat_axis=0, tiled=True)]
    dot_general x9, matrix products: 6.94 us -> 4.87 us  [on_device(): jnp.einsum('nhwo,co->nhwc', grad_window, kernel[row_off, col_off], prefer...]
    unnamed x34 -> x31, local copies, waits for them, and re-layouts: 4.6 us -> 2.74 us
    reshape x2 -> x1, local copies, waits for them, and re-layouts: 1.59 us -> 0.01 us  [on_device(): codes = got[:, cap:, 128:].reshape(slots, zch)]
  transfers between devices with their start and end apart: 26 -> 28, of which waited for: 8 -> 9; matrix products, arithmetic and copies ran while one was open for 22% -> 12% of each run, Pallas kernels for 7% -> 8%
where the time goes in v3:
time: 98.6 us; the launch traced here: 98.2 us
  waiting for transfers between devices  34.3 us (35%)
  starting transfers between devices  32.6 us (33%)
  Pallas kernels  15.4 us (16%)
  matrix products  10.4 us (11%)
  local copies, waits for them, and re-layouts  2.87 us (3%)
  other arithmetic  1.49 us (2%)
  between operations  1.19 us (1%)
    ppermute x26, waiting for transfers between devices, send(): return lax.ppermute(x, AXES, perm)  27.1 us
    ppermute x26, starting transfers between devices, send(): return lax.ppermute(x, AXES, perm)  22.7 us
    all_to_all x2, starting transfers between devices, spread(): return lax.all_to_all(x, AXES, split_axis=0, concat_axis=0, tiled=True)  9.93 us
    all_to_all x2, waiting for transfers between devices, spread(): return lax.all_to_all(x, AXES, split_axis=0, concat_axis=0, tiled=True)  7.27 us
    pallas_call x1, Pallas kernels, group_weights(): pl.pallas_call(functools.partial(weights_kernel, grid, cap), out_shape=ja...  5.03 us
    dot_general x9, matrix products, on_device(): jnp.einsum('nhwo,co->nhwc', grad_window, kernel[row_off, col_off], prefer...  4.87 us
    pallas_call x1, Pallas kernels, finish(): pl.pallas_call(functools.partial(finish_kernel, krows, counts), out_shape...  3.71 us
    dot_general x9, matrix products, on_device(): jnp.einsum('nhwc,co->nhwo', window, kernel[row_off, col_off], preferred_e...  3.48 us
  transfers between devices with their start and end apart: 28, of which 9 were waited for; matrix products, arithmetic and copies ran while one was open for 12% of the time, Pallas kernels for 8%

profile of v3, /device:TPU:0, one launch (start us, length us, event | category | flops | bytes accessed | tf_op | source)
XLA Modules:
  0.0 98.2 jit_solution(2257004813290914987)
XLA Ops:
  0.7 0.7 pad_add_fusion.place_ref
  1.3 3.0 %shard_map.128 = (bf16[528,256]{1,0:T(8,128)(2,1)}, bf16[528,256]{1,0:T(8,128)(2,1)}, s32[1,512]{1,0:T(1,128)}, f32[32,8,384]{2,1,0:T(8,128)}) custom-call(s32[2]{0:T(128)} %pad_add_fusion.place_ref, s32[32,16]{1,0:T(8,128)} %bitcast.137, s32[1,32]{1,0:T(1,128)} %counts_hbm.1, s32[8,32]{1,0:T(8,128)} %bitcast.138, bf16[512,256]{1,0:T(8,128)(2,1)} %bitcast.130, ...), custom_call_target="tpu_custom_call" | custom-call | flops 67108864 | bytes 2097152 | tf_op jit(solution)/shard_map/pallas_call | solution.py:161
  4.4 7.3 %all-to-all-start = ((f32[32,8,384]{2,1,0:T(8,128)}), f32[32,8,384]{2,1,0:T(8,128)S(1)}, u32[]{:S(2)}, u32[]{:S(2)}) async-start(f32[32,8,384]{2,1,0:T(8,128)} %get-tuple-element.35), calls=%async_computation | async-start | bytes 786432 | tf_op jit(solution)/shard_map/all_to_all | solution.py:85
  11.7 0.3 collective-permute-start.5
  12.0 1.7 %collective-permute-start = (bf16[528,256]{1,0:T(8,128)(2,1)}, bf16[528,256]{1,0:T(8,128)(2,1)}, u32[]{:S(2)}, u32[]{:S(2)}) collective-permute-start(bf16[528,256]{1,0:T(8,128)(2,1)} %get-tuple-element.36.refs_0_), channel_id=1, source_target_pairs={{0,2},{1,3},{2,0},{3,1},{4,6},{5,7},{6,4},{7,5},{8,10},{9,11},{10,... | collective-permute-start | bytes 811016 | tf_op jit(solution)/shard_map/ppermute | solution.py:55
  13.7 1.5 %collective-permute-start.1 = (bf16[528,256]{1,0:T(8,128)(2,1)}, bf16[528,256]{1,0:T(8,128)(2,1)}, u32[]{:S(2)}, u32[]{:S(2)}) collective-permute-start(bf16[528,256]{1,0:T(8,128)(2,1)} %get-tuple-element.37), channel_id=1, source_target_pairs={{0,4},{1,5},{2,6},{3,7},{4,0},{5,1},{6,2},{7,3},{8,12},{9,13},{10,... | collective-permute-start | bytes 811016 | tf_op jit(solution)/shard_map/ppermute | solution.py:55
  15.2 0.7 convert_element_type.52
  15.8 1.8 %convolution_convert_fusion.codes_ref = bf16[784,256]{1,0:T(8,128)(2,1)S(1)} fusion(bf16[784,768]{1,0:T(8,128)(2,1)} %book_ref.1, bf16[768,256]{1,0:T(8,128)(2,1)S(1)} %copy-done), kind=kOutput, calls=%fused_computation.18 | convolution fusion | flops 308482048 | bytes 1998848 | tf_op jit(solution)/shard_map/dot_general | solution.py:496
  17.6 7.3 %all-to-all-done.asked_ref = f32[32,8,384]{2,1,0:T(8,128)S(1)} async-done(((f32[32,8,384]{2,1,0:T(8,128)}), f32[32,8,384]{2,1,0:T(8,128)S(1)}, u32[]{:S(2)}, u32[]{:S(2)}) %all-to-all-start) | async-done | bytes 393248 | tf_op jit(solution)/shard_map/all_to_all | solution.py:85
  24.9 1.2 %shard_map.129 = bf16[32,16,384]{2,1,0:T(8,128)(2,1)} custom-call(f32[32,8,384]{2,1,0:T(8,128)S(1)} %all-to-all-done.asked_ref, bf16[784,256]{1,0:T(8,128)(2,1)S(1)} %convolution_convert_fusion.codes_ref), custom_call_target="tpu_custom_call" | custom-call | flops 102760448 | bytes 2097152 | tf_op jit(solution)/shard_map/pallas_call | solution.py:218
  26.1 2.6 %all-to-all-start.1 = ((bf16[32,16,384]{2,1,0:T(8,128)(2,1)}), bf16[32,16,384]{2,1,0:T(8,128)(2,1)S(1)}, u32[]{:S(2)}, u32[]{:S(2)}) async-start(bf16[32,16,384]{2,1,0:T(8,128)(2,1)} %shard_map.129), calls=%async_computation.1 | async-start | bytes 786432 | tf_op jit(solution)/shard_map/all_to_all | solution.py:85
  28.8 0.3 collective-permute-start.7
  29.1 1.7 %collective-permute-start.4 = (bf16[528,256]{1,0:T(8,128)(2,1)}, bf16[528,256]{1,0:T(8,128)(2,1)S(1)}, u32[]{:S(2)}, u32[]{:S(2)}) collective-permute-start(bf16[528,256]{1,0:T(8,128)(2,1)} %collective-permute-done.1.refs_2_), channel_id=1, source_target_pairs={{0,2},{1,3},{2,0},{3,1},{4,6},{5,7},{6,4},{7,5},{8,10},{9,11},{10,... | collective-permute-start | bytes 811016 | tf_op jit(solution)/shard_map/ppermute | solution.py:55
  30.8 1.7 %shard_map.130 = (f32[768,128]{1,0:T(8,128)S(1)}, f32[768,128]{1,0:T(8,128)S(1)}) custom-call(s32[2]{0:T(128)S(1)} %copy-done.2, f32[32,8,384]{2,1,0:T(8,128)S(1)} %all-to-all-done.asked_ref, bf16[784,768]{1,0:T(8,128)(2,1)S(1)} %copy-done.1, bf16[784,256]{1,0:T(8,128)(2,1)S(1)} %convolution_convert_fusion.codes_ref), custom_call_target="tpu_custom_call" | custom-call | flops 509607936 | bytes 4194304 | tf_op jit(solution)/shard_map/pallas_call | solution.py:250
  32.5 0.1 collective-permute-start.6
  32.6 0.5 collective-permute-start.2
  33.1 1.4 %fusion.4 = f32[2,16,16,256]{3,2,1,0:T(8,128)S(1)} fusion(bf16[2,16,16,512]{3,2,1,0:T(8,128)(2,1)} %param.17, bf16[3,3,256,512]{3,2,1,0:T(8,128)(2,1)} %param.15), kind=kOutput, calls=%fused_computation.38 | convolution fusion | flops 134217728 | bytes 1310720 | tf_op jit(solution)/shard_map/nhwo,co->nhwc/dot_general | solution.py:536
  34.6 0.3 convolution_add_fusion.15
  34.9 0.3 convolution_add_fusion.14
  35.2 0.3 convolution_add_fusion.13
  35.6 0.3 convolution_add_fusion.12
  35.9 0.4 convolution_add_fusion.11
  36.3 0.4 convolution_add_fusion.10
  36.7 0.4 collective-permute-start.3
  37.2 0.3 convolution_add_fusion.9
  37.5 4.6 %collective-permute-done.4.refs_3_ = bf16[528,256]{1,0:T(8,128)(2,1)S(1)} collective-permute-done((bf16[528,256]{1,0:T(8,128)(2,1)}, bf16[528,256]{1,0:T(8,128)(2,1)S(1)}, u32[]{:S(2)}, u32[]{:S(2)}) %collective-permute-start.4) | collective-permute-done | bytes 270368 | tf_op jit(solution)/shard_map/ppermute | solution.py:55
  42.1 1.6 %collective-permute-done.3 = bf16[2,4,48,128]{3,2,1,0:T(8,128)(2,1)S(1)} collective-permute-done((bf16[2,4,48,128]{3,2,1,0:T(8,128)(2,1)S(1)}, bf16[2,4,48,128]{3,2,1,0:T(8,128)(2,1)S(1)}, u32[]{:S(2)}, u32[]{:S(2)}) %collective-permute-start.3) | collective-permute-done | bytes 98336 | tf_op jit(solution)/shard_map/ppermute | solution.py:55
  43.8 1.5 %collective-permute-start.9 = (bf16[4,48,128]{2,1,0:T(8,128)(2,1)S(1)}, bf16[4,48,128]{2,1,0:T(8,128)(2,1)S(1)}, u32[]{:S(2)}, u32[]{:S(2)}) collective-permute-start(bf16[4,48,128]{2,1,0:T(8,128)(2,1)S(1)} %fusion.44), channel_id=1, source_target_pairs={{0,4},{1,5},{2,6},{3,7},{4,0},{5,1},{6,2},{7,3},{8,12},{9,13},{10,... | collective-permute-start | bytes 147464 | tf_op jit(solution)/shard_map/ppermute | solution.py:55
  45.3 0.7 copy-done.4
  46.1 0.9 copy-done.5
  47.0 1.0 copy-done.7
  48.0 5.0 %shard_map.131.acc_ref = f32[592,256]{1,0:T(8,128)S(1)} custom-call(s32[2]{0:T(128)S(1)} %copy-done.2, bf16[32,16,384]{2,1,0:T(8,128)(2,1)S(1)} %all-to-all-done.1.got_ref, bf16[528,256]{1,0:T(8,128)(2,1)S(1)} %copy-done.3, bf16[528,256]{1,0:T(8,128)(2,1)} %collective-permute-done.refs_1_, bf16[528,256]{1,0:T(8,128)(2,1)} %collective-permute-done.1.refs_2_, ...), custom_call_target="tpu_custom_call" | custom-call | flops 1207959552 | bytes 8388608 | tf_op jit(solution)/shard_map/pallas_call | solution.py:339
  53.0 0.6 shard_map.132
  53.7 1.5 %collective-permute-start.10 = (bf16[352,128]{1,0:T(8,128)(2,1)S(1)}, bf16[352,128]{1,0:T(8,128)(2,1)S(1)}, u32[]{:S(2)}, u32[]{:S(2)}) collective-permute-start(bf16[352,128]{1,0:T(8,128)(2,1)S(1)} %get-tuple-element.50), channel_id=1, source_target_pairs={{0,8},{1,9},{2,10},{3,11},{4,12},{5,13},{6,14},{7,15},{8,16},{9,17... | collective-permute-start | bytes 270344 | tf_op jit(solution)/shard_map/ppermute | solution.py:55
  55.2 2.4 %collective-permute-start.11 = (bf16[352,128]{1,0:T(8,128)(2,1)S(1)}, bf16[352,128]{1,0:T(8,128)(2,1)S(1)}, u32[]{:S(2)}, u32[]{:S(2)}) collective-permute-start(bf16[352,128]{1,0:T(8,128)(2,1)S(1)} %get-tuple-element.51), channel_id=1, source_target_pairs={{0,16},{1,17},{2,18},{3,19},{4,20},{5,21},{6,22},{7,23},{8,24},{9,... | collective-permute-start | bytes 270344 | tf_op jit(solution)/shard_map/ppermute | solution.py:55
  57.6 1.5 %collective-permute-start.12 = (bf16[352,128]{1,0:T(8,128)(2,1)S(1)}, bf16[352,128]{1,0:T(8,128)(2,1)S(1)}, u32[]{:S(2)}, u32[]{:S(2)}) collective-permute-start(bf16[352,128]{1,0:T(8,128)(2,1)S(1)} %get-tuple-element.52), channel_id=1, source_target_pairs={{0,24},{1,25},{2,26},{3,27},{4,28},{5,29},{6,30},{7,31},{8,0},{9,1... | collective-permute-start | bytes 270344 | tf_op jit(solution)/shard_map/ppermute | solution.py:55
  59.0 0.3 convolution_convert_fusion.1
  59.3 0.3 fusion.5
  59.6 0.3 convolution_add_fusion.7
  59.9 0.3 convolution_add_fusion.6
  60.2 0.3 convolution_add_fusion.5
  60.5 0.3 convolution_add_fusion.4
  60.8 0.3 convolution_add_fusion.3
  61.1 0.3 convolution_add_fusion.2
  61.5 0.3 convolution_add_fusion.1
  61.8 1.9 %collective-permute-done.11.refs_1_ = bf16[352,128]{1,0:T(8,128)(2,1)S(1)} collective-permute-done((bf16[352,128]{1,0:T(8,128)(2,1)S(1)}, bf16[352,128]{1,0:T(8,128)(2,1)S(1)}, u32[]{:S(2)}, u32[]{:S(2)}) %collective-permute-start.11) | collective-permute-done | bytes 90144 | tf_op jit(solution)/shard_map/ppermute | solution.py:55
  63.6 0.2 collective-permute-done.12.refs_2_
  63.9 3.4 %collective-permute-start.18 = (bf16[352,128]{1,0:T(8,128)(2,1)S(1)}, bf16[352,128]{1,0:T(8,128)(2,1)S(1)}, u32[]{:S(2)}, u32[]{:S(2)}) collective-permute-start(bf16[352,128]{1,0:T(8,128)(2,1)S(1)} %shard_map.133), channel_id=1, source_target_pairs={{0,24},{1,25},{2,26},{3,27},{4,28},{5,29},{6,30},{7,31},{8,0},{9,1... | collective-permute-start | bytes 270344 | tf_op jit(solution)/shard_map/ppermute | solution.py:55
  67.3 0.3 collective-permute-start.17
  67.6 0.3 collective-permute-start.16
  67.9 1.1 %fusion.1 = bf16[2,16,16,512]{3,2,1,0:T(8,128)(2,1)} fusion(f32[2,16,16,512]{3,2,1,0:T(8,128)S(1)} %convolution_add_fusion.1, f32[512]{0:T(512)S(1)} %convert_element_type.52, bf16[2,16,16,256]{3,2,1,0:T(8,128)(2,1)S(1)} %bitcast.126, bf16[3,3,256,512]{3,2,1,0:T(8,128)(2,1)S(1)} %copy-done.11), kind=kOutput, calls=%fused_computation.17 | convolution fusion | flops 135004160 | bytes 2099200 | tf_op jit(solution)/shard_map/nhwc,co->nhwo/dot_general | solution.py:527
  69.0 0.3 collective-permute-start.14
  69.3 0.9 collective-permute-start.13
  70.3 5.7 %collective-permute-done.17 = bf16[352,128]{1,0:T(8,128)(2,1)S(1)} collective-permute-done((bf16[352,128]{1,0:T(8,128)(2,1)S(1)}, bf16[352,128]{1,0:T(8,128)(2,1)S(1)}, u32[]{:S(2)}, u32[]{:S(2)}) %collective-permute-start.17) | collective-permute-done | bytes 90144 | tf_op jit(solution)/shard_map/ppermute | solution.py:55
  76.0 0.2 collective-permute-start.20
  76.2 0.9 collective-permute-start.19
  77.1 1.5 %collective-permute-start.15 = (bf16[352,128]{1,0:T(8,128)(2,1)S(1)}, bf16[352,128]{1,0:T(8,128)(2,1)S(1)}, u32[]{:S(2)}, u32[]{:S(2)}) collective-permute-start(bf16[352,128]{1,0:T(8,128)(2,1)S(1)} %collective-permute-done.13), channel_id=1, source_target_pairs={{0,4},{1,5},{2,6},{3,7},{4,0},{5,1},{6,2},{7,3},{8,12},{9,13},{10,... | collective-permute-start | bytes 270344 | tf_op jit(solution)/shard_map/ppermute | solution.py:55
  78.7 1.1 %fusion.3 = bf16[2,16,16,256]{3,2,1,0:T(8,128)(2,1)} fusion(f32[2,16,16,256]{3,2,1,0:T(8,128)S(1)} %convolution_add_fusion.9, bf16[2,16,16,512]{3,2,1,0:T(8,128)(2,1)S(1)} %copy-done.9, bf16[2,16,16,256]{3,2,1,0:T(8,128)(2,1)S(1)} %bitcast.127, bf16[2,16,16,256]{3,2,1,0:T(8,128)(2,1)S(1)} %copy-done.12, bf16[3,3,256,512]{3,2,1,0:T(8,128)(2,1)S(1)} %copy-done.11), kind=kOutput, calls=%fused_computation.28 | convolution fusion | flops 135135232 | bytes 2097152 | tf_op jit(solution)/shard_map/nhwo,co->nhwc/dot_general | solution.py:536
  79.7 5.8 %collective-permute-done.15 = bf16[352,128]{1,0:T(8,128)(2,1)S(1)} collective-permute-done((bf16[352,128]{1,0:T(8,128)(2,1)S(1)}, bf16[352,128]{1,0:T(8,128)(2,1)S(1)}, u32[]{:S(2)}, u32[]{:S(2)}) %collective-permute-start.15) | collective-permute-done | bytes 90144 | tf_op jit(solution)/shard_map/ppermute | solution.py:55
  85.8 1.0 collective-permute-start.21
  86.8 0.3 collective-permute-start.22
  87.1 5.7 %collective-permute-done.21 = bf16[2,352,128]{2,1,0:T(8,128)(2,1)S(1)} collective-permute-done((bf16[2,352,128]{2,1,0:T(8,128)(2,1)S(1)}, bf16[2,352,128]{2,1,0:T(8,128)(2,1)S(1)}, u32[]{:S(2)}, u32[]{:S(2)}) %collective-permute-start.21) | collective-permute-done | bytes 180256 | tf_op jit(solution)/shard_map/ppermute | solution.py:55
  93.0 1.5 %collective-permute-done.25.refs_5_ = bf16[3,352,128]{2,1,0:T(8,128)(2,1)S(1)} collective-permute-done((bf16[3,352,128]{2,1,0:T(8,128)(2,1)S(1)}, bf16[3,352,128]{2,1,0:T(8,128)(2,1)S(1)}, u32[]{:S(2)}, u32[]{:S(2)}) %collective-permute-start.25) | collective-permute-done | bytes 270368 | tf_op jit(solution)/shard_map/ppermute | solution.py:55
  94.5 3.7 %shard_map.134 = (f32[9,256,512]{2,1,0:T(8,128)}, f32[768,256]{1,0:T(8,128)}, f32[1,512]{1,0:T(1,128)}) custom-call(s32[2]{0:T(128)S(1)} %copy-done.2, bf16[4,352,128]{2,1,0:T(8,128)(2,1)S(1)} %pad_maximum_fusion.refs_0_, bf16[9,352,128]{2,1,0:T(8,128)(2,1)S(1)} %constant_dynamic-update-slice_fusion.refs_1_, ...), custom_call_target="tpu_custom_call" | custom-call | tf_op jit(solution)/shard_map/pallas_call | solution.py:451
  (65 shorter events, 0.7 us)
Async XLA Ops:
  0.6 15.2 %copy-start = (bf16[768,256]{1,0:T(8,128)(2,1)S(1)}, bf16[768,256]{1,0:T(8,128)(2,1)}, u32[]{:S(2)}) copy-start(bf16[768,256]{1,0:T(8,128)(2,1)} %param.10) | copy-start | bytes 1179652
  4.4 26.4 %copy-start.1 = (bf16[784,768]{1,0:T(8,128)(2,1)S(1)}, bf16[784,768]{1,0:T(8,128)(2,1)}, u32[]{:S(2)}) copy-start(bf16[784,768]{1,0:T(8,128)(2,1)} %book_ref.1) | copy-start | bytes 3612676
  4.4 26.4 %copy-start.2 = (s32[2]{0:T(128)S(1)}, s32[2]{0:T(128)}, u32[]{:S(2)}) copy-start(s32[2]{0:T(128)} %pad_add_fusion.place_ref) | copy-start | bytes 28
  4.4 20.5 %all-to-all-start = ((f32[32,8,384]{2,1,0:T(8,128)}), f32[32,8,384]{2,1,0:T(8,128)S(1)}, u32[]{:S(2)}, u32[]{:S(2)}) async-start(f32[32,8,384]{2,1,0:T(8,128)} %get-tuple-element.35), calls=%async_computation | async-start | bytes 786432 | tf_op jit(solution)/shard_map/all_to_all | solution.py:85
  11.7 33.6 %collective-permute-start.5 = (bf16[528,256]{1,0:T(8,128)(2,1)}, bf16[528,256]{1,0:T(8,128)(2,1)S(1)}, u32[]{:S(2)}, u32[]{:S(2)}) collective-permute-start(bf16[528,256]{1,0:T(8,128)(2,1)} %get-tuple-element.36.refs_0_), channel_id=1, source_target_pairs={{0,1},{1,0},{2,3},{3,2},{4,5},{5,4},{6,7},{7,6},{8,9},{9,8},{10,11... | collective-permute-start | bytes 811016 | tf_op jit(solution)/shard_map/ppermute | solution.py:55
  12.0 16.7 %collective-permute-start = (bf16[528,256]{1,0:T(8,128)(2,1)}, bf16[528,256]{1,0:T(8,128)(2,1)}, u32[]{:S(2)}, u32[]{:S(2)}) collective-permute-start(bf16[528,256]{1,0:T(8,128)(2,1)} %get-tuple-element.36.refs_0_), channel_id=1, source_target_pairs={{0,2},{1,3},{2,0},{3,1},{4,6},{5,7},{6,4},{7,5},{8,10},{9,11},{10,... | collective-permute-start | bytes 811016 | tf_op jit(solution)/shard_map/ppermute | solution.py:55
  13.7 15.0 %collective-permute-start.1 = (bf16[528,256]{1,0:T(8,128)(2,1)}, bf16[528,256]{1,0:T(8,128)(2,1)}, u32[]{:S(2)}, u32[]{:S(2)}) collective-permute-start(bf16[528,256]{1,0:T(8,128)(2,1)} %get-tuple-element.37), channel_id=1, source_target_pairs={{0,4},{1,5},{2,6},{3,7},{4,0},{5,1},{6,2},{7,3},{8,12},{9,13},{10,... | collective-permute-start | bytes 811016 | tf_op jit(solution)/shard_map/ppermute | solution.py:55
  26.1 20.0 %all-to-all-start.1 = ((bf16[32,16,384]{2,1,0:T(8,128)(2,1)}), bf16[32,16,384]{2,1,0:T(8,128)(2,1)S(1)}, u32[]{:S(2)}, u32[]{:S(2)}) async-start(bf16[32,16,384]{2,1,0:T(8,128)(2,1)} %shard_map.129), calls=%async_computation.1 | async-start | bytes 786432 | tf_op jit(solution)/shard_map/all_to_all | solution.py:85
  28.7 5.8 %copy-start.8 = (bf16[2,16,16,512]{3,2,1,0:T(8,128)(2,1)S(1)}, bf16[2,16,16,512]{3,2,1,0:T(8,128)(2,1)}, u32[]{:S(2)}) copy-start(bf16[2,16,16,512]{3,2,1,0:T(8,128)(2,1)} %param.17) | copy-start | bytes 1572868
  28.7 5.8 %copy-start.10 = (bf16[3,3,256,512]{3,2,1,0:T(8,128)(2,1)S(1)}, bf16[3,3,256,512]{3,2,1,0:T(8,128)(2,1)}, u32[]{:S(2)}) copy-start(bf16[3,3,256,512]{3,2,1,0:T(8,128)(2,1)} %param.15) | copy-start | bytes 7077892
  28.8 16.6 %collective-permute-start.7 = (bf16[528,256]{1,0:T(8,128)(2,1)}, bf16[528,256]{1,0:T(8,128)(2,1)S(1)}, u32[]{:S(2)}, u32[]{:S(2)}) collective-permute-start(bf16[528,256]{1,0:T(8,128)(2,1)} %collective-permute-done.1.refs_2_), channel_id=1, source_target_pairs={{0,1},{1,0},{2,3},{3,2},{4,5},{5,4},{6,7},{7,6},{8,9},{9,8},{10,11... | collective-permute-start | bytes 811016 | tf_op jit(solution)/shard_map/ppermute | solution.py:55
  29.1 13.0 %collective-permute-start.4 = (bf16[528,256]{1,0:T(8,128)(2,1)}, bf16[528,256]{1,0:T(8,128)(2,1)S(1)}, u32[]{:S(2)}, u32[]{:S(2)}) collective-permute-start(bf16[528,256]{1,0:T(8,128)(2,1)} %collective-permute-done.1.refs_2_), channel_id=1, source_target_pairs={{0,2},{1,3},{2,0},{3,1},{4,6},{5,7},{6,4},{7,5},{8,10},{9,11},{10,... | collective-permute-start | bytes 811016 | tf_op jit(solution)/shard_map/ppermute | solution.py:55
  32.5 12.8 %collective-permute-start.6 = (bf16[528,256]{1,0:T(8,128)(2,1)}, bf16[528,256]{1,0:T(8,128)(2,1)S(1)}, u32[]{:S(2)}, u32[]{:S(2)}) collective-permute-start(bf16[528,256]{1,0:T(8,128)(2,1)} %collective-permute-done.refs_1_), channel_id=1, source_target_pairs={{0,1},{1,0},{2,3},{3,2},{4,5},{5,4},{6,7},{7,6},{8,9},{9,8},{10,11... | collective-permute-start | bytes 811016 | tf_op jit(solution)/shard_map/ppermute | solution.py:55
  32.6 4.0 %collective-permute-start.2 = (f32[768,128]{1,0:T(8,128)S(1)}, f32[768,128]{1,0:T(8,128)S(1)}, u32[]{:S(2)}, u32[]{:S(2)}) collective-permute-start(f32[768,128]{1,0:T(8,128)S(1)} %get-tuple-element.40), channel_id=1, source_target_pairs={{0,1},{1,0},{2,3},{3,2},{4,5},{5,4},{6,7},{7,6},{8,9},{9,8},{10,11... | collective-permute-start | bytes 1179656 | tf_op jit(solution)/shard_map/ppermute | solution.py:55
  36.6 9.4 %copy-start.3 = (bf16[528,256]{1,0:T(8,128)(2,1)S(1)}, bf16[528,256]{1,0:T(8,128)(2,1)}, u32[]{:S(2)}) copy-start(bf16[528,256]{1,0:T(8,128)(2,1)} %get-tuple-element.36.refs_0_) | copy-start | bytes 811012
  36.7 7.0 %collective-permute-start.3 = (bf16[2,4,48,128]{3,2,1,0:T(8,128)(2,1)S(1)}, bf16[2,4,48,128]{3,2,1,0:T(8,128)(2,1)S(1)}, u32[]{:S(2)}, u32[]{:S(2)}) collective-permute-start(bf16[2,4,48,128]{3,2,1,0:T(8,128)(2,1)S(1)} %fusion.43), channel_id=1, source_target_pairs={{0,2},{1,3},{2,0},{3,1},{4,6},{5,7},{6,4},{7,5},{8,10},{9,11},{10,... | collective-permute-start | bytes 294920 | tf_op jit(solution)/shard_map/ppermute | solution.py:55
  42.1 3.2 %copy-start.6 = (bf16[528,256]{1,0:T(8,128)(2,1)}, bf16[528,256]{1,0:T(8,128)(2,1)S(1)}, u32[]{:S(2)}) copy-start(bf16[528,256]{1,0:T(8,128)(2,1)S(1)} %collective-permute-done.4.refs_3_) | copy-start | bytes 811012
  42.1 4.0 %collective-permute-start.8 = (bf16[528,256]{1,0:T(8,128)(2,1)S(1)}, bf16[528,256]{1,0:T(8,128)(2,1)S(1)}, u32[]{:S(2)}, u32[]{:S(2)}) collective-permute-start(bf16[528,256]{1,0:T(8,128)(2,1)S(1)} %collective-permute-done.4.refs_3_), channel_id=1, source_target_pairs={{0,1},{1,0},{2,3},{3,2},{4,5},{5,4},{6,7},{7,6},{8,9},{9,8},{10,11... | collective-permute-start | bytes 811016 | tf_op jit(solution)/shard_map/ppermute | solution.py:55
  43.8 9.3 %collective-permute-start.9 = (bf16[4,48,128]{2,1,0:T(8,128)(2,1)S(1)}, bf16[4,48,128]{2,1,0:T(8,128)(2,1)S(1)}, u32[]{:S(2)}, u32[]{:S(2)}) collective-permute-start(bf16[4,48,128]{2,1,0:T(8,128)(2,1)S(1)} %fusion.44), channel_id=1, source_target_pairs={{0,4},{1,5},{2,6},{3,7},{4,0},{5,1},{6,2},{7,3},{8,12},{9,13},{10,... | collective-permute-start | bytes 147464 | tf_op jit(solution)/shard_map/ppermute | solution.py:55
  45.3 13.7 %copy-start.13 = (s32[1,512]{1,0:T(1,128)S(1)}, s32[1,512]{1,0:T(1,128)}, u32[]{:S(2)}) copy-start(s32[1,512]{1,0:T(1,128)} %get-tuple-element.53) | copy-start | bytes 6148
  45.3 0.7 copy-start.4
  46.1 1.0 copy-start.5
  47.0 1.0 copy-start.7
  48.0 11.3 %copy-start.11 = (bf16[3,3,256,512]{3,2,1,0:T(8,128)(2,1)S(1)}, bf16[3,3,256,512]{3,2,1,0:T(8,128)(2,1)}, u32[]{:S(2)}) copy-start(bf16[3,3,256,512]{3,2,1,0:T(8,128)(2,1)} %param.15) | copy-start | bytes 7077892
  53.7 8.1 %collective-permute-start.10 = (bf16[352,128]{1,0:T(8,128)(2,1)S(1)}, bf16[352,128]{1,0:T(8,128)(2,1)S(1)}, u32[]{:S(2)}, u32[]{:S(2)}) collective-permute-start(bf16[352,128]{1,0:T(8,128)(2,1)S(1)} %get-tuple-element.50), channel_id=1, source_target_pairs={{0,8},{1,9},{2,10},{3,11},{4,12},{5,13},{6,14},{7,15},{8,16},{9,17... | collective-permute-start | bytes 270344 | tf_op jit(solution)/shard_map/ppermute | solution.py:55
  55.2 8.5 %collective-permute-start.11 = (bf16[352,128]{1,0:T(8,128)(2,1)S(1)}, bf16[352,128]{1,0:T(8,128)(2,1)S(1)}, u32[]{:S(2)}, u32[]{:S(2)}) collective-permute-start(bf16[352,128]{1,0:T(8,128)(2,1)S(1)} %get-tuple-element.51), channel_id=1, source_target_pairs={{0,16},{1,17},{2,18},{3,19},{4,20},{5,21},{6,22},{7,23},{8,24},{9,... | collective-permute-start | bytes 270344 | tf_op jit(solution)/shard_map/ppermute | solution.py:55
  57.6 6.3 %collective-permute-start.12 = (bf16[352,128]{1,0:T(8,128)(2,1)S(1)}, bf16[352,128]{1,0:T(8,128)(2,1)S(1)}, u32[]{:S(2)}, u32[]{:S(2)}) collective-permute-start(bf16[352,128]{1,0:T(8,128)(2,1)S(1)} %get-tuple-element.52), channel_id=1, source_target_pairs={{0,24},{1,25},{2,26},{3,27},{4,28},{5,29},{6,30},{7,31},{8,0},{9,1... | collective-permute-start | bytes 270344 | tf_op jit(solution)/shard_map/ppermute | solution.py:55
  61.5 17.2 %copy-start.9 = (bf16[2,16,16,512]{3,2,1,0:T(8,128)(2,1)S(1)}, bf16[2,16,16,512]{3,2,1,0:T(8,128)(2,1)}, u32[]{:S(2)}) copy-start(bf16[2,16,16,512]{3,2,1,0:T(8,128)(2,1)} %param.17) | copy-start | bytes 1572868
  61.5 17.2 %copy-start.12 = (bf16[2,16,16,256]{3,2,1,0:T(8,128)(2,1)S(1)}, bf16[2,16,16,256]{3,2,1,0:T(8,128)(2,1)}, u32[]{:S(2)}) copy-start(bf16[2,16,16,256]{3,2,1,0:T(8,128)(2,1)} %param.11) | copy-start | bytes 786436
  63.9 6.4 %collective-permute-start.18 = (bf16[352,128]{1,0:T(8,128)(2,1)S(1)}, bf16[352,128]{1,0:T(8,128)(2,1)S(1)}, u32[]{:S(2)}, u32[]{:S(2)}) collective-permute-start(bf16[352,128]{1,0:T(8,128)(2,1)S(1)} %shard_map.133), channel_id=1, source_target_pairs={{0,24},{1,25},{2,26},{3,27},{4,28},{5,29},{6,30},{7,31},{8,0},{9,1... | collective-permute-start | bytes 270344 | tf_op jit(solution)/shard_map/ppermute | solution.py:55
  67.3 8.7 %collective-permute-start.17 = (bf16[352,128]{1,0:T(8,128)(2,1)S(1)}, bf16[352,128]{1,0:T(8,128)(2,1)S(1)}, u32[]{:S(2)}, u32[]{:S(2)}) collective-permute-start(bf16[352,128]{1,0:T(8,128)(2,1)S(1)} %shard_map.133), channel_id=1, source_target_pairs={{0,16},{1,17},{2,18},{3,19},{4,20},{5,21},{6,22},{7,23},{8,24},{9,... | collective-permute-start | bytes 270344 | tf_op jit(solution)/shard_map/ppermute | solution.py:55
  67.6 8.3 %collective-permute-start.16 = (bf16[352,128]{1,0:T(8,128)(2,1)S(1)}, bf16[352,128]{1,0:T(8,128)(2,1)S(1)}, u32[]{:S(2)}, u32[]{:S(2)}) collective-permute-start(bf16[352,128]{1,0:T(8,128)(2,1)S(1)} %shard_map.133), channel_id=1, source_target_pairs={{0,8},{1,9},{2,10},{3,11},{4,12},{5,13},{6,14},{7,15},{8,16},{9,17... | collective-permute-start | bytes 270344 | tf_op jit(solution)/shard_map/ppermute | solution.py:55
  69.0 10.7 %collective-permute-start.14 = (bf16[352,128]{1,0:T(8,128)(2,1)S(1)}, bf16[352,128]{1,0:T(8,128)(2,1)S(1)}, u32[]{:S(2)}, u32[]{:S(2)}) collective-permute-start(bf16[352,128]{1,0:T(8,128)(2,1)S(1)} %shard_map.133), channel_id=1, source_target_pairs={{0,4},{1,5},{2,6},{3,7},{4,0},{5,1},{6,2},{7,3},{8,12},{9,13},{10,... | collective-permute-start | bytes 270344 | tf_op jit(solution)/shard_map/ppermute | solution.py:55
  69.3 7.8 %collective-permute-start.13 = (bf16[352,128]{1,0:T(8,128)(2,1)S(1)}, bf16[352,128]{1,0:T(8,128)(2,1)S(1)}, u32[]{:S(2)}, u32[]{:S(2)}) collective-permute-start(bf16[352,128]{1,0:T(8,128)(2,1)S(1)} %shard_map.133), channel_id=1, source_target_pairs={{0,2},{1,3},{2,0},{3,1},{4,6},{5,7},{6,4},{7,5},{8,10},{9,11},{10,... | collective-permute-start | bytes 270344 | tf_op jit(solution)/shard_map/ppermute | solution.py:55
  76.0 9.6 %collective-permute-start.20 = (bf16[3,352,128]{2,1,0:T(8,128)(2,1)S(1)}, bf16[3,352,128]{2,1,0:T(8,128)(2,1)S(1)}, u32[]{:S(2)}, u32[]{:S(2)}) collective-permute-start(bf16[3,352,128]{2,1,0:T(8,128)(2,1)S(1)} %pad_maximum_fusion.1), channel_id=1, source_target_pairs={{0,4},{1,5},{2,6},{3,7},{4,0},{5,1},{6,2},{7,3},{8,12},{9,13},{10,... | collective-permute-start | bytes 811016 | tf_op jit(solution)/shard_map/ppermute | solution.py:55
  76.2 9.4 %collective-permute-start.19 = (bf16[3,352,128]{2,1,0:T(8,128)(2,1)S(1)}, bf16[3,352,128]{2,1,0:T(8,128)(2,1)S(1)}, u32[]{:S(2)}, u32[]{:S(2)}) collective-permute-start(bf16[3,352,128]{2,1,0:T(8,128)(2,1)S(1)} %pad_maximum_fusion.1), channel_id=1, source_target_pairs={{0,2},{1,3},{2,0},{3,1},{4,6},{5,7},{6,4},{7,5},{8,10},{9,11},{10,... | collective-permute-start | bytes 811016 | tf_op jit(solution)/shard_map/ppermute | solution.py:55
  77.1 8.4 %collective-permute-start.15 = (bf16[352,128]{1,0:T(8,128)(2,1)S(1)}, bf16[352,128]{1,0:T(8,128)(2,1)S(1)}, u32[]{:S(2)}, u32[]{:S(2)}) collective-permute-start(bf16[352,128]{1,0:T(8,128)(2,1)S(1)} %collective-permute-done.13), channel_id=1, source_target_pairs={{0,4},{1,5},{2,6},{3,7},{4,0},{5,1},{6,2},{7,3},{8,12},{9,13},{10,... | collective-permute-start | bytes 270344 | tf_op jit(solution)/shard_map/ppermute | solution.py:55
  85.7 8.8 %collective-permute-start.24 = (bf16[9,352,128]{2,1,0:T(8,128)(2,1)S(1)}, bf16[9,352,128]{2,1,0:T(8,128)(2,1)S(1)}, u32[]{:S(2)}, u32[]{:S(2)}) collective-permute-start(bf16[9,352,128]{2,1,0:T(8,128)(2,1)S(1)} %constant_dynamic-update-slice_fusion.refs_1_), channel_id=1, source_target_pairs={{0,1},{1,0},{2,3},{3,2},{4,5},{5,4},{6,7},{7,6},{8,9},{9,8},{10,11... | collective-permute-start | bytes 2433032 | tf_op jit(solution)/shard_map/ppermute | solution.py:55
  85.8 7.0 %collective-permute-start.21 = (bf16[2,352,128]{2,1,0:T(8,128)(2,1)S(1)}, bf16[2,352,128]{2,1,0:T(8,128)(2,1)S(1)}, u32[]{:S(2)}, u32[]{:S(2)}) collective-permute-start(bf16[2,352,128]{2,1,0:T(8,128)(2,1)S(1)} %slice.121), channel_id=1, source_target_pairs={{0,2},{1,3},{2,0},{3,1},{4,6},{5,7},{6,4},{7,5},{8,10},{9,11},{10,... | collective-permute-start | bytes 540680 | tf_op jit(solution)/shard_map/ppermute | solution.py:55
  86.8 6.1 %collective-permute-start.22 = (bf16[1,352,128]{2,1,0:T(8,128)(2,1)S(1)}, bf16[1,352,128]{2,1,0:T(8,128)(2,1)S(1)}, u32[]{:S(2)}, u32[]{:S(2)}) collective-permute-start(bf16[1,352,128]{2,1,0:T(8,128)(2,1)S(1)} %slice.122), channel_id=1, source_target_pairs={{0,4},{1,5},{2,6},{3,7},{4,0},{5,1},{6,2},{7,3},{8,12},{9,13},{10,... | collective-permute-start | bytes 270344 | tf_op jit(solution)/shard_map/ppermute | solution.py:55
  87.1 5.9 %collective-permute-start.23 = (bf16[4,352,128]{2,1,0:T(8,128)(2,1)S(1)}, bf16[4,352,128]{2,1,0:T(8,128)(2,1)S(1)}, u32[]{:S(2)}, u32[]{:S(2)}) collective-permute-start(bf16[4,352,128]{2,1,0:T(8,128)(2,1)S(1)} %pad_maximum_fusion.refs_0_), channel_id=1, source_target_pairs={{0,1},{1,0},{2,3},{3,2},{4,5},{5,4},{6,7},{7,6},{8,9},{9,8},{10,11... | collective-permute-start | bytes 1081352 | tf_op jit(solution)/shard_map/ppermute | solution.py:55
  92.9 1.6 %collective-permute-start.25 = (bf16[3,352,128]{2,1,0:T(8,128)(2,1)S(1)}, bf16[3,352,128]{2,1,0:T(8,128)(2,1)S(1)}, u32[]{:S(2)}, u32[]{:S(2)}) collective-permute-start(bf16[3,352,128]{2,1,0:T(8,128)(2,1)S(1)} %constant_dynamic-update-slice_fusion.3.refs_2_), channel_id=1, source_target_pairs={{0,1},{1,0},{2,3},{3,2},{4,5},{5,4},{6,7},{7,6},{8,9},{9,8},{10,11... | collective-permute-start | bytes 811016 | tf_op jit(solution)/shard_map/ppermute | solution.py:55

commit v4 on v3

--- a/solution.py
+++ b/solution.py
@@ -463,12 +463,7 @@
 
 
 def gather_near(grid, near, far):
-    return send(near, grid.flip(2)), send(far, grid.flip(4))
-
-
-def gather_rest(grid, near, col, row):
-    mine = [near, col, row, send(row, grid.flip(2))]
-    return mine + [send(x, grid.flip(1)) for x in mine]
+    return [near, send(near, grid.flip(2)), send(far, grid.flip(4)), send(far, grid.flip(6))]
 
 
 def on_device(
@@ -492,7 +487,7 @@
         cotangent.reshape(tokens, channels),
     )
     asked = spread(ask, grid)
-    col, row = gather_near(grid, near, far)
+    cots = gather_near(grid, near, far)
     local_codes = jnp.dot(codebook, projector, preferred_element_type=jnp.float32).astype(
         jnp.bfloat16
     )
@@ -500,8 +495,8 @@
     onehot = (slot.reshape(tokens, 1) == slot_ids[None, :]).astype(jnp.bfloat16)
     replies = answer(grid, asked, local_codes)
     got = spread(replies, grid)
-    asked, col, row, _ = lax.optimization_barrier((asked, col, row, replies))
-    cots = gather_rest(grid, near, col, row)
+    asked, _, *cots = lax.optimization_barrier((asked, replies, *cots))
+    cots = cots + [send(x, grid.flip(1)) for x in cots]
     kept, sent = proj_part(place, asked, codebook, local_codes)
     proj = (kept + send(sent, grid.flip(1))).reshape(2, 2, PARTS, feat // 16, 128)
     cotangent, _ = lax.optimization_barrier((cotangent, replies))

time: 98.6 us -> 95.1 us (0.965)
  local copies, waits for them, and re-layouts: 2.87 us -> 0.26 us
    unnamed x31 -> x23, local copies, waits for them, and re-layouts: 2.74 us -> 0.13 us
where the time goes in v4:
time: 95.1 us; the launch traced here: 94.7 us
  waiting for transfers between devices  34.4 us (36%)
  starting transfers between devices  31.7 us (33%)
  Pallas kernels  15.4 us (16%)
  matrix products  10.4 us (11%)
  other arithmetic  1.41 us (1%)
  between operations  1.19 us (1%)
    ppermute x26, waiting for transfers between devices, send(): return lax.ppermute(x, AXES, perm)  27.3 us
    ppermute x26, starting transfers between devices, send(): return lax.ppermute(x, AXES, perm)  21.8 us
    all_to_all x2, starting transfers between devices, spread(): return lax.all_to_all(x, AXES, split_axis=0, concat_axis=0, tiled=True)  9.92 us
    all_to_all x2, waiting for transfers between devices, spread(): return lax.all_to_all(x, AXES, split_axis=0, concat_axis=0, tiled=True)  7.18 us
    pallas_call x1, Pallas kernels, group_weights(): pl.pallas_call(functools.partial(weights_kernel, grid, cap), out_shape=ja...  5.03 us
    dot_general x9, matrix products, on_device(): jnp.einsum('nhwo,co->nhwc', grad_window, kernel[row_off, col_off], prefer...  4.87 us
    pallas_call x1, Pallas kernels, finish(): pl.pallas_call(functools.partial(finish_kernel, krows, counts), out_shape...  3.71 us
    dot_general x9, matrix products, on_device(): jnp.einsum('nhwc,co->nhwo', window, kernel[row_off, col_off], preferred_e...  3.46 us
  transfers between devices with their start and end apart: 28, of which 9 were waited for; matrix products, arithmetic and copies ran while one was open for 12% of the time, Pallas kernels for 8%

profile of v4, /device:TPU:0, one launch (start us, length us, event | category | flops | bytes accessed | tf_op | source)
XLA Modules:
  0.0 94.7 jit_solution(17214437885122248834)
XLA Ops:
  0.7 0.6 pad_add_fusion.place_ref
  1.3 3.0 %shard_map.128 = (bf16[528,256]{1,0:T(8,128)(2,1)}, bf16[528,256]{1,0:T(8,128)(2,1)}, s32[1,512]{1,0:T(1,128)}, f32[32,8,384]{2,1,0:T(8,128)}) custom-call(s32[2]{0:T(128)} %pad_add_fusion.place_ref, s32[32,16]{1,0:T(8,128)} %bitcast.137, s32[1,32]{1,0:T(1,128)} %counts_hbm.1, s32[8,32]{1,0:T(8,128)} %bitcast.138, bf16[512,256]{1,0:T(8,128)(2,1)} %bitcast.130, ...), custom_call_target="tpu_custom_call" | custom-call | flops 67108864 | bytes 2097152 | tf_op jit(solution)/shard_map/pallas_call | solution.py:161
  4.3 7.3 %all-to-all-start = ((f32[32,8,384]{2,1,0:T(8,128)}), f32[32,8,384]{2,1,0:T(8,128)S(1)}, u32[]{:S(2)}, u32[]{:S(2)}) async-start(f32[32,8,384]{2,1,0:T(8,128)} %get-tuple-element.37), calls=%async_computation | async-start | bytes 786432 | tf_op jit(solution)/shard_map/all_to_all | solution.py:85
  11.6 2.7 %collective-permute-start.2 = (bf16[528,256]{1,0:T(8,128)(2,1)}, bf16[528,256]{1,0:T(8,128)(2,1)S(1)}, u32[]{:S(2)}, u32[]{:S(2)}) collective-permute-start(bf16[528,256]{1,0:T(8,128)(2,1)} %get-tuple-element.39), channel_id=1, source_target_pairs={{0,6},{1,7},{2,4},{3,5},{4,2},{5,3},{6,0},{7,1},{8,14},{9,15},{10,... | collective-permute-start | bytes 811016 | tf_op jit(solution)/shard_map/ppermute | solution.py:55
  14.4 0.6 collective-permute-start.1
  14.9 0.3 collective-permute-start
  15.2 0.7 convert_element_type.52
  15.9 1.8 %convolution_convert_fusion.codes_ref = bf16[784,256]{1,0:T(8,128)(2,1)S(1)} fusion(bf16[784,768]{1,0:T(8,128)(2,1)} %book_ref.1, bf16[768,256]{1,0:T(8,128)(2,1)S(1)} %copy-done), kind=kOutput, calls=%fused_computation.18 | convolution fusion | flops 308482048 | bytes 1998848 | tf_op jit(solution)/shard_map/dot_general | solution.py:491
  17.6 7.2 %all-to-all-done.asked_ref = f32[32,8,384]{2,1,0:T(8,128)S(1)} async-done(((f32[32,8,384]{2,1,0:T(8,128)}), f32[32,8,384]{2,1,0:T(8,128)S(1)}, u32[]{:S(2)}, u32[]{:S(2)}) %all-to-all-start) | async-done | bytes 393248 | tf_op jit(solution)/shard_map/all_to_all | solution.py:85
  24.8 1.2 %shard_map.129 = bf16[32,16,384]{2,1,0:T(8,128)(2,1)} custom-call(f32[32,8,384]{2,1,0:T(8,128)S(1)} %all-to-all-done.asked_ref, bf16[784,256]{1,0:T(8,128)(2,1)S(1)} %convolution_convert_fusion.codes_ref), custom_call_target="tpu_custom_call" | custom-call | flops 102760448 | bytes 2097152 | tf_op jit(solution)/shard_map/pallas_call | solution.py:218
  26.0 2.6 %all-to-all-start.1 = ((bf16[32,16,384]{2,1,0:T(8,128)(2,1)}), bf16[32,16,384]{2,1,0:T(8,128)(2,1)S(1)}, u32[]{:S(2)}, u32[]{:S(2)}) async-start(bf16[32,16,384]{2,1,0:T(8,128)(2,1)} %shard_map.129), calls=%async_computation.1 | async-start | bytes 786432 | tf_op jit(solution)/shard_map/all_to_all | solution.py:85
  28.7 2.0 %collective-permute-done.refs_1_ = bf16[528,256]{1,0:T(8,128)(2,1)} collective-permute-done((bf16[528,256]{1,0:T(8,128)(2,1)}, bf16[528,256]{1,0:T(8,128)(2,1)}, u32[]{:S(2)}, u32[]{:S(2)}) %collective-permute-start) | collective-permute-done | bytes 270368 | tf_op jit(solution)/shard_map/ppermute | solution.py:55
  30.6 0.4 collective-permute-done.1.refs_2_
  31.0 1.7 %shard_map.130 = (f32[768,128]{1,0:T(8,128)S(1)}, f32[768,128]{1,0:T(8,128)S(1)}) custom-call(s32[2]{0:T(128)S(1)} %copy-done.2, f32[32,8,384]{2,1,0:T(8,128)S(1)} %all-to-all-done.asked_ref, bf16[784,768]{1,0:T(8,128)(2,1)S(1)} %copy-done.1, bf16[784,256]{1,0:T(8,128)(2,1)S(1)} %convolution_convert_fusion.codes_ref), custom_call_target="tpu_custom_call" | custom-call | flops 509607936 | bytes 4194304 | tf_op jit(solution)/shard_map/pallas_call | solution.py:250
  32.8 0.1 collective-permute-start.5
  32.9 0.5 collective-permute-start.6
  33.4 0.1 collective-permute-start.7
  33.5 0.4 collective-permute-start.8
  33.9 0.1 collective-permute-start.3
  34.0 1.4 %fusion.4 = f32[2,16,16,256]{3,2,1,0:T(8,128)S(1)} fusion(bf16[2,16,16,512]{3,2,1,0:T(8,128)(2,1)} %param.17, bf16[3,3,256,512]{3,2,1,0:T(8,128)(2,1)} %param.15), kind=kOutput, calls=%fused_computation.38 | convolution fusion | flops 134217728 | bytes 1310720 | tf_op jit(solution)/shard_map/nhwo,co->nhwc/dot_general | solution.py:531
  35.4 0.3 convolution_add_fusion.15
  35.8 0.4 convolution_add_fusion.14
  36.1 0.3 convolution_add_fusion.13
  36.5 0.3 convolution_add_fusion.12
  36.8 0.4 convolution_add_fusion.11
  37.2 0.4 convolution_add_fusion.10
  37.6 1.0 %collective-permute-start.4 = (bf16[2,4,48,128]{3,2,1,0:T(8,128)(2,1)S(1)}, bf16[2,4,48,128]{3,2,1,0:T(8,128)(2,1)S(1)}, u32[]{:S(2)}, u32[]{:S(2)}) collective-permute-start(bf16[2,4,48,128]{3,2,1,0:T(8,128)(2,1)S(1)} %fusion.43), channel_id=1, source_target_pairs={{0,2},{1,3},{2,0},{3,1},{4,6},{5,7},{6,4},{7,5},{8,10},{9,11},{10,... | collective-permute-start | bytes 294920 | tf_op jit(solution)/shard_map/ppermute | solution.py:55
  38.6 0.3 convolution_add_fusion.9
  39.0 4.0 %collective-permute-done.4 = bf16[2,4,48,128]{3,2,1,0:T(8,128)(2,1)S(1)} collective-permute-done((bf16[2,4,48,128]{3,2,1,0:T(8,128)(2,1)S(1)}, bf16[2,4,48,128]{3,2,1,0:T(8,128)(2,1)S(1)}, u32[]{:S(2)}, u32[]{:S(2)}) %collective-permute-start.4) | collective-permute-done | bytes 98336 | tf_op jit(solution)/shard_map/ppermute | solution.py:55
  43.0 1.4 %collective-permute-start.9 = (bf16[4,48,128]{2,1,0:T(8,128)(2,1)S(1)}, bf16[4,48,128]{2,1,0:T(8,128)(2,1)S(1)}, u32[]{:S(2)}, u32[]{:S(2)}) collective-permute-start(bf16[4,48,128]{2,1,0:T(8,128)(2,1)S(1)} %fusion.44), channel_id=1, source_target_pairs={{0,4},{1,5},{2,6},{3,7},{4,0},{5,1},{6,2},{7,3},{8,12},{9,13},{10,... | collective-permute-start | bytes 147464 | tf_op jit(solution)/shard_map/ppermute | solution.py:55
  44.5 5.0 %shard_map.131.acc_ref = f32[592,256]{1,0:T(8,128)S(1)} custom-call(s32[2]{0:T(128)S(1)} %copy-done.2, bf16[32,16,384]{2,1,0:T(8,128)(2,1)S(1)} %all-to-all-done.1.got_ref, bf16[528,256]{1,0:T(8,128)(2,1)S(1)} %copy-done.3, bf16[528,256]{1,0:T(8,128)(2,1)} %collective-permute-done.refs_1_, bf16[528,256]{1,0:T(8,128)(2,1)} %collective-permute-done.1.refs_2_, ...), custom_call_target="tpu_custom_call" | custom-call | flops 1207959552 | bytes 8388608 | tf_op jit(solution)/shard_map/pallas_call | solution.py:339
  49.5 0.6 shard_map.132
  50.2 1.3 %collective-permute-start.10 = (bf16[352,128]{1,0:T(8,128)(2,1)S(1)}, bf16[352,128]{1,0:T(8,128)(2,1)S(1)}, u32[]{:S(2)}, u32[]{:S(2)}) collective-permute-start(bf16[352,128]{1,0:T(8,128)(2,1)S(1)} %get-tuple-element.54), channel_id=1, source_target_pairs={{0,8},{1,9},{2,10},{3,11},{4,12},{5,13},{6,14},{7,15},{8,16},{9,17... | collective-permute-start | bytes 270344 | tf_op jit(solution)/shard_map/ppermute | solution.py:55
  51.4 2.3 %collective-permute-start.11 = (bf16[352,128]{1,0:T(8,128)(2,1)S(1)}, bf16[352,128]{1,0:T(8,128)(2,1)S(1)}, u32[]{:S(2)}, u32[]{:S(2)}) collective-permute-start(bf16[352,128]{1,0:T(8,128)(2,1)S(1)} %get-tuple-element.55), channel_id=1, source_target_pairs={{0,16},{1,17},{2,18},{3,19},{4,20},{5,21},{6,22},{7,23},{8,24},{9,... | collective-permute-start | bytes 270344 | tf_op jit(solution)/shard_map/ppermute | solution.py:55
  53.8 1.2 %collective-permute-start.12 = (bf16[352,128]{1,0:T(8,128)(2,1)S(1)}, bf16[352,128]{1,0:T(8,128)(2,1)S(1)}, u32[]{:S(2)}, u32[]{:S(2)}) collective-permute-start(bf16[352,128]{1,0:T(8,128)(2,1)S(1)} %get-tuple-element.56), channel_id=1, source_target_pairs={{0,24},{1,25},{2,26},{3,27},{4,28},{5,29},{6,30},{7,31},{8,0},{9,1... | collective-permute-start | bytes 270344 | tf_op jit(solution)/shard_map/ppermute | solution.py:55
  55.0 0.3 convolution_convert_fusion.1
  55.3 0.3 fusion.5
  55.6 0.3 convolution_add_fusion.7
  55.9 0.3 convolution_add_fusion.6
  56.2 0.3 convolution_add_fusion.5
  56.5 0.3 convolution_add_fusion.4
  56.8 0.3 convolution_add_fusion.3
  57.1 0.3 convolution_add_fusion.2
  57.4 0.3 convolution_add_fusion.1
  57.7 2.5 %collective-permute-done.11.refs_1_ = bf16[352,128]{1,0:T(8,128)(2,1)S(1)} collective-permute-done((bf16[352,128]{1,0:T(8,128)(2,1)S(1)}, bf16[352,128]{1,0:T(8,128)(2,1)S(1)}, u32[]{:S(2)}, u32[]{:S(2)}) %collective-permute-start.11) | collective-permute-done | bytes 90144 | tf_op jit(solution)/shard_map/ppermute | solution.py:55
  60.2 0.1 shard_map.133
  60.3 3.1 %collective-permute-start.18 = (bf16[352,128]{1,0:T(8,128)(2,1)S(1)}, bf16[352,128]{1,0:T(8,128)(2,1)S(1)}, u32[]{:S(2)}, u32[]{:S(2)}) collective-permute-start(bf16[352,128]{1,0:T(8,128)(2,1)S(1)} %shard_map.133), channel_id=1, source_target_pairs={{0,24},{1,25},{2,26},{3,27},{4,28},{5,29},{6,30},{7,31},{8,0},{9,1... | collective-permute-start | bytes 270344 | tf_op jit(solution)/shard_map/ppermute | solution.py:55
  63.4 0.6 collective-permute-start.17
  64.1 1.1 %fusion.1 = bf16[2,16,16,512]{3,2,1,0:T(8,128)(2,1)} fusion(f32[2,16,16,512]{3,2,1,0:T(8,128)S(1)} %convolution_add_fusion.1, f32[512]{0:T(512)S(1)} %convert_element_type.52, bf16[2,16,16,256]{3,2,1,0:T(8,128)(2,1)S(1)} %bitcast.126, bf16[3,3,256,512]{3,2,1,0:T(8,128)(2,1)S(1)} %copy-done.7), kind=kOutput, calls=%fused_computation.17 | convolution fusion | flops 135004160 | bytes 2099200 | tf_op jit(solution)/shard_map/nhwc,co->nhwo/dot_general | solution.py:522
  65.2 0.8 collective-permute-start.14
  66.0 0.8 collective-permute-start.13
  66.8 5.3 %collective-permute-done.17 = bf16[352,128]{1,0:T(8,128)(2,1)S(1)} collective-permute-done((bf16[352,128]{1,0:T(8,128)(2,1)S(1)}, bf16[352,128]{1,0:T(8,128)(2,1)S(1)}, u32[]{:S(2)}, u32[]{:S(2)}) %collective-permute-start.17) | collective-permute-done | bytes 90144 | tf_op jit(solution)/shard_map/ppermute | solution.py:55
  72.2 0.7 collective-permute-start.20
  72.9 0.9 collective-permute-start.19
  73.9 1.2 %collective-permute-start.15 = (bf16[352,128]{1,0:T(8,128)(2,1)S(1)}, bf16[352,128]{1,0:T(8,128)(2,1)S(1)}, u32[]{:S(2)}, u32[]{:S(2)}) collective-permute-start(bf16[352,128]{1,0:T(8,128)(2,1)S(1)} %collective-permute-done.13), channel_id=1, source_target_pairs={{0,4},{1,5},{2,6},{3,7},{4,0},{5,1},{6,2},{7,3},{8,12},{9,13},{10,... | collective-permute-start | bytes 270344 | tf_op jit(solution)/shard_map/ppermute | solution.py:55
  75.0 1.1 %fusion.3 = bf16[2,16,16,256]{3,2,1,0:T(8,128)(2,1)} fusion(f32[2,16,16,256]{3,2,1,0:T(8,128)S(1)} %convolution_add_fusion.9, bf16[2,16,16,512]{3,2,1,0:T(8,128)(2,1)S(1)} %copy-done.5, bf16[2,16,16,256]{3,2,1,0:T(8,128)(2,1)S(1)} %bitcast.127, bf16[2,16,16,256]{3,2,1,0:T(8,128)(2,1)S(1)} %copy-done.8, bf16[3,3,256,512]{3,2,1,0:T(8,128)(2,1)S(1)} %copy-done.7), kind=kOutput, calls=%fused_computation.28 | convolution fusion | flops 135135232 | bytes 2097152 | tf_op jit(solution)/shard_map/nhwo,co->nhwc/dot_general | solution.py:531
  76.1 5.9 %collective-permute-done.15 = bf16[352,128]{1,0:T(8,128)(2,1)S(1)} collective-permute-done((bf16[352,128]{1,0:T(8,128)(2,1)S(1)}, bf16[352,128]{1,0:T(8,128)(2,1)S(1)}, u32[]{:S(2)}, u32[]{:S(2)}) %collective-permute-start.15) | collective-permute-done | bytes 90144 | tf_op jit(solution)/shard_map/ppermute | solution.py:55
  82.2 0.1 collective-permute-start.24
  82.3 0.6 collective-permute-start.21
  82.9 0.8 collective-permute-start.22
  83.7 5.6 %collective-permute-done.21 = bf16[2,352,128]{2,1,0:T(8,128)(2,1)S(1)} collective-permute-done((bf16[2,352,128]{2,1,0:T(8,128)(2,1)S(1)}, bf16[2,352,128]{2,1,0:T(8,128)(2,1)S(1)}, u32[]{:S(2)}, u32[]{:S(2)}) %collective-permute-start.21) | collective-permute-done | bytes 180256 | tf_op jit(solution)/shard_map/ppermute | solution.py:55
  89.4 0.1 collective-permute-start.25
  89.5 1.5 %collective-permute-done.25.refs_5_ = bf16[3,352,128]{2,1,0:T(8,128)(2,1)S(1)} collective-permute-done((bf16[3,352,128]{2,1,0:T(8,128)(2,1)S(1)}, bf16[3,352,128]{2,1,0:T(8,128)(2,1)S(1)}, u32[]{:S(2)}, u32[]{:S(2)}) %collective-permute-start.25) | collective-permute-done | bytes 270368 | tf_op jit(solution)/shard_map/ppermute | solution.py:55
  91.0 3.7 %shard_map.134 = (f32[9,256,512]{2,1,0:T(8,128)}, f32[768,256]{1,0:T(8,128)}, f32[1,512]{1,0:T(1,128)}) custom-call(s32[2]{0:T(128)S(1)} %copy-done.2, bf16[4,352,128]{2,1,0:T(8,128)(2,1)S(1)} %pad_maximum_fusion.refs_0_, bf16[9,352,128]{2,1,0:T(8,128)(2,1)S(1)} %constant_dynamic-update-slice_fusion.refs_1_, ...), custom_call_target="tpu_custom_call" | custom-call | tf_op jit(solution)/shard_map/pallas_call | solution.py:451
  (57 shorter events, 0.5 us)
Async XLA Ops:
  0.6 15.2 %copy-start = (bf16[768,256]{1,0:T(8,128)(2,1)S(1)}, bf16[768,256]{1,0:T(8,128)(2,1)}, u32[]{:S(2)}) copy-start(bf16[768,256]{1,0:T(8,128)(2,1)} %param.10) | copy-start | bytes 1179652
  4.3 26.7 %copy-start.1 = (bf16[784,768]{1,0:T(8,128)(2,1)S(1)}, bf16[784,768]{1,0:T(8,128)(2,1)}, u32[]{:S(2)}) copy-start(bf16[784,768]{1,0:T(8,128)(2,1)} %book_ref.1) | copy-start | bytes 3612676
  4.3 26.7 %copy-start.2 = (s32[2]{0:T(128)S(1)}, s32[2]{0:T(128)}, u32[]{:S(2)}) copy-start(s32[2]{0:T(128)} %pad_add_fusion.place_ref) | copy-start | bytes 28
  4.3 20.5 %all-to-all-start = ((f32[32,8,384]{2,1,0:T(8,128)}), f32[32,8,384]{2,1,0:T(8,128)S(1)}, u32[]{:S(2)}, u32[]{:S(2)}) async-start(f32[32,8,384]{2,1,0:T(8,128)} %get-tuple-element.37), calls=%async_computation | async-start | bytes 786432 | tf_op jit(solution)/shard_map/all_to_all | solution.py:85
  11.6 19.0 %collective-permute-start.2 = (bf16[528,256]{1,0:T(8,128)(2,1)}, bf16[528,256]{1,0:T(8,128)(2,1)S(1)}, u32[]{:S(2)}, u32[]{:S(2)}) collective-permute-start(bf16[528,256]{1,0:T(8,128)(2,1)} %get-tuple-element.39), channel_id=1, source_target_pairs={{0,6},{1,7},{2,4},{3,5},{4,2},{5,3},{6,0},{7,1},{8,14},{9,15},{10,... | collective-permute-start | bytes 811016 | tf_op jit(solution)/shard_map/ppermute | solution.py:55
  14.4 16.7 %collective-permute-start.1 = (bf16[528,256]{1,0:T(8,128)(2,1)}, bf16[528,256]{1,0:T(8,128)(2,1)}, u32[]{:S(2)}, u32[]{:S(2)}) collective-permute-start(bf16[528,256]{1,0:T(8,128)(2,1)} %get-tuple-element.39), channel_id=1, source_target_pairs={{0,4},{1,5},{2,6},{3,7},{4,0},{5,1},{6,2},{7,3},{8,12},{9,13},{10,... | collective-permute-start | bytes 811016 | tf_op jit(solution)/shard_map/ppermute | solution.py:55
  14.9 15.7 %collective-permute-start = (bf16[528,256]{1,0:T(8,128)(2,1)}, bf16[528,256]{1,0:T(8,128)(2,1)}, u32[]{:S(2)}, u32[]{:S(2)}) collective-permute-start(bf16[528,256]{1,0:T(8,128)(2,1)} %get-tuple-element.43.refs_0_), channel_id=1, source_target_pairs={{0,2},{1,3},{2,0},{3,1},{4,6},{5,7},{6,4},{7,5},{8,10},{9,11},{10,... | collective-permute-start | bytes 811016 | tf_op jit(solution)/shard_map/ppermute | solution.py:55
  17.6 15.2 %copy-start.3 = (bf16[528,256]{1,0:T(8,128)(2,1)S(1)}, bf16[528,256]{1,0:T(8,128)(2,1)}, u32[]{:S(2)}) copy-start(bf16[528,256]{1,0:T(8,128)(2,1)} %get-tuple-element.43.refs_0_) | copy-start | bytes 811012
  26.0 18.4 %all-to-all-start.1 = ((bf16[32,16,384]{2,1,0:T(8,128)(2,1)}), bf16[32,16,384]{2,1,0:T(8,128)(2,1)S(1)}, u32[]{:S(2)}, u32[]{:S(2)}) async-start(bf16[32,16,384]{2,1,0:T(8,128)(2,1)} %shard_map.129), calls=%async_computation.1 | async-start | bytes 786432 | tf_op jit(solution)/shard_map/all_to_all | solution.py:85
  28.6 6.8 %copy-start.4 = (bf16[2,16,16,512]{3,2,1,0:T(8,128)(2,1)S(1)}, bf16[2,16,16,512]{3,2,1,0:T(8,128)(2,1)}, u32[]{:S(2)}) copy-start(bf16[2,16,16,512]{3,2,1,0:T(8,128)(2,1)} %param.17) | copy-start | bytes 1572868
  28.7 6.8 %copy-start.6 = (bf16[3,3,256,512]{3,2,1,0:T(8,128)(2,1)S(1)}, bf16[3,3,256,512]{3,2,1,0:T(8,128)(2,1)}, u32[]{:S(2)}) copy-start(bf16[3,3,256,512]{3,2,1,0:T(8,128)(2,1)} %param.15) | copy-start | bytes 7077892
  32.8 11.6 %collective-permute-start.5 = (bf16[528,256]{1,0:T(8,128)(2,1)S(1)}, bf16[528,256]{1,0:T(8,128)(2,1)S(1)}, u32[]{:S(2)}, u32[]{:S(2)}) collective-permute-start(bf16[528,256]{1,0:T(8,128)(2,1)S(1)} %copy-done.3), channel_id=1, source_target_pairs={{0,1},{1,0},{2,3},{3,2},{4,5},{5,4},{6,7},{7,6},{8,9},{9,8},{10,11... | collective-permute-start | bytes 811016 | tf_op jit(solution)/shard_map/ppermute | solution.py:55
  32.9 11.6 %collective-permute-start.6 = (bf16[528,256]{1,0:T(8,128)(2,1)}, bf16[528,256]{1,0:T(8,128)(2,1)S(1)}, u32[]{:S(2)}, u32[]{:S(2)}) collective-permute-start(bf16[528,256]{1,0:T(8,128)(2,1)} %collective-permute-done.refs_1_), channel_id=1, source_target_pairs={{0,1},{1,0},{2,3},{3,2},{4,5},{5,4},{6,7},{7,6},{8,9},{9,8},{10,11... | collective-permute-start | bytes 811016 | tf_op jit(solution)/shard_map/ppermute | solution.py:55
  33.4 11.1 %collective-permute-start.7 = (bf16[528,256]{1,0:T(8,128)(2,1)}, bf16[528,256]{1,0:T(8,128)(2,1)S(1)}, u32[]{:S(2)}, u32[]{:S(2)}) collective-permute-start(bf16[528,256]{1,0:T(8,128)(2,1)} %collective-permute-done.1.refs_2_), channel_id=1, source_target_pairs={{0,1},{1,0},{2,3},{3,2},{4,5},{5,4},{6,7},{7,6},{8,9},{9,8},{10,11... | collective-permute-start | bytes 811016 | tf_op jit(solution)/shard_map/ppermute | solution.py:55
  33.5 11.0 %collective-permute-start.8 = (bf16[528,256]{1,0:T(8,128)(2,1)S(1)}, bf16[528,256]{1,0:T(8,128)(2,1)S(1)}, u32[]{:S(2)}, u32[]{:S(2)}) collective-permute-start(bf16[528,256]{1,0:T(8,128)(2,1)S(1)} %collective-permute-done.2.refs_3_), channel_id=1, source_target_pairs={{0,1},{1,0},{2,3},{3,2},{4,5},{5,4},{6,7},{7,6},{8,9},{9,8},{10,11... | collective-permute-start | bytes 811016 | tf_op jit(solution)/shard_map/ppermute | solution.py:55
  33.9 3.6 %collective-permute-start.3 = (f32[768,128]{1,0:T(8,128)S(1)}, f32[768,128]{1,0:T(8,128)S(1)}, u32[]{:S(2)}, u32[]{:S(2)}) collective-permute-start(f32[768,128]{1,0:T(8,128)S(1)} %get-tuple-element.42), channel_id=1, source_target_pairs={{0,1},{1,0},{2,3},{3,2},{4,5},{5,4},{6,7},{7,6},{8,9},{9,8},{10,11... | collective-permute-start | bytes 1179656 | tf_op jit(solution)/shard_map/ppermute | solution.py:55
  37.6 5.3 %collective-permute-start.4 = (bf16[2,4,48,128]{3,2,1,0:T(8,128)(2,1)S(1)}, bf16[2,4,48,128]{3,2,1,0:T(8,128)(2,1)S(1)}, u32[]{:S(2)}, u32[]{:S(2)}) collective-permute-start(bf16[2,4,48,128]{3,2,1,0:T(8,128)(2,1)S(1)} %fusion.43), channel_id=1, source_target_pairs={{0,2},{1,3},{2,0},{3,1},{4,6},{5,7},{6,4},{7,5},{8,10},{9,11},{10,... | collective-permute-start | bytes 294920 | tf_op jit(solution)/shard_map/ppermute | solution.py:55
  43.0 6.5 %collective-permute-start.9 = (bf16[4,48,128]{2,1,0:T(8,128)(2,1)S(1)}, bf16[4,48,128]{2,1,0:T(8,128)(2,1)S(1)}, u32[]{:S(2)}, u32[]{:S(2)}) collective-permute-start(bf16[4,48,128]{2,1,0:T(8,128)(2,1)S(1)} %fusion.44), channel_id=1, source_target_pairs={{0,4},{1,5},{2,6},{3,7},{4,0},{5,1},{6,2},{7,3},{8,12},{9,13},{10,... | collective-permute-start | bytes 147464 | tf_op jit(solution)/shard_map/ppermute | solution.py:55
  44.4 10.6 %copy-start.9 = (s32[1,512]{1,0:T(1,128)S(1)}, s32[1,512]{1,0:T(1,128)}, u32[]{:S(2)}) copy-start(s32[1,512]{1,0:T(1,128)} %get-tuple-element.57) | copy-start | bytes 6148
  44.5 10.8 %copy-start.7 = (bf16[3,3,256,512]{3,2,1,0:T(8,128)(2,1)S(1)}, bf16[3,3,256,512]{3,2,1,0:T(8,128)(2,1)}, u32[]{:S(2)}) copy-start(bf16[3,3,256,512]{3,2,1,0:T(8,128)(2,1)} %param.15) | copy-start | bytes 7077892
  50.2 7.5 %collective-permute-start.10 = (bf16[352,128]{1,0:T(8,128)(2,1)S(1)}, bf16[352,128]{1,0:T(8,128)(2,1)S(1)}, u32[]{:S(2)}, u32[]{:S(2)}) collective-permute-start(bf16[352,128]{1,0:T(8,128)(2,1)S(1)} %get-tuple-element.54), channel_id=1, source_target_pairs={{0,8},{1,9},{2,10},{3,11},{4,12},{5,13},{6,14},{7,15},{8,16},{9,17... | collective-permute-start | bytes 270344 | tf_op jit(solution)/shard_map/ppermute | solution.py:55
  51.4 8.7 %collective-permute-start.11 = (bf16[352,128]{1,0:T(8,128)(2,1)S(1)}, bf16[352,128]{1,0:T(8,128)(2,1)S(1)}, u32[]{:S(2)}, u32[]{:S(2)}) collective-permute-start(bf16[352,128]{1,0:T(8,128)(2,1)S(1)} %get-tuple-element.55), channel_id=1, source_target_pairs={{0,16},{1,17},{2,18},{3,19},{4,20},{5,21},{6,22},{7,23},{8,24},{9,... | collective-permute-start | bytes 270344 | tf_op jit(solution)/shard_map/ppermute | solution.py:55
  53.8 6.4 %collective-permute-start.12 = (bf16[352,128]{1,0:T(8,128)(2,1)S(1)}, bf16[352,128]{1,0:T(8,128)(2,1)S(1)}, u32[]{:S(2)}, u32[]{:S(2)}) collective-permute-start(bf16[352,128]{1,0:T(8,128)(2,1)S(1)} %get-tuple-element.56), channel_id=1, source_target_pairs={{0,24},{1,25},{2,26},{3,27},{4,28},{5,29},{6,30},{7,31},{8,0},{9,1... | collective-permute-start | bytes 270344 | tf_op jit(solution)/shard_map/ppermute | solution.py:55
  57.4 17.6 %copy-start.5 = (bf16[2,16,16,512]{3,2,1,0:T(8,128)(2,1)S(1)}, bf16[2,16,16,512]{3,2,1,0:T(8,128)(2,1)}, u32[]{:S(2)}) copy-start(bf16[2,16,16,512]{3,2,1,0:T(8,128)(2,1)} %param.17) | copy-start | bytes 1572868
  57.4 17.6 %copy-start.8 = (bf16[2,16,16,256]{3,2,1,0:T(8,128)(2,1)S(1)}, bf16[2,16,16,256]{3,2,1,0:T(8,128)(2,1)}, u32[]{:S(2)}) copy-start(bf16[2,16,16,256]{3,2,1,0:T(8,128)(2,1)} %param.11) | copy-start | bytes 786436
  60.3 6.6 %collective-permute-start.18 = (bf16[352,128]{1,0:T(8,128)(2,1)S(1)}, bf16[352,128]{1,0:T(8,128)(2,1)S(1)}, u32[]{:S(2)}, u32[]{:S(2)}) collective-permute-start(bf16[352,128]{1,0:T(8,128)(2,1)S(1)} %shard_map.133), channel_id=1, source_target_pairs={{0,24},{1,25},{2,26},{3,27},{4,28},{5,29},{6,30},{7,31},{8,0},{9,1... | collective-permute-start | bytes 270344 | tf_op jit(solution)/shard_map/ppermute | solution.py:55
  63.4 8.7 %collective-permute-start.17 = (bf16[352,128]{1,0:T(8,128)(2,1)S(1)}, bf16[352,128]{1,0:T(8,128)(2,1)S(1)}, u32[]{:S(2)}, u32[]{:S(2)}) collective-permute-start(bf16[352,128]{1,0:T(8,128)(2,1)S(1)} %shard_map.133), channel_id=1, source_target_pairs={{0,16},{1,17},{2,18},{3,19},{4,20},{5,21},{6,22},{7,23},{8,24},{9,... | collective-permute-start | bytes 270344 | tf_op jit(solution)/shard_map/ppermute | solution.py:55
  64.0 8.2 %collective-permute-start.16 = (bf16[352,128]{1,0:T(8,128)(2,1)S(1)}, bf16[352,128]{1,0:T(8,128)(2,1)S(1)}, u32[]{:S(2)}, u32[]{:S(2)}) collective-permute-start(bf16[352,128]{1,0:T(8,128)(2,1)S(1)} %shard_map.133), channel_id=1, source_target_pairs={{0,8},{1,9},{2,10},{3,11},{4,12},{5,13},{6,14},{7,15},{8,16},{9,17... | collective-permute-start | bytes 270344 | tf_op jit(solution)/shard_map/ppermute | solution.py:55
  65.2 10.9 %collective-permute-start.14 = (bf16[352,128]{1,0:T(8,128)(2,1)S(1)}, bf16[352,128]{1,0:T(8,128)(2,1)S(1)}, u32[]{:S(2)}, u32[]{:S(2)}) collective-permute-start(bf16[352,128]{1,0:T(8,128)(2,1)S(1)} %shard_map.133), channel_id=1, source_target_pairs={{0,4},{1,5},{2,6},{3,7},{4,0},{5,1},{6,2},{7,3},{8,12},{9,13},{10,... | collective-permute-start | bytes 270344 | tf_op jit(solution)/shard_map/ppermute | solution.py:55
  66.0 7.9 %collective-permute-start.13 = (bf16[352,128]{1,0:T(8,128)(2,1)S(1)}, bf16[352,128]{1,0:T(8,128)(2,1)S(1)}, u32[]{:S(2)}, u32[]{:S(2)}) collective-permute-start(bf16[352,128]{1,0:T(8,128)(2,1)S(1)} %shard_map.133), channel_id=1, source_target_pairs={{0,2},{1,3},{2,0},{3,1},{4,6},{5,7},{6,4},{7,5},{8,10},{9,11},{10,... | collective-permute-start | bytes 270344 | tf_op jit(solution)/shard_map/ppermute | solution.py:55
  72.2 9.9 %collective-permute-start.20 = (bf16[3,352,128]{2,1,0:T(8,128)(2,1)S(1)}, bf16[3,352,128]{2,1,0:T(8,128)(2,1)S(1)}, u32[]{:S(2)}, u32[]{:S(2)}) collective-permute-start(bf16[3,352,128]{2,1,0:T(8,128)(2,1)S(1)} %pad_maximum_fusion.1), channel_id=1, source_target_pairs={{0,4},{1,5},{2,6},{3,7},{4,0},{5,1},{6,2},{7,3},{8,12},{9,13},{10,... | collective-permute-start | bytes 811016 | tf_op jit(solution)/shard_map/ppermute | solution.py:55
  72.9 9.1 %collective-permute-start.19 = (bf16[3,352,128]{2,1,0:T(8,128)(2,1)S(1)}, bf16[3,352,128]{2,1,0:T(8,128)(2,1)S(1)}, u32[]{:S(2)}, u32[]{:S(2)}) collective-permute-start(bf16[3,352,128]{2,1,0:T(8,128)(2,1)S(1)} %pad_maximum_fusion.1), channel_id=1, source_target_pairs={{0,2},{1,3},{2,0},{3,1},{4,6},{5,7},{6,4},{7,5},{8,10},{9,11},{10,... | collective-permute-start | bytes 811016 | tf_op jit(solution)/shard_map/ppermute | solution.py:55
  73.9 8.2 %collective-permute-start.15 = (bf16[352,128]{1,0:T(8,128)(2,1)S(1)}, bf16[352,128]{1,0:T(8,128)(2,1)S(1)}, u32[]{:S(2)}, u32[]{:S(2)}) collective-permute-start(bf16[352,128]{1,0:T(8,128)(2,1)S(1)} %collective-permute-done.13), channel_id=1, source_target_pairs={{0,4},{1,5},{2,6},{3,7},{4,0},{5,1},{6,2},{7,3},{8,12},{9,13},{10,... | collective-permute-start | bytes 270344 | tf_op jit(solution)/shard_map/ppermute | solution.py:55
  82.2 8.8 %collective-permute-start.24 = (bf16[9,352,128]{2,1,0:T(8,128)(2,1)S(1)}, bf16[9,352,128]{2,1,0:T(8,128)(2,1)S(1)}, u32[]{:S(2)}, u32[]{:S(2)}) collective-permute-start(bf16[9,352,128]{2,1,0:T(8,128)(2,1)S(1)} %constant_dynamic-update-slice_fusion.refs_1_), channel_id=1, source_target_pairs={{0,1},{1,0},{2,3},{3,2},{4,5},{5,4},{6,7},{7,6},{8,9},{9,8},{10,11... | collective-permute-start | bytes 2433032 | tf_op jit(solution)/shard_map/ppermute | solution.py:55
  82.3 7.0 %collective-permute-start.21 = (bf16[2,352,128]{2,1,0:T(8,128)(2,1)S(1)}, bf16[2,352,128]{2,1,0:T(8,128)(2,1)S(1)}, u32[]{:S(2)}, u32[]{:S(2)}) collective-permute-start(bf16[2,352,128]{2,1,0:T(8,128)(2,1)S(1)} %slice.121), channel_id=1, source_target_pairs={{0,2},{1,3},{2,0},{3,1},{4,6},{5,7},{6,4},{7,5},{8,10},{9,11},{10,... | collective-permute-start | bytes 540680 | tf_op jit(solution)/shard_map/ppermute | solution.py:55
  82.9 6.4 %collective-permute-start.22 = (bf16[1,352,128]{2,1,0:T(8,128)(2,1)S(1)}, bf16[1,352,128]{2,1,0:T(8,128)(2,1)S(1)}, u32[]{:S(2)}, u32[]{:S(2)}) collective-permute-start(bf16[1,352,128]{2,1,0:T(8,128)(2,1)S(1)} %slice.122), channel_id=1, source_target_pairs={{0,4},{1,5},{2,6},{3,7},{4,0},{5,1},{6,2},{7,3},{8,12},{9,13},{10,... | collective-permute-start | bytes 270344 | tf_op jit(solution)/shard_map/ppermute | solution.py:55
  83.7 5.8 %collective-permute-start.23 = (bf16[4,352,128]{2,1,0:T(8,128)(2,1)S(1)}, bf16[4,352,128]{2,1,0:T(8,128)(2,1)S(1)}, u32[]{:S(2)}, u32[]{:S(2)}) collective-permute-start(bf16[4,352,128]{2,1,0:T(8,128)(2,1)S(1)} %pad_maximum_fusion.refs_0_), channel_id=1, source_target_pairs={{0,1},{1,0},{2,3},{3,2},{4,5},{5,4},{6,7},{7,6},{8,9},{9,8},{10,11... | collective-permute-start | bytes 1081352 | tf_op jit(solution)/shard_map/ppermute | solution.py:55
  89.4 1.6 %collective-permute-start.25 = (bf16[3,352,128]{2,1,0:T(8,128)(2,1)S(1)}, bf16[3,352,128]{2,1,0:T(8,128)(2,1)S(1)}, u32[]{:S(2)}, u32[]{:S(2)}) collective-permute-start(bf16[3,352,128]{2,1,0:T(8,128)(2,1)S(1)} %constant_dynamic-update-slice_fusion.3.refs_2_), channel_id=1, source_target_pairs={{0,1},{1,0},{2,3},{3,2},{4,5},{5,4},{6,7},{7,6},{8,9},{9,8},{10,11... | collective-permute-start | bytes 811016 | tf_op jit(solution)/shard_map/ppermute | solution.py:55

commit v5 on v4

--- a/solution.py
+++ b/solution.py
@@ -258,13 +258,32 @@
     )(place, asked, book, codes)
 
 
-def half(x, axis, index):
-    return lax.dynamic_index_in_dim(x, index, axis, keepdims=False)
-
-
-def exchange(x, own, perm):
-    sent = half(x, 0, 1 - own).astype(jnp.bfloat16)
-    return half(x, 0, own) + send(sent, perm).astype(jnp.float32)
+def proj_split_kernel(place_ref, kept_ref, got_ref, own_ref, *rest):
+    send_refs, all_ref = rest[:-1], rest[-1]
+    all_ref[...] = kept_ref[...] + got_ref[...]
+    i = place_ref[0]
+    size = all_ref.shape[0] // 4
+
+    def quarter(place):
+        start = (place // 2 % 2 * 2 + place // 4) * size
+        return all_ref[pl.ds(pl.multiple_of(start, 8), size), :].reshape(own_ref.shape)
+
+    own_ref[...] = quarter(i)
+    for bits, send_ref in zip((2, 4, 6), send_refs):
+        send_ref[...] = quarter(i ^ bits).astype(jnp.bfloat16)
+
+
+def proj_split(place, kept, got):
+    shape = (PARTS, kept.shape[0] // 16, 128)
+    return pl.pallas_call(
+        proj_split_kernel,
+        out_shape=[jax.ShapeDtypeStruct(shape, jnp.float32)]
+        + [jax.ShapeDtypeStruct(shape, jnp.bfloat16)] * 3,
+        in_specs=[SMEM_SPEC] + vmem(2),
+        out_specs=vmem(4),
+        scratch_shapes=[pltpu.VMEM(kept.shape, jnp.float32)],
+        compiler_params=LIMIT,
+    )(place, kept, got)
 
 
 def proj_place(i, q, prows):
@@ -313,8 +332,12 @@
             acc_ref[...] += value
 
 
-def pack_kernel(krows, place_ref, acc_ref, proj_ref, own_ref, *send_refs):
+def pack_kernel(krows, place_ref, acc_ref, *refs):
+    proj_refs, (own_ref, *send_refs) = refs[:4], refs[4:]
     part = place_ref[1]
+
+    def proj(q):
+        return sum(ref[q].astype(jnp.float32) for ref in proj_refs)
 
     def piece(q):
         lanes = pl.ds(pl.multiple_of(q % 2 * 128, 128), 128)
@@ -322,7 +345,7 @@
         return acc_ref[rows, lanes], acc_ref[2 * krows :, lanes]
 
     own_ref[:krows], own_ref[krows : krows + 16] = piece(part)
-    own_ref[krows + 16 :] = proj_ref[part]
+    own_ref[krows + 16 :] = proj(part)
     row = lax.broadcasted_iota(jnp.int32, (16, 128), 0)
     for k, send_ref in enumerate(send_refs, 1):
         value, last = piece((part + k) % PARTS)
@@ -330,7 +353,7 @@
         lower = (last - upper)[0:1]
         send_ref[:krows] = value.astype(jnp.bfloat16)
         send_ref[krows : krows + 16] = jnp.where(row == 1, lower, last).astype(jnp.bfloat16)
-        send_ref[krows + 16 :] = proj_ref[(part + k) % PARTS].astype(jnp.bfloat16)
+        send_ref[krows + 16 :] = proj((part + k) % PARTS).astype(jnp.bfloat16)
 
 
 def group_weights(grid, place, got, cots, cap):
@@ -349,15 +372,15 @@
 
 def pack(place, acc, proj):
     krows = (acc.shape[0] - 16) // 2
-    height = krows + 16 + proj.shape[1]
+    height = krows + 16 + proj[0].shape[1]
     return pl.pallas_call(
         functools.partial(pack_kernel, krows),
         out_shape=[jax.ShapeDtypeStruct((height, 128), jnp.float32)]
         + [jax.ShapeDtypeStruct((height, 128), jnp.bfloat16)] * (PARTS - 1),
-        in_specs=[SMEM_SPEC] + vmem(2),
+        in_specs=[SMEM_SPEC] + vmem(5),
         out_specs=vmem(PARTS),
         compiler_params=LIMIT,
-    )(place, acc, proj)
+    )(place, acc, *proj)
 
 
 def combine_kernel(krows, own_ref, *refs):
@@ -498,13 +521,11 @@
     asked, _, *cots = lax.optimization_barrier((asked, replies, *cots))
     cots = cots + [send(x, grid.flip(1)) for x in cots]
     kept, sent = proj_part(place, asked, codebook, local_codes)
-    proj = (kept + send(sent, grid.flip(1))).reshape(2, 2, PARTS, feat // 16, 128)
+    proj = proj_split(place, kept, send(sent, grid.flip(1)))
     cotangent, _ = lax.optimization_barrier((cotangent, replies))
-    proj = exchange(proj, i // 2 % 2, grid.flip(2))
-    got_half = send(half(proj, 0, 1 - i // 4).astype(jnp.bfloat16), grid.flip(4))
+    gains = [send(x, grid.flip(bits)) for x, bits in zip(proj[1:], (2, 4, 6))]
     acc = group_weights(grid, place, got, cots, cap)
-    kept, acc = lax.optimization_barrier((half(proj, 0, i // 4), acc))
-    own, *sends = pack(place, acc, kept + got_half.astype(jnp.float32))
+    own, *sends = pack(place, acc, [proj[0]] + gains)
     codes = got[:, cap:, 128:].reshape(slots, zch)
     codes, own, *sends = lax.optimization_barrier((codes, own, *sends))
     own, received = reduce_planes(grid, own, sends, r)

time: 95.1 us -> 93.7 us (0.985)
  waiting for transfers between devices: 34.4 us -> 32.5 us
    ppermute x26 -> x27, waiting for transfers between devices: 27.3 us -> 23 us  [send(): return lax.ppermute(x, AXES, perm)]
    all_to_all x2, waiting for transfers between devices: 7.18 us -> 9.51 us  [spread(): return lax.all_to_all(x, AXES, split_axis=0, concat_axis=0, tiled=True)]
    ppermute x26 -> x27, starting transfers between devices: 21.8 us -> 21.8 us  [send(): return lax.ppermute(x, AXES, perm)]
  transfers between devices with their start and end apart: 28 -> 29, of which waited for: 9 -> 10; matrix products, arithmetic and copies ran while one was open for 12% -> 12% of each run, Pallas kernels for 8% -> 9%
where the time goes in v5:
time: 93.7 us; the launch traced here: 93.2 us
  waiting for transfers between devices  32.5 us (35%)
  starting transfers between devices  31.7 us (34%)
  Pallas kernels  15.9 us (17%)
  matrix products  10.4 us (11%)
  other arithmetic  1.41 us (2%)
  between operations  1.12 us (1%)
    ppermute x27, waiting for transfers between devices, send(): return lax.ppermute(x, AXES, perm)  23 us
    ppermute x27, starting transfers between devices, send(): return lax.ppermute(x, AXES, perm)  21.8 us
    all_to_all x2, starting transfers between devices, spread(): return lax.all_to_all(x, AXES, split_axis=0, concat_axis=0, tiled=True)  9.92 us
    all_to_all x2, waiting for transfers between devices, spread(): return lax.all_to_all(x, AXES, split_axis=0, concat_axis=0, tiled=True)  9.51 us
    pallas_call x1, Pallas kernels, group_weights(): pl.pallas_call(functools.partial(weights_kernel, grid, cap), out_shape=ja...  4.96 us
    dot_general x9, matrix products, on_device(): jnp.einsum('nhwo,co->nhwc', grad_window, kernel[row_off, col_off], prefer...  4.88 us
    pallas_call x1, Pallas kernels, finish(): pl.pallas_call(functools.partial(finish_kernel, krows, counts), out_shape...  3.71 us
    dot_general x9, matrix products, on_device(): jnp.einsum('nhwc,co->nhwo', window, kernel[row_off, col_off], preferred_e...  3.45 us
  transfers between devices with their start and end apart: 29, of which 10 were waited for; matrix products, arithmetic and copies ran while one was open for 12% of the time, Pallas kernels for 9%

profile of v5, /device:TPU:0, one launch (start us, length us, event | category | flops | bytes accessed | tf_op | source)
XLA Modules:
  0.0 93.2 jit_solution(6692185961556475257)
XLA Ops:
  0.7 0.7 pad_add_fusion.place_ref
  1.4 3.0 %shard_map.128 = (bf16[528,256]{1,0:T(8,128)(2,1)}, bf16[528,256]{1,0:T(8,128)(2,1)}, s32[1,512]{1,0:T(1,128)}, f32[32,8,384]{2,1,0:T(8,128)}) custom-call(s32[2]{0:T(128)} %pad_add_fusion.place_ref, s32[32,16]{1,0:T(8,128)} %bitcast.126, s32[1,32]{1,0:T(1,128)} %counts_hbm.1, s32[8,32]{1,0:T(8,128)} %bitcast.127, bf16[512,256]{1,0:T(8,128)(2,1)} %bitcast.119, ...), custom_call_target="tpu_custom_call" | custom-call | flops 67108864 | bytes 2097152 | tf_op jit(solution)/shard_map/pallas_call | solution.py:161
  4.4 7.3 %all-to-all-start = ((f32[32,8,384]{2,1,0:T(8,128)}), f32[32,8,384]{2,1,0:T(8,128)S(1)}, u32[]{:S(2)}, u32[]{:S(2)}) async-start(f32[32,8,384]{2,1,0:T(8,128)} %get-tuple-element.39), calls=%async_computation | async-start | bytes 786432 | tf_op jit(solution)/shard_map/all_to_all | solution.py:85
  11.7 2.7 %collective-permute-start.2 = (bf16[528,256]{1,0:T(8,128)(2,1)}, bf16[528,256]{1,0:T(8,128)(2,1)}, u32[]{:S(2)}, u32[]{:S(2)}) collective-permute-start(bf16[528,256]{1,0:T(8,128)(2,1)} %get-tuple-element.41), channel_id=1, source_target_pairs={{0,6},{1,7},{2,4},{3,5},{4,2},{5,3},{6,0},{7,1},{8,14},{9,15},{10,... | collective-permute-start | bytes 811016 | tf_op jit(solution)/shard_map/ppermute | solution.py:55
  14.4 0.6 collective-permute-start.1
  15.0 0.3 collective-permute-start
  15.3 0.7 convert_element_type.28
  15.9 1.8 %convolution_convert_fusion.codes_ref = bf16[784,256]{1,0:T(8,128)(2,1)S(1)} fusion(bf16[784,768]{1,0:T(8,128)(2,1)} %book_ref.1, bf16[768,256]{1,0:T(8,128)(2,1)S(1)} %copy-done), kind=kOutput, calls=%fused_computation.18 | convolution fusion | flops 308482048 | bytes 1998848 | tf_op jit(solution)/shard_map/dot_general | solution.py:514
  17.7 7.2 %all-to-all-done.asked_ref = f32[32,8,384]{2,1,0:T(8,128)S(1)} async-done(((f32[32,8,384]{2,1,0:T(8,128)}), f32[32,8,384]{2,1,0:T(8,128)S(1)}, u32[]{:S(2)}, u32[]{:S(2)}) %all-to-all-start) | async-done | bytes 393248 | tf_op jit(solution)/shard_map/all_to_all | solution.py:85
  24.9 1.2 %shard_map.129 = bf16[32,16,384]{2,1,0:T(8,128)(2,1)} custom-call(f32[32,8,384]{2,1,0:T(8,128)S(1)} %all-to-all-done.asked_ref, bf16[784,256]{1,0:T(8,128)(2,1)S(1)} %convolution_convert_fusion.codes_ref), custom_call_target="tpu_custom_call" | custom-call | flops 102760448 | bytes 2097152 | tf_op jit(solution)/shard_map/pallas_call | solution.py:218
  26.1 2.6 %all-to-all-start.1 = ((bf16[32,16,384]{2,1,0:T(8,128)(2,1)}), bf16[32,16,384]{2,1,0:T(8,128)(2,1)S(1)}, u32[]{:S(2)}, u32[]{:S(2)}) async-start(bf16[32,16,384]{2,1,0:T(8,128)(2,1)} %shard_map.129), calls=%async_computation.1 | async-start | bytes 786432 | tf_op jit(solution)/shard_map/all_to_all | solution.py:85
  28.7 2.0 %collective-permute-done.refs_1_ = bf16[528,256]{1,0:T(8,128)(2,1)} collective-permute-done((bf16[528,256]{1,0:T(8,128)(2,1)}, bf16[528,256]{1,0:T(8,128)(2,1)}, u32[]{:S(2)}, u32[]{:S(2)}) %collective-permute-start) | collective-permute-done | bytes 270368 | tf_op jit(solution)/shard_map/ppermute | solution.py:55
  30.7 0.4 collective-permute-done.1.refs_2_
  31.1 1.7 %shard_map.131 = (f32[768,128]{1,0:T(8,128)S(1)}, f32[768,128]{1,0:T(8,128)S(1)}) custom-call(s32[2]{0:T(128)S(1)} %copy-done.2, f32[32,8,384]{2,1,0:T(8,128)S(1)} %all-to-all-done.asked_ref, bf16[784,768]{1,0:T(8,128)(2,1)S(1)} %copy-done.1, bf16[784,256]{1,0:T(8,128)(2,1)S(1)} %convolution_convert_fusion.codes_ref), custom_call_target="tpu_custom_call" | custom-call | flops 509607936 | bytes 4194304 | tf_op jit(solution)/shard_map/pallas_call | solution.py:250
  33.0 0.5 collective-permute-start.4
  33.5 0.1 collective-permute-start.5
  33.5 0.4 collective-permute-start.6
  34.0 0.1 collective-permute-start.7
  34.0 1.4 %fusion.4 = f32[2,16,16,256]{3,2,1,0:T(8,128)S(1)} fusion(bf16[2,16,16,512]{3,2,1,0:T(8,128)(2,1)} %param.17, bf16[3,3,256,512]{3,2,1,0:T(8,128)(2,1)} %param.15), kind=kOutput, calls=%fused_computation.38 | convolution fusion | flops 134217728 | bytes 1310720 | tf_op jit(solution)/shard_map/nhwo,co->nhwc/dot_general | solution.py:552
  35.5 0.3 convolution_add_fusion.15
  35.9 0.3 convolution_add_fusion.14
  36.2 0.3 convolution_add_fusion.13
  36.6 0.3 convolution_add_fusion.12
  36.9 0.4 convolution_add_fusion.11
  37.3 0.4 convolution_add_fusion.10
  37.6 0.3 convolution_add_fusion.9
  38.0 0.6 shard_map.132
  38.6 1.0 %collective-permute-start.8 = (bf16[4,48,128]{2,1,0:T(8,128)(2,1)S(1)}, bf16[4,48,128]{2,1,0:T(8,128)(2,1)S(1)}, u32[]{:S(2)}, u32[]{:S(2)}) collective-permute-start(bf16[4,48,128]{2,1,0:T(8,128)(2,1)S(1)} %get-tuple-element.50), channel_id=1, source_target_pairs={{0,2},{1,3},{2,0},{3,1},{4,6},{5,7},{6,4},{7,5},{8,10},{9,11},{10,... | collective-permute-start | bytes 147464 | tf_op jit(solution)/shard_map/ppermute | solution.py:55
  39.6 2.3 %all-to-all-done.1.got_ref = bf16[32,16,384]{2,1,0:T(8,128)(2,1)S(1)} async-done(((bf16[32,16,384]{2,1,0:T(8,128)(2,1)}), bf16[32,16,384]{2,1,0:T(8,128)(2,1)S(1)}, u32[]{:S(2)}, u32[]{:S(2)}) %all-to-all-start.1) | async-done | bytes 393248 | tf_op jit(solution)/shard_map/all_to_all | solution.py:85
  41.9 1.0 %collective-permute-start.9 = (bf16[4,48,128]{2,1,0:T(8,128)(2,1)S(1)}, bf16[4,48,128]{2,1,0:T(8,128)(2,1)S(1)}, u32[]{:S(2)}, u32[]{:S(2)}) collective-permute-start(bf16[4,48,128]{2,1,0:T(8,128)(2,1)S(1)} %get-tuple-element.51), channel_id=1, source_target_pairs={{0,4},{1,5},{2,6},{3,7},{4,0},{5,1},{6,2},{7,3},{8,12},{9,13},{10,... | collective-permute-start | bytes 147464 | tf_op jit(solution)/shard_map/ppermute | solution.py:55
  43.0 1.0 %collective-permute-start.10 = (bf16[4,48,128]{2,1,0:T(8,128)(2,1)S(1)}, bf16[4,48,128]{2,1,0:T(8,128)(2,1)S(1)}, u32[]{:S(2)}, u32[]{:S(2)}) collective-permute-start(bf16[4,48,128]{2,1,0:T(8,128)(2,1)S(1)} %get-tuple-element.52), channel_id=1, source_target_pairs={{0,6},{1,7},{2,4},{3,5},{4,2},{5,3},{6,0},{7,1},{8,14},{9,15},{10,... | collective-permute-start | bytes 147464 | tf_op jit(solution)/shard_map/ppermute | solution.py:55
  43.9 5.0 %shard_map.130.acc_ref = f32[592,256]{1,0:T(8,128)S(1)} custom-call(s32[2]{0:T(128)S(1)} %copy-done.2, bf16[32,16,384]{2,1,0:T(8,128)(2,1)S(1)} %all-to-all-done.1.got_ref, bf16[528,256]{1,0:T(8,128)(2,1)S(1)} %copy-done.3, bf16[528,256]{1,0:T(8,128)(2,1)} %collective-permute-done.refs_1_, bf16[528,256]{1,0:T(8,128)(2,1)} %collective-permute-done.1.refs_2_, ...), custom_call_target="tpu_custom_call" | custom-call | flops 1207959552 | bytes 8388608 | tf_op jit(solution)/shard_map/pallas_call | solution.py:362
  48.9 0.6 shard_map.133
  49.6 0.8 collective-permute-start.11
  50.4 1.5 %collective-permute-start.12 = (bf16[352,128]{1,0:T(8,128)(2,1)S(1)}, bf16[352,128]{1,0:T(8,128)(2,1)S(1)}, u32[]{:S(2)}, u32[]{:S(2)}) collective-permute-start(bf16[352,128]{1,0:T(8,128)(2,1)S(1)} %get-tuple-element.59), channel_id=1, source_target_pairs={{0,16},{1,17},{2,18},{3,19},{4,20},{5,21},{6,22},{7,23},{8,24},{9,... | collective-permute-start | bytes 270344 | tf_op jit(solution)/shard_map/ppermute | solution.py:55
  51.8 1.8 %collective-permute-start.13 = (bf16[352,128]{1,0:T(8,128)(2,1)S(1)}, bf16[352,128]{1,0:T(8,128)(2,1)S(1)}, u32[]{:S(2)}, u32[]{:S(2)}) collective-permute-start(bf16[352,128]{1,0:T(8,128)(2,1)S(1)} %get-tuple-element.60), channel_id=1, source_target_pairs={{0,24},{1,25},{2,26},{3,27},{4,28},{5,29},{6,30},{7,31},{8,0},{9,1... | collective-permute-start | bytes 270344 | tf_op jit(solution)/shard_map/ppermute | solution.py:55
  53.6 0.3 convolution_convert_fusion.1
  53.9 0.3 fusion.5
  54.2 0.3 convolution_add_fusion.7
  54.5 0.3 convolution_add_fusion.6
  54.8 0.3 convolution_add_fusion.5
  55.1 0.3 convolution_add_fusion.4
  55.4 0.3 convolution_add_fusion.3
  55.7 0.3 convolution_add_fusion.2
  56.0 0.3 convolution_add_fusion.1
  56.3 0.6 collective-permute-done.11.refs_0_
  56.9 2.9 %collective-permute-done.12.refs_1_ = bf16[352,128]{1,0:T(8,128)(2,1)S(1)} collective-permute-done((bf16[352,128]{1,0:T(8,128)(2,1)S(1)}, bf16[352,128]{1,0:T(8,128)(2,1)S(1)}, u32[]{:S(2)}, u32[]{:S(2)}) %collective-permute-start.12) | collective-permute-done | bytes 90144 | tf_op jit(solution)/shard_map/ppermute | solution.py:55
  59.9 0.1 shard_map.134
  59.9 2.1 %collective-permute-start.19 = (bf16[352,128]{1,0:T(8,128)(2,1)S(1)}, bf16[352,128]{1,0:T(8,128)(2,1)S(1)}, u32[]{:S(2)}, u32[]{:S(2)}) collective-permute-start(bf16[352,128]{1,0:T(8,128)(2,1)S(1)} %shard_map.134), channel_id=1, source_target_pairs={{0,24},{1,25},{2,26},{3,27},{4,28},{5,29},{6,30},{7,31},{8,0},{9,1... | collective-permute-start | bytes 270344 | tf_op jit(solution)/shard_map/ppermute | solution.py:55
  62.0 1.3 %collective-permute-start.18 = (bf16[352,128]{1,0:T(8,128)(2,1)S(1)}, bf16[352,128]{1,0:T(8,128)(2,1)S(1)}, u32[]{:S(2)}, u32[]{:S(2)}) collective-permute-start(bf16[352,128]{1,0:T(8,128)(2,1)S(1)} %shard_map.134), channel_id=1, source_target_pairs={{0,16},{1,17},{2,18},{3,19},{4,20},{5,21},{6,22},{7,23},{8,24},{9,... | collective-permute-start | bytes 270344 | tf_op jit(solution)/shard_map/ppermute | solution.py:55
  63.3 1.1 %fusion.1 = bf16[2,16,16,512]{3,2,1,0:T(8,128)(2,1)} fusion(f32[2,16,16,512]{3,2,1,0:T(8,128)S(1)} %convolution_add_fusion.1, f32[512]{0:T(512)S(1)} %convert_element_type.28, bf16[2,16,16,256]{3,2,1,0:T(8,128)(2,1)S(1)} %bitcast.117, bf16[3,3,256,512]{3,2,1,0:T(8,128)(2,1)S(1)} %copy-done.7), kind=kOutput, calls=%fused_computation.17 | convolution fusion | flops 135004160 | bytes 2099200 | tf_op jit(solution)/shard_map/nhwc,co->nhwo/dot_general | solution.py:543
  64.4 0.4 collective-permute-start.15
  64.8 1.5 %collective-permute-start.14 = (bf16[352,128]{1,0:T(8,128)(2,1)S(1)}, bf16[352,128]{1,0:T(8,128)(2,1)S(1)}, u32[]{:S(2)}, u32[]{:S(2)}) collective-permute-start(bf16[352,128]{1,0:T(8,128)(2,1)S(1)} %shard_map.134), channel_id=1, source_target_pairs={{0,2},{1,3},{2,0},{3,1},{4,6},{5,7},{6,4},{7,5},{8,10},{9,11},{10,... | collective-permute-start | bytes 270344 | tf_op jit(solution)/shard_map/ppermute | solution.py:55
  66.3 5.0 %collective-permute-done.18 = bf16[352,128]{1,0:T(8,128)(2,1)S(1)} collective-permute-done((bf16[352,128]{1,0:T(8,128)(2,1)S(1)}, bf16[352,128]{1,0:T(8,128)(2,1)S(1)}, u32[]{:S(2)}, u32[]{:S(2)}) %collective-permute-start.18) | collective-permute-done | bytes 90144 | tf_op jit(solution)/shard_map/ppermute | solution.py:55
  71.3 0.4 collective-permute-start.21
  71.7 1.7 %collective-permute-start.20 = (bf16[3,352,128]{2,1,0:T(8,128)(2,1)S(1)}, bf16[3,352,128]{2,1,0:T(8,128)(2,1)S(1)}, u32[]{:S(2)}, u32[]{:S(2)}) collective-permute-start(bf16[3,352,128]{2,1,0:T(8,128)(2,1)S(1)} %pad_maximum_fusion.1), channel_id=1, source_target_pairs={{0,2},{1,3},{2,0},{3,1},{4,6},{5,7},{6,4},{7,5},{8,10},{9,11},{10,... | collective-permute-start | bytes 811016 | tf_op jit(solution)/shard_map/ppermute | solution.py:55
  73.4 0.6 collective-permute-start.16
  74.0 1.1 %fusion.3 = bf16[2,16,16,256]{3,2,1,0:T(8,128)(2,1)} fusion(f32[2,16,16,256]{3,2,1,0:T(8,128)S(1)} %convolution_add_fusion.9, bf16[2,16,16,512]{3,2,1,0:T(8,128)(2,1)S(1)} %copy-done.5, bf16[2,16,16,256]{3,2,1,0:T(8,128)(2,1)S(1)} %bitcast.118, bf16[2,16,16,256]{3,2,1,0:T(8,128)(2,1)S(1)} %copy-done.8, bf16[3,3,256,512]{3,2,1,0:T(8,128)(2,1)S(1)} %copy-done.7), kind=kOutput, calls=%fused_computation.28 | convolution fusion | flops 135135232 | bytes 2097152 | tf_op jit(solution)/shard_map/nhwo,co->nhwc/dot_general | solution.py:552
  75.1 5.5 %collective-permute-done.16 = bf16[352,128]{1,0:T(8,128)(2,1)S(1)} collective-permute-done((bf16[352,128]{1,0:T(8,128)(2,1)S(1)}, bf16[352,128]{1,0:T(8,128)(2,1)S(1)}, u32[]{:S(2)}, u32[]{:S(2)}) %collective-permute-start.16) | collective-permute-done | bytes 90144 | tf_op jit(solution)/shard_map/ppermute | solution.py:55
  80.8 1.1 %collective-permute-start.22 = (bf16[2,352,128]{2,1,0:T(8,128)(2,1)S(1)}, bf16[2,352,128]{2,1,0:T(8,128)(2,1)S(1)}, u32[]{:S(2)}, u32[]{:S(2)}) collective-permute-start(bf16[2,352,128]{2,1,0:T(8,128)(2,1)S(1)} %slice.121), channel_id=1, source_target_pairs={{0,2},{1,3},{2,0},{3,1},{4,6},{5,7},{6,4},{7,5},{8,10},{9,11},{10,... | collective-permute-start | bytes 540680 | tf_op jit(solution)/shard_map/ppermute | solution.py:55
  81.9 0.9 collective-permute-start.23
  82.8 5.0 %collective-permute-done.22 = bf16[2,352,128]{2,1,0:T(8,128)(2,1)S(1)} collective-permute-done((bf16[2,352,128]{2,1,0:T(8,128)(2,1)S(1)}, bf16[2,352,128]{2,1,0:T(8,128)(2,1)S(1)}, u32[]{:S(2)}, u32[]{:S(2)}) %collective-permute-start.22) | collective-permute-done | bytes 180256 | tf_op jit(solution)/shard_map/ppermute | solution.py:55
  88.0 1.5 %collective-permute-done.26.refs_5_ = bf16[3,352,128]{2,1,0:T(8,128)(2,1)S(1)} collective-permute-done((bf16[3,352,128]{2,1,0:T(8,128)(2,1)S(1)}, bf16[3,352,128]{2,1,0:T(8,128)(2,1)S(1)}, u32[]{:S(2)}, u32[]{:S(2)}) %collective-permute-start.26) | collective-permute-done | bytes 270368 | tf_op jit(solution)/shard_map/ppermute | solution.py:55
  89.5 3.7 %shard_map.135 = (f32[9,256,512]{2,1,0:T(8,128)}, f32[768,256]{1,0:T(8,128)}, f32[1,512]{1,0:T(1,128)}) custom-call(s32[2]{0:T(128)S(1)} %copy-done.2, bf16[4,352,128]{2,1,0:T(8,128)(2,1)S(1)} %pad_maximum_fusion.refs_0_, bf16[9,352,128]{2,1,0:T(8,128)(2,1)S(1)} %constant_dynamic-update-slice_fusion.refs_1_, ...), custom_call_target="tpu_custom_call" | custom-call | tf_op jit(solution)/shard_map/pallas_call | solution.py:474
  (54 shorter events, 0.6 us)
Async XLA Ops:
  0.6 15.3 %copy-start = (bf16[768,256]{1,0:T(8,128)(2,1)S(1)}, bf16[768,256]{1,0:T(8,128)(2,1)}, u32[]{:S(2)}) copy-start(bf16[768,256]{1,0:T(8,128)(2,1)} %param.10) | copy-start | bytes 1179652
  4.4 26.7 %copy-start.1 = (bf16[784,768]{1,0:T(8,128)(2,1)S(1)}, bf16[784,768]{1,0:T(8,128)(2,1)}, u32[]{:S(2)}) copy-start(bf16[784,768]{1,0:T(8,128)(2,1)} %book_ref.1) | copy-start | bytes 3612676
  4.4 26.7 %copy-start.2 = (s32[2]{0:T(128)S(1)}, s32[2]{0:T(128)}, u32[]{:S(2)}) copy-start(s32[2]{0:T(128)} %pad_add_fusion.place_ref) | copy-start | bytes 28
  4.4 20.5 %all-to-all-start = ((f32[32,8,384]{2,1,0:T(8,128)}), f32[32,8,384]{2,1,0:T(8,128)S(1)}, u32[]{:S(2)}, u32[]{:S(2)}) async-start(f32[32,8,384]{2,1,0:T(8,128)} %get-tuple-element.39), calls=%async_computation | async-start | bytes 786432 | tf_op jit(solution)/shard_map/all_to_all | solution.py:85
  11.7 19.0 %collective-permute-start.2 = (bf16[528,256]{1,0:T(8,128)(2,1)}, bf16[528,256]{1,0:T(8,128)(2,1)}, u32[]{:S(2)}, u32[]{:S(2)}) collective-permute-start(bf16[528,256]{1,0:T(8,128)(2,1)} %get-tuple-element.41), channel_id=1, source_target_pairs={{0,6},{1,7},{2,4},{3,5},{4,2},{5,3},{6,0},{7,1},{8,14},{9,15},{10,... | collective-permute-start | bytes 811016 | tf_op jit(solution)/shard_map/ppermute | solution.py:55
  14.4 16.7 %collective-permute-start.1 = (bf16[528,256]{1,0:T(8,128)(2,1)}, bf16[528,256]{1,0:T(8,128)(2,1)}, u32[]{:S(2)}, u32[]{:S(2)}) collective-permute-start(bf16[528,256]{1,0:T(8,128)(2,1)} %get-tuple-element.41), channel_id=1, source_target_pairs={{0,4},{1,5},{2,6},{3,7},{4,0},{5,1},{6,2},{7,3},{8,12},{9,13},{10,... | collective-permute-start | bytes 811016 | tf_op jit(solution)/shard_map/ppermute | solution.py:55
  15.0 15.7 %collective-permute-start = (bf16[528,256]{1,0:T(8,128)(2,1)}, bf16[528,256]{1,0:T(8,128)(2,1)}, u32[]{:S(2)}, u32[]{:S(2)}) collective-permute-start(bf16[528,256]{1,0:T(8,128)(2,1)} %get-tuple-element.42.refs_0_), channel_id=1, source_target_pairs={{0,2},{1,3},{2,0},{3,1},{4,6},{5,7},{6,4},{7,5},{8,10},{9,11},{10,... | collective-permute-start | bytes 811016 | tf_op jit(solution)/shard_map/ppermute | solution.py:55
  17.7 15.2 %copy-start.3 = (bf16[528,256]{1,0:T(8,128)(2,1)S(1)}, bf16[528,256]{1,0:T(8,128)(2,1)}, u32[]{:S(2)}) copy-start(bf16[528,256]{1,0:T(8,128)(2,1)} %get-tuple-element.42.refs_0_) | copy-start | bytes 811012
  26.1 15.8 %all-to-all-start.1 = ((bf16[32,16,384]{2,1,0:T(8,128)(2,1)}), bf16[32,16,384]{2,1,0:T(8,128)(2,1)S(1)}, u32[]{:S(2)}, u32[]{:S(2)}) async-start(bf16[32,16,384]{2,1,0:T(8,128)(2,1)} %shard_map.129), calls=%async_computation.1 | async-start | bytes 786432 | tf_op jit(solution)/shard_map/all_to_all | solution.py:85
  28.7 6.8 %copy-start.4 = (bf16[2,16,16,512]{3,2,1,0:T(8,128)(2,1)S(1)}, bf16[2,16,16,512]{3,2,1,0:T(8,128)(2,1)}, u32[]{:S(2)}) copy-start(bf16[2,16,16,512]{3,2,1,0:T(8,128)(2,1)} %param.17) | copy-start | bytes 1572868
  28.7 6.8 %copy-start.6 = (bf16[3,3,256,512]{3,2,1,0:T(8,128)(2,1)S(1)}, bf16[3,3,256,512]{3,2,1,0:T(8,128)(2,1)}, u32[]{:S(2)}) copy-start(bf16[3,3,256,512]{3,2,1,0:T(8,128)(2,1)} %param.15) | copy-start | bytes 7077892
  32.9 9.0 %collective-permute-start.3 = (bf16[528,256]{1,0:T(8,128)(2,1)S(1)}, bf16[528,256]{1,0:T(8,128)(2,1)S(1)}, u32[]{:S(2)}, u32[]{:S(2)}) collective-permute-start(bf16[528,256]{1,0:T(8,128)(2,1)S(1)} %copy-done.3), channel_id=1, source_target_pairs={{0,1},{1,0},{2,3},{3,2},{4,5},{5,4},{6,7},{7,6},{8,9},{9,8},{10,11... | collective-permute-start | bytes 811016 | tf_op jit(solution)/shard_map/ppermute | solution.py:55
  33.0 10.0 %collective-permute-start.4 = (bf16[528,256]{1,0:T(8,128)(2,1)}, bf16[528,256]{1,0:T(8,128)(2,1)S(1)}, u32[]{:S(2)}, u32[]{:S(2)}) collective-permute-start(bf16[528,256]{1,0:T(8,128)(2,1)} %collective-permute-done.refs_1_), channel_id=1, source_target_pairs={{0,1},{1,0},{2,3},{3,2},{4,5},{5,4},{6,7},{7,6},{8,9},{9,8},{10,11... | collective-permute-start | bytes 811016 | tf_op jit(solution)/shard_map/ppermute | solution.py:55
  33.5 10.5 %collective-permute-start.5 = (bf16[528,256]{1,0:T(8,128)(2,1)}, bf16[528,256]{1,0:T(8,128)(2,1)S(1)}, u32[]{:S(2)}, u32[]{:S(2)}) collective-permute-start(bf16[528,256]{1,0:T(8,128)(2,1)} %collective-permute-done.1.refs_2_), channel_id=1, source_target_pairs={{0,1},{1,0},{2,3},{3,2},{4,5},{5,4},{6,7},{7,6},{8,9},{9,8},{10,11... | collective-permute-start | bytes 811016 | tf_op jit(solution)/shard_map/ppermute | solution.py:55
  33.5 10.4 %collective-permute-start.6 = (bf16[528,256]{1,0:T(8,128)(2,1)}, bf16[528,256]{1,0:T(8,128)(2,1)S(1)}, u32[]{:S(2)}, u32[]{:S(2)}) collective-permute-start(bf16[528,256]{1,0:T(8,128)(2,1)} %collective-permute-done.2.refs_3_), channel_id=1, source_target_pairs={{0,1},{1,0},{2,3},{3,2},{4,5},{5,4},{6,7},{7,6},{8,9},{9,8},{10,11... | collective-permute-start | bytes 811016 | tf_op jit(solution)/shard_map/ppermute | solution.py:55
  34.0 4.0 %collective-permute-start.7 = (f32[768,128]{1,0:T(8,128)S(1)}, f32[768,128]{1,0:T(8,128)S(1)}, u32[]{:S(2)}, u32[]{:S(2)}) collective-permute-start(f32[768,128]{1,0:T(8,128)S(1)} %get-tuple-element.48), channel_id=1, source_target_pairs={{0,1},{1,0},{2,3},{3,2},{4,5},{5,4},{6,7},{7,6},{8,9},{9,8},{10,11... | collective-permute-start | bytes 1179656 | tf_op jit(solution)/shard_map/ppermute | solution.py:55
  38.6 10.3 %collective-permute-start.8 = (bf16[4,48,128]{2,1,0:T(8,128)(2,1)S(1)}, bf16[4,48,128]{2,1,0:T(8,128)(2,1)S(1)}, u32[]{:S(2)}, u32[]{:S(2)}) collective-permute-start(bf16[4,48,128]{2,1,0:T(8,128)(2,1)S(1)} %get-tuple-element.50), channel_id=1, source_target_pairs={{0,2},{1,3},{2,0},{3,1},{4,6},{5,7},{6,4},{7,5},{8,10},{9,11},{10,... | collective-permute-start | bytes 147464 | tf_op jit(solution)/shard_map/ppermute | solution.py:55
  41.9 7.0 %collective-permute-start.9 = (bf16[4,48,128]{2,1,0:T(8,128)(2,1)S(1)}, bf16[4,48,128]{2,1,0:T(8,128)(2,1)S(1)}, u32[]{:S(2)}, u32[]{:S(2)}) collective-permute-start(bf16[4,48,128]{2,1,0:T(8,128)(2,1)S(1)} %get-tuple-element.51), channel_id=1, source_target_pairs={{0,4},{1,5},{2,6},{3,7},{4,0},{5,1},{6,2},{7,3},{8,12},{9,13},{10,... | collective-permute-start | bytes 147464 | tf_op jit(solution)/shard_map/ppermute | solution.py:55
  43.0 10.6 %copy-start.9 = (s32[1,512]{1,0:T(1,128)S(1)}, s32[1,512]{1,0:T(1,128)}, u32[]{:S(2)}) copy-start(s32[1,512]{1,0:T(1,128)} %get-tuple-element.61) | copy-start | bytes 6148
  43.0 10.9 %copy-start.7 = (bf16[3,3,256,512]{3,2,1,0:T(8,128)(2,1)S(1)}, bf16[3,3,256,512]{3,2,1,0:T(8,128)(2,1)}, u32[]{:S(2)}) copy-start(bf16[3,3,256,512]{3,2,1,0:T(8,128)(2,1)} %param.15) | copy-start | bytes 7077892
  43.0 6.0 %collective-permute-start.10 = (bf16[4,48,128]{2,1,0:T(8,128)(2,1)S(1)}, bf16[4,48,128]{2,1,0:T(8,128)(2,1)S(1)}, u32[]{:S(2)}, u32[]{:S(2)}) collective-permute-start(bf16[4,48,128]{2,1,0:T(8,128)(2,1)S(1)} %get-tuple-element.52), channel_id=1, source_target_pairs={{0,6},{1,7},{2,4},{3,5},{4,2},{5,3},{6,0},{7,1},{8,14},{9,15},{10,... | collective-permute-start | bytes 147464 | tf_op jit(solution)/shard_map/ppermute | solution.py:55
  49.6 7.4 %collective-permute-start.11 = (bf16[352,128]{1,0:T(8,128)(2,1)S(1)}, bf16[352,128]{1,0:T(8,128)(2,1)S(1)}, u32[]{:S(2)}, u32[]{:S(2)}) collective-permute-start(bf16[352,128]{1,0:T(8,128)(2,1)S(1)} %get-tuple-element.58), channel_id=1, source_target_pairs={{0,8},{1,9},{2,10},{3,11},{4,12},{5,13},{6,14},{7,15},{8,16},{9,17... | collective-permute-start | bytes 270344 | tf_op jit(solution)/shard_map/ppermute | solution.py:55
  50.4 9.5 %collective-permute-start.12 = (bf16[352,128]{1,0:T(8,128)(2,1)S(1)}, bf16[352,128]{1,0:T(8,128)(2,1)S(1)}, u32[]{:S(2)}, u32[]{:S(2)}) collective-permute-start(bf16[352,128]{1,0:T(8,128)(2,1)S(1)} %get-tuple-element.59), channel_id=1, source_target_pairs={{0,16},{1,17},{2,18},{3,19},{4,20},{5,21},{6,22},{7,23},{8,24},{9,... | collective-permute-start | bytes 270344 | tf_op jit(solution)/shard_map/ppermute | solution.py:55
  51.8 8.1 %collective-permute-start.13 = (bf16[352,128]{1,0:T(8,128)(2,1)S(1)}, bf16[352,128]{1,0:T(8,128)(2,1)S(1)}, u32[]{:S(2)}, u32[]{:S(2)}) collective-permute-start(bf16[352,128]{1,0:T(8,128)(2,1)S(1)} %get-tuple-element.60), channel_id=1, source_target_pairs={{0,24},{1,25},{2,26},{3,27},{4,28},{5,29},{6,30},{7,31},{8,0},{9,1... | collective-permute-start | bytes 270344 | tf_op jit(solution)/shard_map/ppermute | solution.py:55
  56.0 18.0 %copy-start.5 = (bf16[2,16,16,512]{3,2,1,0:T(8,128)(2,1)S(1)}, bf16[2,16,16,512]{3,2,1,0:T(8,128)(2,1)}, u32[]{:S(2)}) copy-start(bf16[2,16,16,512]{3,2,1,0:T(8,128)(2,1)} %param.17) | copy-start | bytes 1572868
  56.0 18.0 %copy-start.8 = (bf16[2,16,16,256]{3,2,1,0:T(8,128)(2,1)S(1)}, bf16[2,16,16,256]{3,2,1,0:T(8,128)(2,1)}, u32[]{:S(2)}) copy-start(bf16[2,16,16,256]{3,2,1,0:T(8,128)(2,1)} %param.11) | copy-start | bytes 786436
  59.9 6.4 %collective-permute-start.19 = (bf16[352,128]{1,0:T(8,128)(2,1)S(1)}, bf16[352,128]{1,0:T(8,128)(2,1)S(1)}, u32[]{:S(2)}, u32[]{:S(2)}) collective-permute-start(bf16[352,128]{1,0:T(8,128)(2,1)S(1)} %shard_map.134), channel_id=1, source_target_pairs={{0,24},{1,25},{2,26},{3,27},{4,28},{5,29},{6,30},{7,31},{8,0},{9,1... | collective-permute-start | bytes 270344 | tf_op jit(solution)/shard_map/ppermute | solution.py:55
  62.0 9.3 %collective-permute-start.18 = (bf16[352,128]{1,0:T(8,128)(2,1)S(1)}, bf16[352,128]{1,0:T(8,128)(2,1)S(1)}, u32[]{:S(2)}, u32[]{:S(2)}) collective-permute-start(bf16[352,128]{1,0:T(8,128)(2,1)S(1)} %shard_map.134), channel_id=1, source_target_pairs={{0,16},{1,17},{2,18},{3,19},{4,20},{5,21},{6,22},{7,23},{8,24},{9,... | collective-permute-start | bytes 270344 | tf_op jit(solution)/shard_map/ppermute | solution.py:55
  63.3 8.0 %collective-permute-start.17 = (bf16[352,128]{1,0:T(8,128)(2,1)S(1)}, bf16[352,128]{1,0:T(8,128)(2,1)S(1)}, u32[]{:S(2)}, u32[]{:S(2)}) collective-permute-start(bf16[352,128]{1,0:T(8,128)(2,1)S(1)} %shard_map.134), channel_id=1, source_target_pairs={{0,8},{1,9},{2,10},{3,11},{4,12},{5,13},{6,14},{7,15},{8,16},{9,17... | collective-permute-start | bytes 270344 | tf_op jit(solution)/shard_map/ppermute | solution.py:55
  64.4 10.7 %collective-permute-start.15 = (bf16[352,128]{1,0:T(8,128)(2,1)S(1)}, bf16[352,128]{1,0:T(8,128)(2,1)S(1)}, u32[]{:S(2)}, u32[]{:S(2)}) collective-permute-start(bf16[352,128]{1,0:T(8,128)(2,1)S(1)} %shard_map.134), channel_id=1, source_target_pairs={{0,4},{1,5},{2,6},{3,7},{4,0},{5,1},{6,2},{7,3},{8,12},{9,13},{10,... | collective-permute-start | bytes 270344 | tf_op jit(solution)/shard_map/ppermute | solution.py:55
  64.8 8.6 %collective-permute-start.14 = (bf16[352,128]{1,0:T(8,128)(2,1)S(1)}, bf16[352,128]{1,0:T(8,128)(2,1)S(1)}, u32[]{:S(2)}, u32[]{:S(2)}) collective-permute-start(bf16[352,128]{1,0:T(8,128)(2,1)S(1)} %shard_map.134), channel_id=1, source_target_pairs={{0,2},{1,3},{2,0},{3,1},{4,6},{5,7},{6,4},{7,5},{8,10},{9,11},{10,... | collective-permute-start | bytes 270344 | tf_op jit(solution)/shard_map/ppermute | solution.py:55
  71.3 9.3 %collective-permute-start.21 = (bf16[3,352,128]{2,1,0:T(8,128)(2,1)S(1)}, bf16[3,352,128]{2,1,0:T(8,128)(2,1)S(1)}, u32[]{:S(2)}, u32[]{:S(2)}) collective-permute-start(bf16[3,352,128]{2,1,0:T(8,128)(2,1)S(1)} %pad_maximum_fusion.1), channel_id=1, source_target_pairs={{0,4},{1,5},{2,6},{3,7},{4,0},{5,1},{6,2},{7,3},{8,12},{9,13},{10,... | collective-permute-start | bytes 811016 | tf_op jit(solution)/shard_map/ppermute | solution.py:55
  71.7 8.9 %collective-permute-start.20 = (bf16[3,352,128]{2,1,0:T(8,128)(2,1)S(1)}, bf16[3,352,128]{2,1,0:T(8,128)(2,1)S(1)}, u32[]{:S(2)}, u32[]{:S(2)}) collective-permute-start(bf16[3,352,128]{2,1,0:T(8,128)(2,1)S(1)} %pad_maximum_fusion.1), channel_id=1, source_target_pairs={{0,2},{1,3},{2,0},{3,1},{4,6},{5,7},{6,4},{7,5},{8,10},{9,11},{10,... | collective-permute-start | bytes 811016 | tf_op jit(solution)/shard_map/ppermute | solution.py:55
  73.4 7.1 %collective-permute-start.16 = (bf16[352,128]{1,0:T(8,128)(2,1)S(1)}, bf16[352,128]{1,0:T(8,128)(2,1)S(1)}, u32[]{:S(2)}, u32[]{:S(2)}) collective-permute-start(bf16[352,128]{1,0:T(8,128)(2,1)S(1)} %collective-permute-done.14), channel_id=1, source_target_pairs={{0,4},{1,5},{2,6},{3,7},{4,0},{5,1},{6,2},{7,3},{8,12},{9,13},{10,... | collective-permute-start | bytes 270344 | tf_op jit(solution)/shard_map/ppermute | solution.py:55
  80.7 8.8 %collective-permute-start.25 = (bf16[9,352,128]{2,1,0:T(8,128)(2,1)S(1)}, bf16[9,352,128]{2,1,0:T(8,128)(2,1)S(1)}, u32[]{:S(2)}, u32[]{:S(2)}) collective-permute-start(bf16[9,352,128]{2,1,0:T(8,128)(2,1)S(1)} %constant_dynamic-update-slice_fusion.refs_1_), channel_id=1, source_target_pairs={{0,1},{1,0},{2,3},{3,2},{4,5},{5,4},{6,7},{7,6},{8,9},{9,8},{10,11... | collective-permute-start | bytes 2433032 | tf_op jit(solution)/shard_map/ppermute | solution.py:55
  80.8 7.0 %collective-permute-start.22 = (bf16[2,352,128]{2,1,0:T(8,128)(2,1)S(1)}, bf16[2,352,128]{2,1,0:T(8,128)(2,1)S(1)}, u32[]{:S(2)}, u32[]{:S(2)}) collective-permute-start(bf16[2,352,128]{2,1,0:T(8,128)(2,1)S(1)} %slice.121), channel_id=1, source_target_pairs={{0,2},{1,3},{2,0},{3,1},{4,6},{5,7},{6,4},{7,5},{8,10},{9,11},{10,... | collective-permute-start | bytes 540680 | tf_op jit(solution)/shard_map/ppermute | solution.py:55
  81.9 5.9 %collective-permute-start.23 = (bf16[1,352,128]{2,1,0:T(8,128)(2,1)S(1)}, bf16[1,352,128]{2,1,0:T(8,128)(2,1)S(1)}, u32[]{:S(2)}, u32[]{:S(2)}) collective-permute-start(bf16[1,352,128]{2,1,0:T(8,128)(2,1)S(1)} %slice.122), channel_id=1, source_target_pairs={{0,4},{1,5},{2,6},{3,7},{4,0},{5,1},{6,2},{7,3},{8,12},{9,13},{10,... | collective-permute-start | bytes 270344 | tf_op jit(solution)/shard_map/ppermute | solution.py:55
  82.8 5.1 %collective-permute-start.24 = (bf16[4,352,128]{2,1,0:T(8,128)(2,1)S(1)}, bf16[4,352,128]{2,1,0:T(8,128)(2,1)S(1)}, u32[]{:S(2)}, u32[]{:S(2)}) collective-permute-start(bf16[4,352,128]{2,1,0:T(8,128)(2,1)S(1)} %pad_maximum_fusion.refs_0_), channel_id=1, source_target_pairs={{0,1},{1,0},{2,3},{3,2},{4,5},{5,4},{6,7},{7,6},{8,9},{9,8},{10,11... | collective-permute-start | bytes 1081352 | tf_op jit(solution)/shard_map/ppermute | solution.py:55
  87.9 1.6 %collective-permute-start.26 = (bf16[3,352,128]{2,1,0:T(8,128)(2,1)S(1)}, bf16[3,352,128]{2,1,0:T(8,128)(2,1)S(1)}, u32[]{:S(2)}, u32[]{:S(2)}) collective-permute-start(bf16[3,352,128]{2,1,0:T(8,128)(2,1)S(1)} %constant_dynamic-update-slice_fusion.3.refs_2_), channel_id=1, source_target_pairs={{0,1},{1,0},{2,3},{3,2},{4,5},{5,4},{6,7},{7,6},{8,9},{9,8},{10,11... | collective-permute-start | bytes 811016 | tf_op jit(solution)/shard_map/ppermute | solution.py:55

commit v6 on v5

--- a/solution.py
+++ b/solution.py
@@ -85,23 +85,10 @@
     return lax.all_to_all(x, AXES, split_axis=0, concat_axis=0, tiled=True)
 
 
-def token_kernel(
-    cap, place_ref, pick_hbm, counts_hbm, wanted_hbm, latents_hbm, cot_hbm, near_ref, far_ref, slot_ref, ask_ref, *rest
-):
-    pick_ref, counts_ref, wanted_ref, latents_ref, cot_ref, sems = rest
-    sources = (pick_hbm, counts_hbm, wanted_hbm, latents_hbm, cot_hbm)
-    copies = [
-        pltpu.make_async_copy(source, target, sems.at[n])
-        for n, (source, target) in enumerate(zip(sources, rest[:-1]))
-    ]
-    for copy in copies:
-        copy.start()
-    for copy in copies[:4]:
-        copy.wait()
-    lines, width = pick_ref.shape
-    devices = counts_ref.shape[1]
+def token_slots(cap, pick, counts):
+    lines, width = pick.shape
+    devices = counts.shape[1]
     tokens = lines * width
-    pick = pick_ref[...]
     owner = pick // cap
     first = pick - owner * cap
     token = lax.broadcasted_iota(jnp.int32, (width, tokens), 1)
@@ -118,7 +105,7 @@
     owner, entry = flat(owner), flat(first)
     row = lax.broadcasted_iota(jnp.int32, (devices, devices), 0)
     col = lax.broadcasted_iota(jnp.int32, (devices, devices), 1)
-    counts = jnp.where(row == col, counts_ref[...].astype(jnp.float32), 0.0)
+    counts = jnp.where(row == col, counts.astype(jnp.float32), 0.0)
     counts = jnp.sum(counts, axis=1, keepdims=True)
     owner_id = lax.broadcasted_iota(jnp.int32, (devices, tokens), 0)
     count = jnp.sum(
@@ -126,20 +113,31 @@
     )
     for _ in range(cap - 1):
         entry = jnp.where(entry >= count, entry - count, entry)
+    return owner, entry
+
+
+def fetch(sources, targets, sems):
+    copies = [
+        pltpu.make_async_copy(source, target, sems.at[n])
+        for n, (source, target) in enumerate(zip(sources, targets))
+    ]
+    for copy in copies:
+        copy.start()
+    for copy in copies:
+        copy.wait()
+
+
+def token_kernel(cap, pick_hbm, counts_hbm, wanted_hbm, latents_hbm, slot_ref, parts_ref, ask_ref, *rest):
+    pick_ref, counts_ref, wanted_ref, latents_ref, sems = rest
+    fetch((pick_hbm, counts_hbm, wanted_hbm, latents_hbm), rest[:-1], sems)
+    owner, entry = token_slots(cap, pick_ref[...], counts_ref[...])
+    tokens, devices = owner.shape[1], counts_ref.shape[1]
+    slots = devices * cap
     slot = (owner * cap + entry).astype(jnp.int32)
     slot_ref[...] = slot
-    place = lax.broadcasted_iota(jnp.int32, (16, tokens), 0)
-    wide = cot_ref.shape[1] // 2
-    place = place[:, :wide]
-    extra = jnp.zeros((16, wide), jnp.float32)
-    for n, row in enumerate((owner[:, :wide], owner[:, wide:], entry[:, :wide], entry[:, wide:])):
-        extra = jnp.where(place == n, row, extra)
-    copies[4].wait()
-    for ref, side in ((near_ref, place_ref[0] // 4), (far_ref, 1 - place_ref[0] // 4)):
-        ref[:tokens] = cot_ref[:, pl.ds(pl.multiple_of(side * wide, wide), wide)]
-        ref[tokens:] = extra.astype(jnp.bfloat16)
-    hit = (lax.broadcasted_iota(jnp.int32, (devices * cap, tokens), 0) == slot).astype(jnp.float32)
-    slots = devices * cap
+    row = lax.broadcasted_iota(jnp.int32, (8, tokens), 0)
+    parts_ref[...] = jnp.where(row == 0, owner, jnp.where(row == 1, entry, 0.0))
+    hit = (lax.broadcasted_iota(jnp.int32, (slots, tokens), 0) == slot).astype(jnp.float32)
     uses = jnp.sum(hit, axis=1, keepdims=True)
     sums = jnp.dot(hit.astype(jnp.bfloat16), latents_ref[...], preferred_element_type=jnp.float32)
     zch = sums.shape[1]
@@ -154,27 +152,50 @@
     ask_ref[:, :, zch:] = last.reshape(devices, cap, 128)
 
 
-def token_part(place, pick, counts, wanted, latents, cots):
-    tokens, channels = cots.shape
+def token_part(pick, counts, wanted, latents):
     cap, devices = wanted.shape
+    tokens = pick.shape[0] * pick.shape[1]
     slots = devices * cap
     return pl.pallas_call(
         functools.partial(token_kernel, cap),
         out_shape=(
-            jax.ShapeDtypeStruct((tokens + 16, channels // 2), jnp.bfloat16),
-            jax.ShapeDtypeStruct((tokens + 16, channels // 2), jnp.bfloat16),
             jax.ShapeDtypeStruct((1, tokens), jnp.int32),
+            jax.ShapeDtypeStruct((8, tokens), jnp.float32),
             jax.ShapeDtypeStruct((devices, cap, latents.shape[1] + 128), jnp.float32),
         ),
-        in_specs=[SMEM_SPEC] + [pl.BlockSpec(memory_space=pltpu.HBM)] * 5,
-        out_specs=tuple(vmem(4)),
-        scratch_shapes=[
-            pltpu.VMEM(x.shape, x.dtype) for x in (pick, counts, wanted, latents, cots)
-        ]
-        + [pltpu.SemaphoreType.DMA((5,))],
+        in_specs=[pl.BlockSpec(memory_space=pltpu.HBM)] * 4,
+        out_specs=tuple(vmem(3)),
+        scratch_shapes=[pltpu.VMEM(x.shape, x.dtype) for x in (pick, counts, wanted, latents)]
+        + [pltpu.SemaphoreType.DMA((4,))],
         compiler_params=pltpu.CompilerParams(vmem_limit_bytes=62 << 20),
         cost_estimate=cost(2 * slots * tokens * latents.shape[1], 2 << 20),
-    )(place, pick, counts, wanted, latents, cots)
+    )(pick, counts, wanted, latents)
+
+
+def block_kernel(parts_ref, cot_ref, near_ref, far_ref):
+    tokens, channels = cot_ref.shape
+    wide = channels // 2
+    place = lax.broadcasted_iota(jnp.int32, (16, wide), 0)
+    extra = jnp.zeros((16, wide), jnp.float32)
+    rows = [parts_ref[n : n + 1, m * wide : (m + 1) * wide] for n in range(2) for m in range(2)]
+    for n, row in enumerate(rows):
+        extra = jnp.where(place == n, row, extra)
+    side = lax.axis_index("dp") % 2
+    for ref, side in ((near_ref, side), (far_ref, 1 - side)):
+        ref[:tokens] = cot_ref[:, pl.ds(pl.multiple_of(side * wide, wide), wide)]
+        ref[tokens:] = extra.astype(jnp.bfloat16)
+
+
+def block_part(parts, cots):
+    tokens, channels = cots.shape
+    return pl.pallas_call(
+        block_kernel,
+        out_shape=(jax.ShapeDtypeStruct((tokens + 16, channels // 2), jnp.bfloat16),) * 2,
+        in_specs=vmem(2),
+        out_specs=tuple(vmem(2)),
+        compiler_params=LIMIT,
+        cost_estimate=cost(0, 1 << 20),
+    )(parts, cots)
 
 
 def select_rows(asked, zch, entries):
@@ -501,14 +522,13 @@
     tokens = images * rows * width
     r, i = grid.place()
     place = jnp.stack([i, r % PARTS]).astype(jnp.int32)
-    near, far, slot, ask = token_part(
-        place,
+    slot, parts, ask = token_part(
         token_pick.reshape(images * rows, width),
         wanted_count,
         jnp.swapaxes(wanted.reshape(devices, cap), 0, 1),
         latents.reshape(tokens, zch),
-        cotangent.reshape(tokens, channels),
     )
+    near, far = block_part(parts, cotangent.reshape(tokens, channels))
     asked = spread(ask, grid)
     cots = gather_near(grid, near, far)
     local_codes = jnp.dot(codebook, projector, preferred_element_type=jnp.float32).astype(

time: 93.7 us -> 92.3 us (0.985)
  waiting for transfers between devices: 32.5 us -> 27.4 us
  local copies, waits for them, and re-layouts: 0.21 us -> 1.95 us
  starting transfers between devices: 31.7 us -> 33.3 us
    all_to_all x2, waiting for transfers between devices: 9.51 us -> 6.93 us  [spread(): return lax.all_to_all(x, AXES, split_axis=0, concat_axis=0, tiled=True)]
    ppermute x27, waiting for transfers between devices: 23 us -> 20.4 us  [send(): return lax.ppermute(x, AXES, perm)]
    unnamed x23 -> x21, local copies, waits for them, and re-layouts: 0.13 us -> 1.86 us
    ppermute x27, starting transfers between devices: 21.8 us -> 23.4 us  [send(): return lax.ppermute(x, AXES, perm)]
    dot_general x9, matrix products: 4.88 us -> 5.83 us  [on_device(): jnp.einsum('nhwo,co->nhwc', grad_window, kernel[row_off, col_off], prefer...]
  transfers between devices with their start and end apart: 29 -> 29, of which waited for: 10 -> 9; matrix products, arithmetic and copies ran while one was open for 12% -> 13% of each run, Pallas kernels for 9% -> 10%
where the time goes in v6:
time: 92.3 us; the launch traced here: 91.8 us
  starting transfers between devices  33.3 us (36%)
  waiting for transfers between devices  27.4 us (30%)
  Pallas kernels  16 us (17%)
  matrix products  11.3 us (12%)
  local copies, waits for them, and re-layouts  1.95 us (2%)
  between operations  1.05 us (1%)
    ppermute x27, starting transfers between devices, send(): return lax.ppermute(x, AXES, perm)  23.4 us
    ppermute x27, waiting for transfers between devices, send(): return lax.ppermute(x, AXES, perm)  20.4 us
    all_to_all x2, starting transfers between devices, spread(): return lax.all_to_all(x, AXES, split_axis=0, concat_axis=0, tiled=True)  9.92 us
    all_to_all x2, waiting for transfers between devices, spread(): return lax.all_to_all(x, AXES, split_axis=0, concat_axis=0, tiled=True)  6.93 us
    dot_general x9, matrix products, on_device(): jnp.einsum('nhwo,co->nhwc', grad_window, kernel[row_off, col_off], prefer...  5.83 us
    pallas_call x1, Pallas kernels, group_weights(): pl.pallas_call(functools.partial(weights_kernel, grid, cap), out_shape=ja...  5.03 us
    pallas_call x1, Pallas kernels, finish(): pl.pallas_call(functools.partial(finish_kernel, krows, counts), out_shape...  3.71 us
    dot_general x9, matrix products, on_device(): jnp.einsum('nhwc,co->nhwo', window, kernel[row_off, col_off], preferred_e...  3.46 us
  transfers between devices with their start and end apart: 29, of which 9 were waited for; matrix products, arithmetic and copies ran while one was open for 13% of the time, Pallas kernels for 10%

profile of v6, /device:TPU:0, one launch (start us, length us, event | category | flops | bytes accessed | tf_op | source)
XLA Modules:
  0.0 91.8 jit_solution(5234387643116709800)
XLA Ops:
  0.6 2.2 %shard_map.128 = (s32[1,512]{1,0:T(1,128)}, f32[8,512]{1,0:T(8,128)}, f32[32,8,384]{2,1,0:T(8,128)}) custom-call(s32[32,16]{1,0:T(8,128)} %bitcast.126, s32[1,32]{1,0:T(1,128)} %counts_hbm.1, s32[8,32]{1,0:T(8,128)} %bitcast.127, bf16[512,256]{1,0:T(8,128)(2,1)} %bitcast.119), custom_call_target="tpu_custom_call" | custom-call | flops 67108864 | bytes 2097152 | tf_op jit(solution)/shard_map/pallas_call | solution.py:159
  2.9 7.3 %all-to-all-start = ((f32[32,8,384]{2,1,0:T(8,128)}), f32[32,8,384]{2,1,0:T(8,128)S(1)}, u32[]{:S(2)}, u32[]{:S(2)}) async-start(f32[32,8,384]{2,1,0:T(8,128)} %get-tuple-element.40), calls=%async_computation | async-start | bytes 786432 | tf_op jit(solution)/shard_map/all_to_all | solution.py:85
  10.2 1.0 %copy-done.1 = bf16[2,16,16,512]{3,2,1,0:T(8,128)(2,1)S(1)} copy-done((bf16[2,16,16,512]{3,2,1,0:T(8,128)(2,1)S(1)}, bf16[2,16,16,512]{3,2,1,0:T(8,128)(2,1)}, u32[]{:S(2)}) %copy-start.1) | copy-done | bytes 524312
  11.3 0.7 copy-done.4
  12.0 0.7 shard_map.130
  12.7 2.7 %collective-permute-start.2 = (bf16[528,256]{1,0:T(8,128)(2,1)}, bf16[528,256]{1,0:T(8,128)(2,1)S(1)}, u32[]{:S(2)}, u32[]{:S(2)}) collective-permute-start(bf16[528,256]{1,0:T(8,128)(2,1)} %get-tuple-element.43), channel_id=1, source_target_pairs={{0,6},{1,7},{2,4},{3,5},{4,2},{5,3},{6,0},{7,1},{8,14},{9,15},{10,... | collective-permute-start | bytes 811016 | tf_op jit(solution)/shard_map/ppermute | solution.py:55
  15.4 0.6 collective-permute-start.1
  16.0 0.3 collective-permute-start
  16.2 0.7 convert_element_type.28
  17.0 1.8 %convolution_convert_fusion.codes_ref = bf16[784,256]{1,0:T(8,128)(2,1)S(1)} fusion(bf16[784,768]{1,0:T(8,128)(2,1)} %book_ref.1, bf16[768,256]{1,0:T(8,128)(2,1)S(1)} %copy-done), kind=kOutput, calls=%fused_computation.18 | convolution fusion | flops 308482048 | bytes 1998848 | tf_op jit(solution)/shard_map/dot_general | solution.py:534
  18.7 4.7 %all-to-all-done.asked_ref = f32[32,8,384]{2,1,0:T(8,128)S(1)} async-done(((f32[32,8,384]{2,1,0:T(8,128)}), f32[32,8,384]{2,1,0:T(8,128)S(1)}, u32[]{:S(2)}, u32[]{:S(2)}) %all-to-all-start) | async-done | bytes 393248 | tf_op jit(solution)/shard_map/all_to_all | solution.py:85
  23.4 1.2 %shard_map.129 = bf16[32,16,384]{2,1,0:T(8,128)(2,1)} custom-call(f32[32,8,384]{2,1,0:T(8,128)S(1)} %all-to-all-done.asked_ref, bf16[784,256]{1,0:T(8,128)(2,1)S(1)} %convolution_convert_fusion.codes_ref), custom_call_target="tpu_custom_call" | custom-call | flops 102760448 | bytes 2097152 | tf_op jit(solution)/shard_map/pallas_call | solution.py:239
  24.6 2.6 %all-to-all-start.1 = ((bf16[32,16,384]{2,1,0:T(8,128)(2,1)}), bf16[32,16,384]{2,1,0:T(8,128)(2,1)S(1)}, u32[]{:S(2)}, u32[]{:S(2)}) async-start(bf16[32,16,384]{2,1,0:T(8,128)(2,1)} %shard_map.129), calls=%async_computation.1 | async-start | bytes 786432 | tf_op jit(solution)/shard_map/all_to_all | solution.py:85
  27.2 1.4 %fusion.4 = f32[2,16,16,256]{3,2,1,0:T(8,128)S(1)} fusion(bf16[2,16,16,512]{3,2,1,0:T(8,128)(2,1)S(1)} %copy-done.2, bf16[3,3,256,512]{3,2,1,0:T(8,128)(2,1)} %param.15), kind=kOutput, calls=%fused_computation.38 | convolution fusion | flops 134217728 | bytes 1310720 | tf_op jit(solution)/shard_map/nhwo,co->nhwc/dot_general | solution.py:572
  28.7 1.3 %convolution_add_fusion.15 = f32[2,16,16,256]{3,2,1,0:T(8,128)S(1)} fusion(f32[2,16,16,256]{3,2,1,0:T(8,128)S(1)} %fusion.4, bf16[2,16,16,512]{3,2,1,0:T(8,128)(2,1)S(1)} %copy-done.2, bf16[3,3,256,512]{3,2,1,0:T(8,128)(2,1)} %param.15), kind=kOutput, calls=%fused_computation.27 | convolution fusion | flops 134348800 | bytes 1835008 | tf_op jit(solution)/shard_map/nhwo,co->nhwc/dot_general | solution.py:572
  30.0 0.3 convolution_add_fusion.14
  30.4 0.3 convolution_add_fusion.13
  30.7 0.3 convolution_add_fusion.12
  31.1 0.3 collective-permute-start.3
  31.6 0.3 collective-permute-start.5
  31.9 0.2 collective-permute-start.6
  32.2 1.7 %shard_map.132 = (f32[768,128]{1,0:T(8,128)S(1)}, f32[768,128]{1,0:T(8,128)S(1)}) custom-call(s32[2]{0:T(128)S(1)} %pad_add_fusion.place_ref, f32[32,8,384]{2,1,0:T(8,128)S(1)} %all-to-all-done.asked_ref, bf16[784,768]{1,0:T(8,128)(2,1)S(1)} %copy-done.3, bf16[784,256]{1,0:T(8,128)(2,1)S(1)} %convolution_convert_fusion.codes_ref), custom_call_target="tpu_custom_call" | custom-call | flops 509607936 | bytes 4194304 | tf_op jit(solution)/shard_map/pallas_call | solution.py:271
  33.9 0.3 collective-permute-start.7
  34.2 0.4 convolution_add_fusion.11
  34.6 0.4 convolution_add_fusion.10
  34.9 0.3 convolution_add_fusion.9
  35.3 0.4 collective-permute-done.7.got_ref
  35.7 0.6 shard_map.133
  36.3 1.8 %collective-permute-start.8 = (bf16[4,48,128]{2,1,0:T(8,128)(2,1)S(1)}, bf16[4,48,128]{2,1,0:T(8,128)(2,1)S(1)}, u32[]{:S(2)}, u32[]{:S(2)}) collective-permute-start(bf16[4,48,128]{2,1,0:T(8,128)(2,1)S(1)} %get-tuple-element.52), channel_id=1, source_target_pairs={{0,2},{1,3},{2,0},{3,1},{4,6},{5,7},{6,4},{7,5},{8,10},{9,11},{10,... | collective-permute-start | bytes 147464 | tf_op jit(solution)/shard_map/ppermute | solution.py:55
  38.1 2.3 %all-to-all-done.1.got_ref = bf16[32,16,384]{2,1,0:T(8,128)(2,1)S(1)} async-done(((bf16[32,16,384]{2,1,0:T(8,128)(2,1)}), bf16[32,16,384]{2,1,0:T(8,128)(2,1)S(1)}, u32[]{:S(2)}, u32[]{:S(2)}) %all-to-all-start.1) | async-done | bytes 393248 | tf_op jit(solution)/shard_map/all_to_all | solution.py:85
  40.4 1.0 %collective-permute-start.9 = (bf16[4,48,128]{2,1,0:T(8,128)(2,1)S(1)}, bf16[4,48,128]{2,1,0:T(8,128)(2,1)S(1)}, u32[]{:S(2)}, u32[]{:S(2)}) collective-permute-start(bf16[4,48,128]{2,1,0:T(8,128)(2,1)S(1)} %get-tuple-element.53), channel_id=1, source_target_pairs={{0,4},{1,5},{2,6},{3,7},{4,0},{5,1},{6,2},{7,3},{8,12},{9,13},{10,... | collective-permute-start | bytes 147464 | tf_op jit(solution)/shard_map/ppermute | solution.py:55
  41.5 1.0 %collective-permute-start.10 = (bf16[4,48,128]{2,1,0:T(8,128)(2,1)S(1)}, bf16[4,48,128]{2,1,0:T(8,128)(2,1)S(1)}, u32[]{:S(2)}, u32[]{:S(2)}) collective-permute-start(bf16[4,48,128]{2,1,0:T(8,128)(2,1)S(1)} %get-tuple-element.54), channel_id=1, source_target_pairs={{0,6},{1,7},{2,4},{3,5},{4,2},{5,3},{6,0},{7,1},{8,14},{9,15},{10,... | collective-permute-start | bytes 147464 | tf_op jit(solution)/shard_map/ppermute | solution.py:55
  42.4 5.0 %shard_map.131.acc_ref = f32[592,256]{1,0:T(8,128)S(1)} custom-call(s32[2]{0:T(128)S(1)} %pad_add_fusion.place_ref, bf16[32,16,384]{2,1,0:T(8,128)(2,1)S(1)} %all-to-all-done.1.got_ref, bf16[528,256]{1,0:T(8,128)(2,1)S(1)} %get-tuple-element.44.refs_0_, bf16[528,256]{1,0:T(8,128)(2,1)S(1)} %collective-permute-done.refs_1_, ...), custom_call_target="tpu_custom_call" | custom-call | flops 1207959552 | bytes 8388608 | tf_op jit(solution)/shard_map/pallas_call | solution.py:383
  47.5 0.6 shard_map.134
  48.1 0.8 collective-permute-start.11
  48.9 1.3 %collective-permute-start.12 = (bf16[352,128]{1,0:T(8,128)(2,1)S(1)}, bf16[352,128]{1,0:T(8,128)(2,1)S(1)}, u32[]{:S(2)}, u32[]{:S(2)}) collective-permute-start(bf16[352,128]{1,0:T(8,128)(2,1)S(1)} %get-tuple-element.61), channel_id=1, source_target_pairs={{0,16},{1,17},{2,18},{3,19},{4,20},{5,21},{6,22},{7,23},{8,24},{9,... | collective-permute-start | bytes 270344 | tf_op jit(solution)/shard_map/ppermute | solution.py:55
  50.2 1.9 %collective-permute-start.13 = (bf16[352,128]{1,0:T(8,128)(2,1)S(1)}, bf16[352,128]{1,0:T(8,128)(2,1)S(1)}, u32[]{:S(2)}, u32[]{:S(2)}) collective-permute-start(bf16[352,128]{1,0:T(8,128)(2,1)S(1)} %get-tuple-element.62), channel_id=1, source_target_pairs={{0,24},{1,25},{2,26},{3,27},{4,28},{5,29},{6,30},{7,31},{8,0},{9,1... | collective-permute-start | bytes 270344 | tf_op jit(solution)/shard_map/ppermute | solution.py:55
  52.2 0.3 convolution_convert_fusion.1
  52.4 0.3 fusion.5
  52.7 0.3 convolution_add_fusion.7
  53.0 0.3 convolution_add_fusion.6
  53.3 0.3 convolution_add_fusion.5
  53.6 0.3 convolution_add_fusion.4
  53.9 0.3 convolution_add_fusion.3
  54.2 0.3 convolution_add_fusion.2
  54.6 0.3 convolution_add_fusion.1
  54.9 0.6 collective-permute-done.11.refs_0_
  55.5 2.9 %collective-permute-done.12.refs_1_ = bf16[352,128]{1,0:T(8,128)(2,1)S(1)} collective-permute-done((bf16[352,128]{1,0:T(8,128)(2,1)S(1)}, bf16[352,128]{1,0:T(8,128)(2,1)S(1)}, u32[]{:S(2)}, u32[]{:S(2)}) %collective-permute-start.12) | collective-permute-done | bytes 90144 | tf_op jit(solution)/shard_map/ppermute | solution.py:55
  58.5 2.1 %collective-permute-start.19 = (bf16[352,128]{1,0:T(8,128)(2,1)S(1)}, bf16[352,128]{1,0:T(8,128)(2,1)S(1)}, u32[]{:S(2)}, u32[]{:S(2)}) collective-permute-start(bf16[352,128]{1,0:T(8,128)(2,1)S(1)} %shard_map.135), channel_id=1, source_target_pairs={{0,24},{1,25},{2,26},{3,27},{4,28},{5,29},{6,30},{7,31},{8,0},{9,1... | collective-permute-start | bytes 270344 | tf_op jit(solution)/shard_map/ppermute | solution.py:55
  60.6 1.3 %collective-permute-start.18 = (bf16[352,128]{1,0:T(8,128)(2,1)S(1)}, bf16[352,128]{1,0:T(8,128)(2,1)S(1)}, u32[]{:S(2)}, u32[]{:S(2)}) collective-permute-start(bf16[352,128]{1,0:T(8,128)(2,1)S(1)} %shard_map.135), channel_id=1, source_target_pairs={{0,16},{1,17},{2,18},{3,19},{4,20},{5,21},{6,22},{7,23},{8,24},{9,... | collective-permute-start | bytes 270344 | tf_op jit(solution)/shard_map/ppermute | solution.py:55
  61.9 1.1 %fusion.1 = bf16[2,16,16,512]{3,2,1,0:T(8,128)(2,1)} fusion(f32[2,16,16,512]{3,2,1,0:T(8,128)S(1)} %convolution_add_fusion.1, f32[512]{0:T(512)S(1)} %convert_element_type.28, bf16[2,16,16,256]{3,2,1,0:T(8,128)(2,1)S(1)} %bitcast.117, bf16[3,3,256,512]{3,2,1,0:T(8,128)(2,1)S(1)} %copy-done.6), kind=kOutput, calls=%fused_computation.17 | convolution fusion | flops 135004160 | bytes 2099200 | tf_op jit(solution)/shard_map/nhwc,co->nhwo/dot_general | solution.py:563
  63.0 0.4 collective-permute-start.15
  63.4 1.5 %collective-permute-start.14 = (bf16[352,128]{1,0:T(8,128)(2,1)S(1)}, bf16[352,128]{1,0:T(8,128)(2,1)S(1)}, u32[]{:S(2)}, u32[]{:S(2)}) collective-permute-start(bf16[352,128]{1,0:T(8,128)(2,1)S(1)} %shard_map.135), channel_id=1, source_target_pairs={{0,2},{1,3},{2,0},{3,1},{4,6},{5,7},{6,4},{7,5},{8,10},{9,11},{10,... | collective-permute-start | bytes 270344 | tf_op jit(solution)/shard_map/ppermute | solution.py:55
  64.9 5.0 %collective-permute-done.18 = bf16[352,128]{1,0:T(8,128)(2,1)S(1)} collective-permute-done((bf16[352,128]{1,0:T(8,128)(2,1)S(1)}, bf16[352,128]{1,0:T(8,128)(2,1)S(1)}, u32[]{:S(2)}, u32[]{:S(2)}) %collective-permute-start.18) | collective-permute-done | bytes 90144 | tf_op jit(solution)/shard_map/ppermute | solution.py:55
  69.9 0.4 collective-permute-start.21
  70.3 1.8 %collective-permute-start.20 = (bf16[3,352,128]{2,1,0:T(8,128)(2,1)S(1)}, bf16[3,352,128]{2,1,0:T(8,128)(2,1)S(1)}, u32[]{:S(2)}, u32[]{:S(2)}) collective-permute-start(bf16[3,352,128]{2,1,0:T(8,128)(2,1)S(1)} %pad_maximum_fusion.1), channel_id=1, source_target_pairs={{0,2},{1,3},{2,0},{3,1},{4,6},{5,7},{6,4},{7,5},{8,10},{9,11},{10,... | collective-permute-start | bytes 811016 | tf_op jit(solution)/shard_map/ppermute | solution.py:55
  72.1 0.5 collective-permute-start.16
  72.6 1.1 %fusion.3 = bf16[2,16,16,256]{3,2,1,0:T(8,128)(2,1)} fusion(f32[2,16,16,256]{3,2,1,0:T(8,128)S(1)} %convolution_add_fusion.9, bf16[2,16,16,512]{3,2,1,0:T(8,128)(2,1)S(1)} %copy-done.2, bf16[2,16,16,256]{3,2,1,0:T(8,128)(2,1)S(1)} %bitcast.118, bf16[2,16,16,256]{3,2,1,0:T(8,128)(2,1)S(1)} %copy-done.7, bf16[3,3,256,512]{3,2,1,0:T(8,128)(2,1)S(1)} %copy-done.6), kind=kOutput, calls=%fused_computation.28 | convolution fusion | flops 135135232 | bytes 2097152 | tf_op jit(solution)/shard_map/nhwo,co->nhwc/dot_general | solution.py:572
  73.6 5.5 %collective-permute-done.16 = bf16[352,128]{1,0:T(8,128)(2,1)S(1)} collective-permute-done((bf16[352,128]{1,0:T(8,128)(2,1)S(1)}, bf16[352,128]{1,0:T(8,128)(2,1)S(1)}, u32[]{:S(2)}, u32[]{:S(2)}) %collective-permute-start.16) | collective-permute-done | bytes 90144 | tf_op jit(solution)/shard_map/ppermute | solution.py:55
  79.4 1.1 %collective-permute-start.22 = (bf16[2,352,128]{2,1,0:T(8,128)(2,1)S(1)}, bf16[2,352,128]{2,1,0:T(8,128)(2,1)S(1)}, u32[]{:S(2)}, u32[]{:S(2)}) collective-permute-start(bf16[2,352,128]{2,1,0:T(8,128)(2,1)S(1)} %slice.121), channel_id=1, source_target_pairs={{0,2},{1,3},{2,0},{3,1},{4,6},{5,7},{6,4},{7,5},{8,10},{9,11},{10,... | collective-permute-start | bytes 540680 | tf_op jit(solution)/shard_map/ppermute | solution.py:55
  80.5 1.5 %collective-permute-start.23 = (bf16[1,352,128]{2,1,0:T(8,128)(2,1)S(1)}, bf16[1,352,128]{2,1,0:T(8,128)(2,1)S(1)}, u32[]{:S(2)}, u32[]{:S(2)}) collective-permute-start(bf16[1,352,128]{2,1,0:T(8,128)(2,1)S(1)} %slice.122), channel_id=1, source_target_pairs={{0,4},{1,5},{2,6},{3,7},{4,0},{5,1},{6,2},{7,3},{8,12},{9,13},{10,... | collective-permute-start | bytes 270344 | tf_op jit(solution)/shard_map/ppermute | solution.py:55
  82.1 4.4 %collective-permute-done.22 = bf16[2,352,128]{2,1,0:T(8,128)(2,1)S(1)} collective-permute-done((bf16[2,352,128]{2,1,0:T(8,128)(2,1)S(1)}, bf16[2,352,128]{2,1,0:T(8,128)(2,1)S(1)}, u32[]{:S(2)}, u32[]{:S(2)}) %collective-permute-start.22) | collective-permute-done | bytes 180256 | tf_op jit(solution)/shard_map/ppermute | solution.py:55
  86.6 1.5 %collective-permute-done.26.refs_5_ = bf16[3,352,128]{2,1,0:T(8,128)(2,1)S(1)} collective-permute-done((bf16[3,352,128]{2,1,0:T(8,128)(2,1)S(1)}, bf16[3,352,128]{2,1,0:T(8,128)(2,1)S(1)}, u32[]{:S(2)}, u32[]{:S(2)}) %collective-permute-start.26) | collective-permute-done | bytes 270368 | tf_op jit(solution)/shard_map/ppermute | solution.py:55
  88.1 3.7 %shard_map.136 = (f32[9,256,512]{2,1,0:T(8,128)}, f32[768,256]{1,0:T(8,128)}, f32[1,512]{1,0:T(1,128)}) custom-call(s32[2]{0:T(128)S(1)} %pad_add_fusion.place_ref, bf16[4,352,128]{2,1,0:T(8,128)(2,1)S(1)} %pad_maximum_fusion.refs_0_, bf16[9,352,128]{2,1,0:T(8,128)(2,1)S(1)} %constant_dynamic-update-slice_fusion.refs_1_, ...), custom_call_target="tpu_custom_call" | custom-call | tf_op jit(solution)/shard_map/pallas_call | solution.py:495
  (53 shorter events, 0.9 us)
Async XLA Ops:
  0.6 16.3 %copy-start = (bf16[768,256]{1,0:T(8,128)(2,1)S(1)}, bf16[768,256]{1,0:T(8,128)(2,1)}, u32[]{:S(2)}) copy-start(bf16[768,256]{1,0:T(8,128)(2,1)} %param.10) | copy-start | bytes 1179652
  2.9 20.5 %all-to-all-start = ((f32[32,8,384]{2,1,0:T(8,128)}), f32[32,8,384]{2,1,0:T(8,128)S(1)}, u32[]{:S(2)}, u32[]{:S(2)}) async-start(f32[32,8,384]{2,1,0:T(8,128)} %get-tuple-element.40), calls=%async_computation | async-start | bytes 786432 | tf_op jit(solution)/shard_map/all_to_all | solution.py:85
  10.2 1.0 %copy-start.1 = (bf16[2,16,16,512]{3,2,1,0:T(8,128)(2,1)S(1)}, bf16[2,16,16,512]{3,2,1,0:T(8,128)(2,1)}, u32[]{:S(2)}) copy-start(bf16[2,16,16,512]{3,2,1,0:T(8,128)(2,1)} %param.17) | copy-start | bytes 1572868
  11.3 0.7 copy-start.4
  12.0 15.3 %copy-start.2 = (bf16[2,16,16,512]{3,2,1,0:T(8,128)(2,1)S(1)}, bf16[2,16,16,512]{3,2,1,0:T(8,128)(2,1)}, u32[]{:S(2)}) copy-start(bf16[2,16,16,512]{3,2,1,0:T(8,128)(2,1)} %param.17) | copy-start | bytes 1572868
  12.7 18.3 %collective-permute-start.2 = (bf16[528,256]{1,0:T(8,128)(2,1)}, bf16[528,256]{1,0:T(8,128)(2,1)S(1)}, u32[]{:S(2)}, u32[]{:S(2)}) collective-permute-start(bf16[528,256]{1,0:T(8,128)(2,1)} %get-tuple-element.43), channel_id=1, source_target_pairs={{0,6},{1,7},{2,4},{3,5},{4,2},{5,3},{6,0},{7,1},{8,14},{9,15},{10,... | collective-permute-start | bytes 811016 | tf_op jit(solution)/shard_map/ppermute | solution.py:55
  15.4 15.7 %collective-permute-start.1 = (bf16[528,256]{1,0:T(8,128)(2,1)}, bf16[528,256]{1,0:T(8,128)(2,1)S(1)}, u32[]{:S(2)}, u32[]{:S(2)}) collective-permute-start(bf16[528,256]{1,0:T(8,128)(2,1)} %get-tuple-element.43), channel_id=1, source_target_pairs={{0,4},{1,5},{2,6},{3,7},{4,0},{5,1},{6,2},{7,3},{8,12},{9,13},{10,... | collective-permute-start | bytes 811016 | tf_op jit(solution)/shard_map/ppermute | solution.py:55
  16.0 15.1 %collective-permute-start = (bf16[528,256]{1,0:T(8,128)(2,1)S(1)}, bf16[528,256]{1,0:T(8,128)(2,1)S(1)}, u32[]{:S(2)}, u32[]{:S(2)}) collective-permute-start(bf16[528,256]{1,0:T(8,128)(2,1)S(1)} %get-tuple-element.44.refs_0_), channel_id=1, source_target_pairs={{0,2},{1,3},{2,0},{3,1},{4,6},{5,7},{6,4},{7,5},{8,10},{9,11},{10,... | collective-permute-start | bytes 811016 | tf_op jit(solution)/shard_map/ppermute | solution.py:55
  24.6 15.8 %all-to-all-start.1 = ((bf16[32,16,384]{2,1,0:T(8,128)(2,1)}), bf16[32,16,384]{2,1,0:T(8,128)(2,1)S(1)}, u32[]{:S(2)}, u32[]{:S(2)}) async-start(bf16[32,16,384]{2,1,0:T(8,128)(2,1)} %shard_map.129), calls=%async_computation.1 | async-start | bytes 786432 | tf_op jit(solution)/shard_map/all_to_all | solution.py:85
  27.2 2.7 %copy-start.5 = (bf16[3,3,256,512]{3,2,1,0:T(8,128)(2,1)S(1)}, bf16[3,3,256,512]{3,2,1,0:T(8,128)(2,1)}, u32[]{:S(2)}) copy-start(bf16[3,3,256,512]{3,2,1,0:T(8,128)(2,1)} %param.15) | copy-start | bytes 7077892
  30.0 2.2 %copy-start.3 = (bf16[784,768]{1,0:T(8,128)(2,1)S(1)}, bf16[784,768]{1,0:T(8,128)(2,1)}, u32[]{:S(2)}) copy-start(bf16[784,768]{1,0:T(8,128)(2,1)} %book_ref.1) | copy-start | bytes 3612676
  31.1 9.4 %collective-permute-start.3 = (bf16[528,256]{1,0:T(8,128)(2,1)S(1)}, bf16[528,256]{1,0:T(8,128)(2,1)}, u32[]{:S(2)}, u32[]{:S(2)}) collective-permute-start(bf16[528,256]{1,0:T(8,128)(2,1)S(1)} %get-tuple-element.44.refs_0_), channel_id=1, source_target_pairs={{0,1},{1,0},{2,3},{3,2},{4,5},{5,4},{6,7},{7,6},{8,9},{9,8},{10,11... | collective-permute-start | bytes 811016 | tf_op jit(solution)/shard_map/ppermute | solution.py:55
  31.4 10.1 %collective-permute-start.4 = (bf16[528,256]{1,0:T(8,128)(2,1)S(1)}, bf16[528,256]{1,0:T(8,128)(2,1)}, u32[]{:S(2)}, u32[]{:S(2)}) collective-permute-start(bf16[528,256]{1,0:T(8,128)(2,1)S(1)} %collective-permute-done.refs_1_), channel_id=1, source_target_pairs={{0,1},{1,0},{2,3},{3,2},{4,5},{5,4},{6,7},{7,6},{8,9},{9,8},{10,11... | collective-permute-start | bytes 811016 | tf_op jit(solution)/shard_map/ppermute | solution.py:55
  31.6 10.8 %collective-permute-start.5 = (bf16[528,256]{1,0:T(8,128)(2,1)S(1)}, bf16[528,256]{1,0:T(8,128)(2,1)}, u32[]{:S(2)}, u32[]{:S(2)}) collective-permute-start(bf16[528,256]{1,0:T(8,128)(2,1)S(1)} %collective-permute-done.1.refs_2_), channel_id=1, source_target_pairs={{0,1},{1,0},{2,3},{3,2},{4,5},{5,4},{6,7},{7,6},{8,9},{9,8},{10,11... | collective-permute-start | bytes 811016 | tf_op jit(solution)/shard_map/ppermute | solution.py:55
  31.9 10.5 %collective-permute-start.6 = (bf16[528,256]{1,0:T(8,128)(2,1)S(1)}, bf16[528,256]{1,0:T(8,128)(2,1)}, u32[]{:S(2)}, u32[]{:S(2)}) collective-permute-start(bf16[528,256]{1,0:T(8,128)(2,1)S(1)} %collective-permute-done.2.refs_3_), channel_id=1, source_target_pairs={{0,1},{1,0},{2,3},{3,2},{4,5},{5,4},{6,7},{7,6},{8,9},{9,8},{10,11... | collective-permute-start | bytes 811016 | tf_op jit(solution)/shard_map/ppermute | solution.py:55
  33.9 1.8 %collective-permute-start.7 = (f32[768,128]{1,0:T(8,128)S(1)}, f32[768,128]{1,0:T(8,128)S(1)}, u32[]{:S(2)}, u32[]{:S(2)}) collective-permute-start(f32[768,128]{1,0:T(8,128)S(1)} %get-tuple-element.50), channel_id=1, source_target_pairs={{0,1},{1,0},{2,3},{3,2},{4,5},{5,4},{6,7},{7,6},{8,9},{9,8},{10,11... | collective-permute-start | bytes 1179656 | tf_op jit(solution)/shard_map/ppermute | solution.py:55
  36.3 11.2 %collective-permute-start.8 = (bf16[4,48,128]{2,1,0:T(8,128)(2,1)S(1)}, bf16[4,48,128]{2,1,0:T(8,128)(2,1)S(1)}, u32[]{:S(2)}, u32[]{:S(2)}) collective-permute-start(bf16[4,48,128]{2,1,0:T(8,128)(2,1)S(1)} %get-tuple-element.52), channel_id=1, source_target_pairs={{0,2},{1,3},{2,0},{3,1},{4,6},{5,7},{6,4},{7,5},{8,10},{9,11},{10,... | collective-permute-start | bytes 147464 | tf_op jit(solution)/shard_map/ppermute | solution.py:55
  40.4 7.1 %collective-permute-start.9 = (bf16[4,48,128]{2,1,0:T(8,128)(2,1)S(1)}, bf16[4,48,128]{2,1,0:T(8,128)(2,1)S(1)}, u32[]{:S(2)}, u32[]{:S(2)}) collective-permute-start(bf16[4,48,128]{2,1,0:T(8,128)(2,1)S(1)} %get-tuple-element.53), channel_id=1, source_target_pairs={{0,4},{1,5},{2,6},{3,7},{4,0},{5,1},{6,2},{7,3},{8,12},{9,13},{10,... | collective-permute-start | bytes 147464 | tf_op jit(solution)/shard_map/ppermute | solution.py:55
  41.5 10.7 %copy-start.8 = (s32[1,512]{1,0:T(1,128)S(1)}, s32[1,512]{1,0:T(1,128)}, u32[]{:S(2)}) copy-start(s32[1,512]{1,0:T(1,128)} %get-tuple-element.63) | copy-start | bytes 6148
  41.5 11.0 %copy-start.6 = (bf16[3,3,256,512]{3,2,1,0:T(8,128)(2,1)S(1)}, bf16[3,3,256,512]{3,2,1,0:T(8,128)(2,1)}, u32[]{:S(2)}) copy-start(bf16[3,3,256,512]{3,2,1,0:T(8,128)(2,1)} %param.15) | copy-start | bytes 7077892
  41.5 6.0 %collective-permute-start.10 = (bf16[4,48,128]{2,1,0:T(8,128)(2,1)S(1)}, bf16[4,48,128]{2,1,0:T(8,128)(2,1)S(1)}, u32[]{:S(2)}, u32[]{:S(2)}) collective-permute-start(bf16[4,48,128]{2,1,0:T(8,128)(2,1)S(1)} %get-tuple-element.54), channel_id=1, source_target_pairs={{0,6},{1,7},{2,4},{3,5},{4,2},{5,3},{6,0},{7,1},{8,14},{9,15},{10,... | collective-permute-start | bytes 147464 | tf_op jit(solution)/shard_map/ppermute | solution.py:55
  48.1 7.4 %collective-permute-start.11 = (bf16[352,128]{1,0:T(8,128)(2,1)S(1)}, bf16[352,128]{1,0:T(8,128)(2,1)S(1)}, u32[]{:S(2)}, u32[]{:S(2)}) collective-permute-start(bf16[352,128]{1,0:T(8,128)(2,1)S(1)} %get-tuple-element.60), channel_id=1, source_target_pairs={{0,8},{1,9},{2,10},{3,11},{4,12},{5,13},{6,14},{7,15},{8,16},{9,17... | collective-permute-start | bytes 270344 | tf_op jit(solution)/shard_map/ppermute | solution.py:55
  48.9 9.5 %collective-permute-start.12 = (bf16[352,128]{1,0:T(8,128)(2,1)S(1)}, bf16[352,128]{1,0:T(8,128)(2,1)S(1)}, u32[]{:S(2)}, u32[]{:S(2)}) collective-permute-start(bf16[352,128]{1,0:T(8,128)(2,1)S(1)} %get-tuple-element.61), channel_id=1, source_target_pairs={{0,16},{1,17},{2,18},{3,19},{4,20},{5,21},{6,22},{7,23},{8,24},{9,... | collective-permute-start | bytes 270344 | tf_op jit(solution)/shard_map/ppermute | solution.py:55
  50.2 8.2 %collective-permute-start.13 = (bf16[352,128]{1,0:T(8,128)(2,1)S(1)}, bf16[352,128]{1,0:T(8,128)(2,1)S(1)}, u32[]{:S(2)}, u32[]{:S(2)}) collective-permute-start(bf16[352,128]{1,0:T(8,128)(2,1)S(1)} %get-tuple-element.62), channel_id=1, source_target_pairs={{0,24},{1,25},{2,26},{3,27},{4,28},{5,29},{6,30},{7,31},{8,0},{9,1... | collective-permute-start | bytes 270344 | tf_op jit(solution)/shard_map/ppermute | solution.py:55
  54.6 18.0 %copy-start.7 = (bf16[2,16,16,256]{3,2,1,0:T(8,128)(2,1)S(1)}, bf16[2,16,16,256]{3,2,1,0:T(8,128)(2,1)}, u32[]{:S(2)}) copy-start(bf16[2,16,16,256]{3,2,1,0:T(8,128)(2,1)} %param.11) | copy-start | bytes 786436
  58.5 6.4 %collective-permute-start.19 = (bf16[352,128]{1,0:T(8,128)(2,1)S(1)}, bf16[352,128]{1,0:T(8,128)(2,1)S(1)}, u32[]{:S(2)}, u32[]{:S(2)}) collective-permute-start(bf16[352,128]{1,0:T(8,128)(2,1)S(1)} %shard_map.135), channel_id=1, source_target_pairs={{0,24},{1,25},{2,26},{3,27},{4,28},{5,29},{6,30},{7,31},{8,0},{9,1... | collective-permute-start | bytes 270344 | tf_op jit(solution)/shard_map/ppermute | solution.py:55
  60.6 9.3 %collective-permute-start.18 = (bf16[352,128]{1,0:T(8,128)(2,1)S(1)}, bf16[352,128]{1,0:T(8,128)(2,1)S(1)}, u32[]{:S(2)}, u32[]{:S(2)}) collective-permute-start(bf16[352,128]{1,0:T(8,128)(2,1)S(1)} %shard_map.135), channel_id=1, source_target_pairs={{0,16},{1,17},{2,18},{3,19},{4,20},{5,21},{6,22},{7,23},{8,24},{9,... | collective-permute-start | bytes 270344 | tf_op jit(solution)/shard_map/ppermute | solution.py:55
  61.9 8.0 %collective-permute-start.17 = (bf16[352,128]{1,0:T(8,128)(2,1)S(1)}, bf16[352,128]{1,0:T(8,128)(2,1)S(1)}, u32[]{:S(2)}, u32[]{:S(2)}) collective-permute-start(bf16[352,128]{1,0:T(8,128)(2,1)S(1)} %shard_map.135), channel_id=1, source_target_pairs={{0,8},{1,9},{2,10},{3,11},{4,12},{5,13},{6,14},{7,15},{8,16},{9,17... | collective-permute-start | bytes 270344 | tf_op jit(solution)/shard_map/ppermute | solution.py:55
  63.0 10.6 %collective-permute-start.15 = (bf16[352,128]{1,0:T(8,128)(2,1)S(1)}, bf16[352,128]{1,0:T(8,128)(2,1)S(1)}, u32[]{:S(2)}, u32[]{:S(2)}) collective-permute-start(bf16[352,128]{1,0:T(8,128)(2,1)S(1)} %shard_map.135), channel_id=1, source_target_pairs={{0,4},{1,5},{2,6},{3,7},{4,0},{5,1},{6,2},{7,3},{8,12},{9,13},{10,... | collective-permute-start | bytes 270344 | tf_op jit(solution)/shard_map/ppermute | solution.py:55
  63.4 8.7 %collective-permute-start.14 = (bf16[352,128]{1,0:T(8,128)(2,1)S(1)}, bf16[352,128]{1,0:T(8,128)(2,1)S(1)}, u32[]{:S(2)}, u32[]{:S(2)}) collective-permute-start(bf16[352,128]{1,0:T(8,128)(2,1)S(1)} %shard_map.135), channel_id=1, source_target_pairs={{0,2},{1,3},{2,0},{3,1},{4,6},{5,7},{6,4},{7,5},{8,10},{9,11},{10,... | collective-permute-start | bytes 270344 | tf_op jit(solution)/shard_map/ppermute | solution.py:55
  69.9 9.3 %collective-permute-start.21 = (bf16[3,352,128]{2,1,0:T(8,128)(2,1)S(1)}, bf16[3,352,128]{2,1,0:T(8,128)(2,1)S(1)}, u32[]{:S(2)}, u32[]{:S(2)}) collective-permute-start(bf16[3,352,128]{2,1,0:T(8,128)(2,1)S(1)} %pad_maximum_fusion.1), channel_id=1, source_target_pairs={{0,4},{1,5},{2,6},{3,7},{4,0},{5,1},{6,2},{7,3},{8,12},{9,13},{10,... | collective-permute-start | bytes 811016 | tf_op jit(solution)/shard_map/ppermute | solution.py:55
  70.3 8.9 %collective-permute-start.20 = (bf16[3,352,128]{2,1,0:T(8,128)(2,1)S(1)}, bf16[3,352,128]{2,1,0:T(8,128)(2,1)S(1)}, u32[]{:S(2)}, u32[]{:S(2)}) collective-permute-start(bf16[3,352,128]{2,1,0:T(8,128)(2,1)S(1)} %pad_maximum_fusion.1), channel_id=1, source_target_pairs={{0,2},{1,3},{2,0},{3,1},{4,6},{5,7},{6,4},{7,5},{8,10},{9,11},{10,... | collective-permute-start | bytes 811016 | tf_op jit(solution)/shard_map/ppermute | solution.py:55
  72.1 7.0 %collective-permute-start.16 = (bf16[352,128]{1,0:T(8,128)(2,1)S(1)}, bf16[352,128]{1,0:T(8,128)(2,1)S(1)}, u32[]{:S(2)}, u32[]{:S(2)}) collective-permute-start(bf16[352,128]{1,0:T(8,128)(2,1)S(1)} %collective-permute-done.14), channel_id=1, source_target_pairs={{0,4},{1,5},{2,6},{3,7},{4,0},{5,1},{6,2},{7,3},{8,12},{9,13},{10,... | collective-permute-start | bytes 270344 | tf_op jit(solution)/shard_map/ppermute | solution.py:55
  79.3 8.8 %collective-permute-start.25 = (bf16[9,352,128]{2,1,0:T(8,128)(2,1)S(1)}, bf16[9,352,128]{2,1,0:T(8,128)(2,1)S(1)}, u32[]{:S(2)}, u32[]{:S(2)}) collective-permute-start(bf16[9,352,128]{2,1,0:T(8,128)(2,1)S(1)} %constant_dynamic-update-slice_fusion.refs_1_), channel_id=1, source_target_pairs={{0,1},{1,0},{2,3},{3,2},{4,5},{5,4},{6,7},{7,6},{8,9},{9,8},{10,11... | collective-permute-start | bytes 2433032 | tf_op jit(solution)/shard_map/ppermute | solution.py:55
  79.4 7.0 %collective-permute-start.22 = (bf16[2,352,128]{2,1,0:T(8,128)(2,1)S(1)}, bf16[2,352,128]{2,1,0:T(8,128)(2,1)S(1)}, u32[]{:S(2)}, u32[]{:S(2)}) collective-permute-start(bf16[2,352,128]{2,1,0:T(8,128)(2,1)S(1)} %slice.121), channel_id=1, source_target_pairs={{0,2},{1,3},{2,0},{3,1},{4,6},{5,7},{6,4},{7,5},{8,10},{9,11},{10,... | collective-permute-start | bytes 540680 | tf_op jit(solution)/shard_map/ppermute | solution.py:55
  80.5 5.9 %collective-permute-start.23 = (bf16[1,352,128]{2,1,0:T(8,128)(2,1)S(1)}, bf16[1,352,128]{2,1,0:T(8,128)(2,1)S(1)}, u32[]{:S(2)}, u32[]{:S(2)}) collective-permute-start(bf16[1,352,128]{2,1,0:T(8,128)(2,1)S(1)} %slice.122), channel_id=1, source_target_pairs={{0,4},{1,5},{2,6},{3,7},{4,0},{5,1},{6,2},{7,3},{8,12},{9,13},{10,... | collective-permute-start | bytes 270344 | tf_op jit(solution)/shard_map/ppermute | solution.py:55
  82.0 4.5 %collective-permute-start.24 = (bf16[4,352,128]{2,1,0:T(8,128)(2,1)S(1)}, bf16[4,352,128]{2,1,0:T(8,128)(2,1)S(1)}, u32[]{:S(2)}, u32[]{:S(2)}) collective-permute-start(bf16[4,352,128]{2,1,0:T(8,128)(2,1)S(1)} %pad_maximum_fusion.refs_0_), channel_id=1, source_target_pairs={{0,1},{1,0},{2,3},{3,2},{4,5},{5,4},{6,7},{7,6},{8,9},{9,8},{10,11... | collective-permute-start | bytes 1081352 | tf_op jit(solution)/shard_map/ppermute | solution.py:55
  86.5 1.6 %collective-permute-start.26 = (bf16[3,352,128]{2,1,0:T(8,128)(2,1)S(1)}, bf16[3,352,128]{2,1,0:T(8,128)(2,1)S(1)}, u32[]{:S(2)}, u32[]{:S(2)}) collective-permute-start(bf16[3,352,128]{2,1,0:T(8,128)(2,1)S(1)} %constant_dynamic-update-slice_fusion.3.refs_2_), channel_id=1, source_target_pairs={{0,1},{1,0},{2,3},{3,2},{4,5},{5,4},{6,7},{7,6},{8,9},{9,8},{10,11... | collective-permute-start | bytes 811016 | tf_op jit(solution)/shard_map/ppermute | solution.py:55

commit v7 on v6

--- a/solution.py
+++ b/solution.py
@@ -58,14 +58,18 @@
 def gather_planes(grid, own):
     zs = [send(own, grid.turn(k)) for k in range(1, PARTS)]
     x, y = send(own, grid.flip(2)), send(own, grid.flip(4))
-    early = jnp.stack([own, x, y, send(x, grid.flip(4))])
+    early = jnp.stack([own, x, y, send(own, grid.flip(6))])
     zs = jnp.stack(zs)
     return early, zs, send(zs, grid.flip(2)), send(zs, grid.flip(4))
 
 
 def gather_places(grid, early, zs, xs, ys):
-    second, first = send(ys[:2], grid.flip(2)), send(xs[2:], grid.flip(4))
-    mine = [early, jnp.concatenate([zs, xs, ys]), jnp.concatenate([second, first])]
+    count, height, wide = zs.shape
+    cut = count * height // 2
+    second = send(ys.reshape(-1, wide)[:cut], grid.flip(2))
+    first = send(xs.reshape(-1, wide)[cut:], grid.flip(4))
+    last = jnp.concatenate([second, first]).reshape(zs.shape)
+    mine = [early, jnp.concatenate([zs, xs, ys]), last]
     return mine + [send(x, grid.flip(1)) for x in mine]
 
 

time: 92.3 us -> 91.1 us (0.987)
  waiting for transfers between devices: 27.4 us -> 25.3 us
    ppermute x27, waiting for transfers between devices: 20.4 us -> 18.4 us  [send(): return lax.ppermute(x, AXES, perm)]
    unnamed x21 -> x20, local copies, waits for them, and re-layouts: 1.86 us -> 1.85 us
  transfers between devices with their start and end apart: 29 -> 29, of which waited for: 9 -> 11; matrix products, arithmetic and copies ran while one was open for 13% -> 14% of each run, Pallas kernels for 10% -> 10%
where the time goes in v7:
time: 91.1 us; the launch traced here: 90.6 us
  starting transfers between devices  34.1 us (37%)
  waiting for transfers between devices  25.3 us (28%)
  Pallas kernels  16 us (18%)
  matrix products  11.4 us (13%)
  local copies, waits for them, and re-layouts  1.92 us (2%)
  between operations  1.03 us (1%)
    ppermute x27, starting transfers between devices, send(): return lax.ppermute(x, AXES, perm)  24.2 us
    ppermute x27, waiting for transfers between devices, send(): return lax.ppermute(x, AXES, perm)  18.4 us
    all_to_all x2, starting transfers between devices, spread(): return lax.all_to_all(x, AXES, split_axis=0, concat_axis=0, tiled=True)  9.92 us
    all_to_all x2, waiting for transfers between devices, spread(): return lax.all_to_all(x, AXES, split_axis=0, concat_axis=0, tiled=True)  6.93 us
    dot_general x9, matrix products, on_device(): jnp.einsum('nhwo,co->nhwc', grad_window, kernel[row_off, col_off], prefer...  5.84 us
    pallas_call x1, Pallas kernels, group_weights(): pl.pallas_call(functools.partial(weights_kernel, grid, cap), out_shape=ja...  5.03 us
    pallas_call x1, Pallas kernels, finish(): pl.pallas_call(functools.partial(finish_kernel, krows, counts), out_shape...  3.71 us
    dot_general x9, matrix products, on_device(): jnp.einsum('nhwc,co->nhwo', window, kernel[row_off, col_off], preferred_e...  3.49 us
  transfers between devices with their start and end apart: 29, of which 11 were waited for; matrix products, arithmetic and copies ran while one was open for 14% of the time, Pallas kernels for 10%

profile of v7, /device:TPU:0, one launch (start us, length us, event | category | flops | bytes accessed | tf_op | source)
XLA Modules:
  0.0 90.6 jit_solution(3054385410034601553)
XLA Ops:
  0.6 2.2 %shard_map.128 = (s32[1,512]{1,0:T(1,128)}, f32[8,512]{1,0:T(8,128)}, f32[32,8,384]{2,1,0:T(8,128)}) custom-call(s32[32,16]{1,0:T(8,128)} %bitcast.133, s32[1,32]{1,0:T(1,128)} %counts_hbm.1, s32[8,32]{1,0:T(8,128)} %bitcast.134, bf16[512,256]{1,0:T(8,128)(2,1)} %bitcast.124), custom_call_target="tpu_custom_call" | custom-call | flops 67108864 | bytes 2097152 | tf_op jit(solution)/shard_map/pallas_call | solution.py:163
  2.9 7.3 %all-to-all-start = ((f32[32,8,384]{2,1,0:T(8,128)}), f32[32,8,384]{2,1,0:T(8,128)S(1)}, u32[]{:S(2)}, u32[]{:S(2)}) async-start(f32[32,8,384]{2,1,0:T(8,128)} %get-tuple-element.40), calls=%async_computation | async-start | bytes 786432 | tf_op jit(solution)/shard_map/all_to_all | solution.py:89
  10.2 1.0 %copy-done.1 = bf16[2,16,16,512]{3,2,1,0:T(8,128)(2,1)S(1)} copy-done((bf16[2,16,16,512]{3,2,1,0:T(8,128)(2,1)S(1)}, bf16[2,16,16,512]{3,2,1,0:T(8,128)(2,1)}, u32[]{:S(2)}) %copy-start.1) | copy-done | bytes 524312
  11.3 0.7 copy-done.4
  12.0 0.7 shard_map.130
  12.7 2.7 %collective-permute-start.2 = (bf16[528,256]{1,0:T(8,128)(2,1)}, bf16[528,256]{1,0:T(8,128)(2,1)S(1)}, u32[]{:S(2)}, u32[]{:S(2)}) collective-permute-start(bf16[528,256]{1,0:T(8,128)(2,1)} %get-tuple-element.43), channel_id=1, source_target_pairs={{0,6},{1,7},{2,4},{3,5},{4,2},{5,3},{6,0},{7,1},{8,14},{9,15},{10,... | collective-permute-start | bytes 811016 | tf_op jit(solution)/shard_map/ppermute | solution.py:55
  15.4 0.6 collective-permute-start.1
  16.0 0.3 collective-permute-start
  16.2 0.7 convert_element_type.28
  17.0 1.8 %convolution_convert_fusion.codes_ref = bf16[784,256]{1,0:T(8,128)(2,1)S(1)} fusion(bf16[784,768]{1,0:T(8,128)(2,1)} %book_ref.1, bf16[768,256]{1,0:T(8,128)(2,1)S(1)} %copy-done), kind=kOutput, calls=%fused_computation.18 | convolution fusion | flops 308482048 | bytes 1998848 | tf_op jit(solution)/shard_map/dot_general | solution.py:538
  18.7 4.7 %all-to-all-done.asked_ref = f32[32,8,384]{2,1,0:T(8,128)S(1)} async-done(((f32[32,8,384]{2,1,0:T(8,128)}), f32[32,8,384]{2,1,0:T(8,128)S(1)}, u32[]{:S(2)}, u32[]{:S(2)}) %all-to-all-start) | async-done | bytes 393248 | tf_op jit(solution)/shard_map/all_to_all | solution.py:89
  23.4 1.2 %shard_map.129 = bf16[32,16,384]{2,1,0:T(8,128)(2,1)} custom-call(f32[32,8,384]{2,1,0:T(8,128)S(1)} %all-to-all-done.asked_ref, bf16[784,256]{1,0:T(8,128)(2,1)S(1)} %convolution_convert_fusion.codes_ref), custom_call_target="tpu_custom_call" | custom-call | flops 102760448 | bytes 2097152 | tf_op jit(solution)/shard_map/pallas_call | solution.py:243
  24.6 2.6 %all-to-all-start.1 = ((bf16[32,16,384]{2,1,0:T(8,128)(2,1)}), bf16[32,16,384]{2,1,0:T(8,128)(2,1)S(1)}, u32[]{:S(2)}, u32[]{:S(2)}) async-start(bf16[32,16,384]{2,1,0:T(8,128)(2,1)} %shard_map.129), calls=%async_computation.1 | async-start | bytes 786432 | tf_op jit(solution)/shard_map/all_to_all | solution.py:89
  27.2 1.4 %fusion.4 = f32[2,16,16,256]{3,2,1,0:T(8,128)S(1)} fusion(bf16[2,16,16,512]{3,2,1,0:T(8,128)(2,1)S(1)} %copy-done.2, bf16[3,3,256,512]{3,2,1,0:T(8,128)(2,1)} %param.15), kind=kOutput, calls=%fused_computation.38 | convolution fusion | flops 134217728 | bytes 1310720 | tf_op jit(solution)/shard_map/nhwo,co->nhwc/dot_general | solution.py:576
  28.7 1.3 %convolution_add_fusion.15 = f32[2,16,16,256]{3,2,1,0:T(8,128)S(1)} fusion(f32[2,16,16,256]{3,2,1,0:T(8,128)S(1)} %fusion.4, bf16[2,16,16,512]{3,2,1,0:T(8,128)(2,1)S(1)} %copy-done.2, bf16[3,3,256,512]{3,2,1,0:T(8,128)(2,1)} %param.15), kind=kOutput, calls=%fused_computation.27 | convolution fusion | flops 134348800 | bytes 1835008 | tf_op jit(solution)/shard_map/nhwo,co->nhwc/dot_general | solution.py:576
  30.0 0.3 convolution_add_fusion.14
  30.4 0.3 convolution_add_fusion.13
  30.7 0.3 convolution_add_fusion.12
  31.1 0.3 collective-permute-start.3
  31.6 0.3 collective-permute-start.5
  32.2 1.7 %shard_map.132 = (f32[768,128]{1,0:T(8,128)S(1)}, f32[768,128]{1,0:T(8,128)S(1)}) custom-call(s32[2]{0:T(128)S(1)} %pad_add_fusion.place_ref, f32[32,8,384]{2,1,0:T(8,128)S(1)} %all-to-all-done.asked_ref, bf16[784,768]{1,0:T(8,128)(2,1)S(1)} %copy-done.3, bf16[784,256]{1,0:T(8,128)(2,1)S(1)} %convolution_convert_fusion.codes_ref), custom_call_target="tpu_custom_call" | custom-call | flops 509607936 | bytes 4194304 | tf_op jit(solution)/shard_map/pallas_call | solution.py:275
  33.9 0.3 collective-permute-start.7
  34.2 0.4 convolution_add_fusion.11
  34.6 0.4 convolution_add_fusion.10
  34.9 0.3 convolution_add_fusion.9
  35.3 0.4 collective-permute-done.7.got_ref
  35.7 0.6 shard_map.133
  36.3 1.8 %collective-permute-start.8 = (bf16[4,48,128]{2,1,0:T(8,128)(2,1)S(1)}, bf16[4,48,128]{2,1,0:T(8,128)(2,1)S(1)}, u32[]{:S(2)}, u32[]{:S(2)}) collective-permute-start(bf16[4,48,128]{2,1,0:T(8,128)(2,1)S(1)} %get-tuple-element.52), channel_id=1, source_target_pairs={{0,2},{1,3},{2,0},{3,1},{4,6},{5,7},{6,4},{7,5},{8,10},{9,11},{10,... | collective-permute-start | bytes 147464 | tf_op jit(solution)/shard_map/ppermute | solution.py:55
  38.1 2.3 %all-to-all-done.1.got_ref = bf16[32,16,384]{2,1,0:T(8,128)(2,1)S(1)} async-done(((bf16[32,16,384]{2,1,0:T(8,128)(2,1)}), bf16[32,16,384]{2,1,0:T(8,128)(2,1)S(1)}, u32[]{:S(2)}, u32[]{:S(2)}) %all-to-all-start.1) | async-done | bytes 393248 | tf_op jit(solution)/shard_map/all_to_all | solution.py:89
  40.4 1.0 %collective-permute-start.9 = (bf16[4,48,128]{2,1,0:T(8,128)(2,1)S(1)}, bf16[4,48,128]{2,1,0:T(8,128)(2,1)S(1)}, u32[]{:S(2)}, u32[]{:S(2)}) collective-permute-start(bf16[4,48,128]{2,1,0:T(8,128)(2,1)S(1)} %get-tuple-element.53), channel_id=1, source_target_pairs={{0,4},{1,5},{2,6},{3,7},{4,0},{5,1},{6,2},{7,3},{8,12},{9,13},{10,... | collective-permute-start | bytes 147464 | tf_op jit(solution)/shard_map/ppermute | solution.py:55
  41.5 1.0 %collective-permute-start.10 = (bf16[4,48,128]{2,1,0:T(8,128)(2,1)S(1)}, bf16[4,48,128]{2,1,0:T(8,128)(2,1)S(1)}, u32[]{:S(2)}, u32[]{:S(2)}) collective-permute-start(bf16[4,48,128]{2,1,0:T(8,128)(2,1)S(1)} %get-tuple-element.54), channel_id=1, source_target_pairs={{0,6},{1,7},{2,4},{3,5},{4,2},{5,3},{6,0},{7,1},{8,14},{9,15},{10,... | collective-permute-start | bytes 147464 | tf_op jit(solution)/shard_map/ppermute | solution.py:55
  42.4 5.0 %shard_map.131.acc_ref = f32[592,256]{1,0:T(8,128)S(1)} custom-call(s32[2]{0:T(128)S(1)} %pad_add_fusion.place_ref, bf16[32,16,384]{2,1,0:T(8,128)(2,1)S(1)} %all-to-all-done.1.got_ref, bf16[528,256]{1,0:T(8,128)(2,1)S(1)} %get-tuple-element.44.refs_0_, bf16[528,256]{1,0:T(8,128)(2,1)S(1)} %collective-permute-done.refs_1_, ...), custom_call_target="tpu_custom_call" | custom-call | flops 1207959552 | bytes 8388608 | tf_op jit(solution)/shard_map/pallas_call | solution.py:387
  47.5 0.6 shard_map.134
  48.1 0.8 collective-permute-start.11
  48.9 1.3 %collective-permute-start.12 = (bf16[352,128]{1,0:T(8,128)(2,1)S(1)}, bf16[352,128]{1,0:T(8,128)(2,1)S(1)}, u32[]{:S(2)}, u32[]{:S(2)}) collective-permute-start(bf16[352,128]{1,0:T(8,128)(2,1)S(1)} %get-tuple-element.61), channel_id=1, source_target_pairs={{0,16},{1,17},{2,18},{3,19},{4,20},{5,21},{6,22},{7,23},{8,24},{9,... | collective-permute-start | bytes 270344 | tf_op jit(solution)/shard_map/ppermute | solution.py:55
  50.2 1.9 %collective-permute-start.13 = (bf16[352,128]{1,0:T(8,128)(2,1)S(1)}, bf16[352,128]{1,0:T(8,128)(2,1)S(1)}, u32[]{:S(2)}, u32[]{:S(2)}) collective-permute-start(bf16[352,128]{1,0:T(8,128)(2,1)S(1)} %get-tuple-element.62), channel_id=1, source_target_pairs={{0,24},{1,25},{2,26},{3,27},{4,28},{5,29},{6,30},{7,31},{8,0},{9,1... | collective-permute-start | bytes 270344 | tf_op jit(solution)/shard_map/ppermute | solution.py:55
  52.2 0.3 convolution_convert_fusion.1
  52.4 0.3 fusion.5
  52.7 0.3 convolution_add_fusion.7
  53.1 0.3 convolution_add_fusion.6
  53.4 0.3 convolution_add_fusion.5
  53.7 0.3 convolution_add_fusion.4
  54.0 0.3 convolution_add_fusion.3
  54.3 0.3 convolution_add_fusion.2
  54.6 0.3 convolution_add_fusion.1
  54.9 0.6 collective-permute-done.11.refs_0_
  55.5 2.9 %collective-permute-done.12.refs_1_ = bf16[352,128]{1,0:T(8,128)(2,1)S(1)} collective-permute-done((bf16[352,128]{1,0:T(8,128)(2,1)S(1)}, bf16[352,128]{1,0:T(8,128)(2,1)S(1)}, u32[]{:S(2)}, u32[]{:S(2)}) %collective-permute-start.12) | collective-permute-done | bytes 90144 | tf_op jit(solution)/shard_map/ppermute | solution.py:55
  58.5 2.1 %collective-permute-start.19 = (bf16[352,128]{1,0:T(8,128)(2,1)S(1)}, bf16[352,128]{1,0:T(8,128)(2,1)S(1)}, u32[]{:S(2)}, u32[]{:S(2)}) collective-permute-start(bf16[352,128]{1,0:T(8,128)(2,1)S(1)} %shard_map.135), channel_id=1, source_target_pairs={{0,24},{1,25},{2,26},{3,27},{4,28},{5,29},{6,30},{7,31},{8,0},{9,1... | collective-permute-start | bytes 270344 | tf_op jit(solution)/shard_map/ppermute | solution.py:55
  60.6 1.3 %collective-permute-start.18 = (bf16[352,128]{1,0:T(8,128)(2,1)S(1)}, bf16[352,128]{1,0:T(8,128)(2,1)S(1)}, u32[]{:S(2)}, u32[]{:S(2)}) collective-permute-start(bf16[352,128]{1,0:T(8,128)(2,1)S(1)} %shard_map.135), channel_id=1, source_target_pairs={{0,16},{1,17},{2,18},{3,19},{4,20},{5,21},{6,22},{7,23},{8,24},{9,... | collective-permute-start | bytes 270344 | tf_op jit(solution)/shard_map/ppermute | solution.py:55
  61.9 1.1 %fusion.1 = bf16[2,16,16,512]{3,2,1,0:T(8,128)(2,1)} fusion(f32[2,16,16,512]{3,2,1,0:T(8,128)S(1)} %convolution_add_fusion.1, f32[512]{0:T(512)S(1)} %convert_element_type.28, bf16[2,16,16,256]{3,2,1,0:T(8,128)(2,1)S(1)} %bitcast.122, bf16[3,3,256,512]{3,2,1,0:T(8,128)(2,1)S(1)} %copy-done.6), kind=kOutput, calls=%fused_computation.17 | convolution fusion | flops 135004160 | bytes 2099200 | tf_op jit(solution)/shard_map/nhwc,co->nhwo/dot_general | solution.py:567
  63.0 1.3 %collective-permute-start.16 = (bf16[352,128]{1,0:T(8,128)(2,1)S(1)}, bf16[352,128]{1,0:T(8,128)(2,1)S(1)}, u32[]{:S(2)}, u32[]{:S(2)}) collective-permute-start(bf16[352,128]{1,0:T(8,128)(2,1)S(1)} %shard_map.135), channel_id=1, source_target_pairs={{0,6},{1,7},{2,4},{3,5},{4,2},{5,3},{6,0},{7,1},{8,14},{9,15},{10,... | collective-permute-start | bytes 270344 | tf_op jit(solution)/shard_map/ppermute | solution.py:55
  64.3 0.7 collective-permute-start.15
  65.0 1.5 %collective-permute-start.14 = (bf16[352,128]{1,0:T(8,128)(2,1)S(1)}, bf16[352,128]{1,0:T(8,128)(2,1)S(1)}, u32[]{:S(2)}, u32[]{:S(2)}) collective-permute-start(bf16[352,128]{1,0:T(8,128)(2,1)S(1)} %shard_map.135), channel_id=1, source_target_pairs={{0,2},{1,3},{2,0},{3,1},{4,6},{5,7},{6,4},{7,5},{8,10},{9,11},{10,... | collective-permute-start | bytes 270344 | tf_op jit(solution)/shard_map/ppermute | solution.py:55
  66.5 3.4 %collective-permute-done.18 = bf16[352,128]{1,0:T(8,128)(2,1)S(1)} collective-permute-done((bf16[352,128]{1,0:T(8,128)(2,1)S(1)}, bf16[352,128]{1,0:T(8,128)(2,1)S(1)}, u32[]{:S(2)}, u32[]{:S(2)}) %collective-permute-start.18) | collective-permute-done | bytes 90144 | tf_op jit(solution)/shard_map/ppermute | solution.py:55
  69.9 0.4 collective-permute-start.21
  70.3 1.8 %collective-permute-start.20 = (bf16[3,352,128]{2,1,0:T(8,128)(2,1)S(1)}, bf16[3,352,128]{2,1,0:T(8,128)(2,1)S(1)}, u32[]{:S(2)}, u32[]{:S(2)}) collective-permute-start(bf16[3,352,128]{2,1,0:T(8,128)(2,1)S(1)} %pad_maximum_fusion.1), channel_id=1, source_target_pairs={{0,2},{1,3},{2,0},{3,1},{4,6},{5,7},{6,4},{7,5},{8,10},{9,11},{10,... | collective-permute-start | bytes 811016 | tf_op jit(solution)/shard_map/ppermute | solution.py:55
  72.1 1.1 %fusion.3 = bf16[2,16,16,256]{3,2,1,0:T(8,128)(2,1)} fusion(f32[2,16,16,256]{3,2,1,0:T(8,128)S(1)} %convolution_add_fusion.9, bf16[2,16,16,512]{3,2,1,0:T(8,128)(2,1)S(1)} %copy-done.2, bf16[2,16,16,256]{3,2,1,0:T(8,128)(2,1)S(1)} %bitcast.123, bf16[2,16,16,256]{3,2,1,0:T(8,128)(2,1)S(1)} %copy-done.7, bf16[3,3,256,512]{3,2,1,0:T(8,128)(2,1)S(1)} %copy-done.6), kind=kOutput, calls=%fused_computation.28 | convolution fusion | flops 135135232 | bytes 2097152 | tf_op jit(solution)/shard_map/nhwo,co->nhwc/dot_general | solution.py:576
  73.2 4.3 %collective-permute-done.21 = bf16[3,352,128]{2,1,0:T(8,128)(2,1)S(1)} collective-permute-done((bf16[3,352,128]{2,1,0:T(8,128)(2,1)S(1)}, bf16[3,352,128]{2,1,0:T(8,128)(2,1)S(1)}, u32[]{:S(2)}, u32[]{:S(2)}) %collective-permute-start.21) | collective-permute-done | bytes 270368 | tf_op jit(solution)/shard_map/ppermute | solution.py:55
  78.0 1.6 %collective-permute-start.23 = (bf16[528,128]{1,0:T(8,128)(2,1)S(1)}, bf16[528,128]{1,0:T(8,128)(2,1)S(1)}, u32[]{:S(2)}, u32[]{:S(2)}) collective-permute-start(bf16[528,128]{1,0:T(8,128)(2,1)S(1)} %slice.125), channel_id=1, source_target_pairs={{0,4},{1,5},{2,6},{3,7},{4,0},{5,1},{6,2},{7,3},{8,12},{9,13},{10,... | collective-permute-start | bytes 405512 | tf_op jit(solution)/shard_map/ppermute | solution.py:55
  79.5 0.7 collective-permute-start.22
  80.3 3.7 %collective-permute-done.23 = bf16[528,128]{1,0:T(8,128)(2,1)S(1)} collective-permute-done((bf16[528,128]{1,0:T(8,128)(2,1)S(1)}, bf16[528,128]{1,0:T(8,128)(2,1)S(1)}, u32[]{:S(2)}, u32[]{:S(2)}) %collective-permute-start.23) | collective-permute-done | bytes 135200 | tf_op jit(solution)/shard_map/ppermute | solution.py:55
  84.0 1.2 %collective-permute-done.22 = bf16[528,128]{1,0:T(8,128)(2,1)S(1)} collective-permute-done((bf16[528,128]{1,0:T(8,128)(2,1)S(1)}, bf16[528,128]{1,0:T(8,128)(2,1)S(1)}, u32[]{:S(2)}, u32[]{:S(2)}) %collective-permute-start.22) | collective-permute-done | bytes 135200 | tf_op jit(solution)/shard_map/ppermute | solution.py:55
  85.4 1.5 %collective-permute-done.26.refs_5_ = bf16[3,352,128]{2,1,0:T(8,128)(2,1)S(1)} collective-permute-done((bf16[3,352,128]{2,1,0:T(8,128)(2,1)S(1)}, bf16[3,352,128]{2,1,0:T(8,128)(2,1)S(1)}, u32[]{:S(2)}, u32[]{:S(2)}) %collective-permute-start.26) | collective-permute-done | bytes 270368 | tf_op jit(solution)/shard_map/ppermute | solution.py:55
  86.9 3.7 %shard_map.136 = (f32[9,256,512]{2,1,0:T(8,128)}, f32[768,256]{1,0:T(8,128)}, f32[1,512]{1,0:T(1,128)}) custom-call(s32[2]{0:T(128)S(1)} %pad_add_fusion.place_ref, bf16[4,352,128]{2,1,0:T(8,128)(2,1)S(1)} %pad_maximum_fusion.refs_0_, bf16[9,352,128]{2,1,0:T(8,128)(2,1)S(1)} %constant_dynamic-update-slice_fusion.refs_1_, bf16[3,352,128]{2,1,0:T(8,128)(2,1)S(1)} %bitcast.112, ...), custom_call_target="tpu_custom_call" | custom-call | tf_op jit(solution)/shard_map/pallas_call | solution.py:499
  (52 shorter events, 1.3 us)
Async XLA Ops:
  0.6 16.3 %copy-start = (bf16[768,256]{1,0:T(8,128)(2,1)S(1)}, bf16[768,256]{1,0:T(8,128)(2,1)}, u32[]{:S(2)}) copy-start(bf16[768,256]{1,0:T(8,128)(2,1)} %param.10) | copy-start | bytes 1179652
  2.9 20.5 %all-to-all-start = ((f32[32,8,384]{2,1,0:T(8,128)}), f32[32,8,384]{2,1,0:T(8,128)S(1)}, u32[]{:S(2)}, u32[]{:S(2)}) async-start(f32[32,8,384]{2,1,0:T(8,128)} %get-tuple-element.40), calls=%async_computation | async-start | bytes 786432 | tf_op jit(solution)/shard_map/all_to_all | solution.py:89
  10.2 1.0 %copy-start.1 = (bf16[2,16,16,512]{3,2,1,0:T(8,128)(2,1)S(1)}, bf16[2,16,16,512]{3,2,1,0:T(8,128)(2,1)}, u32[]{:S(2)}) copy-start(bf16[2,16,16,512]{3,2,1,0:T(8,128)(2,1)} %param.17) | copy-start | bytes 1572868
  11.3 0.7 copy-start.4
  12.0 15.3 %copy-start.2 = (bf16[2,16,16,512]{3,2,1,0:T(8,128)(2,1)S(1)}, bf16[2,16,16,512]{3,2,1,0:T(8,128)(2,1)}, u32[]{:S(2)}) copy-start(bf16[2,16,16,512]{3,2,1,0:T(8,128)(2,1)} %param.17) | copy-start | bytes 1572868
  12.7 18.3 %collective-permute-start.2 = (bf16[528,256]{1,0:T(8,128)(2,1)}, bf16[528,256]{1,0:T(8,128)(2,1)S(1)}, u32[]{:S(2)}, u32[]{:S(2)}) collective-permute-start(bf16[528,256]{1,0:T(8,128)(2,1)} %get-tuple-element.43), channel_id=1, source_target_pairs={{0,6},{1,7},{2,4},{3,5},{4,2},{5,3},{6,0},{7,1},{8,14},{9,15},{10,... | collective-permute-start | bytes 811016 | tf_op jit(solution)/shard_map/ppermute | solution.py:55
  15.4 15.7 %collective-permute-start.1 = (bf16[528,256]{1,0:T(8,128)(2,1)}, bf16[528,256]{1,0:T(8,128)(2,1)S(1)}, u32[]{:S(2)}, u32[]{:S(2)}) collective-permute-start(bf16[528,256]{1,0:T(8,128)(2,1)} %get-tuple-element.43), channel_id=1, source_target_pairs={{0,4},{1,5},{2,6},{3,7},{4,0},{5,1},{6,2},{7,3},{8,12},{9,13},{10,... | collective-permute-start | bytes 811016 | tf_op jit(solution)/shard_map/ppermute | solution.py:55
  16.0 15.1 %collective-permute-start = (bf16[528,256]{1,0:T(8,128)(2,1)S(1)}, bf16[528,256]{1,0:T(8,128)(2,1)S(1)}, u32[]{:S(2)}, u32[]{:S(2)}) collective-permute-start(bf16[528,256]{1,0:T(8,128)(2,1)S(1)} %get-tuple-element.44.refs_0_), channel_id=1, source_target_pairs={{0,2},{1,3},{2,0},{3,1},{4,6},{5,7},{6,4},{7,5},{8,10},{9,11},{10,... | collective-permute-start | bytes 811016 | tf_op jit(solution)/shard_map/ppermute | solution.py:55
  24.6 15.8 %all-to-all-start.1 = ((bf16[32,16,384]{2,1,0:T(8,128)(2,1)}), bf16[32,16,384]{2,1,0:T(8,128)(2,1)S(1)}, u32[]{:S(2)}, u32[]{:S(2)}) async-start(bf16[32,16,384]{2,1,0:T(8,128)(2,1)} %shard_map.129), calls=%async_computation.1 | async-start | bytes 786432 | tf_op jit(solution)/shard_map/all_to_all | solution.py:89
  27.2 2.7 %copy-start.5 = (bf16[3,3,256,512]{3,2,1,0:T(8,128)(2,1)S(1)}, bf16[3,3,256,512]{3,2,1,0:T(8,128)(2,1)}, u32[]{:S(2)}) copy-start(bf16[3,3,256,512]{3,2,1,0:T(8,128)(2,1)} %param.15) | copy-start | bytes 7077892
  30.0 2.2 %copy-start.3 = (bf16[784,768]{1,0:T(8,128)(2,1)S(1)}, bf16[784,768]{1,0:T(8,128)(2,1)}, u32[]{:S(2)}) copy-start(bf16[784,768]{1,0:T(8,128)(2,1)} %book_ref.1) | copy-start | bytes 3612676
  31.1 9.4 %collective-permute-start.3 = (bf16[528,256]{1,0:T(8,128)(2,1)S(1)}, bf16[528,256]{1,0:T(8,128)(2,1)}, u32[]{:S(2)}, u32[]{:S(2)}) collective-permute-start(bf16[528,256]{1,0:T(8,128)(2,1)S(1)} %get-tuple-element.44.refs_0_), channel_id=1, source_target_pairs={{0,1},{1,0},{2,3},{3,2},{4,5},{5,4},{6,7},{7,6},{8,9},{9,8},{10,11... | collective-permute-start | bytes 811016 | tf_op jit(solution)/shard_map/ppermute | solution.py:55
  31.4 10.1 %collective-permute-start.4 = (bf16[528,256]{1,0:T(8,128)(2,1)S(1)}, bf16[528,256]{1,0:T(8,128)(2,1)}, u32[]{:S(2)}, u32[]{:S(2)}) collective-permute-start(bf16[528,256]{1,0:T(8,128)(2,1)S(1)} %collective-permute-done.refs_1_), channel_id=1, source_target_pairs={{0,1},{1,0},{2,3},{3,2},{4,5},{5,4},{6,7},{7,6},{8,9},{9,8},{10,11... | collective-permute-start | bytes 811016 | tf_op jit(solution)/shard_map/ppermute | solution.py:55
  31.6 10.8 %collective-permute-start.5 = (bf16[528,256]{1,0:T(8,128)(2,1)S(1)}, bf16[528,256]{1,0:T(8,128)(2,1)}, u32[]{:S(2)}, u32[]{:S(2)}) collective-permute-start(bf16[528,256]{1,0:T(8,128)(2,1)S(1)} %collective-permute-done.1.refs_2_), channel_id=1, source_target_pairs={{0,1},{1,0},{2,3},{3,2},{4,5},{5,4},{6,7},{7,6},{8,9},{9,8},{10,11... | collective-permute-start | bytes 811016 | tf_op jit(solution)/shard_map/ppermute | solution.py:55
  31.9 10.5 %collective-permute-start.6 = (bf16[528,256]{1,0:T(8,128)(2,1)S(1)}, bf16[528,256]{1,0:T(8,128)(2,1)}, u32[]{:S(2)}, u32[]{:S(2)}) collective-permute-start(bf16[528,256]{1,0:T(8,128)(2,1)S(1)} %collective-permute-done.2.refs_3_), channel_id=1, source_target_pairs={{0,1},{1,0},{2,3},{3,2},{4,5},{5,4},{6,7},{7,6},{8,9},{9,8},{10,11... | collective-permute-start | bytes 811016 | tf_op jit(solution)/shard_map/ppermute | solution.py:55
  33.9 1.8 %collective-permute-start.7 = (f32[768,128]{1,0:T(8,128)S(1)}, f32[768,128]{1,0:T(8,128)S(1)}, u32[]{:S(2)}, u32[]{:S(2)}) collective-permute-start(f32[768,128]{1,0:T(8,128)S(1)} %get-tuple-element.50), channel_id=1, source_target_pairs={{0,1},{1,0},{2,3},{3,2},{4,5},{5,4},{6,7},{7,6},{8,9},{9,8},{10,11... | collective-permute-start | bytes 1179656 | tf_op jit(solution)/shard_map/ppermute | solution.py:55
  36.3 11.2 %collective-permute-start.8 = (bf16[4,48,128]{2,1,0:T(8,128)(2,1)S(1)}, bf16[4,48,128]{2,1,0:T(8,128)(2,1)S(1)}, u32[]{:S(2)}, u32[]{:S(2)}) collective-permute-start(bf16[4,48,128]{2,1,0:T(8,128)(2,1)S(1)} %get-tuple-element.52), channel_id=1, source_target_pairs={{0,2},{1,3},{2,0},{3,1},{4,6},{5,7},{6,4},{7,5},{8,10},{9,11},{10,... | collective-permute-start | bytes 147464 | tf_op jit(solution)/shard_map/ppermute | solution.py:55
  40.4 7.1 %collective-permute-start.9 = (bf16[4,48,128]{2,1,0:T(8,128)(2,1)S(1)}, bf16[4,48,128]{2,1,0:T(8,128)(2,1)S(1)}, u32[]{:S(2)}, u32[]{:S(2)}) collective-permute-start(bf16[4,48,128]{2,1,0:T(8,128)(2,1)S(1)} %get-tuple-element.53), channel_id=1, source_target_pairs={{0,4},{1,5},{2,6},{3,7},{4,0},{5,1},{6,2},{7,3},{8,12},{9,13},{10,... | collective-permute-start | bytes 147464 | tf_op jit(solution)/shard_map/ppermute | solution.py:55
  41.5 10.7 %copy-start.8 = (s32[1,512]{1,0:T(1,128)S(1)}, s32[1,512]{1,0:T(1,128)}, u32[]{:S(2)}) copy-start(s32[1,512]{1,0:T(1,128)} %get-tuple-element.63) | copy-start | bytes 6148
  41.5 11.0 %copy-start.6 = (bf16[3,3,256,512]{3,2,1,0:T(8,128)(2,1)S(1)}, bf16[3,3,256,512]{3,2,1,0:T(8,128)(2,1)}, u32[]{:S(2)}) copy-start(bf16[3,3,256,512]{3,2,1,0:T(8,128)(2,1)} %param.15) | copy-start | bytes 7077892
  41.5 6.0 %collective-permute-start.10 = (bf16[4,48,128]{2,1,0:T(8,128)(2,1)S(1)}, bf16[4,48,128]{2,1,0:T(8,128)(2,1)S(1)}, u32[]{:S(2)}, u32[]{:S(2)}) collective-permute-start(bf16[4,48,128]{2,1,0:T(8,128)(2,1)S(1)} %get-tuple-element.54), channel_id=1, source_target_pairs={{0,6},{1,7},{2,4},{3,5},{4,2},{5,3},{6,0},{7,1},{8,14},{9,15},{10,... | collective-permute-start | bytes 147464 | tf_op jit(solution)/shard_map/ppermute | solution.py:55
  48.1 7.4 %collective-permute-start.11 = (bf16[352,128]{1,0:T(8,128)(2,1)S(1)}, bf16[352,128]{1,0:T(8,128)(2,1)S(1)}, u32[]{:S(2)}, u32[]{:S(2)}) collective-permute-start(bf16[352,128]{1,0:T(8,128)(2,1)S(1)} %get-tuple-element.60), channel_id=1, source_target_pairs={{0,8},{1,9},{2,10},{3,11},{4,12},{5,13},{6,14},{7,15},{8,16},{9,17... | collective-permute-start | bytes 270344 | tf_op jit(solution)/shard_map/ppermute | solution.py:55
  48.9 9.5 %collective-permute-start.12 = (bf16[352,128]{1,0:T(8,128)(2,1)S(1)}, bf16[352,128]{1,0:T(8,128)(2,1)S(1)}, u32[]{:S(2)}, u32[]{:S(2)}) collective-permute-start(bf16[352,128]{1,0:T(8,128)(2,1)S(1)} %get-tuple-element.61), channel_id=1, source_target_pairs={{0,16},{1,17},{2,18},{3,19},{4,20},{5,21},{6,22},{7,23},{8,24},{9,... | collective-permute-start | bytes 270344 | tf_op jit(solution)/shard_map/ppermute | solution.py:55
  50.2 8.2 %collective-permute-start.13 = (bf16[352,128]{1,0:T(8,128)(2,1)S(1)}, bf16[352,128]{1,0:T(8,128)(2,1)S(1)}, u32[]{:S(2)}, u32[]{:S(2)}) collective-permute-start(bf16[352,128]{1,0:T(8,128)(2,1)S(1)} %get-tuple-element.62), channel_id=1, source_target_pairs={{0,24},{1,25},{2,26},{3,27},{4,28},{5,29},{6,30},{7,31},{8,0},{9,1... | collective-permute-start | bytes 270344 | tf_op jit(solution)/shard_map/ppermute | solution.py:55
  54.6 17.5 %copy-start.7 = (bf16[2,16,16,256]{3,2,1,0:T(8,128)(2,1)S(1)}, bf16[2,16,16,256]{3,2,1,0:T(8,128)(2,1)}, u32[]{:S(2)}) copy-start(bf16[2,16,16,256]{3,2,1,0:T(8,128)(2,1)} %param.11) | copy-start | bytes 786436
  58.5 6.5 %collective-permute-start.19 = (bf16[352,128]{1,0:T(8,128)(2,1)S(1)}, bf16[352,128]{1,0:T(8,128)(2,1)S(1)}, u32[]{:S(2)}, u32[]{:S(2)}) collective-permute-start(bf16[352,128]{1,0:T(8,128)(2,1)S(1)} %shard_map.135), channel_id=1, source_target_pairs={{0,24},{1,25},{2,26},{3,27},{4,28},{5,29},{6,30},{7,31},{8,0},{9,1... | collective-permute-start | bytes 270344 | tf_op jit(solution)/shard_map/ppermute | solution.py:55
  60.6 9.3 %collective-permute-start.18 = (bf16[352,128]{1,0:T(8,128)(2,1)S(1)}, bf16[352,128]{1,0:T(8,128)(2,1)S(1)}, u32[]{:S(2)}, u32[]{:S(2)}) collective-permute-start(bf16[352,128]{1,0:T(8,128)(2,1)S(1)} %shard_map.135), channel_id=1, source_target_pairs={{0,16},{1,17},{2,18},{3,19},{4,20},{5,21},{6,22},{7,23},{8,24},{9,... | collective-permute-start | bytes 270344 | tf_op jit(solution)/shard_map/ppermute | solution.py:55
  61.9 8.0 %collective-permute-start.17 = (bf16[352,128]{1,0:T(8,128)(2,1)S(1)}, bf16[352,128]{1,0:T(8,128)(2,1)S(1)}, u32[]{:S(2)}, u32[]{:S(2)}) collective-permute-start(bf16[352,128]{1,0:T(8,128)(2,1)S(1)} %shard_map.135), channel_id=1, source_target_pairs={{0,8},{1,9},{2,10},{3,11},{4,12},{5,13},{6,14},{7,15},{8,16},{9,17... | collective-permute-start | bytes 270344 | tf_op jit(solution)/shard_map/ppermute | solution.py:55
  63.0 10.2 %collective-permute-start.16 = (bf16[352,128]{1,0:T(8,128)(2,1)S(1)}, bf16[352,128]{1,0:T(8,128)(2,1)S(1)}, u32[]{:S(2)}, u32[]{:S(2)}) collective-permute-start(bf16[352,128]{1,0:T(8,128)(2,1)S(1)} %shard_map.135), channel_id=1, source_target_pairs={{0,6},{1,7},{2,4},{3,5},{4,2},{5,3},{6,0},{7,1},{8,14},{9,15},{10,... | collective-permute-start | bytes 270344 | tf_op jit(solution)/shard_map/ppermute | solution.py:55
  64.3 8.9 %collective-permute-start.15 = (bf16[352,128]{1,0:T(8,128)(2,1)S(1)}, bf16[352,128]{1,0:T(8,128)(2,1)S(1)}, u32[]{:S(2)}, u32[]{:S(2)}) collective-permute-start(bf16[352,128]{1,0:T(8,128)(2,1)S(1)} %shard_map.135), channel_id=1, source_target_pairs={{0,4},{1,5},{2,6},{3,7},{4,0},{5,1},{6,2},{7,3},{8,12},{9,13},{10,... | collective-permute-start | bytes 270344 | tf_op jit(solution)/shard_map/ppermute | solution.py:55
  65.0 8.2 %collective-permute-start.14 = (bf16[352,128]{1,0:T(8,128)(2,1)S(1)}, bf16[352,128]{1,0:T(8,128)(2,1)S(1)}, u32[]{:S(2)}, u32[]{:S(2)}) collective-permute-start(bf16[352,128]{1,0:T(8,128)(2,1)S(1)} %shard_map.135), channel_id=1, source_target_pairs={{0,2},{1,3},{2,0},{3,1},{4,6},{5,7},{6,4},{7,5},{8,10},{9,11},{10,... | collective-permute-start | bytes 270344 | tf_op jit(solution)/shard_map/ppermute | solution.py:55
  69.9 7.6 %collective-permute-start.21 = (bf16[3,352,128]{2,1,0:T(8,128)(2,1)S(1)}, bf16[3,352,128]{2,1,0:T(8,128)(2,1)S(1)}, u32[]{:S(2)}, u32[]{:S(2)}) collective-permute-start(bf16[3,352,128]{2,1,0:T(8,128)(2,1)S(1)} %pad_maximum_fusion.1), channel_id=1, source_target_pairs={{0,4},{1,5},{2,6},{3,7},{4,0},{5,1},{6,2},{7,3},{8,12},{9,13},{10,... | collective-permute-start | bytes 811016 | tf_op jit(solution)/shard_map/ppermute | solution.py:55
  70.3 7.4 %collective-permute-start.20 = (bf16[3,352,128]{2,1,0:T(8,128)(2,1)S(1)}, bf16[3,352,128]{2,1,0:T(8,128)(2,1)S(1)}, u32[]{:S(2)}, u32[]{:S(2)}) collective-permute-start(bf16[3,352,128]{2,1,0:T(8,128)(2,1)S(1)} %pad_maximum_fusion.1), channel_id=1, source_target_pairs={{0,2},{1,3},{2,0},{3,1},{4,6},{5,7},{6,4},{7,5},{8,10},{9,11},{10,... | collective-permute-start | bytes 811016 | tf_op jit(solution)/shard_map/ppermute | solution.py:55
  77.8 9.0 %collective-permute-start.25 = (bf16[9,352,128]{2,1,0:T(8,128)(2,1)S(1)}, bf16[9,352,128]{2,1,0:T(8,128)(2,1)S(1)}, u32[]{:S(2)}, u32[]{:S(2)}) collective-permute-start(bf16[9,352,128]{2,1,0:T(8,128)(2,1)S(1)} %constant_dynamic-update-slice_fusion.refs_1_), channel_id=1, source_target_pairs={{0,1},{1,0},{2,3},{3,2},{4,5},{5,4},{6,7},{7,6},{8,9},{9,8},{10,11... | collective-permute-start | bytes 2433032 | tf_op jit(solution)/shard_map/ppermute | solution.py:55
  78.0 6.0 %collective-permute-start.23 = (bf16[528,128]{1,0:T(8,128)(2,1)S(1)}, bf16[528,128]{1,0:T(8,128)(2,1)S(1)}, u32[]{:S(2)}, u32[]{:S(2)}) collective-permute-start(bf16[528,128]{1,0:T(8,128)(2,1)S(1)} %slice.125), channel_id=1, source_target_pairs={{0,4},{1,5},{2,6},{3,7},{4,0},{5,1},{6,2},{7,3},{8,12},{9,13},{10,... | collective-permute-start | bytes 405512 | tf_op jit(solution)/shard_map/ppermute | solution.py:55
  79.5 5.7 %collective-permute-start.22 = (bf16[528,128]{1,0:T(8,128)(2,1)S(1)}, bf16[528,128]{1,0:T(8,128)(2,1)S(1)}, u32[]{:S(2)}, u32[]{:S(2)}) collective-permute-start(bf16[528,128]{1,0:T(8,128)(2,1)S(1)} %slice.124), channel_id=1, source_target_pairs={{0,2},{1,3},{2,0},{3,1},{4,6},{5,7},{6,4},{7,5},{8,10},{9,11},{10,... | collective-permute-start | bytes 405512 | tf_op jit(solution)/shard_map/ppermute | solution.py:55
  80.3 5.1 %collective-permute-start.24 = (bf16[4,352,128]{2,1,0:T(8,128)(2,1)S(1)}, bf16[4,352,128]{2,1,0:T(8,128)(2,1)S(1)}, u32[]{:S(2)}, u32[]{:S(2)}) collective-permute-start(bf16[4,352,128]{2,1,0:T(8,128)(2,1)S(1)} %pad_maximum_fusion.refs_0_), channel_id=1, source_target_pairs={{0,1},{1,0},{2,3},{3,2},{4,5},{5,4},{6,7},{7,6},{8,9},{9,8},{10,11... | collective-permute-start | bytes 1081352 | tf_op jit(solution)/shard_map/ppermute | solution.py:55
  85.3 1.6 %collective-permute-start.26 = (bf16[3,352,128]{2,1,0:T(8,128)(2,1)S(1)}, bf16[3,352,128]{2,1,0:T(8,128)(2,1)S(1)}, u32[]{:S(2)}, u32[]{:S(2)}) collective-permute-start(bf16[3,352,128]{2,1,0:T(8,128)(2,1)S(1)} %bitcast.111), channel_id=1, source_target_pairs={{0,1},{1,0},{2,3},{3,2},{4,5},{5,4},{6,7},{7,6},{8,9},{9,8},{10,11... | collective-permute-start | bytes 811016 | tf_op jit(solution)/shard_map/ppermute | solution.py:55

commit v8 on v7

--- a/solution.py
+++ b/solution.py
@@ -542,9 +542,10 @@
     onehot = (slot.reshape(tokens, 1) == slot_ids[None, :]).astype(jnp.bfloat16)
     replies = answer(grid, asked, local_codes)
     got = spread(replies, grid)
-    asked, _, *cots = lax.optimization_barrier((asked, replies, *cots))
+    asked, _ = lax.optimization_barrier((asked, replies))
+    kept, sent = proj_part(place, asked, codebook, local_codes)
+    kept, sent, *cots = lax.optimization_barrier((kept, sent, *cots))
     cots = cots + [send(x, grid.flip(1)) for x in cots]
-    kept, sent = proj_part(place, asked, codebook, local_codes)
     proj = proj_split(place, kept, send(sent, grid.flip(1)))
     cotangent, _ = lax.optimization_barrier((cotangent, replies))
     gains = [send(x, grid.flip(bits)) for x, bits in zip(proj[1:], (2, 4, 6))]

time: 91.1 us -> 91.1 us (level)
  no operation moved by 1% of the time
where the time goes in v8:
time: 91.1 us; the launch traced here: 90.6 us
  starting transfers between devices  34 us (37%)
  waiting for transfers between devices  25.4 us (28%)
  Pallas kernels  16 us (18%)
  matrix products  11.4 us (13%)
  local copies, waits for them, and re-layouts  1.92 us (2%)
  between operations  1.04 us (1%)
    ppermute x27, starting transfers between devices, send(): return lax.ppermute(x, AXES, perm)  24.1 us
    ppermute x27, waiting for transfers between devices, send(): return lax.ppermute(x, AXES, perm)  19 us
    all_to_all x2, starting transfers between devices, spread(): return lax.all_to_all(x, AXES, split_axis=0, concat_axis=0, tiled=True)  9.92 us
    all_to_all x2, waiting for transfers between devices, spread(): return lax.all_to_all(x, AXES, split_axis=0, concat_axis=0, tiled=True)  6.37 us
    dot_general x9, matrix products, on_device(): jnp.einsum('nhwo,co->nhwc', grad_window, kernel[row_off, col_off], prefer...  5.92 us
    pallas_call x1, Pallas kernels, group_weights(): pl.pallas_call(functools.partial(weights_kernel, grid, cap), out_shape=ja...  5.03 us
    pallas_call x1, Pallas kernels, finish(): pl.pallas_call(functools.partial(finish_kernel, krows, counts), out_shape...  3.71 us
    dot_general x9, matrix products, on_device(): jnp.einsum('nhwc,co->nhwo', window, kernel[row_off, col_off], preferred_e...  3.49 us
  transfers between devices with their start and end apart: 29, of which 11 were waited for; matrix products, arithmetic and copies ran while one was open for 14% of the time, Pallas kernels for 10%

profile of v8, /device:TPU:0, one launch (start us, length us, event | category | flops | bytes accessed | tf_op | source)
XLA Modules:
  0.0 90.6 jit_solution(2058107459834789025)
XLA Ops:
  0.6 2.2 %shard_map.128 = (s32[1,512]{1,0:T(1,128)}, f32[8,512]{1,0:T(8,128)}, f32[32,8,384]{2,1,0:T(8,128)}) custom-call(s32[32,16]{1,0:T(8,128)} %bitcast.133, s32[1,32]{1,0:T(1,128)} %counts_hbm.1, s32[8,32]{1,0:T(8,128)} %bitcast.134, bf16[512,256]{1,0:T(8,128)(2,1)} %bitcast.124), custom_call_target="tpu_custom_call" | custom-call | flops 67108864 | bytes 2097152 | tf_op jit(solution)/shard_map/pallas_call | solution.py:163
  2.9 7.3 %all-to-all-start = ((f32[32,8,384]{2,1,0:T(8,128)}), f32[32,8,384]{2,1,0:T(8,128)S(1)}, u32[]{:S(2)}, u32[]{:S(2)}) async-start(f32[32,8,384]{2,1,0:T(8,128)} %get-tuple-element.42), calls=%async_computation | async-start | bytes 786432 | tf_op jit(solution)/shard_map/all_to_all | solution.py:89
  10.2 1.0 %copy-done.1 = bf16[2,16,16,512]{3,2,1,0:T(8,128)(2,1)S(1)} copy-done((bf16[2,16,16,512]{3,2,1,0:T(8,128)(2,1)S(1)}, bf16[2,16,16,512]{3,2,1,0:T(8,128)(2,1)}, u32[]{:S(2)}) %copy-start.1) | copy-done | bytes 524312
  11.3 0.7 copy-done.4
  12.0 0.7 shard_map.131
  12.7 2.7 %collective-permute-start.2 = (bf16[528,256]{1,0:T(8,128)(2,1)}, bf16[528,256]{1,0:T(8,128)(2,1)S(1)}, u32[]{:S(2)}, u32[]{:S(2)}) collective-permute-start(bf16[528,256]{1,0:T(8,128)(2,1)} %get-tuple-element.48), channel_id=1, source_target_pairs={{0,6},{1,7},{2,4},{3,5},{4,2},{5,3},{6,0},{7,1},{8,14},{9,15},{10,... | collective-permute-start | bytes 811016 | tf_op jit(solution)/shard_map/ppermute | solution.py:55
  15.4 0.6 collective-permute-start.1
  16.0 0.3 collective-permute-start
  16.2 0.7 convert_element_type.28
  17.0 1.8 %convolution_convert_fusion.codes_ref = bf16[784,256]{1,0:T(8,128)(2,1)S(1)} fusion(bf16[784,768]{1,0:T(8,128)(2,1)} %book_ref.1, bf16[768,256]{1,0:T(8,128)(2,1)S(1)} %copy-done), kind=kOutput, calls=%fused_computation.18 | convolution fusion | flops 308482048 | bytes 1998848 | tf_op jit(solution)/shard_map/dot_general | solution.py:538
  18.7 4.7 %all-to-all-done.asked_ref = f32[32,8,384]{2,1,0:T(8,128)S(1)} async-done(((f32[32,8,384]{2,1,0:T(8,128)}), f32[32,8,384]{2,1,0:T(8,128)S(1)}, u32[]{:S(2)}, u32[]{:S(2)}) %all-to-all-start) | async-done | bytes 393248 | tf_op jit(solution)/shard_map/all_to_all | solution.py:89
  23.4 1.2 %shard_map.129 = bf16[32,16,384]{2,1,0:T(8,128)(2,1)} custom-call(f32[32,8,384]{2,1,0:T(8,128)S(1)} %all-to-all-done.asked_ref, bf16[784,256]{1,0:T(8,128)(2,1)S(1)} %convolution_convert_fusion.codes_ref), custom_call_target="tpu_custom_call" | custom-call | flops 102760448 | bytes 2097152 | tf_op jit(solution)/shard_map/pallas_call | solution.py:243
  24.6 2.6 %all-to-all-start.1 = ((bf16[32,16,384]{2,1,0:T(8,128)(2,1)}), bf16[32,16,384]{2,1,0:T(8,128)(2,1)S(1)}, u32[]{:S(2)}, u32[]{:S(2)}) async-start(bf16[32,16,384]{2,1,0:T(8,128)(2,1)} %shard_map.129), calls=%async_computation.1 | async-start | bytes 786432 | tf_op jit(solution)/shard_map/all_to_all | solution.py:89
  27.2 1.4 %fusion.4 = f32[2,16,16,256]{3,2,1,0:T(8,128)S(1)} fusion(bf16[2,16,16,512]{3,2,1,0:T(8,128)(2,1)S(1)} %copy-done.2, bf16[3,3,256,512]{3,2,1,0:T(8,128)(2,1)} %param.15), kind=kOutput, calls=%fused_computation.38 | convolution fusion | flops 134217728 | bytes 1310720 | tf_op jit(solution)/shard_map/nhwo,co->nhwc/dot_general | solution.py:577
  28.7 1.4 %convolution_add_fusion.15 = f32[2,16,16,256]{3,2,1,0:T(8,128)S(1)} fusion(f32[2,16,16,256]{3,2,1,0:T(8,128)S(1)} %fusion.4, bf16[2,16,16,512]{3,2,1,0:T(8,128)(2,1)S(1)} %copy-done.2, bf16[3,3,256,512]{3,2,1,0:T(8,128)(2,1)} %param.15), kind=kOutput, calls=%fused_computation.27 | convolution fusion | flops 134348800 | bytes 1835008 | tf_op jit(solution)/shard_map/nhwo,co->nhwc/dot_general | solution.py:577
  30.1 0.3 convolution_add_fusion.14
  30.5 0.3 convolution_add_fusion.13
  30.8 1.7 %shard_map.130 = (f32[768,128]{1,0:T(8,128)S(1)}, f32[768,128]{1,0:T(8,128)S(1)}) custom-call(s32[2]{0:T(128)S(1)} %pad_add_fusion.place_ref, f32[32,8,384]{2,1,0:T(8,128)S(1)} %all-to-all-done.asked_ref, bf16[784,768]{1,0:T(8,128)(2,1)S(1)} %copy-done.3, bf16[784,256]{1,0:T(8,128)(2,1)S(1)} %convolution_convert_fusion.codes_ref), custom_call_target="tpu_custom_call" | custom-call | flops 509607936 | bytes 4194304 | tf_op jit(solution)/shard_map/pallas_call | solution.py:275
  32.6 0.3 convolution_add_fusion.12
  32.9 0.3 collective-permute-start.3
  33.2 0.3 collective-permute-start.4
  33.7 0.3 collective-permute-start.6
  34.2 0.3 convolution_add_fusion.11
  34.6 0.4 convolution_add_fusion.10
  35.0 0.3 convolution_add_fusion.9
  35.3 1.0 %collective-permute-done.7.got_ref = f32[768,128]{1,0:T(8,128)S(1)} collective-permute-done((f32[768,128]{1,0:T(8,128)S(1)}, f32[768,128]{1,0:T(8,128)S(1)}, u32[]{:S(2)}, u32[]{:S(2)}) %collective-permute-start.7) | collective-permute-done | bytes 393248 | tf_op jit(solution)/shard_map/ppermute | solution.py:55
  36.3 0.6 shard_map.133
  36.9 1.8 %collective-permute-start.8 = (bf16[4,48,128]{2,1,0:T(8,128)(2,1)S(1)}, bf16[4,48,128]{2,1,0:T(8,128)(2,1)S(1)}, u32[]{:S(2)}, u32[]{:S(2)}) collective-permute-start(bf16[4,48,128]{2,1,0:T(8,128)(2,1)S(1)} %get-tuple-element.56), channel_id=1, source_target_pairs={{0,2},{1,3},{2,0},{3,1},{4,6},{5,7},{6,4},{7,5},{8,10},{9,11},{10,... | collective-permute-start | bytes 147464 | tf_op jit(solution)/shard_map/ppermute | solution.py:55
  38.7 1.7 %all-to-all-done.1.got_ref = bf16[32,16,384]{2,1,0:T(8,128)(2,1)S(1)} async-done(((bf16[32,16,384]{2,1,0:T(8,128)(2,1)}), bf16[32,16,384]{2,1,0:T(8,128)(2,1)S(1)}, u32[]{:S(2)}, u32[]{:S(2)}) %all-to-all-start.1) | async-done | bytes 393248 | tf_op jit(solution)/shard_map/all_to_all | solution.py:89
  40.4 1.2 %collective-permute-start.9 = (bf16[4,48,128]{2,1,0:T(8,128)(2,1)S(1)}, bf16[4,48,128]{2,1,0:T(8,128)(2,1)S(1)}, u32[]{:S(2)}, u32[]{:S(2)}) collective-permute-start(bf16[4,48,128]{2,1,0:T(8,128)(2,1)S(1)} %get-tuple-element.57), channel_id=1, source_target_pairs={{0,4},{1,5},{2,6},{3,7},{4,0},{5,1},{6,2},{7,3},{8,12},{9,13},{10,... | collective-permute-start | bytes 147464 | tf_op jit(solution)/shard_map/ppermute | solution.py:55
  41.6 0.9 collective-permute-start.10
  42.4 5.0 %shard_map.132.acc_ref = f32[592,256]{1,0:T(8,128)S(1)} custom-call(s32[2]{0:T(128)S(1)} %pad_add_fusion.place_ref, bf16[32,16,384]{2,1,0:T(8,128)(2,1)S(1)} %all-to-all-done.1.got_ref, bf16[528,256]{1,0:T(8,128)(2,1)S(1)} %get-tuple-element.49.refs_0_, bf16[528,256]{1,0:T(8,128)(2,1)S(1)} %collective-permute-done.refs_1_, ...), custom_call_target="tpu_custom_call" | custom-call | flops 1207959552 | bytes 8388608 | tf_op jit(solution)/shard_map/pallas_call | solution.py:387
  47.5 0.6 shard_map.134
  48.1 0.8 collective-permute-start.11
  48.9 1.7 %collective-permute-start.12 = (bf16[352,128]{1,0:T(8,128)(2,1)S(1)}, bf16[352,128]{1,0:T(8,128)(2,1)S(1)}, u32[]{:S(2)}, u32[]{:S(2)}) collective-permute-start(bf16[352,128]{1,0:T(8,128)(2,1)S(1)} %get-tuple-element.65), channel_id=1, source_target_pairs={{0,16},{1,17},{2,18},{3,19},{4,20},{5,21},{6,22},{7,23},{8,24},{9,... | collective-permute-start | bytes 270344 | tf_op jit(solution)/shard_map/ppermute | solution.py:55
  50.7 1.5 %collective-permute-start.13 = (bf16[352,128]{1,0:T(8,128)(2,1)S(1)}, bf16[352,128]{1,0:T(8,128)(2,1)S(1)}, u32[]{:S(2)}, u32[]{:S(2)}) collective-permute-start(bf16[352,128]{1,0:T(8,128)(2,1)S(1)} %get-tuple-element.66), channel_id=1, source_target_pairs={{0,24},{1,25},{2,26},{3,27},{4,28},{5,29},{6,30},{7,31},{8,0},{9,1... | collective-permute-start | bytes 270344 | tf_op jit(solution)/shard_map/ppermute | solution.py:55
  52.2 0.3 convolution_convert_fusion.1
  52.4 0.3 fusion.5
  52.7 0.3 convolution_add_fusion.7
  53.1 0.3 convolution_add_fusion.6
  53.4 0.3 convolution_add_fusion.5
  53.7 0.3 convolution_add_fusion.4
  54.0 0.3 convolution_add_fusion.3
  54.3 0.3 convolution_add_fusion.2
  54.6 0.3 convolution_add_fusion.1
  54.9 0.6 collective-permute-done.11.refs_0_
  55.5 2.9 %collective-permute-done.12.refs_1_ = bf16[352,128]{1,0:T(8,128)(2,1)S(1)} collective-permute-done((bf16[352,128]{1,0:T(8,128)(2,1)S(1)}, bf16[352,128]{1,0:T(8,128)(2,1)S(1)}, u32[]{:S(2)}, u32[]{:S(2)}) %collective-permute-start.12) | collective-permute-done | bytes 90144 | tf_op jit(solution)/shard_map/ppermute | solution.py:55
  58.5 2.1 %collective-permute-start.19 = (bf16[352,128]{1,0:T(8,128)(2,1)S(1)}, bf16[352,128]{1,0:T(8,128)(2,1)S(1)}, u32[]{:S(2)}, u32[]{:S(2)}) collective-permute-start(bf16[352,128]{1,0:T(8,128)(2,1)S(1)} %shard_map.135), channel_id=1, source_target_pairs={{0,24},{1,25},{2,26},{3,27},{4,28},{5,29},{6,30},{7,31},{8,0},{9,1... | collective-permute-start | bytes 270344 | tf_op jit(solution)/shard_map/ppermute | solution.py:55
  60.6 1.3 %collective-permute-start.18 = (bf16[352,128]{1,0:T(8,128)(2,1)S(1)}, bf16[352,128]{1,0:T(8,128)(2,1)S(1)}, u32[]{:S(2)}, u32[]{:S(2)}) collective-permute-start(bf16[352,128]{1,0:T(8,128)(2,1)S(1)} %shard_map.135), channel_id=1, source_target_pairs={{0,16},{1,17},{2,18},{3,19},{4,20},{5,21},{6,22},{7,23},{8,24},{9,... | collective-permute-start | bytes 270344 | tf_op jit(solution)/shard_map/ppermute | solution.py:55
  61.9 1.1 %fusion.1 = bf16[2,16,16,512]{3,2,1,0:T(8,128)(2,1)} fusion(f32[2,16,16,512]{3,2,1,0:T(8,128)S(1)} %convolution_add_fusion.1, f32[512]{0:T(512)S(1)} %convert_element_type.28, bf16[2,16,16,256]{3,2,1,0:T(8,128)(2,1)S(1)} %bitcast.122, bf16[3,3,256,512]{3,2,1,0:T(8,128)(2,1)S(1)} %copy-done.6), kind=kOutput, calls=%fused_computation.17 | convolution fusion | flops 135004160 | bytes 2099200 | tf_op jit(solution)/shard_map/nhwc,co->nhwo/dot_general | solution.py:568
  63.0 1.4 %collective-permute-start.16 = (bf16[352,128]{1,0:T(8,128)(2,1)S(1)}, bf16[352,128]{1,0:T(8,128)(2,1)S(1)}, u32[]{:S(2)}, u32[]{:S(2)}) collective-permute-start(bf16[352,128]{1,0:T(8,128)(2,1)S(1)} %shard_map.135), channel_id=1, source_target_pairs={{0,6},{1,7},{2,4},{3,5},{4,2},{5,3},{6,0},{7,1},{8,14},{9,15},{10,... | collective-permute-start | bytes 270344 | tf_op jit(solution)/shard_map/ppermute | solution.py:55
  64.4 0.6 collective-permute-start.15
  65.0 1.5 %collective-permute-start.14 = (bf16[352,128]{1,0:T(8,128)(2,1)S(1)}, bf16[352,128]{1,0:T(8,128)(2,1)S(1)}, u32[]{:S(2)}, u32[]{:S(2)}) collective-permute-start(bf16[352,128]{1,0:T(8,128)(2,1)S(1)} %shard_map.135), channel_id=1, source_target_pairs={{0,2},{1,3},{2,0},{3,1},{4,6},{5,7},{6,4},{7,5},{8,10},{9,11},{10,... | collective-permute-start | bytes 270344 | tf_op jit(solution)/shard_map/ppermute | solution.py:55
  66.5 3.4 %collective-permute-done.18 = bf16[352,128]{1,0:T(8,128)(2,1)S(1)} collective-permute-done((bf16[352,128]{1,0:T(8,128)(2,1)S(1)}, bf16[352,128]{1,0:T(8,128)(2,1)S(1)}, u32[]{:S(2)}, u32[]{:S(2)}) %collective-permute-start.18) | collective-permute-done | bytes 90144 | tf_op jit(solution)/shard_map/ppermute | solution.py:55
  70.2 1.9 %collective-permute-start.20 = (bf16[3,352,128]{2,1,0:T(8,128)(2,1)S(1)}, bf16[3,352,128]{2,1,0:T(8,128)(2,1)S(1)}, u32[]{:S(2)}, u32[]{:S(2)}) collective-permute-start(bf16[3,352,128]{2,1,0:T(8,128)(2,1)S(1)} %pad_maximum_fusion.1), channel_id=1, source_target_pairs={{0,2},{1,3},{2,0},{3,1},{4,6},{5,7},{6,4},{7,5},{8,10},{9,11},{10,... | collective-permute-start | bytes 811016 | tf_op jit(solution)/shard_map/ppermute | solution.py:55
  72.1 1.1 %fusion.3 = bf16[2,16,16,256]{3,2,1,0:T(8,128)(2,1)} fusion(f32[2,16,16,256]{3,2,1,0:T(8,128)S(1)} %convolution_add_fusion.9, bf16[2,16,16,512]{3,2,1,0:T(8,128)(2,1)S(1)} %copy-done.2, bf16[2,16,16,256]{3,2,1,0:T(8,128)(2,1)S(1)} %bitcast.123, bf16[2,16,16,256]{3,2,1,0:T(8,128)(2,1)S(1)} %copy-done.7, bf16[3,3,256,512]{3,2,1,0:T(8,128)(2,1)S(1)} %copy-done.6), kind=kOutput, calls=%fused_computation.28 | convolution fusion | flops 135135232 | bytes 2097152 | tf_op jit(solution)/shard_map/nhwo,co->nhwc/dot_general | solution.py:577
  73.2 4.3 %collective-permute-done.21 = bf16[3,352,128]{2,1,0:T(8,128)(2,1)S(1)} collective-permute-done((bf16[3,352,128]{2,1,0:T(8,128)(2,1)S(1)}, bf16[3,352,128]{2,1,0:T(8,128)(2,1)S(1)}, u32[]{:S(2)}, u32[]{:S(2)}) %collective-permute-start.21) | collective-permute-done | bytes 270368 | tf_op jit(solution)/shard_map/ppermute | solution.py:55
  77.5 0.4 collective-permute-done.20
  78.1 1.4 %collective-permute-start.23 = (bf16[528,128]{1,0:T(8,128)(2,1)S(1)}, bf16[528,128]{1,0:T(8,128)(2,1)S(1)}, u32[]{:S(2)}, u32[]{:S(2)}) collective-permute-start(bf16[528,128]{1,0:T(8,128)(2,1)S(1)} %slice.125), channel_id=1, source_target_pairs={{0,4},{1,5},{2,6},{3,7},{4,0},{5,1},{6,2},{7,3},{8,12},{9,13},{10,... | collective-permute-start | bytes 405512 | tf_op jit(solution)/shard_map/ppermute | solution.py:55
  79.5 0.9 collective-permute-start.22
  80.4 3.8 %collective-permute-done.23 = bf16[528,128]{1,0:T(8,128)(2,1)S(1)} collective-permute-done((bf16[528,128]{1,0:T(8,128)(2,1)S(1)}, bf16[528,128]{1,0:T(8,128)(2,1)S(1)}, u32[]{:S(2)}, u32[]{:S(2)}) %collective-permute-start.23) | collective-permute-done | bytes 135200 | tf_op jit(solution)/shard_map/ppermute | solution.py:55
  84.2 1.1 %collective-permute-done.22 = bf16[528,128]{1,0:T(8,128)(2,1)S(1)} collective-permute-done((bf16[528,128]{1,0:T(8,128)(2,1)S(1)}, bf16[528,128]{1,0:T(8,128)(2,1)S(1)}, u32[]{:S(2)}, u32[]{:S(2)}) %collective-permute-start.22) | collective-permute-done | bytes 135200 | tf_op jit(solution)/shard_map/ppermute | solution.py:55
  85.4 1.5 %collective-permute-done.26.refs_5_ = bf16[3,352,128]{2,1,0:T(8,128)(2,1)S(1)} collective-permute-done((bf16[3,352,128]{2,1,0:T(8,128)(2,1)S(1)}, bf16[3,352,128]{2,1,0:T(8,128)(2,1)S(1)}, u32[]{:S(2)}, u32[]{:S(2)}) %collective-permute-start.26) | collective-permute-done | bytes 270368 | tf_op jit(solution)/shard_map/ppermute | solution.py:55
  86.9 3.7 %shard_map.136 = (f32[9,256,512]{2,1,0:T(8,128)}, f32[768,256]{1,0:T(8,128)}, f32[1,512]{1,0:T(1,128)}) custom-call(s32[2]{0:T(128)S(1)} %pad_add_fusion.place_ref, bf16[4,352,128]{2,1,0:T(8,128)(2,1)S(1)} %pad_maximum_fusion.refs_0_, bf16[9,352,128]{2,1,0:T(8,128)(2,1)S(1)} %constant_dynamic-update-slice_fusion.refs_1_, bf16[3,352,128]{2,1,0:T(8,128)(2,1)S(1)} %bitcast.112, ...), custom_call_target="tpu_custom_call" | custom-call | tf_op jit(solution)/shard_map/pallas_call | solution.py:499
  (52 shorter events, 1.3 us)
Async XLA Ops:
  0.6 16.3 %copy-start = (bf16[768,256]{1,0:T(8,128)(2,1)S(1)}, bf16[768,256]{1,0:T(8,128)(2,1)}, u32[]{:S(2)}) copy-start(bf16[768,256]{1,0:T(8,128)(2,1)} %param.10) | copy-start | bytes 1179652
  2.9 20.5 %all-to-all-start = ((f32[32,8,384]{2,1,0:T(8,128)}), f32[32,8,384]{2,1,0:T(8,128)S(1)}, u32[]{:S(2)}, u32[]{:S(2)}) async-start(f32[32,8,384]{2,1,0:T(8,128)} %get-tuple-element.42), calls=%async_computation | async-start | bytes 786432 | tf_op jit(solution)/shard_map/all_to_all | solution.py:89
  10.2 1.0 %copy-start.1 = (bf16[2,16,16,512]{3,2,1,0:T(8,128)(2,1)S(1)}, bf16[2,16,16,512]{3,2,1,0:T(8,128)(2,1)}, u32[]{:S(2)}) copy-start(bf16[2,16,16,512]{3,2,1,0:T(8,128)(2,1)} %param.17) | copy-start | bytes 1572868
  11.3 0.7 copy-start.4
  12.0 15.3 %copy-start.2 = (bf16[2,16,16,512]{3,2,1,0:T(8,128)(2,1)S(1)}, bf16[2,16,16,512]{3,2,1,0:T(8,128)(2,1)}, u32[]{:S(2)}) copy-start(bf16[2,16,16,512]{3,2,1,0:T(8,128)(2,1)} %param.17) | copy-start | bytes 1572868
  12.7 20.2 %collective-permute-start.2 = (bf16[528,256]{1,0:T(8,128)(2,1)}, bf16[528,256]{1,0:T(8,128)(2,1)S(1)}, u32[]{:S(2)}, u32[]{:S(2)}) collective-permute-start(bf16[528,256]{1,0:T(8,128)(2,1)} %get-tuple-element.48), channel_id=1, source_target_pairs={{0,6},{1,7},{2,4},{3,5},{4,2},{5,3},{6,0},{7,1},{8,14},{9,15},{10,... | collective-permute-start | bytes 811016 | tf_op jit(solution)/shard_map/ppermute | solution.py:55
  15.4 17.5 %collective-permute-start.1 = (bf16[528,256]{1,0:T(8,128)(2,1)}, bf16[528,256]{1,0:T(8,128)(2,1)S(1)}, u32[]{:S(2)}, u32[]{:S(2)}) collective-permute-start(bf16[528,256]{1,0:T(8,128)(2,1)} %get-tuple-element.48), channel_id=1, source_target_pairs={{0,4},{1,5},{2,6},{3,7},{4,0},{5,1},{6,2},{7,3},{8,12},{9,13},{10,... | collective-permute-start | bytes 811016 | tf_op jit(solution)/shard_map/ppermute | solution.py:55
  16.0 16.9 %collective-permute-start = (bf16[528,256]{1,0:T(8,128)(2,1)S(1)}, bf16[528,256]{1,0:T(8,128)(2,1)S(1)}, u32[]{:S(2)}, u32[]{:S(2)}) collective-permute-start(bf16[528,256]{1,0:T(8,128)(2,1)S(1)} %get-tuple-element.49.refs_0_), channel_id=1, source_target_pairs={{0,2},{1,3},{2,0},{3,1},{4,6},{5,7},{6,4},{7,5},{8,10},{9,11},{10,... | collective-permute-start | bytes 811016 | tf_op jit(solution)/shard_map/ppermute | solution.py:55
  24.6 15.8 %all-to-all-start.1 = ((bf16[32,16,384]{2,1,0:T(8,128)(2,1)}), bf16[32,16,384]{2,1,0:T(8,128)(2,1)S(1)}, u32[]{:S(2)}, u32[]{:S(2)}) async-start(bf16[32,16,384]{2,1,0:T(8,128)(2,1)} %shard_map.129), calls=%async_computation.1 | async-start | bytes 786432 | tf_op jit(solution)/shard_map/all_to_all | solution.py:89
  27.2 2.9 %copy-start.5 = (bf16[3,3,256,512]{3,2,1,0:T(8,128)(2,1)S(1)}, bf16[3,3,256,512]{3,2,1,0:T(8,128)(2,1)}, u32[]{:S(2)}) copy-start(bf16[3,3,256,512]{3,2,1,0:T(8,128)(2,1)} %param.15) | copy-start | bytes 7077892
  28.7 2.1 %copy-start.3 = (bf16[784,768]{1,0:T(8,128)(2,1)S(1)}, bf16[784,768]{1,0:T(8,128)(2,1)}, u32[]{:S(2)}) copy-start(bf16[784,768]{1,0:T(8,128)(2,1)} %book_ref.1) | copy-start | bytes 3612676
  32.9 7.5 %collective-permute-start.3 = (bf16[528,256]{1,0:T(8,128)(2,1)S(1)}, bf16[528,256]{1,0:T(8,128)(2,1)}, u32[]{:S(2)}, u32[]{:S(2)}) collective-permute-start(bf16[528,256]{1,0:T(8,128)(2,1)S(1)} %get-tuple-element.49.refs_0_), channel_id=1, source_target_pairs={{0,1},{1,0},{2,3},{3,2},{4,5},{5,4},{6,7},{7,6},{8,9},{9,8},{10,11... | collective-permute-start | bytes 811016 | tf_op jit(solution)/shard_map/ppermute | solution.py:55
  33.2 8.4 %collective-permute-start.4 = (bf16[528,256]{1,0:T(8,128)(2,1)S(1)}, bf16[528,256]{1,0:T(8,128)(2,1)}, u32[]{:S(2)}, u32[]{:S(2)}) collective-permute-start(bf16[528,256]{1,0:T(8,128)(2,1)S(1)} %collective-permute-done.refs_1_), channel_id=1, source_target_pairs={{0,1},{1,0},{2,3},{3,2},{4,5},{5,4},{6,7},{7,6},{8,9},{9,8},{10,11... | collective-permute-start | bytes 811016 | tf_op jit(solution)/shard_map/ppermute | solution.py:55
  33.5 8.9 %collective-permute-start.5 = (bf16[528,256]{1,0:T(8,128)(2,1)S(1)}, bf16[528,256]{1,0:T(8,128)(2,1)}, u32[]{:S(2)}, u32[]{:S(2)}) collective-permute-start(bf16[528,256]{1,0:T(8,128)(2,1)S(1)} %collective-permute-done.1.refs_2_), channel_id=1, source_target_pairs={{0,1},{1,0},{2,3},{3,2},{4,5},{5,4},{6,7},{7,6},{8,9},{9,8},{10,11... | collective-permute-start | bytes 811016 | tf_op jit(solution)/shard_map/ppermute | solution.py:55
  33.7 8.7 %collective-permute-start.6 = (bf16[528,256]{1,0:T(8,128)(2,1)S(1)}, bf16[528,256]{1,0:T(8,128)(2,1)}, u32[]{:S(2)}, u32[]{:S(2)}) collective-permute-start(bf16[528,256]{1,0:T(8,128)(2,1)S(1)} %collective-permute-done.2.refs_3_), channel_id=1, source_target_pairs={{0,1},{1,0},{2,3},{3,2},{4,5},{5,4},{6,7},{7,6},{8,9},{9,8},{10,11... | collective-permute-start | bytes 811016 | tf_op jit(solution)/shard_map/ppermute | solution.py:55
  34.0 2.2 %collective-permute-start.7 = (f32[768,128]{1,0:T(8,128)S(1)}, f32[768,128]{1,0:T(8,128)S(1)}, u32[]{:S(2)}, u32[]{:S(2)}) collective-permute-start(f32[768,128]{1,0:T(8,128)S(1)} %get-tuple-element.54), channel_id=1, source_target_pairs={{0,1},{1,0},{2,3},{3,2},{4,5},{5,4},{6,7},{7,6},{8,9},{9,8},{10,11... | collective-permute-start | bytes 1179656 | tf_op jit(solution)/shard_map/ppermute | solution.py:55
  36.9 10.6 %collective-permute-start.8 = (bf16[4,48,128]{2,1,0:T(8,128)(2,1)S(1)}, bf16[4,48,128]{2,1,0:T(8,128)(2,1)S(1)}, u32[]{:S(2)}, u32[]{:S(2)}) collective-permute-start(bf16[4,48,128]{2,1,0:T(8,128)(2,1)S(1)} %get-tuple-element.56), channel_id=1, source_target_pairs={{0,2},{1,3},{2,0},{3,1},{4,6},{5,7},{6,4},{7,5},{8,10},{9,11},{10,... | collective-permute-start | bytes 147464 | tf_op jit(solution)/shard_map/ppermute | solution.py:55
  40.4 7.1 %collective-permute-start.9 = (bf16[4,48,128]{2,1,0:T(8,128)(2,1)S(1)}, bf16[4,48,128]{2,1,0:T(8,128)(2,1)S(1)}, u32[]{:S(2)}, u32[]{:S(2)}) collective-permute-start(bf16[4,48,128]{2,1,0:T(8,128)(2,1)S(1)} %get-tuple-element.57), channel_id=1, source_target_pairs={{0,4},{1,5},{2,6},{3,7},{4,0},{5,1},{6,2},{7,3},{8,12},{9,13},{10,... | collective-permute-start | bytes 147464 | tf_op jit(solution)/shard_map/ppermute | solution.py:55
  41.6 10.6 %copy-start.8 = (s32[1,512]{1,0:T(1,128)S(1)}, s32[1,512]{1,0:T(1,128)}, u32[]{:S(2)}) copy-start(s32[1,512]{1,0:T(1,128)} %get-tuple-element.67) | copy-start | bytes 6148
  41.6 10.9 %copy-start.6 = (bf16[3,3,256,512]{3,2,1,0:T(8,128)(2,1)S(1)}, bf16[3,3,256,512]{3,2,1,0:T(8,128)(2,1)}, u32[]{:S(2)}) copy-start(bf16[3,3,256,512]{3,2,1,0:T(8,128)(2,1)} %param.15) | copy-start | bytes 7077892
  41.6 5.9 %collective-permute-start.10 = (bf16[4,48,128]{2,1,0:T(8,128)(2,1)S(1)}, bf16[4,48,128]{2,1,0:T(8,128)(2,1)S(1)}, u32[]{:S(2)}, u32[]{:S(2)}) collective-permute-start(bf16[4,48,128]{2,1,0:T(8,128)(2,1)S(1)} %get-tuple-element.58), channel_id=1, source_target_pairs={{0,6},{1,7},{2,4},{3,5},{4,2},{5,3},{6,0},{7,1},{8,14},{9,15},{10,... | collective-permute-start | bytes 147464 | tf_op jit(solution)/shard_map/ppermute | solution.py:55
  48.1 7.4 %collective-permute-start.11 = (bf16[352,128]{1,0:T(8,128)(2,1)S(1)}, bf16[352,128]{1,0:T(8,128)(2,1)S(1)}, u32[]{:S(2)}, u32[]{:S(2)}) collective-permute-start(bf16[352,128]{1,0:T(8,128)(2,1)S(1)} %get-tuple-element.64), channel_id=1, source_target_pairs={{0,8},{1,9},{2,10},{3,11},{4,12},{5,13},{6,14},{7,15},{8,16},{9,17... | collective-permute-start | bytes 270344 | tf_op jit(solution)/shard_map/ppermute | solution.py:55
  48.9 9.5 %collective-permute-start.12 = (bf16[352,128]{1,0:T(8,128)(2,1)S(1)}, bf16[352,128]{1,0:T(8,128)(2,1)S(1)}, u32[]{:S(2)}, u32[]{:S(2)}) collective-permute-start(bf16[352,128]{1,0:T(8,128)(2,1)S(1)} %get-tuple-element.65), channel_id=1, source_target_pairs={{0,16},{1,17},{2,18},{3,19},{4,20},{5,21},{6,22},{7,23},{8,24},{9,... | collective-permute-start | bytes 270344 | tf_op jit(solution)/shard_map/ppermute | solution.py:55
  50.7 7.8 %collective-permute-start.13 = (bf16[352,128]{1,0:T(8,128)(2,1)S(1)}, bf16[352,128]{1,0:T(8,128)(2,1)S(1)}, u32[]{:S(2)}, u32[]{:S(2)}) collective-permute-start(bf16[352,128]{1,0:T(8,128)(2,1)S(1)} %get-tuple-element.66), channel_id=1, source_target_pairs={{0,24},{1,25},{2,26},{3,27},{4,28},{5,29},{6,30},{7,31},{8,0},{9,1... | collective-permute-start | bytes 270344 | tf_op jit(solution)/shard_map/ppermute | solution.py:55
  54.6 17.5 %copy-start.7 = (bf16[2,16,16,256]{3,2,1,0:T(8,128)(2,1)S(1)}, bf16[2,16,16,256]{3,2,1,0:T(8,128)(2,1)}, u32[]{:S(2)}) copy-start(bf16[2,16,16,256]{3,2,1,0:T(8,128)(2,1)} %param.11) | copy-start | bytes 786436
  58.5 6.5 %collective-permute-start.19 = (bf16[352,128]{1,0:T(8,128)(2,1)S(1)}, bf16[352,128]{1,0:T(8,128)(2,1)S(1)}, u32[]{:S(2)}, u32[]{:S(2)}) collective-permute-start(bf16[352,128]{1,0:T(8,128)(2,1)S(1)} %shard_map.135), channel_id=1, source_target_pairs={{0,24},{1,25},{2,26},{3,27},{4,28},{5,29},{6,30},{7,31},{8,0},{9,1... | collective-permute-start | bytes 270344 | tf_op jit(solution)/shard_map/ppermute | solution.py:55
  60.6 9.3 %collective-permute-start.18 = (bf16[352,128]{1,0:T(8,128)(2,1)S(1)}, bf16[352,128]{1,0:T(8,128)(2,1)S(1)}, u32[]{:S(2)}, u32[]{:S(2)}) collective-permute-start(bf16[352,128]{1,0:T(8,128)(2,1)S(1)} %shard_map.135), channel_id=1, source_target_pairs={{0,16},{1,17},{2,18},{3,19},{4,20},{5,21},{6,22},{7,23},{8,24},{9,... | collective-permute-start | bytes 270344 | tf_op jit(solution)/shard_map/ppermute | solution.py:55
  61.9 8.0 %collective-permute-start.17 = (bf16[352,128]{1,0:T(8,128)(2,1)S(1)}, bf16[352,128]{1,0:T(8,128)(2,1)S(1)}, u32[]{:S(2)}, u32[]{:S(2)}) collective-permute-start(bf16[352,128]{1,0:T(8,128)(2,1)S(1)} %shard_map.135), channel_id=1, source_target_pairs={{0,8},{1,9},{2,10},{3,11},{4,12},{5,13},{6,14},{7,15},{8,16},{9,17... | collective-permute-start | bytes 270344 | tf_op jit(solution)/shard_map/ppermute | solution.py:55
  63.0 10.1 %collective-permute-start.16 = (bf16[352,128]{1,0:T(8,128)(2,1)S(1)}, bf16[352,128]{1,0:T(8,128)(2,1)S(1)}, u32[]{:S(2)}, u32[]{:S(2)}) collective-permute-start(bf16[352,128]{1,0:T(8,128)(2,1)S(1)} %shard_map.135), channel_id=1, source_target_pairs={{0,6},{1,7},{2,4},{3,5},{4,2},{5,3},{6,0},{7,1},{8,14},{9,15},{10,... | collective-permute-start | bytes 270344 | tf_op jit(solution)/shard_map/ppermute | solution.py:55
  64.4 8.7 %collective-permute-start.15 = (bf16[352,128]{1,0:T(8,128)(2,1)S(1)}, bf16[352,128]{1,0:T(8,128)(2,1)S(1)}, u32[]{:S(2)}, u32[]{:S(2)}) collective-permute-start(bf16[352,128]{1,0:T(8,128)(2,1)S(1)} %shard_map.135), channel_id=1, source_target_pairs={{0,4},{1,5},{2,6},{3,7},{4,0},{5,1},{6,2},{7,3},{8,12},{9,13},{10,... | collective-permute-start | bytes 270344 | tf_op jit(solution)/shard_map/ppermute | solution.py:55
  65.0 8.1 %collective-permute-start.14 = (bf16[352,128]{1,0:T(8,128)(2,1)S(1)}, bf16[352,128]{1,0:T(8,128)(2,1)S(1)}, u32[]{:S(2)}, u32[]{:S(2)}) collective-permute-start(bf16[352,128]{1,0:T(8,128)(2,1)S(1)} %shard_map.135), channel_id=1, source_target_pairs={{0,2},{1,3},{2,0},{3,1},{4,6},{5,7},{6,4},{7,5},{8,10},{9,11},{10,... | collective-permute-start | bytes 270344 | tf_op jit(solution)/shard_map/ppermute | solution.py:55
  69.9 7.6 %collective-permute-start.21 = (bf16[3,352,128]{2,1,0:T(8,128)(2,1)S(1)}, bf16[3,352,128]{2,1,0:T(8,128)(2,1)S(1)}, u32[]{:S(2)}, u32[]{:S(2)}) collective-permute-start(bf16[3,352,128]{2,1,0:T(8,128)(2,1)S(1)} %pad_maximum_fusion.1), channel_id=1, source_target_pairs={{0,4},{1,5},{2,6},{3,7},{4,0},{5,1},{6,2},{7,3},{8,12},{9,13},{10,... | collective-permute-start | bytes 811016 | tf_op jit(solution)/shard_map/ppermute | solution.py:55
  70.2 7.7 %collective-permute-start.20 = (bf16[3,352,128]{2,1,0:T(8,128)(2,1)S(1)}, bf16[3,352,128]{2,1,0:T(8,128)(2,1)S(1)}, u32[]{:S(2)}, u32[]{:S(2)}) collective-permute-start(bf16[3,352,128]{2,1,0:T(8,128)(2,1)S(1)} %pad_maximum_fusion.1), channel_id=1, source_target_pairs={{0,2},{1,3},{2,0},{3,1},{4,6},{5,7},{6,4},{7,5},{8,10},{9,11},{10,... | collective-permute-start | bytes 811016 | tf_op jit(solution)/shard_map/ppermute | solution.py:55
  78.0 8.9 %collective-permute-start.25 = (bf16[9,352,128]{2,1,0:T(8,128)(2,1)S(1)}, bf16[9,352,128]{2,1,0:T(8,128)(2,1)S(1)}, u32[]{:S(2)}, u32[]{:S(2)}) collective-permute-start(bf16[9,352,128]{2,1,0:T(8,128)(2,1)S(1)} %constant_dynamic-update-slice_fusion.refs_1_), channel_id=1, source_target_pairs={{0,1},{1,0},{2,3},{3,2},{4,5},{5,4},{6,7},{7,6},{8,9},{9,8},{10,11... | collective-permute-start | bytes 2433032 | tf_op jit(solution)/shard_map/ppermute | solution.py:55
  78.1 6.0 %collective-permute-start.23 = (bf16[528,128]{1,0:T(8,128)(2,1)S(1)}, bf16[528,128]{1,0:T(8,128)(2,1)S(1)}, u32[]{:S(2)}, u32[]{:S(2)}) collective-permute-start(bf16[528,128]{1,0:T(8,128)(2,1)S(1)} %slice.125), channel_id=1, source_target_pairs={{0,4},{1,5},{2,6},{3,7},{4,0},{5,1},{6,2},{7,3},{8,12},{9,13},{10,... | collective-permute-start | bytes 405512 | tf_op jit(solution)/shard_map/ppermute | solution.py:55
  79.5 5.7 %collective-permute-start.22 = (bf16[528,128]{1,0:T(8,128)(2,1)S(1)}, bf16[528,128]{1,0:T(8,128)(2,1)S(1)}, u32[]{:S(2)}, u32[]{:S(2)}) collective-permute-start(bf16[528,128]{1,0:T(8,128)(2,1)S(1)} %slice.124), channel_id=1, source_target_pairs={{0,2},{1,3},{2,0},{3,1},{4,6},{5,7},{6,4},{7,5},{8,10},{9,11},{10,... | collective-permute-start | bytes 405512 | tf_op jit(solution)/shard_map/ppermute | solution.py:55
  80.4 4.9 %collective-permute-start.24 = (bf16[4,352,128]{2,1,0:T(8,128)(2,1)S(1)}, bf16[4,352,128]{2,1,0:T(8,128)(2,1)S(1)}, u32[]{:S(2)}, u32[]{:S(2)}) collective-permute-start(bf16[4,352,128]{2,1,0:T(8,128)(2,1)S(1)} %pad_maximum_fusion.refs_0_), channel_id=1, source_target_pairs={{0,1},{1,0},{2,3},{3,2},{4,5},{5,4},{6,7},{7,6},{8,9},{9,8},{10,11... | collective-permute-start | bytes 1081352 | tf_op jit(solution)/shard_map/ppermute | solution.py:55
  85.3 1.6 %collective-permute-start.26 = (bf16[3,352,128]{2,1,0:T(8,128)(2,1)S(1)}, bf16[3,352,128]{2,1,0:T(8,128)(2,1)S(1)}, u32[]{:S(2)}, u32[]{:S(2)}) collective-permute-start(bf16[3,352,128]{2,1,0:T(8,128)(2,1)S(1)} %bitcast.111), channel_id=1, source_target_pairs={{0,1},{1,0},{2,3},{3,2},{4,5},{5,4},{6,7},{7,6},{8,9},{9,8},{10,11... | collective-permute-start | bytes 811016 | tf_op jit(solution)/shard_map/ppermute | solution.py:55
